TPU v7x, 32 devices: a whole 2x2x4 slice. The times are simulated.
32 devices in a mesh: tm: 8 (over y, x, core), space: 4 (over z).
Axes of the slice: x: 2, y: 2, z: 4, core: 2. Of those that a mesh axis runs over, the one named last changes fastest.
Arguments:
- snapshots: bfloat16 [4096, 8192], P('tm', 'space'), may hold values from -6 to 6
- outlier_cols: int32 [32, 16], P('tm', 'space'), may hold values from 0 to 15
- outlier_values: bfloat16 [32, 16, 128, 128], P('tm', 'space'), may hold values from -12 to 12
- threshold: float32 [], replicated, may hold values from 0.3 to 0.9
Outputs:
- gram_band: float32 [4096, 5, 512], P('tm', None, 'space')
Inputs may be any that keep to these rules, and one draw needn't show every extreme that they name: `outlier_cols`: entry k of a row lies in the points of space block k // 4; repeated entries add.
All inputs are finite; a program needn't handle non-finite values.
Results may differ from a plain program's by a relative error of at most 0.0021.
Values may be sent and summed in bfloat16 or wider, within the bound.
No kernel may reach another device: no remote copies, remote signals or barrier semaphores. Data moves between devices by JAX's collectives and lax.ppermute only.
A program may use at most 128 MiB of HBM per device.

v0:
```python
import jax
import jax.numpy as jnp
from jax import lax
from jax.sharding import PartitionSpec as P

ST = 128


def passed_along(x, axis, by):
    size = lax.axis_size(axis)
    return lax.ppermute(x, axis, [(i, (i + by) % size) for i in range(size)])


def tile_product(own, other):
    return lax.dot_general(own, other, (((1,), (1,)), ((), ())), preferred_element_type=jnp.float32)


def local(snapshots, outlier_cols, outlier_values, threshold):
    block_rows, points = snapshots.shape
    tiles_dev = points // ST
    n_loop = lax.axis_size("tm")
    half = n_loop // 2
    onehot = (
        outlier_cols[:, :, None] == jnp.arange(tiles_dev, dtype=jnp.int32)[None, None, :]
    ).astype(jnp.bfloat16)
    dense = jnp.einsum("rkos,rkn->rons", outlier_values, onehot, preferred_element_type=jnp.float32)
    dense = dense.reshape(block_rows, points)
    diff = snapshots.astype(jnp.float32) - dense
    cleaned = (jnp.sign(diff) * jnp.maximum(jnp.abs(diff) - threshold, 0.0)).astype(jnp.bfloat16)
    scale = 1.0 / jnp.sqrt(jnp.float32(points * lax.axis_size("space")))
    kept = []

    def finish(term):
        kept.append(term)

    finish(tile_product(cleaned, cleaned))
    moving = cleaned
    for step in range(half):
        moving = passed_along(moving, "tm", -1)
        finish(tile_product(cleaned, moving))
    band = lax.psum_scatter(jnp.stack(kept, axis=1), "space", scatter_dimension=2, tiled=True)
    return band * scale


def solution(mesh):
    placed = (P("tm", "space"), P("tm", "space"), P("tm", "space", None, None), P())
    return jax.shard_map(
        local, mesh=mesh, in_specs=placed, out_specs=P("tm", None, "space"), check_vma=False
    )
```

profile of v0, /device:TPU:3, one launch (start us, length us, event | category | flops | bytes accessed | tf_op | source)
XLA Modules:
  0.0 223.8 jit_solution(10211343603152342237)
XLA Ops:
  6.5 0.0 copy-start
  6.5 0.0 reduce-scatter.2.cloned.1.call-start
  7.2 0.3 copy-done
  7.6 0.0 copy-start.1
  7.6 1.9 fusion.5
  9.5 0.0 copy-done.1
  9.5 2.5 %multiply_convert_fusion = bf16[512,2048]{1,0:T(8,128)(2,1)S(1)} fusion(f32[64,8,16,128]{3,2,1,0:T(8,128)S(1)} %bitcast.42, bf16[512,2048]{1,0:T(8,128)(2,1)S(1)} %copy-done.1, f32[]{:T(128)S(6)} %copy.17), kind=kLoop, calls=%fused_computation.1 | loop fusion | flops 8388608 | bytes 8388612 | tf_op jit(solution)/shard_map/convert_element_type | solution.py:29
  12.0 0.7 collective-permute-start
  12.7 25.7 %collective-permute-done = bf16[512,2048]{1,0:T(8,128)(2,1)S(1)} collective-permute-done((bf16[512,2048]{1,0:T(8,128)(2,1)S(1)}, bf16[512,2048]{1,0:T(8,128)(2,1)S(1)}, u32[]{:S(2)}, u32[]{:S(2)}) %collective-permute-start) | collective-permute-done | bytes 2097184 | tf_op jit(solution)/shard_map/ppermute | solution.py:11
  38.4 0.0 collective-permute-start.1
  38.4 26.4 %collective-permute-done.1 = bf16[512,2048]{1,0:T(8,128)(2,1)S(1)} collective-permute-done((bf16[512,2048]{1,0:T(8,128)(2,1)S(1)}, bf16[512,2048]{1,0:T(8,128)(2,1)S(1)}, u32[]{:S(2)}, u32[]{:S(2)}) %collective-permute-start.1) | collective-permute-done | bytes 2097184 | tf_op jit(solution)/shard_map/ppermute | solution.py:11
  64.7 0.0 collective-permute-start.2
  64.7 26.4 %collective-permute-done.2 = bf16[512,2048]{1,0:T(8,128)(2,1)S(1)} collective-permute-done((bf16[512,2048]{1,0:T(8,128)(2,1)S(1)}, bf16[512,2048]{1,0:T(8,128)(2,1)S(1)}, u32[]{:S(2)}, u32[]{:S(2)}) %collective-permute-start.2) | collective-permute-done | bytes 2097184 | tf_op jit(solution)/shard_map/ppermute | solution.py:11
  91.1 0.0 collective-permute-start.3
  91.1 2.3 %fusion.4 = f32[512,5,512]{2,0,1:T(8,128)} fusion(bf16[512,2048]{1,0:T(8,128)(2,1)S(1)} %multiply_convert_fusion), kind=kOutput, calls=%fused_computation.11 | convolution fusion | flops 1073741824 | bytes 5242880 | tf_op jit(solution)/shard_map/dot_general | solution.py:15
  93.4 2.4 %fusion.3 = f32[512,5,512]{2,0,1:T(8,128)} fusion(f32[512,5,512]{2,0,1:T(8,128)} %fusion.4, bf16[512,2048]{1,0:T(8,128)(2,1)S(1)} %multiply_convert_fusion, bf16[512,2048]{1,0:T(8,128)(2,1)S(1)} %collective-permute-done), kind=kOutput, calls=%fused_computation.9 | convolution fusion | flops 1073741824 | bytes 5242880 | tf_op jit(solution)/shard_map/dot_general | solution.py:15
  95.8 2.4 %fusion.2 = f32[512,5,512]{2,0,1:T(8,128)} fusion(f32[512,5,512]{2,0,1:T(8,128)} %fusion.3, bf16[512,2048]{1,0:T(8,128)(2,1)S(1)} %multiply_convert_fusion, bf16[512,2048]{1,0:T(8,128)(2,1)S(1)} %collective-permute-done.1), kind=kOutput, calls=%fused_computation.7 | convolution fusion | flops 1073741824 | bytes 5242880 | tf_op jit(solution)/shard_map/dot_general | solution.py:15
  98.2 2.4 %fusion.1 = f32[512,5,512]{2,0,1:T(8,128)} fusion(f32[512,5,512]{2,0,1:T(8,128)} %fusion.2, bf16[512,2048]{1,0:T(8,128)(2,1)S(1)} %multiply_convert_fusion, bf16[512,2048]{1,0:T(8,128)(2,1)S(1)} %collective-permute-done.2), kind=kOutput, calls=%fused_computation.5 | convolution fusion | flops 1073741824 | bytes 5242880 | tf_op jit(solution)/shard_map/dot_general | solution.py:15
  100.5 16.9 %collective-permute-done.3 = bf16[512,2048]{1,0:T(8,128)(2,1)S(1)} collective-permute-done((bf16[512,2048]{1,0:T(8,128)(2,1)S(1)}, bf16[512,2048]{1,0:T(8,128)(2,1)S(1)}, u32[]{:S(2)}, u32[]{:S(2)}) %collective-permute-start.3) | collective-permute-done | bytes 2097184 | tf_op jit(solution)/shard_map/ppermute | solution.py:11
  117.5 2.3 %fusion = f32[512,5,512]{2,0,1:T(8,128)} fusion(f32[512,5,512]{2,0,1:T(8,128)} %fusion.1, bf16[512,2048]{1,0:T(8,128)(2,1)S(1)} %multiply_convert_fusion, bf16[512,2048]{1,0:T(8,128)(2,1)S(1)} %collective-permute-done.3), kind=kOutput, calls=%fused_computation.3 | convolution fusion | flops 1073741824 | bytes 5242880 | tf_op jit(solution)/shard_map/dot_general | solution.py:15
  119.8 0.0 reduce-scatter.2.cloned.1.call-update
  119.8 94.7 %reduce-scatter.2.cloned.1.call-done = f32[512,5,128]{2,0,1:T(8,128)} async-done(((f32[512,5,512]{2,0,1:T(8,128)}), f32[512,5,128]{2,0,1:T(8,128)}) %reduce-scatter.2.cloned.1.call-update) | async-done | bytes 1310736 | tf_op jit(solution)/shard_map/reduce_scatter | solution.py:41
  214.5 2.5 %broadcast_multiply_fusion = f32[512,5,128]{2,0,1:T(8,128)} fusion(f32[512,5,128]{2,0,1:T(8,128)} %reduce-scatter.2.cloned.1.call-done), kind=kLoop, calls=%fused_computation.12 | loop fusion | flops 327680 | bytes 2621440 | tf_op jit(solution)/shard_map/mul | solution.py:42
Async XLA Ops:
  6.5 1.1 copy-start
  6.5 208.0 %reduce-scatter.2.cloned.1.call-start = ((), (), s32[]{:S(2)}) async-start(), calls=%async_computation.1 | async-start | bytes 6553600 | tf_op jit(solution)/shard_map/reduce_scatter | solution.py:41
  7.6 1.9 copy-start.1
  12.0 26.4 %collective-permute-start = (bf16[512,2048]{1,0:T(8,128)(2,1)S(1)}, bf16[512,2048]{1,0:T(8,128)(2,1)S(1)}, u32[]{:S(2)}, u32[]{:S(2)}) collective-permute-start(bf16[512,2048]{1,0:T(8,128)(2,1)S(1)} %multiply_convert_fusion), channel_id=1, source_target_pairs={{0,28},{4,0},{8,4},{12,8},{16,12},{20,16},{24,20},{28,24},{1,29},{... | collective-permute-start | bytes 6291464 | tf_op jit(solution)/shard_map/ppermute | solution.py:11
  38.4 26.4 %collective-permute-start.1 = (bf16[512,2048]{1,0:T(8,128)(2,1)S(1)}, bf16[512,2048]{1,0:T(8,128)(2,1)S(1)}, u32[]{:S(2)}, u32[]{:S(2)}) collective-permute-start(bf16[512,2048]{1,0:T(8,128)(2,1)S(1)} %collective-permute-done), channel_id=1, source_target_pairs={{0,28},{4,0},{8,4},{12,8},{16,12},{20,16},{24,20},{28,24},{1,29},{... | collective-permute-start | bytes 6291464 | tf_op jit(solution)/shard_map/ppermute | solution.py:11
  64.7 26.4 %collective-permute-start.2 = (bf16[512,2048]{1,0:T(8,128)(2,1)S(1)}, bf16[512,2048]{1,0:T(8,128)(2,1)S(1)}, u32[]{:S(2)}, u32[]{:S(2)}) collective-permute-start(bf16[512,2048]{1,0:T(8,128)(2,1)S(1)} %collective-permute-done.1), channel_id=1, source_target_pairs={{0,28},{4,0},{8,4},{12,8},{16,12},{20,16},{24,20},{28,24},{1,29},{... | collective-permute-start | bytes 6291464 | tf_op jit(solution)/shard_map/ppermute | solution.py:11
  91.1 26.4 %collective-permute-start.3 = (bf16[512,2048]{1,0:T(8,128)(2,1)S(1)}, bf16[512,2048]{1,0:T(8,128)(2,1)S(1)}, u32[]{:S(2)}, u32[]{:S(2)}) collective-permute-start(bf16[512,2048]{1,0:T(8,128)(2,1)S(1)} %collective-permute-done.2), channel_id=1, source_target_pairs={{0,28},{4,0},{8,4},{12,8},{16,12},{20,16},{24,20},{28,24},{1,29},{... | collective-permute-start | bytes 6291464 | tf_op jit(solution)/shard_map/ppermute | solution.py:11
Sparse Core Ops, SparseCore 0:
  120.0 94.5 reduce-scatter.1
where the time goes:
time: 225 us; the launch traced here: 224 us
  waiting for transfers between devices  190 us (84%)
  between operations  14.1 us (6%)
  matrix products  13.7 us (6%)
  other arithmetic  4.95 us (2%)
    ppermute x4, waiting for transfers between devices, passed_along(): return lax.ppermute(x, axis, [(i, (i + by) % size) for i in range(size)])  95.3 us
    reduce_scatter x1, waiting for transfers between devices, local(): lax.psum_scatter(jnp.stack(kept, axis=1), 'space', scatter_dimension=2, t...  94.7 us
    dot_general x5, matrix products, tile_product(): lax.dot_general(own, other, (((1,), (1,)), ((), ())), preferred_element_t...  11.8 us
  transfers between devices with their start and end apart: 5, of which 5 were waited for; matrix products, arithmetic and copies ran while one was open for 4% of the time, Pallas kernels for 0%

commit v1 on v0

v1 whole, which is shorter than its diff:
```python
import math

import jax
import jax.numpy as jnp
from jax import lax
from jax.sharding import PartitionSpec as P

ST = 128
SNAP_MAX = 6.0
OUTLIER_MAX = 12.0
PARTS = 2


def swapped(x, axis, bit, only=None):
    pairs = [(i, i ^ bit) for i in range(lax.axis_size(axis)) if only is None or i & only]
    return lax.ppermute(x, axis, pairs)


def passed_along(x, axis, by):
    size = lax.axis_size(axis)
    return lax.ppermute(x, axis, [(i, (i + by) % size) for i in range(size)])


def tile_product(own, other):
    return lax.dot_general(own, other, (((1,), (1,)), ((), ())), preferred_element_type=jnp.float32)


def clean(snapshots, outlier_cols, outlier_values, threshold):
    block_rows, points = snapshots.shape
    tiles_dev = points // ST
    onehot = (
        outlier_cols[:, :, None] == jnp.arange(tiles_dev, dtype=jnp.int32)[None, None, :]
    ).astype(jnp.bfloat16)
    dense = jnp.einsum("rkos,rkn->rons", outlier_values, onehot, preferred_element_type=jnp.float32)
    dense = dense.reshape(block_rows, points)
    diff = snapshots.astype(jnp.float32) - dense
    return (jnp.sign(diff) * jnp.maximum(jnp.abs(diff) - threshold, 0.0)).astype(jnp.bfloat16)


def ring(cleaned):
    kept = [tile_product(cleaned, cleaned)]
    moving = cleaned
    for step in range(lax.axis_size("tm") // 2):
        moving = passed_along(moving, "tm", -1)
        kept.append(tile_product(cleaned, moving))
    return lax.psum_scatter(jnp.stack(kept, axis=1), "space", scatter_dimension=2, tiled=True)


def square(cleaned, most):
    rows, points = cleaned.shape
    quarter = rows // 4
    width = quarter // PARTS
    here = lax.axis_index("space")
    me = lax.axis_index("tm")
    core = me % 2
    far = (me // 2) % 2
    down = 2.0 ** -max(0, math.ceil(math.log2(2 * points * most * most / 6e4)))

    grouped = cleaned.reshape(4, quarter, points)
    own = [grouped[:, r * width : (r + 1) * width].reshape(4 * width, points) for r in range(PARTS)]

    def quarters(part, *which):
        part = part.reshape(4, width, points)
        return jnp.concatenate([lax.dynamic_index_in_dim(part, here ^ q, 0, keepdims=False) for q in which])

    def summed(blocks):
        away = [
            (tile_product(quarters(a, 1, 3), b) * down).astype(jnp.float16)
            for a, b in blocks
        ]
        away = swapped(jnp.stack(away).reshape(len(blocks), 2, width, 4 * width), "space", 1)
        stay = [tile_product(quarters(a, 0, 2), b) * down for a, b in blocks]
        stay = jnp.stack(stay).reshape(len(blocks), 2, width, 4 * width)
        stay = stay + away.astype(jnp.float32)
        away = swapped(stay[:, 1].astype(jnp.float16), "space", 2)
        return stay[:, 0] + away.astype(jnp.float32)

    by_x = [swapped(part, "tm", 2) for part in own]
    by_y = [swapped(part, "tm", 4) for part in own]
    sibling = [swapped(part, "tm", 1) for part in own]

    first = summed([(a, b) for a in own for b in own])
    first = {(r, s): first[r * PARTS + s] for r in range(PARTS) for s in range(PARTS)}
    tiles = {("own", r, s): v for (r, s), v in first.items()}

    left = []
    x_near, x_other = [], []
    for r in range(PARTS):
        x_near.append(by_x[r])
        x_other.append(swapped(by_x[r], "tm", 1))
        y_other = swapped(by_y[r], "tm", 1)
        side = jnp.where(core == 0, sibling[r], y_other)
        left.append(jnp.where(far == 1, by_y[r], own[r]))
        keys, blocks = [], []
        for s in range(PARTS):
            keys.append(("side", r, s))
            blocks.append((side, own[s]))
            keys.append(("y", r, s))
            blocks.append((by_y[r], own[s]))
        n_plain = len(keys)
        for s in range(r + 1):
            pairs = [(r, s)] if s == r else [(r, s), (s, r)]
            for i, j in pairs:
                keys.append(("near", i, j))
                blocks.append((x_near[i], left[j]))
                keys.append(("other", i, j))
                blocks.append((x_other[i], left[j]))
        done = summed(blocks)
        lent = swapped(done[n_plain:].astype(jnp.float16), "tm", 4, only=2).astype(jnp.float32)
        lent = jnp.where(far == 1, lent, done[n_plain:])
        for i, key in enumerate(keys):
            tiles[key] = done[i] if i < n_plain else lent[i - n_plain]

    def whole(name):
        tile = jnp.concatenate(
            [
                jnp.concatenate([tiles[name, r, s].reshape(width, 4, width) for s in range(PARTS)], axis=2)
                for r in range(PARTS)
            ],
            axis=0,
        )
        return tile.reshape(quarter, 4, quarter)

    one, three = whole("side"), whole("other")
    one, three = jnp.where(core == 0, one, three), jnp.where(core == 0, three, one)
    band = jnp.stack([whole("own"), one, whole("near"), three, whole("y")])
    band = band.reshape(5, quarter, rows).transpose(2, 0, 1)
    return band / down


def local(snapshots, outlier_cols, outlier_values, threshold):
    points = snapshots.shape[1]
    cleaned = clean(snapshots, outlier_cols, outlier_values, threshold)
    if lax.axis_size("tm") == 8 and lax.axis_size("space") == 4:
        band = square(cleaned, SNAP_MAX + outlier_cols.shape[1] * OUTLIER_MAX)
    else:
        band = ring(cleaned)
    return band * (1.0 / jnp.sqrt(jnp.float32(points * lax.axis_size("space"))))


def solution(mesh):
    placed = (P("tm", "space"), P("tm", "space"), P("tm", "space", None, None), P())
    return jax.shard_map(
        local, mesh=mesh, in_specs=placed, out_specs=P("tm", None, "space"), check_vma=False
    )
```

time: 225 us -> 150 us (0.67)
  waiting for transfers between devices: 190 us -> 76.4 us
  starting transfers between devices: 0.74 us -> 25 us
  between operations: 14.1 us -> 1.78 us
  local copies, waits for them, and re-layouts: 0.35 us -> 12.5 us
  matrix products: 13.7 us -> 21.6 us
  other arithmetic: 4.95 us -> 11.6 us
    reduce_scatter x1 -> x0, waiting for transfers between devices: 94.7 us -> none  [local(): lax.psum_scatter(jnp.stack(kept, axis=1), 'space', scatter_dimension=2, t...]
    ppermute x4 -> x18, starting transfers between devices: 0.74 us -> 25 us  [swapped(): return lax.ppermute(x, axis, pairs)]
    ppermute x4 -> x18, waiting for transfers between devices: 95.3 us -> 76.4 us  [swapped(): return lax.ppermute(x, axis, pairs)]
    dot_general x5 -> x40, matrix products: 11.8 us -> 19.7 us  [tile_product(): lax.dot_general(own, other, (((1,), (1,)), ((), ())), preferred_element_t...]
    squeeze x0 -> x7, local copies, waits for them, and re-layouts: none -> 5.77 us  [quarters(): lax.dynamic_index_in_dim(part, here ^ q, 0, keepdims=False)]
    another operation x0 -> x25, local copies, waits for them, and re-layouts: none -> 4.37 us  [the longest x20 4.3 us: whole(): tiles[name, r, s].reshape(width, 4, width)]
    select_n x0 -> x6, other arithmetic: none -> 2.97 us  [the longest x2 2.68 us: square(): left.append(jnp.where(far == 1, by_y[r], own[r]))]
    add x0 -> x6, other arithmetic: none -> 2.94 us  [the longest x3 1.8 us: summed(): stay = stay + away.astype(jnp.float32)]
  transfers between devices with their start and end apart: 5 -> 18, of which waited for: 5 -> 11; matrix products, arithmetic and copies ran while one was open for 4% -> 19% of each run, Pallas kernels for 0% -> 0%
where the time goes in v1:
time: 150 us; the launch traced here: 149 us
  waiting for transfers between devices  76.4 us (51%)
  starting transfers between devices  25 us (17%)
  matrix products  21.6 us (14%)
  local copies, waits for them, and re-layouts  12.5 us (8%)
  other arithmetic  11.6 us (8%)
  between operations  1.78 us (1%)
    ppermute x18, waiting for transfers between devices, swapped(): return lax.ppermute(x, axis, pairs)  76.4 us
    ppermute x18, starting transfers between devices, swapped(): return lax.ppermute(x, axis, pairs)  25 us
    dot_general x40, matrix products, tile_product(): lax.dot_general(own, other, (((1,), (1,)), ((), ())), preferred_element_t...  19.7 us
    squeeze x7, local copies, waits for them, and re-layouts, quarters(): lax.dynamic_index_in_dim(part, here ^ q, 0, keepdims=False)  5.77 us
    another operation x20, local copies, waits for them, and re-layouts, whole(): tiles[name, r, s].reshape(width, 4, width)  4.3 us
  transfers between devices with their start and end apart: 18, of which 11 were waited for; matrix products, arithmetic and copies ran while one was open for 19% of the time, Pallas kernels for 0%

profile of v1, /device:TPU:3, one launch (start us, length us, event | category | flops | bytes accessed | tf_op | source)
XLA Modules:
  0.0 148.9 jit_solution(13238954422967417765)
XLA Ops:
  1.1 1.9 %fusion.21 = f32[4,16,128,128]{3,1,2,0:T(8,128)S(1)} fusion(bf16[4,4,128,128]{3,2,1,0:T(8,128)(2,1)S(1)} %copy-done, s32[4,4]{1,0:T(4,128)} %param.5), kind=kOutput, calls=%fused_computation.93 | convolution fusion | flops 8388864 | bytes 4718656 | tf_op jit(solution)/shard_map/rkos,rkn->rons/dot_general | solution.py:34
  3.0 2.5 %multiply_convert_fusion = bf16[512,2048]{1,0:T(8,128)(2,1)S(1)} fusion(f32[64,8,16,128]{3,2,1,0:T(8,128)S(1)} %bitcast.238, bf16[512,2048]{1,0:T(8,128)(2,1)S(1)} %copy-done.1, f32[]{:T(128)S(6)} %copy.91), kind=kLoop, calls=%fused_computation.1 | loop fusion | flops 8388608 | bytes 8388612 | tf_op jit(solution)/shard_map/convert_element_type | solution.py:37
  5.9 0.5 fusion.3
  6.4 0.5 fusion.2
  6.9 0.5 fusion.1
  7.4 0.5 fusion
  8.0 1.6 %collective-permute-start = (f16[4,2,64,256]{3,2,1,0:T(8,128)(2,1)S(1)}, f16[4,2,64,256]{3,2,1,0:T(8,128)(2,1)S(1)}, u32[]{:S(2)}, u32[]{:S(2)}) collective-permute-start(f16[4,2,64,256]{3,2,1,0:T(8,128)(2,1)S(1)} %pad_maximum_fusion.60), channel_id=1, source_target_pairs={{0,1},{1,0},{2,3},{3,2},{4,5},{5,4},{6,7},{7,6},{8,9},{9,8},{10,11... | collective-permute-start | bytes 786440 | tf_op jit(solution)/shard_map/ppermute | solution.py:16
  11.6 3.8 %collective-permute-done = f16[4,2,64,256]{3,2,1,0:T(8,128)(2,1)S(1)} collective-permute-done((f16[4,2,64,256]{3,2,1,0:T(8,128)(2,1)S(1)}, f16[4,2,64,256]{3,2,1,0:T(8,128)(2,1)S(1)}, u32[]{:S(2)}, u32[]{:S(2)}) %collective-permute-start) | collective-permute-done | bytes 262176 | tf_op jit(solution)/shard_map/ppermute | solution.py:16
  15.5 2.2 %collective-permute-start.1 = (f16[4,64,256]{2,1,0:T(8,128)(2,1)S(1)}, f16[4,64,256]{2,1,0:T(8,128)(2,1)S(1)}, u32[]{:S(2)}, u32[]{:S(2)}) collective-permute-start(f16[4,64,256]{2,1,0:T(8,128)(2,1)S(1)} %fusion.27), channel_id=1, source_target_pairs={{0,2},{1,3},{2,0},{3,1},{4,6},{5,7},{6,4},{7,5},{8,10},{9,11},{10,... | collective-permute-start | bytes 393224 | tf_op jit(solution)/shard_map/ppermute | solution.py:16
  17.7 1.2 collective-permute-start.10
  19.0 2.3 %collective-permute-start.9 = (bf16[256,2048]{1,0:T(8,128)(2,1)S(1)}, bf16[256,2048]{1,0:T(8,128)(2,1)}, u32[]{:S(2)}, u32[]{:S(2)}) collective-permute-start(bf16[256,2048]{1,0:T(8,128)(2,1)S(1)} %bitcast.260), channel_id=1, source_target_pairs={{0,4},{4,0},{8,12},{12,8},{16,20},{20,16},{24,28},{28,24},{1,5},{5... | collective-permute-start | bytes 3145736 | tf_op jit(solution)/shard_map/ppermute | solution.py:16
  21.3 1.2 collective-permute-start.5
  22.5 1.3 collective-permute-done.1
  24.4 0.7 constant_dynamic-update-slice_fusion.34
  25.1 4.7 %collective-permute-done.12 = bf16[256,2048]{1,0:T(8,128)(2,1)} collective-permute-done((bf16[256,2048]{1,0:T(8,128)(2,1)S(1)}, bf16[256,2048]{1,0:T(8,128)(2,1)}, u32[]{:S(2)}, u32[]{:S(2)}) %collective-permute-start.12) | collective-permute-done | bytes 1048608 | tf_op jit(solution)/shard_map/ppermute | solution.py:16
  29.8 2.7 %collective-permute-start.2 = (bf16[256,2048]{1,0:T(8,128)(2,1)S(1)}, bf16[256,2048]{1,0:T(8,128)(2,1)S(1)}, u32[]{:S(2)}, u32[]{:S(2)}) collective-permute-start(bf16[256,2048]{1,0:T(8,128)(2,1)S(1)} %bitcast.245), channel_id=1, source_target_pairs={{0,4},{4,0},{8,12},{12,8},{16,20},{20,16},{24,28},{28,24},{1,5},{5... | collective-permute-start | bytes 3145736 | tf_op jit(solution)/shard_map/ppermute | solution.py:16
  32.5 1.3 dynamic-slice_bitcast_fusion.3
  33.7 6.7 %collective-permute-done.10 = bf16[256,2048]{1,0:T(8,128)(2,1)} collective-permute-done((bf16[256,2048]{1,0:T(8,128)(2,1)S(1)}, bf16[256,2048]{1,0:T(8,128)(2,1)}, u32[]{:S(2)}, u32[]{:S(2)}) %collective-permute-start.10) | collective-permute-done | bytes 1048608 | tf_op jit(solution)/shard_map/ppermute | solution.py:16
  40.4 1.3 dynamic-slice_bitcast_fusion.5
  42.2 1.3 broadcast_select_fusion
  43.5 8.7 %collective-permute-done.5 = bf16[256,2048]{1,0:T(8,128)(2,1)} collective-permute-done((bf16[256,2048]{1,0:T(8,128)(2,1)S(1)}, bf16[256,2048]{1,0:T(8,128)(2,1)}, u32[]{:S(2)}, u32[]{:S(2)}) %collective-permute-start.5) | collective-permute-done | bytes 1048608 | tf_op jit(solution)/shard_map/ppermute | solution.py:16
  52.3 1.3 dynamic-slice_bitcast_fusion.19
  54.0 0.5 fusion.18
  55.5 7.4 %collective-permute-done.3 = bf16[256,2048]{1,0:T(8,128)(2,1)} collective-permute-done((bf16[256,2048]{1,0:T(8,128)(2,1)S(1)}, bf16[256,2048]{1,0:T(8,128)(2,1)}, u32[]{:S(2)}, u32[]{:S(2)}) %collective-permute-start.3) | collective-permute-done | bytes 1048608 | tf_op jit(solution)/shard_map/ppermute | solution.py:16
  62.9 1.3 broadcast_select_fusion.1
  64.7 0.5 fusion.16
  66.7 1.3 dynamic-slice_bitcast_fusion.21
  68.5 3.0 %collective-permute-start.13 = (bf16[256,2048]{1,0:T(8,128)(2,1)}, bf16[256,2048]{1,0:T(8,128)(2,1)S(1)}, u32[]{:S(2)}, u32[]{:S(2)}) collective-permute-start(bf16[256,2048]{1,0:T(8,128)(2,1)} %collective-permute-done.12), channel_id=1, source_target_pairs={{0,4},{4,0},{8,12},{12,8},{16,20},{20,16},{24,28},{28,24},{1,5},{5... | collective-permute-start | bytes 3145736 | tf_op jit(solution)/shard_map/ppermute | solution.py:16
  72.1 0.5 collective-permute-start.11
  72.6 0.7 convolution_multiply_fusion.13
  74.9 0.6 collective-permute-done.6
  75.8 0.5 fusion.19
  79.3 0.5 fusion.12
  83.4 1.3 collective-permute-start.7
  86.5 6.0 %collective-permute-done.7 = f16[6,2,64,256]{3,2,1,0:T(8,128)(2,1)S(1)} collective-permute-done((f16[6,2,64,256]{3,2,1,0:T(8,128)(2,1)S(1)}, f16[6,2,64,256]{3,2,1,0:T(8,128)(2,1)S(1)}, u32[]{:S(2)}, u32[]{:S(2)}) %collective-permute-start.7) | collective-permute-done | bytes 393248 | tf_op jit(solution)/shard_map/ppermute | solution.py:16
  92.9 16.9 %collective-permute-done.8 = f16[6,64,256]{2,1,0:T(8,128)(2,1)S(1)} collective-permute-done((f16[6,64,256]{2,1,0:T(8,128)(2,1)S(1)}, f16[6,64,256]{2,1,0:T(8,128)(2,1)S(1)}, u32[]{:S(2)}, u32[]{:S(2)}) %collective-permute-start.8) | collective-permute-done | bytes 196640 | tf_op jit(solution)/shard_map/ppermute | solution.py:16
  109.9 3.2 %collective-permute-start.16 = (f16[2,64,256]{2,1,0:T(8,128)(2,1)S(1)}, f16[2,64,256]{2,1,0:T(8,128)(2,1)S(1)}, u32[]{:S(2)}, u32[]{:S(2)}) collective-permute-start(f16[2,64,256]{2,1,0:T(8,128)(2,1)S(1)} %slice_convert_fusion.4), channel_id=1, source_target_pairs={{8,24},{12,28},{24,8},{28,12},{9,25},{13,29},{25,9},{29,13},{10,26... | collective-permute-start | bytes 196616 | tf_op jit(solution)/shard_map/ppermute | solution.py:16
  113.6 1.7 %convert_add_fusion = f32[10,2,64,256]{3,2,1,0:T(8,128)S(1)} fusion(f32[10,2,64,256]{3,2,1,0:T(8,128)} %copy-done.3, f16[10,2,64,256]{3,2,1,0:T(8,128)(2,1)} %collective-permute-done.14), kind=kLoop, calls=%fused_computation.3 | loop fusion | flops 655360 | bytes 3276800 | tf_op jit(solution)/shard_map/add | solution.py:74
  115.3 2.9 %collective-permute-start.15 = (f16[10,64,256]{2,1,0:T(8,128)(2,1)S(1)}, f16[10,64,256]{2,1,0:T(8,128)(2,1)}, u32[]{:S(2)}, u32[]{:S(2)}) collective-permute-start(f16[10,64,256]{2,1,0:T(8,128)(2,1)S(1)} %fusion.24), channel_id=1, source_target_pairs={{0,2},{1,3},{2,0},{3,1},{4,6},{5,7},{6,4},{7,5},{8,10},{9,11},{10,... | collective-permute-start | bytes 983048 | tf_op jit(solution)/shard_map/ppermute | solution.py:16
  118.4 15.0 %collective-permute-done.15 = f16[10,64,256]{2,1,0:T(8,128)(2,1)} collective-permute-done((f16[10,64,256]{2,1,0:T(8,128)(2,1)S(1)}, f16[10,64,256]{2,1,0:T(8,128)(2,1)}, u32[]{:S(2)}, u32[]{:S(2)}) %collective-permute-start.15) | collective-permute-done | bytes 327712 | tf_op jit(solution)/shard_map/ppermute | solution.py:16
  133.4 1.0 fusion.20
  134.5 2.1 %collective-permute-start.17 = (f16[6,64,256]{2,1,0:T(8,128)(2,1)S(1)}, f16[6,64,256]{2,1,0:T(8,128)(2,1)S(1)}, u32[]{:S(2)}, u32[]{:S(2)}) collective-permute-start(f16[6,64,256]{2,1,0:T(8,128)(2,1)S(1)} %slice_convert_fusion.2), channel_id=1, source_target_pairs={{8,24},{12,28},{24,8},{28,12},{9,25},{13,29},{25,9},{29,13},{10,26... | collective-permute-start | bytes 589832 | tf_op jit(solution)/shard_map/ppermute | solution.py:16
  137.2 5.2 %collective-permute-done.17 = f16[6,64,256]{2,1,0:T(8,128)(2,1)S(1)} collective-permute-done((f16[6,64,256]{2,1,0:T(8,128)(2,1)S(1)}, f16[6,64,256]{2,1,0:T(8,128)(2,1)S(1)}, u32[]{:S(2)}, u32[]{:S(2)}) %collective-permute-start.17) | collective-permute-done | bytes 196640 | tf_op jit(solution)/shard_map/ppermute | solution.py:16
  142.5 0.7 fusion.74
  143.5 1.0 copy.40
  144.6 1.6 %copy.39 = f32[1,64,256]{1,2,0:T(8,128)} copy(f32[1,64,256]{2,1,0:T(8,128)} %get-tuple-element.60) | data formatting | bytes 131072 | tf_op jit(solution)/shard_map/reshape;squeeze | solution.py:117
  146.2 0.9 pad_maximum_fusion.64
  147.8 1.2 multiply_bitcast_fusion
  (134 shorter events, 21.1 us)
Async XLA Ops:
  0.0 1.1 copy-start
  1.1 1.9 %copy-start.1 = (bf16[512,2048]{1,0:T(8,128)(2,1)S(1)}, bf16[512,2048]{1,0:T(8,128)(2,1)}, u32[]{:S(2)}) copy-start(bf16[512,2048]{1,0:T(8,128)(2,1)} %param.4) | copy-start | bytes 6291460
  5.6 24.2 %collective-permute-start.12 = (bf16[256,2048]{1,0:T(8,128)(2,1)S(1)}, bf16[256,2048]{1,0:T(8,128)(2,1)}, u32[]{:S(2)}, u32[]{:S(2)}) collective-permute-start(bf16[256,2048]{1,0:T(8,128)(2,1)S(1)} %bitcast.254), channel_id=1, source_target_pairs={{0,8},{4,12},{8,0},{12,4},{16,24},{20,28},{24,16},{28,20},{1,9},{5... | collective-permute-start | bytes 3145736 | tf_op jit(solution)/shard_map/ppermute | solution.py:16
  8.0 7.4 %collective-permute-start = (f16[4,2,64,256]{3,2,1,0:T(8,128)(2,1)S(1)}, f16[4,2,64,256]{3,2,1,0:T(8,128)(2,1)S(1)}, u32[]{:S(2)}, u32[]{:S(2)}) collective-permute-start(f16[4,2,64,256]{3,2,1,0:T(8,128)(2,1)S(1)} %pad_maximum_fusion.60), channel_id=1, source_target_pairs={{0,1},{1,0},{2,3},{3,2},{4,5},{5,4},{6,7},{7,6},{8,9},{9,8},{10,11... | collective-permute-start | bytes 786440 | tf_op jit(solution)/shard_map/ppermute | solution.py:16
  15.5 8.3 %collective-permute-start.1 = (f16[4,64,256]{2,1,0:T(8,128)(2,1)S(1)}, f16[4,64,256]{2,1,0:T(8,128)(2,1)S(1)}, u32[]{:S(2)}, u32[]{:S(2)}) collective-permute-start(f16[4,64,256]{2,1,0:T(8,128)(2,1)S(1)} %fusion.27), channel_id=1, source_target_pairs={{0,2},{1,3},{2,0},{3,1},{4,6},{5,7},{6,4},{7,5},{8,10},{9,11},{10,... | collective-permute-start | bytes 393224 | tf_op jit(solution)/shard_map/ppermute | solution.py:16
  17.7 22.7 %collective-permute-start.10 = (bf16[256,2048]{1,0:T(8,128)(2,1)S(1)}, bf16[256,2048]{1,0:T(8,128)(2,1)}, u32[]{:S(2)}, u32[]{:S(2)}) collective-permute-start(bf16[256,2048]{1,0:T(8,128)(2,1)S(1)} %bitcast.259), channel_id=1, source_target_pairs={{0,16},{4,20},{8,24},{12,28},{16,0},{20,4},{24,8},{28,12},{1,17},{... | collective-permute-start | bytes 3145736 | tf_op jit(solution)/shard_map/ppermute | solution.py:16
  19.0 59.8 %collective-permute-start.9 = (bf16[256,2048]{1,0:T(8,128)(2,1)S(1)}, bf16[256,2048]{1,0:T(8,128)(2,1)}, u32[]{:S(2)}, u32[]{:S(2)}) collective-permute-start(bf16[256,2048]{1,0:T(8,128)(2,1)S(1)} %bitcast.260), channel_id=1, source_target_pairs={{0,4},{4,0},{8,12},{12,8},{16,20},{20,16},{24,28},{28,24},{1,5},{5... | collective-permute-start | bytes 3145736 | tf_op jit(solution)/shard_map/ppermute | solution.py:16
  21.3 31.0 %collective-permute-start.5 = (bf16[256,2048]{1,0:T(8,128)(2,1)S(1)}, bf16[256,2048]{1,0:T(8,128)(2,1)}, u32[]{:S(2)}, u32[]{:S(2)}) collective-permute-start(bf16[256,2048]{1,0:T(8,128)(2,1)S(1)} %bitcast.243), channel_id=1, source_target_pairs={{0,8},{4,12},{8,0},{12,4},{16,24},{20,28},{24,16},{28,20},{1,9},{5... | collective-permute-start | bytes 3145736 | tf_op jit(solution)/shard_map/ppermute | solution.py:16
  23.8 39.1 %collective-permute-start.3 = (bf16[256,2048]{1,0:T(8,128)(2,1)S(1)}, bf16[256,2048]{1,0:T(8,128)(2,1)}, u32[]{:S(2)}, u32[]{:S(2)}) collective-permute-start(bf16[256,2048]{1,0:T(8,128)(2,1)S(1)} %bitcast.244), channel_id=1, source_target_pairs={{0,16},{4,20},{8,24},{12,28},{16,0},{20,4},{24,8},{28,12},{1,17},{... | collective-permute-start | bytes 3145736 | tf_op jit(solution)/shard_map/ppermute | solution.py:16
  29.8 49.1 %collective-permute-start.2 = (bf16[256,2048]{1,0:T(8,128)(2,1)S(1)}, bf16[256,2048]{1,0:T(8,128)(2,1)S(1)}, u32[]{:S(2)}, u32[]{:S(2)}) collective-permute-start(bf16[256,2048]{1,0:T(8,128)(2,1)S(1)} %bitcast.245), channel_id=1, source_target_pairs={{0,4},{4,0},{8,12},{12,8},{16,20},{20,16},{24,28},{28,24},{1,5},{5... | collective-permute-start | bytes 3145736 | tf_op jit(solution)/shard_map/ppermute | solution.py:16
  68.5 6.3 %collective-permute-start.13 = (bf16[256,2048]{1,0:T(8,128)(2,1)}, bf16[256,2048]{1,0:T(8,128)(2,1)S(1)}, u32[]{:S(2)}, u32[]{:S(2)}) collective-permute-start(bf16[256,2048]{1,0:T(8,128)(2,1)} %collective-permute-done.12), channel_id=1, source_target_pairs={{0,4},{4,0},{8,12},{12,8},{16,20},{20,16},{24,28},{28,24},{1,5},{5... | collective-permute-start | bytes 3145736 | tf_op jit(solution)/shard_map/ppermute | solution.py:16
  71.5 4.0 %collective-permute-start.6 = (bf16[256,2048]{1,0:T(8,128)(2,1)}, bf16[256,2048]{1,0:T(8,128)(2,1)S(1)}, u32[]{:S(2)}, u32[]{:S(2)}) collective-permute-start(bf16[256,2048]{1,0:T(8,128)(2,1)} %collective-permute-done.5), channel_id=1, source_target_pairs={{0,4},{4,0},{8,12},{12,8},{16,20},{20,16},{24,28},{28,24},{1,5},{5... | collective-permute-start | bytes 3145736 | tf_op jit(solution)/shard_map/ppermute | solution.py:16
  72.1 6.7 %collective-permute-start.11 = (bf16[256,2048]{1,0:T(8,128)(2,1)}, bf16[256,2048]{1,0:T(8,128)(2,1)S(1)}, u32[]{:S(2)}, u32[]{:S(2)}) collective-permute-start(bf16[256,2048]{1,0:T(8,128)(2,1)} %collective-permute-done.10), channel_id=1, source_target_pairs={{0,4},{4,0},{8,12},{12,8},{16,20},{20,16},{24,28},{28,24},{1,5},{5... | collective-permute-start | bytes 3145736 | tf_op jit(solution)/shard_map/ppermute | solution.py:16
  74.8 4.2 %collective-permute-start.4 = (bf16[256,2048]{1,0:T(8,128)(2,1)}, bf16[256,2048]{1,0:T(8,128)(2,1)S(1)}, u32[]{:S(2)}, u32[]{:S(2)}) collective-permute-start(bf16[256,2048]{1,0:T(8,128)(2,1)} %collective-permute-done.3), channel_id=1, source_target_pairs={{0,4},{4,0},{8,12},{12,8},{16,20},{20,16},{24,28},{28,24},{1,5},{5... | collective-permute-start | bytes 3145736 | tf_op jit(solution)/shard_map/ppermute | solution.py:16
  83.4 9.1 %collective-permute-start.7 = (f16[6,2,64,256]{3,2,1,0:T(8,128)(2,1)S(1)}, f16[6,2,64,256]{3,2,1,0:T(8,128)(2,1)S(1)}, u32[]{:S(2)}, u32[]{:S(2)}) collective-permute-start(f16[6,2,64,256]{3,2,1,0:T(8,128)(2,1)S(1)} %constant_dynamic-update-slice_fusion.6), channel_id=1, source_target_pairs={{0,1},{1,0},{2,3},{3,2},{4,5},{5,4},{6,7},{7,6},{8,9},{9,8},{10,11... | collective-permute-start | bytes 1179656 | tf_op jit(solution)/shard_map/ppermute | solution.py:16
  85.0 28.6 %collective-permute-start.14 = (f16[10,2,64,256]{3,2,1,0:T(8,128)(2,1)S(1)}, f16[10,2,64,256]{3,2,1,0:T(8,128)(2,1)}, u32[]{:S(2)}, u32[]{:S(2)}) collective-permute-start(f16[10,2,64,256]{3,2,1,0:T(8,128)(2,1)S(1)} %constant_dynamic-update-slice_fusion.22), channel_id=1, source_target_pairs={{0,1},{1,0},{2,3},{3,2},{4,5},{5,4},{6,7},{7,6},{8,9},{9,8},{10,11... | collective-permute-start | bytes 1966088 | tf_op jit(solution)/shard_map/ppermute | solution.py:16
  92.6 17.2 %collective-permute-start.8 = (f16[6,64,256]{2,1,0:T(8,128)(2,1)S(1)}, f16[6,64,256]{2,1,0:T(8,128)(2,1)S(1)}, u32[]{:S(2)}, u32[]{:S(2)}) collective-permute-start(f16[6,64,256]{2,1,0:T(8,128)(2,1)S(1)} %fusion.26), channel_id=1, source_target_pairs={{0,2},{1,3},{2,0},{3,1},{4,6},{5,7},{6,4},{7,5},{8,10},{9,11},{10,... | collective-permute-start | bytes 589832 | tf_op jit(solution)/shard_map/ppermute | solution.py:16
  92.9 17.0 %copy-start.3 = (f32[10,2,64,256]{3,2,1,0:T(8,128)}, f32[10,2,64,256]{3,2,1,0:T(8,128)S(1)}, u32[]{:S(2)}) copy-start(f32[10,2,64,256]{3,2,1,0:T(8,128)S(1)} %constant_dynamic-update-slice_fusion.12) | copy-start | bytes 3932164
  109.9 8.2 %collective-permute-start.16 = (f16[2,64,256]{2,1,0:T(8,128)(2,1)S(1)}, f16[2,64,256]{2,1,0:T(8,128)(2,1)S(1)}, u32[]{:S(2)}, u32[]{:S(2)}) collective-permute-start(f16[2,64,256]{2,1,0:T(8,128)(2,1)S(1)} %slice_convert_fusion.4), channel_id=1, source_target_pairs={{8,24},{12,28},{24,8},{28,12},{9,25},{13,29},{25,9},{29,13},{10,26... | collective-permute-start | bytes 196616 | tf_op jit(solution)/shard_map/ppermute | solution.py:16
  115.3 18.1 %collective-permute-start.15 = (f16[10,64,256]{2,1,0:T(8,128)(2,1)S(1)}, f16[10,64,256]{2,1,0:T(8,128)(2,1)}, u32[]{:S(2)}, u32[]{:S(2)}) collective-permute-start(f16[10,64,256]{2,1,0:T(8,128)(2,1)S(1)} %fusion.24), channel_id=1, source_target_pairs={{0,2},{1,3},{2,0},{3,1},{4,6},{5,7},{6,4},{7,5},{8,10},{9,11},{10,... | collective-permute-start | bytes 983048 | tf_op jit(solution)/shard_map/ppermute | solution.py:16
  134.5 7.9 %collective-permute-start.17 = (f16[6,64,256]{2,1,0:T(8,128)(2,1)S(1)}, f16[6,64,256]{2,1,0:T(8,128)(2,1)S(1)}, u32[]{:S(2)}, u32[]{:S(2)}) collective-permute-start(f16[6,64,256]{2,1,0:T(8,128)(2,1)S(1)} %slice_convert_fusion.2), channel_id=1, source_target_pairs={{8,24},{12,28},{24,8},{28,12},{9,25},{13,29},{25,9},{29,13},{10,26... | collective-permute-start | bytes 589832 | tf_op jit(solution)/shard_map/ppermute | solution.py:16
  143.3 3.9 %copy-start.2 = (f32[5,128,512]{1,2,0:T(8,128)S(1)}, f32[5,128,512]{1,2,0:T(8,128)}, u32[]{:S(2)}) copy-start(f32[5,128,512]{1,2,0:T(8,128)} %constant_dynamic-update-slice_fusion.34) | copy-start | bytes 3932164

commit v2 on v0

v2 whole, which is shorter than its diff:
```python
import functools
import math

import jax
import jax.numpy as jnp
from jax import lax
from jax.experimental import pallas as pl
from jax.experimental.pallas import tpu as pltpu
from jax.sharding import PartitionSpec as P

ST = 128
SNAP_MAX = 6.0
OUTLIER_MAX = 12.0
UNITS = 4


def swapped(x, axis, bit, only=None):
    pairs = [(i, i ^ bit) for i in range(lax.axis_size(axis)) if only is None or only(i)]
    return lax.ppermute(x, axis, pairs)


def passed_along(x, axis, by):
    size = lax.axis_size(axis)
    return lax.ppermute(x, axis, [(i, (i + by) % size) for i in range(size)])


def tile_product(own, other):
    return lax.dot_general(own, other, (((1,), (1,)), ((), ())), preferred_element_type=jnp.float32)


def clean(snapshots, outlier_cols, outlier_values, threshold):
    block_rows, points = snapshots.shape
    tiles_dev = points // ST
    onehot = (
        outlier_cols[:, :, None] == jnp.arange(tiles_dev, dtype=jnp.int32)[None, None, :]
    ).astype(jnp.bfloat16)
    dense = jnp.einsum("rkos,rkn->rons", outlier_values, onehot, preferred_element_type=jnp.float32)
    dense = dense.reshape(block_rows, points)
    diff = snapshots.astype(jnp.float32) - dense
    return (jnp.sign(diff) * jnp.maximum(jnp.abs(diff) - threshold, 0.0)).astype(jnp.bfloat16)


def ring(cleaned):
    kept = [tile_product(cleaned, cleaned)]
    moving = cleaned
    for step in range(lax.axis_size("tm") // 2):
        moving = passed_along(moving, "tm", -1)
        kept.append(tile_product(cleaned, moving))
    return lax.psum_scatter(jnp.stack(kept, axis=1), "space", scatter_dimension=2, tiled=True)


def in_order(body, out_shape, n_in, n_after=0, scratch=()):
    anywhere = pl.BlockSpec(memory_space=pl.ANY)
    whole = pl.BlockSpec(memory_space=pltpu.VMEM)
    return pl.pallas_call(
        body,
        out_shape=out_shape,
        in_specs=[whole] * n_in + [anywhere] * n_after,
        out_specs=jax.tree.map(lambda _: whole, out_shape),
        scratch_shapes=scratch,
        compiler_params=pltpu.CompilerParams(vmem_limit_bytes=40 << 20),
        cost_estimate=pl.CostEstimate(flops=1000, bytes_accessed=1000, transcendentals=0),
    )


def clean_kernel(cols_ref, threshold_ref, snapshots_ref, values_ref, all_ref, *first_refs):
    row = pl.program_id(0)
    threshold = threshold_ref[0]
    listed = values_ref.shape[1]

    def shrunk(d):
        return (d - jnp.clip(d, -threshold, threshold)).astype(jnp.bfloat16)

    width = all_ref.shape[1]

    def put(unit, columns, value):
        all_ref[unit, :, columns] = value
        if unit < len(first_refs):
            first_refs[unit][:, columns] = value

    for unit in range(UNITS):
        rows = slice(unit * width, (unit + 1) * width)
        put(unit, slice(None), shrunk(snapshots_ref[rows, :].astype(jnp.float32)))
    for k in range(listed):
        col = cols_ref[row, k]
        columns = pl.ds(pl.multiple_of(col * ST, ST), ST)
        for unit in range(UNITS):
            rows = slice(unit * width, (unit + 1) * width)
            total = values_ref[0, k, rows, :].astype(jnp.float32)
            for other in range(listed):
                if other != k:
                    same = jnp.where(cols_ref[row, other] == col, 1.0, 0.0)
                    total = total + same * values_ref[0, other, rows, :].astype(jnp.float32)
            put(unit, columns, shrunk(snapshots_ref[rows, columns].astype(jnp.float32) - total))


def clean_units(snapshots, outlier_cols, outlier_values, threshold, first):
    rows, points = snapshots.shape
    tile_rows, listed, height, _ = outlier_values.shape
    width = height // UNITS
    unit = jax.ShapeDtypeStruct((rows // UNITS, points), jnp.bfloat16)
    return pl.pallas_call(
        clean_kernel,
        grid=(tile_rows,),
        out_shape=[jax.ShapeDtypeStruct((UNITS, rows // UNITS, points), jnp.bfloat16)] + [unit] * first,
        in_specs=[
            pl.BlockSpec(memory_space=pltpu.SMEM),
            pl.BlockSpec(memory_space=pltpu.SMEM),
            pl.BlockSpec((height, points), lambda g: (g, 0)),
            pl.BlockSpec((1, listed, height, ST), lambda g: (g, 0, 0, 0)),
        ],
        out_specs=[pl.BlockSpec((UNITS, width, points), lambda g: (0, g, 0))]
        + [pl.BlockSpec((width, points), lambda g: (g, 0))] * first,
        compiler_params=pltpu.CompilerParams(vmem_limit_bytes=40 << 20),
    )(outlier_cols, threshold.reshape(1), snapshots, outlier_values)


def columns_of(ref):
    here = lax.axis_index("space")
    width = ref.shape[0] // 4
    return jnp.concatenate(
        [ref[pl.ds(pl.multiple_of((here ^ q) * width, width), width), :] for q in (0, 2, 1, 3)], axis=0
    )


def multiply(cols, rows, down, stay_ref, away_ref, places):
    product = tile_product(jnp.concatenate(cols, axis=0), jnp.concatenate(rows, axis=0)) * down
    width, length = stay_ref.shape[2:]
    for c, line in enumerate(places):
        for s, place in enumerate(line):
            for q in range(4):
                top = (c * 4 + q) * width
                block = product[top : top + width, s * length : (s + 1) * length]
                (stay_ref, stay_ref, away_ref, away_ref)[q][q % 2, place] = block


def own_kernel(down, all_ref, stay_ref, away_ref):
    for c in range(UNITS):
        places = [[c * UNITS + s for s in range(UNITS)]]
        rows = [all_ref[s] for s in range(UNITS)]
        multiply([columns_of(all_ref.at[c])], rows, down, stay_ref, away_ref, places)


def x_blocks(unit):
    keys = [(name, unit, s) for name in ("near", "other") for s in range(unit + 1)]
    return keys + [(name, s, unit) for s in range(unit) for name in ("near", "other")]


def y_blocks(unit):
    return [(name, unit, s) for name in ("y", "side") for s in range(UNITS)]


def unit_kernel(down, unit, n_after, *refs):
    refs = list(refs)

    def take(n):
        out, refs[:n] = refs[:n], []
        return out

    all_ref, sibling_ref, y_ref, y_other_ref = take(4)
    near, other, left_before = take(unit + 1), take(unit + 1), take(unit)
    take(n_after)
    stay_ref, away_ref, left_ref = take(3)
    next_ref = take(1)[0] if unit + 2 < UNITS else None
    side_ref = refs[0]
    core = lax.rem(lax.axis_index("tm"), 2)
    far = lax.rem(lax.div(lax.axis_index("tm"), 2), 2)

    if next_ref is not None:
        next_ref[...] = all_ref[unit + 2]

    @pl.when(far == 1)
    def _():
        left_ref[...] = y_ref[...]

    @pl.when(far == 0)
    def _():
        left_ref[...] = all_ref[unit]

    @pl.when(core == 0)
    def _():
        side_ref[...] = sibling_ref[unit]

    @pl.when(core == 1)
    def _():
        side_ref[...] = y_other_ref[...]

    place = {key: i for i, key in enumerate(x_blocks(unit) + y_blocks(unit))}
    left = [ref[...] for ref in left_before] + [left_ref[...]]
    multiply(
        [columns_of(near[unit]), columns_of(other[unit])],
        left,
        down,
        stay_ref,
        away_ref,
        [[place[name, unit, s] for s in range(unit + 1)] for name in ("near", "other")],
    )
    if unit > 0:
        multiply(
            [columns_of(ref) for pair in zip(near[:unit], other[:unit]) for ref in pair],
            [left_ref[...]],
            down,
            stay_ref,
            away_ref,
            [[place[name, s, unit]] for s in range(unit) for name in ("near", "other")],
        )
    multiply(
        [columns_of(y_ref), columns_of(side_ref)],
        [all_ref[s] for s in range(UNITS)],
        down,
        stay_ref,
        away_ref,
        [[place[name, unit, s] for s in range(UNITS)] for name in ("y", "side")],
    )


def assemble_kernel(scale, *refs):
    own_ref, x_refs, y_refs, out_ref = refs[0], refs[1 : 1 + UNITS], refs[1 + UNITS : 1 + 2 * UNITS], refs[-1]
    core = lax.rem(lax.axis_index("tm"), 2)
    where = {("own", c, s): (own_ref, c * UNITS + s) for c in range(UNITS) for s in range(UNITS)}
    for unit in range(UNITS):
        where.update({key: (x_refs[unit], i) for i, key in enumerate(x_blocks(unit))})
        where.update({key: (y_refs[unit], i) for i, key in enumerate(y_blocks(unit))})
    width = own_ref.shape[1]
    quarter = width * UNITS

    def put(k, name):
        for s in range(UNITS):
            pieces = [where[name, c, s] for c in range(UNITS)]
            tile = jnp.concatenate([ref[i] for ref, i in pieces], axis=0).T * scale
            for g in range(4):
                out_ref[k, g * quarter + s * width : g * quarter + (s + 1) * width, :] = tile[g * width : (g + 1) * width]

    put(0, "own")
    put(2, "near")
    put(4, "y")

    @pl.when(core == 0)
    def _():
        put(1, "side")
        put(3, "other")

    @pl.when(core == 1)
    def _():
        put(1, "other")
        put(3, "side")


def square(snapshots, outlier_cols, outlier_values, threshold):
    rows, points = snapshots.shape
    width, length = rows // (4 * UNITS), rows // UNITS
    far = (lax.axis_index("tm") // 2) % 2
    most = SNAP_MAX + outlier_cols.shape[1] * OUTLIER_MAX
    down = 2.0 ** -max(0, math.ceil(math.log2(2 * points * most * most / 6e4)))
    scale = 1.0 / (math.sqrt(points * lax.axis_size("space")) * down)

    def message(blocks):
        return [jax.ShapeDtypeStruct((2, blocks, width, length), jnp.float32)] * 2

    def half_summed(stay, away):
        return stay + swapped(away.astype(jnp.float16), "space", 1).astype(jnp.float32)

    def summed(kept):
        return kept[0] + swapped(kept[1].astype(jnp.float16), "space", 2).astype(jnp.float32)

    whole, *sent = clean_units(snapshots, outlier_cols, outlier_values, threshold, 2)
    unit_shape = jax.ShapeDtypeStruct((length, points), jnp.bfloat16)
    sibling = swapped(whole, "tm", 1, lambda i: i % 2 == 1)
    near, other, by_y, left, halves, totals, x_parts, y_parts = [], [], [], [], [], [], [], []
    halves.append(half_summed(*in_order(functools.partial(own_kernel, down), message(UNITS * UNITS), 1)(whole)))
    for unit in range(UNITS):
        near.append(swapped(sent[unit], "tm", 2))
        by_y.append(swapped(sent[unit], "tm", 4))
        other.append(swapped(near[unit], "tm", 1))
        y_other = swapped(by_y[unit], "tm", 1, lambda i: i % 2 == 0)
        operands = [whole, sibling, by_y[unit], y_other, *near, *other, *left]
        after = [halves[-1]] + totals[-1:]
        more = unit + 2 < UNITS
        stay, away, now, *later = in_order(
            functools.partial(unit_kernel, down, unit, len(after)),
            message(len(x_blocks(unit)) + len(y_blocks(unit))) + [unit_shape] * (2 if more else 1),
            len(operands),
            len(after),
            [pltpu.VMEM((length, points), jnp.bfloat16)],
        )(*operands, *after)
        left.append(now)
        sent.extend(later)
        totals.append(summed(halves[-1]))
        halves.append(half_summed(stay, away))
    totals.append(summed(halves[-1]))
    for unit, total in enumerate(totals[1:]):
        n = len(x_blocks(unit))
        lent = swapped(total[:n].astype(jnp.float16), "tm", 4, lambda i: i & 2).astype(jnp.float32)
        x_parts.append(jnp.where(far == 1, lent, total[:n]))
        y_parts.append(total[n:])
    out_shape = jax.ShapeDtypeStruct((5, rows, rows // 4), jnp.float32)
    operands = [totals[0], *x_parts, *y_parts]
    band = in_order(functools.partial(assemble_kernel, scale), out_shape, len(operands))(*operands)
    return band.transpose(1, 0, 2)


def local(snapshots, outlier_cols, outlier_values, threshold):
    if lax.axis_size("tm") == 8 and lax.axis_size("space") == 4:
        return square(snapshots, outlier_cols, outlier_values, threshold)
    points = snapshots.shape[1] * lax.axis_size("space")
    band = ring(clean(snapshots, outlier_cols, outlier_values, threshold))
    return band * (1.0 / jnp.sqrt(jnp.float32(points)))


def solution(mesh):
    placed = (P("tm", "space"), P("tm", "space"), P("tm", "space", None, None), P())
    return jax.shard_map(
        local, mesh=mesh, in_specs=placed, out_specs=P("tm", None, "space"), check_vma=False
    )
```

time: 225 us -> 118 us (0.52)
  the two profiles are of different devices: /device:TPU:3 before, /device:TPU:2 now
where the time goes in v2:
time: 118 us
  starting transfers between devices  50.9 us (43%)
  waiting for transfers between devices  38.7 us (33%)
  Pallas kernels  21.5 us (18%)
  local copies, waits for them, and re-layouts  3.35 us (3%)
  other arithmetic  2.07 us (2%)
    ppermute x31, starting transfers between devices, swapped(): return lax.ppermute(x, axis, pairs)  50.9 us
    ppermute x31, waiting for transfers between devices, swapped(): return lax.ppermute(x, axis, pairs)  38.7 us
    pallas_call x4, Pallas kernels, square(): in_order(functools.partial(unit_kernel, down, unit, len(after)), message(...  14.2 us
    unnamed x8, local copies, waits for them, and re-layouts  3.31 us
    pallas_call x1, Pallas kernels, clean_units(): pl.pallas_call(clean_kernel, grid=(tile_rows,), out_shape=[jax.ShapeDtype...  2.92 us
    pallas_call x1, Pallas kernels, square(): in_order(functools.partial(own_kernel, down), message(UNITS * UNITS), 1)  2.87 us
  transfers between devices with their start and end apart: 31, of which 10 were waited for; matrix products, arithmetic and copies ran while one was open for 2% of the time, Pallas kernels for 14%

profile of v2, /device:TPU:2, one launch (start us, length us, event | category | flops | bytes accessed | tf_op | source)
XLA Modules:
  0.0 117.6 jit_solution(6777035341938382263)
XLA Ops:
  0.7 1.6 %copy-done = bf16[512,2048]{1,0:T(8,128)(2,1)S(1)} copy-done((bf16[512,2048]{1,0:T(8,128)(2,1)S(1)}, bf16[512,2048]{1,0:T(8,128)(2,1)}, u32[]{:S(2)}) %copy-start) | copy-done | bytes 2097176
  2.2 1.0 copy-done.1
  3.3 0.7 copy-done.3
  4.0 2.9 %shard_map.46 = (bf16[4,128,2048]{2,1,0:T(8,128)(2,1)S(1)}, bf16[128,2048]{1,0:T(8,128)(2,1)S(1)}, bf16[128,2048]{1,0:T(8,128)(2,1)}) custom-call(s32[4,4]{1,0:T(4,128)S(1)} %copy-done.3, f32[1]{0:T(128)} %bitcast.32.threshold_ref, bf16[512,2048]{1,0:T(8,128)(2,1)S(1)} %copy-done, bf16[4,4,128,128]{3,2,1,0:T(8,128)(2,1)S(1)} %copy-done.1), custom_call_target="tpu_custom_call" | custom-call | tf_op jit(solution)/shard_map/pallas_call | solution.py:102
  6.9 1.3 %collective-permute-start.2 = (bf16[4,128,2048]{2,1,0:T(8,128)(2,1)S(1)}, bf16[4,128,2048]{2,1,0:T(8,128)(2,1)}, u32[]{:S(2)}, u32[]{:S(2)}) collective-permute-start(bf16[4,128,2048]{2,1,0:T(8,128)(2,1)S(1)} %get-tuple-element.23.all_ref.refs_0_), channel_id=1, source_target_pairs={{4,0},{12,8},{20,16},{28,24},{5,1},{13,9},{21,17},{29,25},{6,2},{1... | collective-permute-start | bytes 6291464 | tf_op jit(solution)/shard_map/ppermute | solution.py:19
  8.3 2.0 %collective-permute-start.3 = (bf16[128,2048]{1,0:T(8,128)(2,1)S(1)}, bf16[128,2048]{1,0:T(8,128)(2,1)}, u32[]{:S(2)}, u32[]{:S(2)}) collective-permute-start(bf16[128,2048]{1,0:T(8,128)(2,1)S(1)} %get-tuple-element.26), channel_id=1, source_target_pairs={{0,16},{4,20},{8,24},{12,28},{16,0},{20,4},{24,8},{28,12},{1,17},{... | collective-permute-start | bytes 1572872 | tf_op jit(solution)/shard_map/ppermute | solution.py:19
  10.3 2.9 %shard_map.47 = (f32[2,16,32,128]{3,2,1,0:T(8,128)S(1)}, f32[2,16,32,128]{3,2,1,0:T(8,128)S(1)}) custom-call(bf16[4,128,2048]{2,1,0:T(8,128)(2,1)S(1)} %get-tuple-element.23.all_ref.refs_0_), custom_call_target="tpu_custom_call" | custom-call | flops 1000 | bytes 1000 | tf_op jit(solution)/shard_map/pallas_call | solution.py:270
  13.2 1.6 %collective-permute-start = (f16[2,16,32,128]{3,2,1,0:T(8,128)(2,1)S(1)}, f16[2,16,32,128]{3,2,1,0:T(8,128)(2,1)S(1)}, u32[]{:S(2)}, u32[]{:S(2)}) collective-permute-start(f16[2,16,32,128]{3,2,1,0:T(8,128)(2,1)S(1)} %convert_element_type.89), channel_id=1, source_target_pairs={{0,1},{1,0},{2,3},{3,2},{4,5},{5,4},{6,7},{7,6},{8,9},{9,8},{10,11... | collective-permute-start | bytes 786440 | tf_op jit(solution)/shard_map/ppermute | solution.py:19
  14.9 6.6 %collective-permute-done.5.refs_4_ = bf16[128,2048]{1,0:T(8,128)(2,1)S(1)} collective-permute-done((bf16[128,2048]{1,0:T(8,128)(2,1)S(1)}, bf16[128,2048]{1,0:T(8,128)(2,1)S(1)}, u32[]{:S(2)}, u32[]{:S(2)}) %collective-permute-start.5) | collective-permute-done | bytes 524320 | tf_op jit(solution)/shard_map/ppermute | solution.py:19
  21.5 1.3 %collective-permute-start.6 = (bf16[128,2048]{1,0:T(8,128)(2,1)S(1)}, bf16[128,2048]{1,0:T(8,128)(2,1)S(1)}, u32[]{:S(2)}, u32[]{:S(2)}) collective-permute-start(bf16[128,2048]{1,0:T(8,128)(2,1)S(1)} %collective-permute-done.5.refs_4_), channel_id=1, source_target_pairs={{0,4},{4,0},{8,12},{12,8},{16,20},{20,16},{24,28},{28,24},{1,5},{5... | collective-permute-start | bytes 1572872 | tf_op jit(solution)/shard_map/ppermute | solution.py:19
  22.9 2.9 %collective-permute-start.4 = (bf16[128,2048]{1,0:T(8,128)(2,1)}, bf16[128,2048]{1,0:T(8,128)(2,1)}, u32[]{:S(2)}, u32[]{:S(2)}) collective-permute-start(bf16[128,2048]{1,0:T(8,128)(2,1)} %collective-permute-done.3.refs_2_), channel_id=1, source_target_pairs={{0,4},{8,12},{16,20},{24,28},{1,5},{9,13},{17,21},{25,29},{2,6},{1... | collective-permute-start | bytes 1572872 | tf_op jit(solution)/shard_map/ppermute | solution.py:19
  25.7 1.9 %collective-permute-start.12 = (bf16[128,2048]{1,0:T(8,128)(2,1)}, bf16[128,2048]{1,0:T(8,128)(2,1)}, u32[]{:S(2)}, u32[]{:S(2)}) collective-permute-start(bf16[128,2048]{1,0:T(8,128)(2,1)} %get-tuple-element.29), channel_id=1, source_target_pairs={{0,8},{4,12},{8,0},{12,4},{16,24},{20,28},{24,16},{28,20},{1,9},{5... | collective-permute-start | bytes 1572872 | tf_op jit(solution)/shard_map/ppermute | solution.py:19
  27.7 1.5 %collective-permute-start.10 = (bf16[128,2048]{1,0:T(8,128)(2,1)}, bf16[128,2048]{1,0:T(8,128)(2,1)}, u32[]{:S(2)}, u32[]{:S(2)}) collective-permute-start(bf16[128,2048]{1,0:T(8,128)(2,1)} %get-tuple-element.29), channel_id=1, source_target_pairs={{0,16},{4,20},{8,24},{12,28},{16,0},{20,4},{24,8},{28,12},{1,17},{... | collective-permute-start | bytes 1572872 | tf_op jit(solution)/shard_map/ppermute | solution.py:19
  29.2 1.1 convert_add_fusion.2.refs_6_
  30.4 2.9 %shard_map.48 = (f32[2,10,32,128]{3,2,1,0:T(8,128)S(1)}, f32[2,10,32,128]{3,2,1,0:T(8,128)S(1)}, bf16[128,2048]{1,0:T(8,128)(2,1)S(1)}, bf16[128,2048]{1,0:T(8,128)(2,1)S(1)}) custom-call(bf16[4,128,2048]{2,1,0:T(8,128)(2,1)S(1)} %get-tuple-element.23.all_ref.refs_0_, bf16[4,128,2048]{2,1,0:T(8,128)(2,1)} %collective-permute-done.2.refs_1_, ...), custom_call_target="tpu_custom_call" | custom-call | flops 1000 | bytes 1000 | tf_op jit(solution)/shard_map/pallas_call | solution.py:279
  33.3 1.6 %collective-permute-start.7 = (f16[2,10,32,128]{3,2,1,0:T(8,128)(2,1)S(1)}, f16[2,10,32,128]{3,2,1,0:T(8,128)(2,1)S(1)}, u32[]{:S(2)}, u32[]{:S(2)}) collective-permute-start(f16[2,10,32,128]{3,2,1,0:T(8,128)(2,1)S(1)} %convert_element_type.93), channel_id=1, source_target_pairs={{0,1},{1,0},{2,3},{3,2},{4,5},{5,4},{6,7},{7,6},{8,9},{9,8},{10,11... | collective-permute-start | bytes 491528 | tf_op jit(solution)/shard_map/ppermute | solution.py:19
  35.0 2.7 %collective-permute-start.1 = (f16[16,32,128]{2,1,0:T(8,128)(2,1)S(1)}, f16[16,32,128]{2,1,0:T(8,128)(2,1)S(1)}, u32[]{:S(2)}, u32[]{:S(2)}) collective-permute-start(f16[16,32,128]{2,1,0:T(8,128)(2,1)S(1)} %fusion.7), channel_id=1, source_target_pairs={{0,2},{1,3},{2,0},{3,1},{4,6},{5,7},{6,4},{7,5},{8,10},{9,11},{10,... | collective-permute-start | bytes 393224 | tf_op jit(solution)/shard_map/ppermute | solution.py:19
  37.6 1.1 collective-permute-done.12.refs_5_
  38.8 1.5 %collective-permute-done.10.refs_2_ = bf16[128,2048]{1,0:T(8,128)(2,1)} collective-permute-done((bf16[128,2048]{1,0:T(8,128)(2,1)}, bf16[128,2048]{1,0:T(8,128)(2,1)}, u32[]{:S(2)}, u32[]{:S(2)}) %collective-permute-start.10) | collective-permute-done | bytes 524320 | tf_op jit(solution)/shard_map/ppermute | solution.py:19
  40.2 1.3 %collective-permute-start.11 = (bf16[128,2048]{1,0:T(8,128)(2,1)}, bf16[128,2048]{1,0:T(8,128)(2,1)S(1)}, u32[]{:S(2)}, u32[]{:S(2)}) collective-permute-start(bf16[128,2048]{1,0:T(8,128)(2,1)} %collective-permute-done.10.refs_2_), channel_id=1, source_target_pairs={{0,4},{8,12},{16,20},{24,28},{1,5},{9,13},{17,21},{25,29},{2,6},{1... | collective-permute-start | bytes 1572872 | tf_op jit(solution)/shard_map/ppermute | solution.py:19
  41.5 1.5 %collective-permute-start.19 = (bf16[128,2048]{1,0:T(8,128)(2,1)S(1)}, bf16[128,2048]{1,0:T(8,128)(2,1)S(1)}, u32[]{:S(2)}, u32[]{:S(2)}) collective-permute-start(bf16[128,2048]{1,0:T(8,128)(2,1)S(1)} %get-tuple-element.33), channel_id=1, source_target_pairs={{0,8},{4,12},{8,0},{12,4},{16,24},{20,28},{24,16},{28,20},{1,9},{5... | collective-permute-start | bytes 1572872 | tf_op jit(solution)/shard_map/ppermute | solution.py:19
  43.0 1.5 %collective-permute-start.17 = (bf16[128,2048]{1,0:T(8,128)(2,1)S(1)}, bf16[128,2048]{1,0:T(8,128)(2,1)S(1)}, u32[]{:S(2)}, u32[]{:S(2)}) collective-permute-start(bf16[128,2048]{1,0:T(8,128)(2,1)S(1)} %get-tuple-element.33), channel_id=1, source_target_pairs={{0,16},{4,20},{8,24},{12,28},{16,0},{20,4},{24,8},{28,12},{1,17},{... | collective-permute-start | bytes 1572872 | tf_op jit(solution)/shard_map/ppermute | solution.py:19
  44.6 2.7 %collective-permute-start.8 = (f16[10,32,128]{2,1,0:T(8,128)(2,1)S(1)}, f16[10,32,128]{2,1,0:T(8,128)(2,1)S(1)}, u32[]{:S(2)}, u32[]{:S(2)}) collective-permute-start(f16[10,32,128]{2,1,0:T(8,128)(2,1)S(1)} %fusion.9), channel_id=1, source_target_pairs={{0,2},{1,3},{2,0},{3,1},{4,6},{5,7},{6,4},{7,5},{8,10},{9,11},{10,... | collective-permute-start | bytes 245768 | tf_op jit(solution)/shard_map/ppermute | solution.py:19
  47.3 3.2 %shard_map.49 = (f32[2,14,32,128]{3,2,1,0:T(8,128)S(1)}, f32[2,14,32,128]{3,2,1,0:T(8,128)S(1)}, bf16[128,2048]{1,0:T(8,128)(2,1)S(1)}, bf16[128,2048]{1,0:T(8,128)(2,1)S(1)}) custom-call(bf16[4,128,2048]{2,1,0:T(8,128)(2,1)S(1)} %get-tuple-element.23.all_ref.refs_0_, bf16[4,128,2048]{2,1,0:T(8,128)(2,1)} %collective-permute-done.2.refs_1_, ...), custom_call_target="tpu_custom_call" | custom-call | flops 1000 | bytes 1000 | tf_op jit(solution)/shard_map/pallas_call | solution.py:279
  50.5 0.6 collective-permute-start.24
  51.1 0.6 collective-permute-start.26
  51.8 1.6 %collective-permute-start.14 = (f16[2,14,32,128]{3,2,1,0:T(8,128)(2,1)S(1)}, f16[2,14,32,128]{3,2,1,0:T(8,128)(2,1)S(1)}, u32[]{:S(2)}, u32[]{:S(2)}) collective-permute-start(f16[2,14,32,128]{3,2,1,0:T(8,128)(2,1)S(1)} %convert_element_type.99), channel_id=1, source_target_pairs={{0,1},{1,0},{2,3},{3,2},{4,5},{5,4},{6,7},{7,6},{8,9},{9,8},{10,11... | collective-permute-start | bytes 688136 | tf_op jit(solution)/shard_map/ppermute | solution.py:19
  53.5 4.4 %collective-permute-done.14 = f16[2,14,32,128]{3,2,1,0:T(8,128)(2,1)S(1)} collective-permute-done((f16[2,14,32,128]{3,2,1,0:T(8,128)(2,1)S(1)}, f16[2,14,32,128]{3,2,1,0:T(8,128)(2,1)S(1)}, u32[]{:S(2)}, u32[]{:S(2)}) %collective-permute-start.14) | collective-permute-done | bytes 229408 | tf_op jit(solution)/shard_map/ppermute | solution.py:19
  57.9 3.4 %collective-permute-start.9 = (f16[2,32,128]{2,1,0:T(8,128)(2,1)S(1)}, f16[2,32,128]{2,1,0:T(8,128)(2,1)S(1)}, u32[]{:S(2)}, u32[]{:S(2)}) collective-permute-start(f16[2,32,128]{2,1,0:T(8,128)(2,1)S(1)} %slice_convert_fusion.8), channel_id=1, source_target_pairs={{8,24},{12,28},{24,8},{28,12},{9,25},{13,29},{25,9},{29,13},{10,26... | collective-permute-start | bytes 49160 | tf_op jit(solution)/shard_map/ppermute | solution.py:19
  61.4 2.4 %collective-permute-start.18 = (bf16[128,2048]{1,0:T(8,128)(2,1)S(1)}, bf16[128,2048]{1,0:T(8,128)(2,1)S(1)}, u32[]{:S(2)}, u32[]{:S(2)}) collective-permute-start(bf16[128,2048]{1,0:T(8,128)(2,1)S(1)} %collective-permute-done.17.refs_2_), channel_id=1, source_target_pairs={{0,4},{8,12},{16,20},{24,28},{1,5},{9,13},{17,21},{25,29},{2,6},{1... | collective-permute-start | bytes 1572872 | tf_op jit(solution)/shard_map/ppermute | solution.py:19
  63.9 3.6 %collective-permute-done.9 = f16[2,32,128]{2,1,0:T(8,128)(2,1)S(1)} collective-permute-done((f16[2,32,128]{2,1,0:T(8,128)(2,1)S(1)}, f16[2,32,128]{2,1,0:T(8,128)(2,1)S(1)}, u32[]{:S(2)}, u32[]{:S(2)}) %collective-permute-start.9) | collective-permute-done | bytes 16416 | tf_op jit(solution)/shard_map/ppermute | solution.py:19
  67.5 2.6 %collective-permute-start.15 = (f16[14,32,128]{2,1,0:T(8,128)(2,1)S(1)}, f16[14,32,128]{2,1,0:T(8,128)(2,1)S(1)}, u32[]{:S(2)}, u32[]{:S(2)}) collective-permute-start(f16[14,32,128]{2,1,0:T(8,128)(2,1)S(1)} %fusion.8), channel_id=1, source_target_pairs={{0,2},{1,3},{2,0},{3,1},{4,6},{5,7},{6,4},{7,5},{8,10},{9,11},{10,... | collective-permute-start | bytes 344072 | tf_op jit(solution)/shard_map/ppermute | solution.py:19
  70.1 3.5 %shard_map.50 = (f32[2,18,32,128]{3,2,1,0:T(8,128)S(1)}, f32[2,18,32,128]{3,2,1,0:T(8,128)S(1)}, bf16[128,2048]{1,0:T(8,128)(2,1)S(1)}) custom-call(bf16[4,128,2048]{2,1,0:T(8,128)(2,1)S(1)} %get-tuple-element.23.all_ref.refs_0_, bf16[4,128,2048]{2,1,0:T(8,128)(2,1)} %collective-permute-done.2.refs_1_, ...), custom_call_target="tpu_custom_call" | custom-call | flops 1000 | bytes 1000 | tf_op jit(solution)/shard_map/pallas_call | solution.py:279
  73.7 1.6 %collective-permute-start.21 = (f16[2,18,32,128]{3,2,1,0:T(8,128)(2,1)S(1)}, f16[2,18,32,128]{3,2,1,0:T(8,128)(2,1)S(1)}, u32[]{:S(2)}, u32[]{:S(2)}) collective-permute-start(f16[2,18,32,128]{3,2,1,0:T(8,128)(2,1)S(1)} %convert_element_type.105), channel_id=1, source_target_pairs={{0,1},{1,0},{2,3},{3,2},{4,5},{5,4},{6,7},{7,6},{8,9},{9,8},{10,11... | collective-permute-start | bytes 884744 | tf_op jit(solution)/shard_map/ppermute | solution.py:19
  75.4 1.3 %collective-permute-start.25 = (bf16[128,2048]{1,0:T(8,128)(2,1)S(1)}, bf16[128,2048]{1,0:T(8,128)(2,1)S(1)}, u32[]{:S(2)}, u32[]{:S(2)}) collective-permute-start(bf16[128,2048]{1,0:T(8,128)(2,1)S(1)} %collective-permute-done.24.refs_2_), channel_id=1, source_target_pairs={{0,4},{8,12},{16,20},{24,28},{1,5},{9,13},{17,21},{25,29},{2,6},{1... | collective-permute-start | bytes 1572872 | tf_op jit(solution)/shard_map/ppermute | solution.py:19
  76.9 3.4 %collective-permute-start.16 = (f16[6,32,128]{2,1,0:T(8,128)(2,1)S(1)}, f16[6,32,128]{2,1,0:T(8,128)(2,1)S(1)}, u32[]{:S(2)}, u32[]{:S(2)}) collective-permute-start(f16[6,32,128]{2,1,0:T(8,128)(2,1)S(1)} %slice_convert_fusion.7), channel_id=1, source_target_pairs={{8,24},{12,28},{24,8},{28,12},{9,25},{13,29},{25,9},{29,13},{10,26... | collective-permute-start | bytes 147464 | tf_op jit(solution)/shard_map/ppermute | solution.py:19
  80.3 0.3 collective-permute-done.21
  80.8 4.5 %shard_map.51 = (f32[2,22,32,128]{3,2,1,0:T(8,128)S(1)}, f32[2,22,32,128]{3,2,1,0:T(8,128)S(1)}, bf16[128,2048]{1,0:T(8,128)(2,1)}) custom-call(bf16[4,128,2048]{2,1,0:T(8,128)(2,1)S(1)} %get-tuple-element.23.all_ref.refs_0_, bf16[4,128,2048]{2,1,0:T(8,128)(2,1)} %collective-permute-done.2.refs_1_, bf16[128,2048]{1,0:T(8,128)(2,1)S(1)} %collective-permute-done.24.refs_2_, ...), custom_call_target="tpu_custom_call" | custom-call | flops 1000 | bytes 1000 | tf_op jit(solution)/shard_map/pallas_call | solution.py:279
  85.4 1.6 %collective-permute-start.28 = (f16[2,22,32,128]{3,2,1,0:T(8,128)(2,1)S(1)}, f16[2,22,32,128]{3,2,1,0:T(8,128)(2,1)S(1)}, u32[]{:S(2)}, u32[]{:S(2)}) collective-permute-start(f16[2,22,32,128]{3,2,1,0:T(8,128)(2,1)S(1)} %convert_element_type.111), channel_id=1, source_target_pairs={{0,1},{1,0},{2,3},{3,2},{4,5},{5,4},{6,7},{7,6},{8,9},{9,8},{10,11... | collective-permute-start | bytes 1081352 | tf_op jit(solution)/shard_map/ppermute | solution.py:19
  87.0 1.6 %collective-permute-start.22 = (f16[18,32,128]{2,1,0:T(8,128)(2,1)S(1)}, f16[18,32,128]{2,1,0:T(8,128)(2,1)S(1)}, u32[]{:S(2)}, u32[]{:S(2)}) collective-permute-start(f16[18,32,128]{2,1,0:T(8,128)(2,1)S(1)} %fusion.6), channel_id=1, source_target_pairs={{0,2},{1,3},{2,0},{3,1},{4,6},{5,7},{6,4},{7,5},{8,10},{9,11},{10,... | collective-permute-start | bytes 442376 | tf_op jit(solution)/shard_map/ppermute | solution.py:19
  88.5 8.2 %collective-permute-done.22 = f16[18,32,128]{2,1,0:T(8,128)(2,1)S(1)} collective-permute-done((f16[18,32,128]{2,1,0:T(8,128)(2,1)S(1)}, f16[18,32,128]{2,1,0:T(8,128)(2,1)S(1)}, u32[]{:S(2)}, u32[]{:S(2)}) %collective-permute-start.22) | collective-permute-done | bytes 147488 | tf_op jit(solution)/shard_map/ppermute | solution.py:19
  96.8 2.0 %collective-permute-done.28 = f16[2,22,32,128]{3,2,1,0:T(8,128)(2,1)S(1)} collective-permute-done((f16[2,22,32,128]{3,2,1,0:T(8,128)(2,1)S(1)}, f16[2,22,32,128]{3,2,1,0:T(8,128)(2,1)S(1)}, u32[]{:S(2)}, u32[]{:S(2)}) %collective-permute-start.28) | collective-permute-done | bytes 360480 | tf_op jit(solution)/shard_map/ppermute | solution.py:19
  99.0 1.5 %collective-permute-start.29 = (f16[22,32,128]{2,1,0:T(8,128)(2,1)S(1)}, f16[22,32,128]{2,1,0:T(8,128)(2,1)S(1)}, u32[]{:S(2)}, u32[]{:S(2)}) collective-permute-start(f16[22,32,128]{2,1,0:T(8,128)(2,1)S(1)} %fusion.4), channel_id=1, source_target_pairs={{0,2},{1,3},{2,0},{3,1},{4,6},{5,7},{6,4},{7,5},{8,10},{9,11},{10,... | collective-permute-start | bytes 540680 | tf_op jit(solution)/shard_map/ppermute | solution.py:19
  100.5 2.4 %collective-permute-start.23 = (f16[10,32,128]{2,1,0:T(8,128)(2,1)S(1)}, f16[10,32,128]{2,1,0:T(8,128)(2,1)S(1)}, u32[]{:S(2)}, u32[]{:S(2)}) collective-permute-start(f16[10,32,128]{2,1,0:T(8,128)(2,1)S(1)} %slice_convert_fusion.6), channel_id=1, source_target_pairs={{8,24},{12,28},{24,8},{28,12},{9,25},{13,29},{25,9},{29,13},{10,26... | collective-permute-start | bytes 245768 | tf_op jit(solution)/shard_map/ppermute | solution.py:19
  102.9 6.4 %collective-permute-done.29 = f16[22,32,128]{2,1,0:T(8,128)(2,1)S(1)} collective-permute-done((f16[22,32,128]{2,1,0:T(8,128)(2,1)S(1)}, f16[22,32,128]{2,1,0:T(8,128)(2,1)S(1)}, u32[]{:S(2)}, u32[]{:S(2)}) %collective-permute-start.29) | collective-permute-done | bytes 180256 | tf_op jit(solution)/shard_map/ppermute | solution.py:19
  109.4 2.1 %collective-permute-start.30 = (f16[14,32,128]{2,1,0:T(8,128)(2,1)S(1)}, f16[14,32,128]{2,1,0:T(8,128)(2,1)S(1)}, u32[]{:S(2)}, u32[]{:S(2)}) collective-permute-start(f16[14,32,128]{2,1,0:T(8,128)(2,1)S(1)} %slice_convert_fusion.4), channel_id=1, source_target_pairs={{8,24},{12,28},{24,8},{28,12},{9,25},{13,29},{25,9},{29,13},{10,26... | collective-permute-start | bytes 344072 | tf_op jit(solution)/shard_map/ppermute | solution.py:19
  111.6 4.5 %collective-permute-done.30 = f16[14,32,128]{2,1,0:T(8,128)(2,1)S(1)} collective-permute-done((f16[14,32,128]{2,1,0:T(8,128)(2,1)S(1)}, f16[14,32,128]{2,1,0:T(8,128)(2,1)S(1)}, u32[]{:S(2)}, u32[]{:S(2)}) %collective-permute-start.30) | collective-permute-done | bytes 114720 | tf_op jit(solution)/shard_map/ppermute | solution.py:19
  116.1 1.5 %shard_map.52 = f32[5,512,128]{2,1,0:T(8,128)} custom-call(f32[16,32,128]{2,1,0:T(8,128)S(1)} %fusion.2.refs_10_.refs_0_, f32[2,32,128]{2,1,0:T(8,128)S(1)} %convert_select_fusion.3.refs_1_, f32[6,32,128]{2,1,0:T(8,128)S(1)} %convert_select_fusion.2.refs_2_, f32[10,32,128]{2,1,0:T(8,128)S(1)} %convert_select_fusion.1.refs_3_, ...), custom_call_target="tpu_custom_call" | custom-call | flops 1000 | bytes 1000 | tf_op jit(solution)/shard_map/pallas_call | solution.py:298
  (61 shorter events, 1.3 us)
Async XLA Ops:
  0.7 1.6 %copy-start = (bf16[512,2048]{1,0:T(8,128)(2,1)S(1)}, bf16[512,2048]{1,0:T(8,128)(2,1)}, u32[]{:S(2)}) copy-start(bf16[512,2048]{1,0:T(8,128)(2,1)} %snapshots_ref.1) | copy-start | bytes 6291460
  2.2 1.0 copy-start.1
  3.3 0.7 copy-start.3
  6.9 23.5 %collective-permute-start.2 = (bf16[4,128,2048]{2,1,0:T(8,128)(2,1)S(1)}, bf16[4,128,2048]{2,1,0:T(8,128)(2,1)}, u32[]{:S(2)}, u32[]{:S(2)}) collective-permute-start(bf16[4,128,2048]{2,1,0:T(8,128)(2,1)S(1)} %get-tuple-element.23.all_ref.refs_0_), channel_id=1, source_target_pairs={{4,0},{12,8},{20,16},{28,24},{5,1},{13,9},{21,17},{29,25},{6,2},{1... | collective-permute-start | bytes 6291464 | tf_op jit(solution)/shard_map/ppermute | solution.py:19
  8.2 13.4 %collective-permute-start.5 = (bf16[128,2048]{1,0:T(8,128)(2,1)S(1)}, bf16[128,2048]{1,0:T(8,128)(2,1)S(1)}, u32[]{:S(2)}, u32[]{:S(2)}) collective-permute-start(bf16[128,2048]{1,0:T(8,128)(2,1)S(1)} %get-tuple-element.26), channel_id=1, source_target_pairs={{0,8},{4,12},{8,0},{12,4},{16,24},{20,28},{24,16},{28,20},{1,9},{5... | collective-permute-start | bytes 1572872 | tf_op jit(solution)/shard_map/ppermute | solution.py:19
  8.3 14.6 %collective-permute-start.3 = (bf16[128,2048]{1,0:T(8,128)(2,1)S(1)}, bf16[128,2048]{1,0:T(8,128)(2,1)}, u32[]{:S(2)}, u32[]{:S(2)}) collective-permute-start(bf16[128,2048]{1,0:T(8,128)(2,1)S(1)} %get-tuple-element.26), channel_id=1, source_target_pairs={{0,16},{4,20},{8,24},{12,28},{16,0},{20,4},{24,8},{28,12},{1,17},{... | collective-permute-start | bytes 1572872 | tf_op jit(solution)/shard_map/ppermute | solution.py:19
  13.2 8.4 %copy-start.2 = (f32[2,16,32,128]{3,2,1,0:T(8,128)}, f32[2,16,32,128]{3,2,1,0:T(8,128)S(1)}, u32[]{:S(2)}) copy-start(f32[2,16,32,128]{3,2,1,0:T(8,128)S(1)} %get-tuple-element.24) | copy-start | bytes 1572868
  13.2 14.4 %collective-permute-start = (f16[2,16,32,128]{3,2,1,0:T(8,128)(2,1)S(1)}, f16[2,16,32,128]{3,2,1,0:T(8,128)(2,1)S(1)}, u32[]{:S(2)}, u32[]{:S(2)}) collective-permute-start(f16[2,16,32,128]{3,2,1,0:T(8,128)(2,1)S(1)} %convert_element_type.89), channel_id=1, source_target_pairs={{0,1},{1,0},{2,3},{3,2},{4,5},{5,4},{6,7},{7,6},{8,9},{9,8},{10,11... | collective-permute-start | bytes 786440 | tf_op jit(solution)/shard_map/ppermute | solution.py:19
  21.5 8.8 %collective-permute-start.6 = (bf16[128,2048]{1,0:T(8,128)(2,1)S(1)}, bf16[128,2048]{1,0:T(8,128)(2,1)S(1)}, u32[]{:S(2)}, u32[]{:S(2)}) collective-permute-start(bf16[128,2048]{1,0:T(8,128)(2,1)S(1)} %collective-permute-done.5.refs_4_), channel_id=1, source_target_pairs={{0,4},{4,0},{8,12},{12,8},{16,20},{20,16},{24,28},{28,24},{1,5},{5... | collective-permute-start | bytes 1572872 | tf_op jit(solution)/shard_map/ppermute | solution.py:19
  22.9 7.5 %collective-permute-start.4 = (bf16[128,2048]{1,0:T(8,128)(2,1)}, bf16[128,2048]{1,0:T(8,128)(2,1)}, u32[]{:S(2)}, u32[]{:S(2)}) collective-permute-start(bf16[128,2048]{1,0:T(8,128)(2,1)} %collective-permute-done.3.refs_2_), channel_id=1, source_target_pairs={{0,4},{8,12},{16,20},{24,28},{1,5},{9,13},{17,21},{25,29},{2,6},{1... | collective-permute-start | bytes 1572872 | tf_op jit(solution)/shard_map/ppermute | solution.py:19
  25.7 13.0 %collective-permute-start.12 = (bf16[128,2048]{1,0:T(8,128)(2,1)}, bf16[128,2048]{1,0:T(8,128)(2,1)}, u32[]{:S(2)}, u32[]{:S(2)}) collective-permute-start(bf16[128,2048]{1,0:T(8,128)(2,1)} %get-tuple-element.29), channel_id=1, source_target_pairs={{0,8},{4,12},{8,0},{12,4},{16,24},{20,28},{24,16},{28,20},{1,9},{5... | collective-permute-start | bytes 1572872 | tf_op jit(solution)/shard_map/ppermute | solution.py:19
  27.7 12.5 %collective-permute-start.10 = (bf16[128,2048]{1,0:T(8,128)(2,1)}, bf16[128,2048]{1,0:T(8,128)(2,1)}, u32[]{:S(2)}, u32[]{:S(2)}) collective-permute-start(bf16[128,2048]{1,0:T(8,128)(2,1)} %get-tuple-element.29), channel_id=1, source_target_pairs={{0,16},{4,20},{8,24},{12,28},{16,0},{20,4},{24,8},{28,12},{1,17},{... | collective-permute-start | bytes 1572872 | tf_op jit(solution)/shard_map/ppermute | solution.py:19
  33.3 9.7 %collective-permute-start.7 = (f16[2,10,32,128]{3,2,1,0:T(8,128)(2,1)S(1)}, f16[2,10,32,128]{3,2,1,0:T(8,128)(2,1)S(1)}, u32[]{:S(2)}, u32[]{:S(2)}) collective-permute-start(f16[2,10,32,128]{3,2,1,0:T(8,128)(2,1)S(1)} %convert_element_type.93), channel_id=1, source_target_pairs={{0,1},{1,0},{2,3},{3,2},{4,5},{5,4},{6,7},{7,6},{8,9},{9,8},{10,11... | collective-permute-start | bytes 491528 | tf_op jit(solution)/shard_map/ppermute | solution.py:19
  35.0 9.6 %collective-permute-start.1 = (f16[16,32,128]{2,1,0:T(8,128)(2,1)S(1)}, f16[16,32,128]{2,1,0:T(8,128)(2,1)S(1)}, u32[]{:S(2)}, u32[]{:S(2)}) collective-permute-start(f16[16,32,128]{2,1,0:T(8,128)(2,1)S(1)} %fusion.7), channel_id=1, source_target_pairs={{0,2},{1,3},{2,0},{3,1},{4,6},{5,7},{6,4},{7,5},{8,10},{9,11},{10,... | collective-permute-start | bytes 393224 | tf_op jit(solution)/shard_map/ppermute | solution.py:19
  38.8 8.6 %collective-permute-start.13 = (bf16[128,2048]{1,0:T(8,128)(2,1)}, bf16[128,2048]{1,0:T(8,128)(2,1)S(1)}, u32[]{:S(2)}, u32[]{:S(2)}) collective-permute-start(bf16[128,2048]{1,0:T(8,128)(2,1)} %collective-permute-done.12.refs_5_), channel_id=1, source_target_pairs={{0,4},{4,0},{8,12},{12,8},{16,20},{20,16},{24,28},{28,24},{1,5},{5... | collective-permute-start | bytes 1572872 | tf_op jit(solution)/shard_map/ppermute | solution.py:19
  40.2 7.1 %collective-permute-start.11 = (bf16[128,2048]{1,0:T(8,128)(2,1)}, bf16[128,2048]{1,0:T(8,128)(2,1)S(1)}, u32[]{:S(2)}, u32[]{:S(2)}) collective-permute-start(bf16[128,2048]{1,0:T(8,128)(2,1)} %collective-permute-done.10.refs_2_), channel_id=1, source_target_pairs={{0,4},{8,12},{16,20},{24,28},{1,5},{9,13},{17,21},{25,29},{2,6},{1... | collective-permute-start | bytes 1572872 | tf_op jit(solution)/shard_map/ppermute | solution.py:19
  41.5 19.8 %collective-permute-start.19 = (bf16[128,2048]{1,0:T(8,128)(2,1)S(1)}, bf16[128,2048]{1,0:T(8,128)(2,1)S(1)}, u32[]{:S(2)}, u32[]{:S(2)}) collective-permute-start(bf16[128,2048]{1,0:T(8,128)(2,1)S(1)} %get-tuple-element.33), channel_id=1, source_target_pairs={{0,8},{4,12},{8,0},{12,4},{16,24},{20,28},{24,16},{28,20},{1,9},{5... | collective-permute-start | bytes 1572872 | tf_op jit(solution)/shard_map/ppermute | solution.py:19
  43.0 18.4 %collective-permute-start.17 = (bf16[128,2048]{1,0:T(8,128)(2,1)S(1)}, bf16[128,2048]{1,0:T(8,128)(2,1)S(1)}, u32[]{:S(2)}, u32[]{:S(2)}) collective-permute-start(bf16[128,2048]{1,0:T(8,128)(2,1)S(1)} %get-tuple-element.33), channel_id=1, source_target_pairs={{0,16},{4,20},{8,24},{12,28},{16,0},{20,4},{24,8},{28,12},{1,17},{... | collective-permute-start | bytes 1572872 | tf_op jit(solution)/shard_map/ppermute | solution.py:19
  44.6 7.2 %collective-permute-start.8 = (f16[10,32,128]{2,1,0:T(8,128)(2,1)S(1)}, f16[10,32,128]{2,1,0:T(8,128)(2,1)S(1)}, u32[]{:S(2)}, u32[]{:S(2)}) collective-permute-start(f16[10,32,128]{2,1,0:T(8,128)(2,1)S(1)} %fusion.9), channel_id=1, source_target_pairs={{0,2},{1,3},{2,0},{3,1},{4,6},{5,7},{6,4},{7,5},{8,10},{9,11},{10,... | collective-permute-start | bytes 245768 | tf_op jit(solution)/shard_map/ppermute | solution.py:19
  50.5 24.9 %collective-permute-start.24 = (bf16[128,2048]{1,0:T(8,128)(2,1)S(1)}, bf16[128,2048]{1,0:T(8,128)(2,1)S(1)}, u32[]{:S(2)}, u32[]{:S(2)}) collective-permute-start(bf16[128,2048]{1,0:T(8,128)(2,1)S(1)} %get-tuple-element.37), channel_id=1, source_target_pairs={{0,16},{4,20},{8,24},{12,28},{16,0},{20,4},{24,8},{28,12},{1,17},{... | collective-permute-start | bytes 1572872 | tf_op jit(solution)/shard_map/ppermute | solution.py:19
  51.1 25.7 %collective-permute-start.26 = (bf16[128,2048]{1,0:T(8,128)(2,1)S(1)}, bf16[128,2048]{1,0:T(8,128)(2,1)S(1)}, u32[]{:S(2)}, u32[]{:S(2)}) collective-permute-start(bf16[128,2048]{1,0:T(8,128)(2,1)S(1)} %get-tuple-element.37), channel_id=1, source_target_pairs={{0,8},{4,12},{8,0},{12,4},{16,24},{20,28},{24,16},{28,20},{1,9},{5... | collective-permute-start | bytes 1572872 | tf_op jit(solution)/shard_map/ppermute | solution.py:19
  51.8 6.1 %collective-permute-start.14 = (f16[2,14,32,128]{3,2,1,0:T(8,128)(2,1)S(1)}, f16[2,14,32,128]{3,2,1,0:T(8,128)(2,1)S(1)}, u32[]{:S(2)}, u32[]{:S(2)}) collective-permute-start(f16[2,14,32,128]{3,2,1,0:T(8,128)(2,1)S(1)} %convert_element_type.99), channel_id=1, source_target_pairs={{0,1},{1,0},{2,3},{3,2},{4,5},{5,4},{6,7},{7,6},{8,9},{9,8},{10,11... | collective-permute-start | bytes 688136 | tf_op jit(solution)/shard_map/ppermute | solution.py:19
  57.9 9.6 %collective-permute-start.9 = (f16[2,32,128]{2,1,0:T(8,128)(2,1)S(1)}, f16[2,32,128]{2,1,0:T(8,128)(2,1)S(1)}, u32[]{:S(2)}, u32[]{:S(2)}) collective-permute-start(f16[2,32,128]{2,1,0:T(8,128)(2,1)S(1)} %slice_convert_fusion.8), channel_id=1, source_target_pairs={{8,24},{12,28},{24,8},{28,12},{9,25},{13,29},{25,9},{29,13},{10,26... | collective-permute-start | bytes 49160 | tf_op jit(solution)/shard_map/ppermute | solution.py:19
  61.3 8.8 %collective-permute-start.20 = (bf16[128,2048]{1,0:T(8,128)(2,1)S(1)}, bf16[128,2048]{1,0:T(8,128)(2,1)S(1)}, u32[]{:S(2)}, u32[]{:S(2)}) collective-permute-start(bf16[128,2048]{1,0:T(8,128)(2,1)S(1)} %collective-permute-done.19.refs_6_), channel_id=1, source_target_pairs={{0,4},{4,0},{8,12},{12,8},{16,20},{20,16},{24,28},{28,24},{1,5},{5... | collective-permute-start | bytes 1572872 | tf_op jit(solution)/shard_map/ppermute | solution.py:19
  61.4 8.7 %collective-permute-start.18 = (bf16[128,2048]{1,0:T(8,128)(2,1)S(1)}, bf16[128,2048]{1,0:T(8,128)(2,1)S(1)}, u32[]{:S(2)}, u32[]{:S(2)}) collective-permute-start(bf16[128,2048]{1,0:T(8,128)(2,1)S(1)} %collective-permute-done.17.refs_2_), channel_id=1, source_target_pairs={{0,4},{8,12},{16,20},{24,28},{1,5},{9,13},{17,21},{25,29},{2,6},{1... | collective-permute-start | bytes 1572872 | tf_op jit(solution)/shard_map/ppermute | solution.py:19
  67.5 7.9 %collective-permute-start.15 = (f16[14,32,128]{2,1,0:T(8,128)(2,1)S(1)}, f16[14,32,128]{2,1,0:T(8,128)(2,1)S(1)}, u32[]{:S(2)}, u32[]{:S(2)}) collective-permute-start(f16[14,32,128]{2,1,0:T(8,128)(2,1)S(1)} %fusion.8), channel_id=1, source_target_pairs={{0,2},{1,3},{2,0},{3,1},{4,6},{5,7},{6,4},{7,5},{8,10},{9,11},{10,... | collective-permute-start | bytes 344072 | tf_op jit(solution)/shard_map/ppermute | solution.py:19
  73.7 6.9 %collective-permute-start.21 = (f16[2,18,32,128]{3,2,1,0:T(8,128)(2,1)S(1)}, f16[2,18,32,128]{3,2,1,0:T(8,128)(2,1)S(1)}, u32[]{:S(2)}, u32[]{:S(2)}) collective-permute-start(f16[2,18,32,128]{3,2,1,0:T(8,128)(2,1)S(1)} %convert_element_type.105), channel_id=1, source_target_pairs={{0,1},{1,0},{2,3},{3,2},{4,5},{5,4},{6,7},{7,6},{8,9},{9,8},{10,11... | collective-permute-start | bytes 884744 | tf_op jit(solution)/shard_map/ppermute | solution.py:19
  75.4 5.3 %collective-permute-start.25 = (bf16[128,2048]{1,0:T(8,128)(2,1)S(1)}, bf16[128,2048]{1,0:T(8,128)(2,1)S(1)}, u32[]{:S(2)}, u32[]{:S(2)}) collective-permute-start(bf16[128,2048]{1,0:T(8,128)(2,1)S(1)} %collective-permute-done.24.refs_2_), channel_id=1, source_target_pairs={{0,4},{8,12},{16,20},{24,28},{1,5},{9,13},{17,21},{25,29},{2,6},{1... | collective-permute-start | bytes 1572872 | tf_op jit(solution)/shard_map/ppermute | solution.py:19
  76.8 4.0 %collective-permute-start.27 = (bf16[128,2048]{1,0:T(8,128)(2,1)S(1)}, bf16[128,2048]{1,0:T(8,128)(2,1)S(1)}, u32[]{:S(2)}, u32[]{:S(2)}) collective-permute-start(bf16[128,2048]{1,0:T(8,128)(2,1)S(1)} %collective-permute-done.26.refs_7_), channel_id=1, source_target_pairs={{0,4},{4,0},{8,12},{12,8},{16,20},{20,16},{24,28},{28,24},{1,5},{5... | collective-permute-start | bytes 1572872 | tf_op jit(solution)/shard_map/ppermute | solution.py:19
  76.9 11.6 %collective-permute-start.16 = (f16[6,32,128]{2,1,0:T(8,128)(2,1)S(1)}, f16[6,32,128]{2,1,0:T(8,128)(2,1)S(1)}, u32[]{:S(2)}, u32[]{:S(2)}) collective-permute-start(f16[6,32,128]{2,1,0:T(8,128)(2,1)S(1)} %slice_convert_fusion.7), channel_id=1, source_target_pairs={{8,24},{12,28},{24,8},{28,12},{9,25},{13,29},{25,9},{29,13},{10,26... | collective-permute-start | bytes 147464 | tf_op jit(solution)/shard_map/ppermute | solution.py:19
  85.4 13.4 %collective-permute-start.28 = (f16[2,22,32,128]{3,2,1,0:T(8,128)(2,1)S(1)}, f16[2,22,32,128]{3,2,1,0:T(8,128)(2,1)S(1)}, u32[]{:S(2)}, u32[]{:S(2)}) collective-permute-start(f16[2,22,32,128]{3,2,1,0:T(8,128)(2,1)S(1)} %convert_element_type.111), channel_id=1, source_target_pairs={{0,1},{1,0},{2,3},{3,2},{4,5},{5,4},{6,7},{7,6},{8,9},{9,8},{10,11... | collective-permute-start | bytes 1081352 | tf_op jit(solution)/shard_map/ppermute | solution.py:19
  87.0 9.8 %collective-permute-start.22 = (f16[18,32,128]{2,1,0:T(8,128)(2,1)S(1)}, f16[18,32,128]{2,1,0:T(8,128)(2,1)S(1)}, u32[]{:S(2)}, u32[]{:S(2)}) collective-permute-start(f16[18,32,128]{2,1,0:T(8,128)(2,1)S(1)} %fusion.6), channel_id=1, source_target_pairs={{0,2},{1,3},{2,0},{3,1},{4,6},{5,7},{6,4},{7,5},{8,10},{9,11},{10,... | collective-permute-start | bytes 442376 | tf_op jit(solution)/shard_map/ppermute | solution.py:19
  99.0 10.3 %collective-permute-start.29 = (f16[22,32,128]{2,1,0:T(8,128)(2,1)S(1)}, f16[22,32,128]{2,1,0:T(8,128)(2,1)S(1)}, u32[]{:S(2)}, u32[]{:S(2)}) collective-permute-start(f16[22,32,128]{2,1,0:T(8,128)(2,1)S(1)} %fusion.4), channel_id=1, source_target_pairs={{0,2},{1,3},{2,0},{3,1},{4,6},{5,7},{6,4},{7,5},{8,10},{9,11},{10,... | collective-permute-start | bytes 540680 | tf_op jit(solution)/shard_map/ppermute | solution.py:19
  100.5 11.0 %collective-permute-start.23 = (f16[10,32,128]{2,1,0:T(8,128)(2,1)S(1)}, f16[10,32,128]{2,1,0:T(8,128)(2,1)S(1)}, u32[]{:S(2)}, u32[]{:S(2)}) collective-permute-start(f16[10,32,128]{2,1,0:T(8,128)(2,1)S(1)} %slice_convert_fusion.6), channel_id=1, source_target_pairs={{8,24},{12,28},{24,8},{28,12},{9,25},{13,29},{25,9},{29,13},{10,26... | collective-permute-start | bytes 245768 | tf_op jit(solution)/shard_map/ppermute | solution.py:19
  109.4 6.7 %collective-permute-start.30 = (f16[14,32,128]{2,1,0:T(8,128)(2,1)S(1)}, f16[14,32,128]{2,1,0:T(8,128)(2,1)S(1)}, u32[]{:S(2)}, u32[]{:S(2)}) collective-permute-start(f16[14,32,128]{2,1,0:T(8,128)(2,1)S(1)} %slice_convert_fusion.4), channel_id=1, source_target_pairs={{8,24},{12,28},{24,8},{28,12},{9,25},{13,29},{25,9},{29,13},{10,26... | collective-permute-start | bytes 344072 | tf_op jit(solution)/shard_map/ppermute | solution.py:19

commit v3 on v2

v3 whole, which is shorter than its diff:
```python
import functools
import math

import jax
import jax.numpy as jnp
from jax import lax
from jax.experimental import pallas as pl
from jax.experimental.pallas import tpu as pltpu
from jax.sharding import PartitionSpec as P

ST = 128
SNAP_MAX = 6.0
OUTLIER_MAX = 12.0
UNITS = 4
STAGES = ((0, 1), (2,), (3,))
GOES = ((0, 2), (2, 3))


def swapped(x, axis, bit, only=None):
    pairs = [(i, i ^ bit) for i in range(lax.axis_size(axis)) if only is None or only(i)]
    return lax.ppermute(x, axis, pairs)


def passed_along(x, axis, by):
    size = lax.axis_size(axis)
    return lax.ppermute(x, axis, [(i, (i + by) % size) for i in range(size)])


def tile_product(own, other):
    return lax.dot_general(own, other, (((1,), (1,)), ((), ())), preferred_element_type=jnp.float32)


def clean(snapshots, outlier_cols, outlier_values, threshold):
    block_rows, points = snapshots.shape
    tiles_dev = points // ST
    onehot = (
        outlier_cols[:, :, None] == jnp.arange(tiles_dev, dtype=jnp.int32)[None, None, :]
    ).astype(jnp.bfloat16)
    dense = jnp.einsum("rkos,rkn->rons", outlier_values, onehot, preferred_element_type=jnp.float32)
    dense = dense.reshape(block_rows, points)
    diff = snapshots.astype(jnp.float32) - dense
    return (jnp.sign(diff) * jnp.maximum(jnp.abs(diff) - threshold, 0.0)).astype(jnp.bfloat16)


def ring(cleaned):
    kept = [tile_product(cleaned, cleaned)]
    moving = cleaned
    for step in range(lax.axis_size("tm") // 2):
        moving = passed_along(moving, "tm", -1)
        kept.append(tile_product(cleaned, moving))
    return lax.psum_scatter(jnp.stack(kept, axis=1), "space", scatter_dimension=2, tiled=True)


def in_order(body, out_shape, n_in, n_after=0):
    anywhere = pl.BlockSpec(memory_space=pl.ANY)
    whole = pl.BlockSpec(memory_space=pltpu.VMEM)
    return pl.pallas_call(
        body,
        out_shape=out_shape,
        in_specs=[whole] * n_in + [anywhere] * n_after,
        out_specs=jax.tree.map(lambda _: whole, out_shape),
        compiler_params=pltpu.CompilerParams(vmem_limit_bytes=40 << 20),
        cost_estimate=pl.CostEstimate(flops=1000, bytes_accessed=1000, transcendentals=0),
    )


def clean_kernel(
    cols_hbm, threshold_ref, snapshots_hbm, values_hbm, all_ref, *refs
):
    *sent_refs, cols_ref, snapshots_ref, values_ref, cols_sem, row_sems, value_sems = refs
    tile_rows, listed, height, _ = values_ref.shape
    width = height // UNITS
    threshold = threshold_ref[0]
    cols_copy = pltpu.make_async_copy(cols_hbm, cols_ref, cols_sem)
    cols_copy.start()
    row_copies, value_copies = [], []
    for g in range(tile_rows):
        rows = pl.ds(g * height, height)
        row_copies.append(pltpu.make_async_copy(snapshots_hbm.at[rows], snapshots_ref.at[rows], row_sems.at[g]))
        value_copies.append(pltpu.make_async_copy(values_hbm.at[g], values_ref.at[g], value_sems.at[g]))
        row_copies[-1].start()
        value_copies[-1].start()
    cols_copy.wait()

    def shrunk(d):
        return (d - jnp.clip(d, -threshold, threshold)).astype(jnp.bfloat16)

    for g in range(tile_rows):
        row_copies[g].wait()

        def put(unit, columns, value):
            all_ref[unit, g * width : (g + 1) * width, columns] = value
            for stage, sent_ref in enumerate(sent_refs):
                if unit in STAGES[stage]:
                    top = (unit - STAGES[stage][0]) * height + g * width
                    sent_ref[top : top + width, columns] = value

        for unit in range(UNITS):
            rows = slice(g * height + unit * width, g * height + (unit + 1) * width)
            put(unit, slice(None), shrunk(snapshots_ref[rows, :].astype(jnp.float32)))
        value_copies[g].wait()
        for k in range(listed):
            col = cols_ref[g, k]
            columns = pl.ds(pl.multiple_of(col * ST, ST), ST)
            for unit in range(UNITS):
                rows = slice(unit * width, (unit + 1) * width)
                total = values_ref[g, k, rows, :].astype(jnp.float32)
                for other in range(listed):
                    if other != k:
                        same = jnp.where(cols_ref[g, other] == col, 1.0, 0.0)
                        total = total + same * values_ref[g, other, rows, :].astype(jnp.float32)
                rows = slice(g * height + unit * width, g * height + (unit + 1) * width)
                put(unit, columns, shrunk(snapshots_ref[rows, columns].astype(jnp.float32) - total))


def clean_units(snapshots, outlier_cols, outlier_values, threshold, first):
    rows, points = snapshots.shape
    tile_rows = outlier_values.shape[0]
    length = rows // UNITS
    out_shape = [jax.ShapeDtypeStruct((UNITS, length, points), jnp.bfloat16)]
    out_shape += [jax.ShapeDtypeStruct((len(units) * length, points), jnp.bfloat16) for units in STAGES[:first]]
    hbm = pl.BlockSpec(memory_space=pltpu.HBM)
    return pl.pallas_call(
        clean_kernel,
        out_shape=out_shape,
        in_specs=[hbm, pl.BlockSpec(memory_space=pltpu.SMEM), hbm, hbm],
        out_specs=[pl.BlockSpec(memory_space=pltpu.VMEM)] * len(out_shape),
        scratch_shapes=[
            pltpu.SMEM(outlier_cols.shape, jnp.int32),
            pltpu.VMEM(snapshots.shape, jnp.bfloat16),
            pltpu.VMEM(outlier_values.shape, jnp.bfloat16),
            pltpu.SemaphoreType.DMA,
            pltpu.SemaphoreType.DMA((tile_rows,)),
            pltpu.SemaphoreType.DMA((tile_rows,)),
        ],
        compiler_params=pltpu.CompilerParams(vmem_limit_bytes=40 << 20),
    )(outlier_cols, threshold.reshape(1), snapshots, outlier_values)


def columns_of(ref):
    here = lax.axis_index("space")
    width = ref.shape[0] // 4
    return [ref[pl.ds(pl.multiple_of((here ^ q) * width, width), width), :] for q in (0, 2, 1, 3)]


def multiply(cols, rows, down, stay_ref, away_ref, places):
    cols = [piece for ref in cols for piece in columns_of(ref)]
    product = tile_product(jnp.concatenate(cols, axis=0), jnp.concatenate([ref[...] for ref in rows], axis=0)) * down
    width, length = stay_ref.shape[2:]
    for c, line in enumerate(places):
        for s, place in enumerate(line):
            for q in range(4):
                top = (c * 4 + q) * width
                block = product[top : top + width, s * length : (s + 1) * length]
                (stay_ref, stay_ref, away_ref, away_ref)[q][q % 2, place] = block


def own_kernel(down, all_ref, stay_ref, away_ref, copy_ref):
    units = [all_ref.at[s] for s in range(UNITS)]
    for c in range(UNITS):
        multiply([units[c]], units, down, stay_ref, away_ref, [[c * UNITS + s for s in range(UNITS)]])
    copy_ref[...] = all_ref[...]


def x_blocks(stage):
    fresh, before = STAGES[stage], range(STAGES[stage][0])
    return [(c, s) for c in fresh for s in [*before, *fresh]] + [(c, s) for c in before for s in fresh]


def y_blocks(stage):
    return [(c, s) for c in STAGES[stage] for s in range(UNITS)]


def stage_blocks(stage):
    names = [("near", key) for key in x_blocks(stage)] + [("cross", key) for key in x_blocks(stage)]
    return names + [("y", key) for key in y_blocks(stage)] + [("side", key) for key in y_blocks(stage)]


def stage_kernel(down, stage, n_after, hands_on, *refs):
    refs = list(refs)

    def take(n):
        out, refs[:n] = refs[:n], []
        return out

    all_ref, sibling_ref, y_ref, y_other_ref = take(4)
    x_refs = take(stage + 1)
    left_before, cross_before = take(stage), take(stage)
    take(n_after)
    stay_ref, away_ref, left_ref, cross_ref, side_ref = take(5)
    core = lax.rem(lax.axis_index("tm"), 2)
    far = lax.rem(lax.div(lax.axis_index("tm"), 2), 2)
    fresh, before = STAGES[stage], STAGES[stage][0]
    first, count = fresh[0], len(fresh)
    length = all_ref.shape[1]

    def unit_of(ref, i):
        return ref.at[pl.ds(i * length, length)]

    def units_of(stage_refs):
        return [unit_of(ref, i) for s, ref in enumerate(stage_refs) for i in range(len(STAGES[s]))]

    if hands_on is not None:
        for i, unit in enumerate(STAGES[hands_on]):
            refs[0][i * length : (i + 1) * length] = all_ref[unit]

    for i, unit in enumerate(fresh):
        rows = slice(i * length, (i + 1) * length)

        @pl.when(far == 1)
        def _():
            left_ref[rows] = y_ref[rows]
            cross_ref[rows] = y_other_ref[rows]

        @pl.when(far == 0)
        def _():
            left_ref[rows] = all_ref[unit]
            cross_ref[rows] = sibling_ref[unit]

        @pl.when(core == 0)
        def _():
            side_ref[rows] = sibling_ref[unit]

        @pl.when(core == 1)
        def _():
            side_ref[rows] = y_other_ref[rows]

    place = {key: i for i, key in enumerate(stage_blocks(stage))}
    x_units = units_of(x_refs)
    left, cross = units_of([*left_before, left_ref]), units_of([*cross_before, cross_ref])
    n = first + count
    multiply(
        x_units[first:],
        left + cross,
        down,
        stay_ref,
        away_ref,
        [[place[name, (c, s)] for name in ("near", "cross") for s in range(n)] for c in fresh],
    )
    if before > 0:
        multiply(
            x_units[:first],
            left[first:] + cross[first:],
            down,
            stay_ref,
            away_ref,
            [[place[name, (c, s)] for name in ("near", "cross") for s in fresh] for c in range(before)],
        )
    multiply(
        [unit_of(ref, i) for ref in (y_ref, side_ref) for i in range(count)],
        [all_ref.at[s] for s in range(UNITS)],
        down,
        stay_ref,
        away_ref,
        [[place[name, (c, s)] for s in range(UNITS)] for name in ("y", "side") for c in fresh],
    )


def assemble_kernel(scale, *refs):
    own_ref, out_ref = refs[0], refs[-1]
    core = lax.rem(lax.axis_index("tm"), 2)
    where = {("own", (c, s)): (own_ref, c * UNITS + s) for c in range(UNITS) for s in range(UNITS)}
    rest = iter(refs[1:-1])
    for first, last in GOES:
        for name in ("near", "cross"):
            keys = [key for stage in range(first, last) for key in x_blocks(stage)]
            ref = next(rest)
            where.update({(name, key): (ref, i) for i, key in enumerate(keys)})
    for stage in range(len(STAGES)):
        ref = next(rest)
        keys = [(name, key) for name in ("y", "side") for key in y_blocks(stage)]
        where.update({key: (ref, i) for i, key in enumerate(keys)})
    width = own_ref.shape[1]
    quarter = width * UNITS

    def put(k, name):
        for s in range(UNITS):
            pieces = [where[name, (c, s)] for c in range(UNITS)]
            tile = jnp.concatenate([ref[i] for ref, i in pieces], axis=0).T * scale
            for g in range(4):
                out_ref[k, g * quarter + s * width : g * quarter + (s + 1) * width, :] = tile[g * width : (g + 1) * width]

    put(0, "own")
    put(2, "near")
    put(4, "y")

    @pl.when(core == 0)
    def _():
        put(1, "side")
        put(3, "cross")

    @pl.when(core == 1)
    def _():
        put(1, "cross")
        put(3, "side")


def square(snapshots, outlier_cols, outlier_values, threshold):
    rows, points = snapshots.shape
    width, length = rows // (4 * UNITS), rows // UNITS
    far = (lax.axis_index("tm") // 2) % 2
    most = SNAP_MAX + outlier_cols.shape[1] * OUTLIER_MAX
    down = 2.0 ** -max(0, math.ceil(math.log2(2 * points * most * most / 6e4)))
    scale = 1.0 / (math.sqrt(points * lax.axis_size("space")) * down)

    def message(blocks):
        return [jax.ShapeDtypeStruct((2, blocks, width, length), jnp.float32)] * 2

    def units(n):
        return jax.ShapeDtypeStruct((n * length, points), jnp.bfloat16)

    def half_summed(stay, away):
        return stay + swapped(away.astype(jnp.float16), "space", 1).astype(jnp.float32)

    def summed(kept):
        return kept[0] + swapped(kept[1].astype(jnp.float16), "space", 2).astype(jnp.float32)

    whole, *sent = clean_units(snapshots, outlier_cols, outlier_values, threshold, 2)
    out_shape = message(UNITS * UNITS) + [jax.ShapeDtypeStruct(whole.shape, whole.dtype)]
    stay, away, lent = in_order(functools.partial(own_kernel, down), out_shape, 1)(whole)
    sibling = swapped(lent, "tm", 1)
    own = summed(half_summed(stay, away))
    x_units, left, cross, totals = [], [], [], []
    for stage, fresh in enumerate(STAGES):
        x_units.append(swapped(sent[stage], "tm", 2))
        y_units = swapped(sent[stage], "tm", 4)
        y_other = swapped(y_units, "tm", 1)
        operands = [whole, sibling, y_units, y_other, *x_units, *left, *cross]
        after = ([], [own], totals[:1])[stage]
        hands_on = stage + 2 if stage + 2 < len(STAGES) else None
        out_shape = message(len(stage_blocks(stage))) + [units(len(fresh))] * 3
        if hands_on is not None:
            out_shape.append(units(len(STAGES[hands_on])))
        stay, away, left_now, cross_now, _, *later = in_order(
            functools.partial(stage_kernel, down, stage, len(after), hands_on), out_shape, len(operands), len(after)
        )(*operands, *after)
        left.append(left_now)
        cross.append(cross_now)
        sent.extend(later)
        totals.append(summed(half_summed(stay, away)))

    parts = []
    for first, last in GOES:
        near, other = [], []
        for stage in range(first, last):
            n = len(x_blocks(stage))
            near.append(totals[stage][:n])
            other.append(totals[stage][n : 2 * n])
        near, other = jnp.concatenate(near), jnp.concatenate(other)
        handed = swapped(near.astype(jnp.float16), "tm", 4, lambda i: i & 2)
        parts.append(jnp.where(far == 1, handed.astype(jnp.float32), near))
        pairs = [(i, i ^ (5 if i & 2 else 1)) for i in range(lax.axis_size("tm"))]
        parts.append(lax.ppermute(other.astype(jnp.float16), "tm", pairs).astype(jnp.float32))
    parts += [total[2 * len(x_blocks(stage)) :] for stage, total in enumerate(totals)]
    out_shape = jax.ShapeDtypeStruct((5, rows, rows // 4), jnp.float32)
    operands = [own, *parts]
    band = in_order(functools.partial(assemble_kernel, scale), out_shape, len(operands))(*operands)
    return band.transpose(1, 0, 2)


def local(snapshots, outlier_cols, outlier_values, threshold):
    if lax.axis_size("tm") == 8 and lax.axis_size("space") == 4:
        return square(snapshots, outlier_cols, outlier_values, threshold)
    points = snapshots.shape[1] * lax.axis_size("space")
    band = ring(clean(snapshots, outlier_cols, outlier_values, threshold))
    return band * (1.0 / jnp.sqrt(jnp.float32(points)))


def solution(mesh):
    placed = (P("tm", "space"), P("tm", "space"), P("tm", "space", None, None), P())
    return jax.shard_map(
        local, mesh=mesh, in_specs=placed, out_specs=P("tm", None, "space"), check_vma=False
    )
```

time: 118 us -> 131 us (1.11)
  the two profiles are of different devices: /device:TPU:2 before, /device:TPU:3 now
where the time goes in v3:
time: 131 us
  waiting for transfers between devices  69.1 us (53%)
  starting transfers between devices  35.1 us (27%)
  Pallas kernels  15.4 us (12%)
  local copies, waits for them, and re-layouts  5.31 us (4%)
  other arithmetic  5.12 us (4%)
    ppermute x20, waiting for transfers between devices, swapped(): return lax.ppermute(x, axis, pairs)  67.3 us
    ppermute x20, starting transfers between devices, swapped(): return lax.ppermute(x, axis, pairs)  29 us
    pallas_call x3, Pallas kernels, square(): in_order(functools.partial(stage_kernel, down, stage, len(after), hands_o...  8.83 us
    ppermute x2, starting transfers between devices, square(): lax.ppermute(other.astype(jnp.float16), 'tm', pairs).astype(jnp.float32)  6.06 us
    unnamed x36, local copies, waits for them, and re-layouts  5.27 us
    pallas_call x1, Pallas kernels, square(): in_order(functools.partial(own_kernel, down), out_shape, 1)(whole)  2.93 us
    add x4, other arithmetic, half_summed(): stay + swapped(away.astype(jnp.float16), 'space', 1).astype(jnp.float32)  2.89 us
  transfers between devices with their start and end apart: 22, of which 9 were waited for; matrix products, arithmetic and copies ran while one was open for 3% of the time, Pallas kernels for 7%

profile of v3, /device:TPU:3, one launch (start us, length us, event | category | flops | bytes accessed | tf_op | source)
XLA Modules:
  0.0 131.0 jit_solution(16892705952769369789)
XLA Ops:
  0.7 1.6 %copy-done.6 = bf16[512,2048]{1,0:T(8,128)(2,1)S(1)} copy-done((bf16[512,2048]{1,0:T(8,128)(2,1)S(1)}, bf16[512,2048]{1,0:T(8,128)(2,1)}, u32[]{:S(2)}) %copy-start.6) | copy-done | bytes 2097176
  2.2 1.0 copy-done.11
  3.3 0.7 copy-done.16
  4.0 2.1 %shard_map.46 = (bf16[4,128,2048]{2,1,0:T(8,128)(2,1)S(1)}, bf16[256,2048]{1,0:T(8,128)(2,1)S(1)}, bf16[128,2048]{1,0:T(8,128)(2,1)S(1)}) custom-call(s32[4,4]{1,0:T(4,128)S(1)} %copy-done.16, f32[1]{0:T(128)} %bitcast.26.threshold_ref, bf16[512,2048]{1,0:T(8,128)(2,1)S(1)} %copy-done.6, bf16[4,4,128,128]{3,2,1,0:T(8,128)(2,1)S(1)} %copy-done.11), custom_call_target="tpu_custom_call" | custom-call | tf_op jit(solution)/shard_map/pallas_call | solution.py:123
  6.1 1.3 collective-permute-start.3
  7.4 2.9 %shard_map.47 = (f32[2,16,32,128]{3,2,1,0:T(8,128)S(1)}, f32[2,16,32,128]{3,2,1,0:T(8,128)S(1)}, bf16[4,128,2048]{2,1,0:T(8,128)(2,1)S(1)}) custom-call(bf16[4,128,2048]{2,1,0:T(8,128)(2,1)S(1)} %get-tuple-element.22.all_ref.refs_0_), custom_call_target="tpu_custom_call" | custom-call | flops 1000 | bytes 1000 | tf_op jit(solution)/shard_map/pallas_call | solution.py:320
  10.3 1.0 collective-permute-start.2
  11.4 1.4 %collective-permute-start = (f16[2,16,32,128]{3,2,1,0:T(8,128)(2,1)S(1)}, f16[2,16,32,128]{3,2,1,0:T(8,128)(2,1)S(1)}, u32[]{:S(2)}, u32[]{:S(2)}) collective-permute-start(f16[2,16,32,128]{3,2,1,0:T(8,128)(2,1)S(1)} %convert_element_type.72), channel_id=1, source_target_pairs={{0,1},{1,0},{2,3},{3,2},{4,5},{5,4},{6,7},{7,6},{8,9},{9,8},{10,11... | collective-permute-start | bytes 786440 | tf_op jit(solution)/shard_map/ppermute | solution.py:21
  12.7 0.2 collective-permute-start.5
  13.0 0.2 collective-permute-start.8
  13.2 16.9 %collective-permute-done.3.refs_2_ = bf16[256,2048]{1,0:T(8,128)(2,1)S(1)} collective-permute-done((bf16[256,2048]{1,0:T(8,128)(2,1)S(1)}, bf16[256,2048]{1,0:T(8,128)(2,1)S(1)}, u32[]{:S(2)}, u32[]{:S(2)}) %collective-permute-start.3) | collective-permute-done | bytes 1048608 | tf_op jit(solution)/shard_map/ppermute | solution.py:21
  30.2 2.7 %collective-permute-start.4 = (bf16[256,2048]{1,0:T(8,128)(2,1)S(1)}, bf16[256,2048]{1,0:T(8,128)(2,1)S(1)}, u32[]{:S(2)}, u32[]{:S(2)}) collective-permute-start(bf16[256,2048]{1,0:T(8,128)(2,1)S(1)} %collective-permute-done.3.refs_2_), channel_id=1, source_target_pairs={{0,4},{4,0},{8,12},{12,8},{16,20},{20,16},{24,28},{28,24},{1,5},{5... | collective-permute-start | bytes 3145736 | tf_op jit(solution)/shard_map/ppermute | solution.py:21
  32.9 0.1 convert_add_fusion.3
  33.0 2.4 %collective-permute-start.1 = (f16[16,32,128]{2,1,0:T(8,128)(2,1)S(1)}, f16[16,32,128]{2,1,0:T(8,128)(2,1)S(1)}, u32[]{:S(2)}, u32[]{:S(2)}) collective-permute-start(f16[16,32,128]{2,1,0:T(8,128)(2,1)S(1)} %fusion.7), channel_id=1, source_target_pairs={{0,2},{1,3},{2,0},{3,1},{4,6},{5,7},{6,4},{7,5},{8,10},{9,11},{10,... | collective-permute-start | bytes 393224 | tf_op jit(solution)/shard_map/ppermute | solution.py:21
  35.3 6.5 %collective-permute-done.1 = f16[16,32,128]{2,1,0:T(8,128)(2,1)S(1)} collective-permute-done((f16[16,32,128]{2,1,0:T(8,128)(2,1)S(1)}, f16[16,32,128]{2,1,0:T(8,128)(2,1)S(1)}, u32[]{:S(2)}, u32[]{:S(2)}) %collective-permute-start.1) | collective-permute-done | bytes 131104 | tf_op jit(solution)/shard_map/ppermute | solution.py:21
  41.9 0.4 collective-permute-start.10
  42.3 0.9 collective-permute-start.9
  43.2 2.7 %shard_map.48 = (f32[2,24,32,128]{3,2,1,0:T(8,128)S(1)}, f32[2,24,32,128]{3,2,1,0:T(8,128)S(1)}, bf16[256,2048]{1,0:T(8,128)(2,1)S(1)}, bf16[256,2048]{1,0:T(8,1...) custom-call(bf16[4,128,2048]{2,1,0:T(8,128)(2,1)S(1)} %get-tuple-element.22.all_ref.refs_0_, ...), custom_call_target="tpu_custom_call" | custom-call | flops 1000 | bytes 1000 | tf_op jit(solution)/shard_map/pallas_call | solution.py:334
  45.9 0.9 copy-done.9
  46.8 7.7 %collective-permute-done.10.refs_5_ = bf16[128,2048]{1,0:T(8,128)(2,1)S(1)} collective-permute-done((bf16[128,2048]{1,0:T(8,128)(2,1)S(1)}, bf16[128,2048]{1,0:T(8,128)(2,1)S(1)}, u32[]{:S(2)}, u32[]{:S(2)}) %collective-permute-start.10) | collective-permute-done | bytes 524320 | tf_op jit(solution)/shard_map/ppermute | solution.py:21
  54.5 2.7 %shard_map.49 = (f32[2,18,32,128]{3,2,1,0:T(8,128)S(1)}, f32[2,18,32,128]{3,2,1,0:T(8,128)S(1)}, bf16[128,2048]{1,0:T(8,128)(2,1)S(1)}, bf16[128,2048]{1,0:T(8,128)(2,1)S(1)}, bf16[128,2048]{1,0:T(8,128)(2,1)}) custom-call(bf16[4,128,2048]{2,1,0:T(8,128)(2,1)S(1)} %get-tuple-element.22.all_ref.refs_0_, ...), custom_call_target="tpu_custom_call" | custom-call | flops 1000 | bytes 1000 | tf_op jit(solution)/shard_map/pallas_call | solution.py:334
  57.3 0.9 convert_element_type.80
  58.2 1.1 collective-permute-start.11
  59.3 0.8 convert_element_type.76
  60.1 0.4 collective-permute-start.6
  60.5 1.2 collective-permute-start.15
  61.7 0.3 collective-permute-start.17
  62.0 3.4 %collective-permute-done.11 = f16[2,18,32,128]{3,2,1,0:T(8,128)(2,1)} collective-permute-done((f16[2,18,32,128]{3,2,1,0:T(8,128)(2,1)}, f16[2,18,32,128]{3,2,1,0:T(8,128)(2,1)}, u32[]{:S(2)}, u32[]{:S(2)}) %collective-permute-start.11) | collective-permute-done | bytes 294944 | tf_op jit(solution)/shard_map/ppermute | solution.py:21
  65.3 1.3 %convert_add_fusion.2 = f32[2,18,32,128]{3,2,1,0:T(8,128)S(1)} fusion(f32[2,18,32,128]{3,2,1,0:T(8,128)} %copy-done.10, f16[2,18,32,128]{3,2,1,0:T(8,128)(2,1)} %collective-permute-done.11), kind=kLoop, calls=%fused_computation.2 | loop fusion | flops 294912 | bytes 1474560 | tf_op jit(solution)/shard_map/add | solution.py:313
  66.7 7.0 %collective-permute-done.6 = f16[2,24,32,128]{3,2,1,0:T(8,128)(2,1)} collective-permute-done((f16[2,24,32,128]{3,2,1,0:T(8,128)(2,1)}, f16[2,24,32,128]{3,2,1,0:T(8,128)(2,1)}, u32[]{:S(2)}, u32[]{:S(2)}) %collective-permute-start.6) | collective-permute-done | bytes 393248 | tf_op jit(solution)/shard_map/ppermute | solution.py:21
  73.8 1.4 %convert_add_fusion = f32[2,24,32,128]{3,2,1,0:T(8,128)S(1)} fusion(f32[2,24,32,128]{3,2,1,0:T(8,128)} %copy-done.9, f16[2,24,32,128]{3,2,1,0:T(8,128)(2,1)} %collective-permute-done.6), kind=kLoop, calls=%fused_computation | loop fusion | flops 393216 | bytes 1966080 | tf_op jit(solution)/shard_map/add | solution.py:313
  75.1 2.7 %collective-permute-start.16 = (bf16[128,2048]{1,0:T(8,128)(2,1)S(1)}, bf16[128,2048]{1,0:T(8,128)(2,1)S(1)}, u32[]{:S(2)}, u32[]{:S(2)}) collective-permute-start(bf16[128,2048]{1,0:T(8,128)(2,1)S(1)} %collective-permute-done.15.refs_2_), channel_id=1, source_target_pairs={{0,4},{4,0},{8,12},{12,8},{16,20},{20,16},{24,28},{28,24},{1,5},{5... | collective-permute-start | bytes 1572872 | tf_op jit(solution)/shard_map/ppermute | solution.py:21
  77.8 2.8 %collective-permute-start.7 = (f16[24,32,128]{2,1,0:T(8,128)(2,1)S(1)}, f16[24,32,128]{2,1,0:T(8,128)(2,1)S(1)}, u32[]{:S(2)}, u32[]{:S(2)}) collective-permute-start(f16[24,32,128]{2,1,0:T(8,128)(2,1)S(1)} %fusion.4), channel_id=1, source_target_pairs={{0,2},{1,3},{2,0},{3,1},{4,6},{5,7},{6,4},{7,5},{8,10},{9,11},{10,... | collective-permute-start | bytes 589832 | tf_op jit(solution)/shard_map/ppermute | solution.py:21
  80.7 0.1 collective-permute-start.12
  80.8 12.5 %collective-permute-done.7 = f16[24,32,128]{2,1,0:T(8,128)(2,1)S(1)} collective-permute-done((f16[24,32,128]{2,1,0:T(8,128)(2,1)S(1)}, f16[24,32,128]{2,1,0:T(8,128)(2,1)S(1)}, u32[]{:S(2)}, u32[]{:S(2)}) %collective-permute-start.7) | collective-permute-done | bytes 196640 | tf_op jit(solution)/shard_map/ppermute | solution.py:21
  93.4 1.0 copy-done.15
  94.5 3.4 %shard_map.50 = (f32[2,22,32,128]{3,2,1,0:T(8,128)S(1)}, f32[2,22,32,128]{3,2,1,0:T(8,128)S(1)}, bf16[128,2048]{1,0:T(8,128)(2,1)}, bf16[128,2048]{1,0:T(8,128)(2,1)}, bf16[128,2048]{1,0:T(8,128)(2,1)}) custom-call(bf16[4,128,2048]{2,1,0:T(8,128)(2,1)S(1)} %get-tuple-element.22.all_ref.refs_0_, bf16[4,128,2048]{2,1,0:T(8,128)(2,1)S(1)} %copy-done.1, ...), custom_call_target="tpu_custom_call" | custom-call | flops 1000 | bytes 1000 | tf_op jit(solution)/shard_map/pallas_call | solution.py:334
  97.9 0.7 collective-permute-start.18
  98.7 8.5 %collective-permute-done.18 = f16[2,22,32,128]{3,2,1,0:T(8,128)(2,1)S(1)} collective-permute-done((f16[2,22,32,128]{3,2,1,0:T(8,128)(2,1)S(1)}, f16[2,22,32,128]{3,2,1,0:T(8,128)(2,1)S(1)}, u32[]{:S(2)}, u32[]{:S(2)}) %collective-permute-start.18) | collective-permute-done | bytes 360480 | tf_op jit(solution)/shard_map/ppermute | solution.py:21
  107.1 0.1 convert_add_fusion.1
  107.3 3.0 %collective-permute-start.19 = (f16[22,32,128]{2,1,0:T(8,128)(2,1)S(1)}, f16[22,32,128]{2,1,0:T(8,128)(2,1)S(1)}, u32[]{:S(2)}, u32[]{:S(2)}) collective-permute-start(f16[22,32,128]{2,1,0:T(8,128)(2,1)S(1)} %fusion.5), channel_id=1, source_target_pairs={{0,2},{1,3},{2,0},{3,1},{4,6},{5,7},{6,4},{7,5},{8,10},{9,11},{10,... | collective-permute-start | bytes 540680 | tf_op jit(solution)/shard_map/ppermute | solution.py:21
  110.3 3.2 %collective-permute-start.13 = (f16[9,32,128]{2,1,0:T(8,128)(2,1)S(1)}, f16[9,32,128]{2,1,0:T(8,128)(2,1)S(1)}, u32[]{:S(2)}, u32[]{:S(2)}) collective-permute-start(f16[9,32,128]{2,1,0:T(8,128)(2,1)S(1)} %fusion.8), channel_id=1, source_target_pairs={{8,24},{12,28},{24,8},{28,12},{9,25},{13,29},{25,9},{29,13},{10,26... | collective-permute-start | bytes 221192 | tf_op jit(solution)/shard_map/ppermute | solution.py:21
  113.5 4.7 %collective-permute-done.19 = f16[22,32,128]{2,1,0:T(8,128)(2,1)S(1)} collective-permute-done((f16[22,32,128]{2,1,0:T(8,128)(2,1)S(1)}, f16[22,32,128]{2,1,0:T(8,128)(2,1)S(1)}, u32[]{:S(2)}, u32[]{:S(2)}) %collective-permute-start.19) | collective-permute-done | bytes 180256 | tf_op jit(solution)/shard_map/ppermute | solution.py:21
  118.3 3.2 %collective-permute-start.20 = (f16[7,32,128]{2,1,0:T(8,128)(2,1)S(1)}, f16[7,32,128]{2,1,0:T(8,128)(2,1)S(1)}, u32[]{:S(2)}, u32[]{:S(2)}) collective-permute-start(f16[7,32,128]{2,1,0:T(8,128)(2,1)S(1)} %slice_convert_fusion.5), channel_id=1, source_target_pairs={{8,24},{12,28},{24,8},{28,12},{9,25},{13,29},{25,9},{29,13},{10,26... | collective-permute-start | bytes 172040 | tf_op jit(solution)/shard_map/ppermute | solution.py:21
  121.5 1.9 %collective-permute-start.14 = (f16[9,32,128]{2,1,0:T(8,128)(2,1)S(1)}, f16[9,32,128]{2,1,0:T(8,128)(2,1)S(1)}, u32[]{:S(2)}, u32[]{:S(2)}) collective-permute-start(f16[9,32,128]{2,1,0:T(8,128)(2,1)S(1)} %pad_maximum_fusion.1), channel_id=1, source_target_pairs={{0,4},{4,0},{8,28},{12,24},{16,20},{20,16},{24,12},{28,8},{1,5},{5... | collective-permute-start | bytes 221192 | tf_op jit(solution)/shard_map/ppermute | solution.py:353
  123.4 4.2 %collective-permute-start.21 = (f16[7,32,128]{2,1,0:T(8,128)(2,1)S(1)}, f16[7,32,128]{2,1,0:T(8,128)(2,1)S(1)}, u32[]{:S(2)}, u32[]{:S(2)}) collective-permute-start(f16[7,32,128]{2,1,0:T(8,128)(2,1)S(1)} %get-tuple-element.41), channel_id=1, source_target_pairs={{0,4},{4,0},{8,28},{12,24},{16,20},{20,16},{24,12},{28,8},{1,5},{5... | collective-permute-start | bytes 172040 | tf_op jit(solution)/shard_map/ppermute | solution.py:353
  127.7 1.8 %collective-permute-done.21 = f16[7,32,128]{2,1,0:T(8,128)(2,1)S(1)} collective-permute-done((f16[7,32,128]{2,1,0:T(8,128)(2,1)S(1)}, f16[7,32,128]{2,1,0:T(8,128)(2,1)S(1)}, u32[]{:S(2)}, u32[]{:S(2)}) %collective-permute-start.21) | collective-permute-done | bytes 57376 | tf_op jit(solution)/shard_map/ppermute | solution.py:353
  129.5 1.5 %shard_map.51 = f32[5,512,128]{2,1,0:T(8,128)} custom-call(f32[16,32,128]{2,1,0:T(8,128)S(1)} %fusion.3.refs_8_.refs_0_, f32[9,32,128]{2,1,0:T(8,128)S(1)} %convert_select_fusion.refs_1_, f32[9,32,128]{2,1,0:T(8,128)S(1)} %convert_element_type.86.refs_2_, f32[7,32,128]{2,1,0:T(8,128)S(1)} %get-tuple-element.42.refs_3_, ...), custom_call_target="tpu_custom_call" | custom-call | flops 1000 | bytes 1000 | tf_op jit(solution)/shard_map/pallas_call | solution.py:357
  (66 shorter events, 0.7 us)
Async XLA Ops:
  0.7 1.6 %copy-start.6 = (bf16[512,2048]{1,0:T(8,128)(2,1)S(1)}, bf16[512,2048]{1,0:T(8,128)(2,1)}, u32[]{:S(2)}) copy-start(bf16[512,2048]{1,0:T(8,128)(2,1)} %snapshots_hbm.1) | copy-start | bytes 6291460
  2.2 1.0 copy-start.11
  3.3 0.7 copy-start.16
  6.1 24.1 %collective-permute-start.3 = (bf16[256,2048]{1,0:T(8,128)(2,1)S(1)}, bf16[256,2048]{1,0:T(8,128)(2,1)S(1)}, u32[]{:S(2)}, u32[]{:S(2)}) collective-permute-start(bf16[256,2048]{1,0:T(8,128)(2,1)S(1)} %get-tuple-element.26), channel_id=1, source_target_pairs={{0,16},{4,20},{8,24},{12,28},{16,0},{20,4},{24,8},{28,12},{1,17},{... | collective-permute-start | bytes 3145736 | tf_op jit(solution)/shard_map/ppermute | solution.py:21
  10.3 32.9 %collective-permute-start.2 = (bf16[4,128,2048]{2,1,0:T(8,128)(2,1)S(1)}, bf16[4,128,2048]{2,1,0:T(8,128)(2,1)S(1)}, u32[]{:S(2)}, u32[]{:S(2)}) collective-permute-start(bf16[4,128,2048]{2,1,0:T(8,128)(2,1)S(1)} %get-tuple-element.25), channel_id=1, source_target_pairs={{0,4},{4,0},{8,12},{12,8},{16,20},{20,16},{24,28},{28,24},{1,5},{5... | collective-permute-start | bytes 6291464 | tf_op jit(solution)/shard_map/ppermute | solution.py:21
  11.4 21.5 %collective-permute-start = (f16[2,16,32,128]{3,2,1,0:T(8,128)(2,1)S(1)}, f16[2,16,32,128]{3,2,1,0:T(8,128)(2,1)S(1)}, u32[]{:S(2)}, u32[]{:S(2)}) collective-permute-start(f16[2,16,32,128]{3,2,1,0:T(8,128)(2,1)S(1)} %convert_element_type.72), channel_id=1, source_target_pairs={{0,1},{1,0},{2,3},{3,2},{4,5},{5,4},{6,7},{7,6},{8,9},{9,8},{10,11... | collective-permute-start | bytes 786440 | tf_op jit(solution)/shard_map/ppermute | solution.py:21
  12.7 30.4 %collective-permute-start.5 = (bf16[256,2048]{1,0:T(8,128)(2,1)S(1)}, bf16[256,2048]{1,0:T(8,128)(2,1)S(1)}, u32[]{:S(2)}, u32[]{:S(2)}) collective-permute-start(bf16[256,2048]{1,0:T(8,128)(2,1)S(1)} %get-tuple-element.26), channel_id=1, source_target_pairs={{0,8},{4,12},{8,0},{12,4},{16,24},{20,28},{24,16},{28,20},{1,9},{5... | collective-permute-start | bytes 3145736 | tf_op jit(solution)/shard_map/ppermute | solution.py:21
  13.0 29.3 %collective-permute-start.8 = (bf16[128,2048]{1,0:T(8,128)(2,1)S(1)}, bf16[128,2048]{1,0:T(8,128)(2,1)S(1)}, u32[]{:S(2)}, u32[]{:S(2)}) collective-permute-start(bf16[128,2048]{1,0:T(8,128)(2,1)S(1)} %get-tuple-element.29), channel_id=1, source_target_pairs={{0,16},{4,20},{8,24},{12,28},{16,0},{20,4},{24,8},{28,12},{1,17},{... | collective-permute-start | bytes 1572872 | tf_op jit(solution)/shard_map/ppermute | solution.py:21
  30.2 13.1 %collective-permute-start.4 = (bf16[256,2048]{1,0:T(8,128)(2,1)S(1)}, bf16[256,2048]{1,0:T(8,128)(2,1)S(1)}, u32[]{:S(2)}, u32[]{:S(2)}) collective-permute-start(bf16[256,2048]{1,0:T(8,128)(2,1)S(1)} %collective-permute-done.3.refs_2_), channel_id=1, source_target_pairs={{0,4},{4,0},{8,12},{12,8},{16,20},{20,16},{24,28},{28,24},{1,5},{5... | collective-permute-start | bytes 3145736 | tf_op jit(solution)/shard_map/ppermute | solution.py:21
  33.0 8.9 %collective-permute-start.1 = (f16[16,32,128]{2,1,0:T(8,128)(2,1)S(1)}, f16[16,32,128]{2,1,0:T(8,128)(2,1)S(1)}, u32[]{:S(2)}, u32[]{:S(2)}) collective-permute-start(f16[16,32,128]{2,1,0:T(8,128)(2,1)S(1)} %fusion.7), channel_id=1, source_target_pairs={{0,2},{1,3},{2,0},{3,1},{4,6},{5,7},{6,4},{7,5},{8,10},{9,11},{10,... | collective-permute-start | bytes 393224 | tf_op jit(solution)/shard_map/ppermute | solution.py:21
  41.9 12.7 %collective-permute-start.10 = (bf16[128,2048]{1,0:T(8,128)(2,1)S(1)}, bf16[128,2048]{1,0:T(8,128)(2,1)S(1)}, u32[]{:S(2)}, u32[]{:S(2)}) collective-permute-start(bf16[128,2048]{1,0:T(8,128)(2,1)S(1)} %get-tuple-element.29), channel_id=1, source_target_pairs={{0,8},{4,12},{8,0},{12,4},{16,24},{20,28},{24,16},{28,20},{1,9},{5... | collective-permute-start | bytes 1572872 | tf_op jit(solution)/shard_map/ppermute | solution.py:21
  42.3 12.3 %collective-permute-start.9 = (bf16[128,2048]{1,0:T(8,128)(2,1)S(1)}, bf16[128,2048]{1,0:T(8,128)(2,1)S(1)}, u32[]{:S(2)}, u32[]{:S(2)}) collective-permute-start(bf16[128,2048]{1,0:T(8,128)(2,1)S(1)} %collective-permute-done.8.refs_2_), channel_id=1, source_target_pairs={{0,4},{4,0},{8,12},{12,8},{16,20},{20,16},{24,28},{28,24},{1,5},{5... | collective-permute-start | bytes 1572872 | tf_op jit(solution)/shard_map/ppermute | solution.py:21
  43.2 11.3 %copy-start = (bf16[4,128,2048]{2,1,0:T(8,128)(2,1)}, bf16[4,128,2048]{2,1,0:T(8,128)(2,1)S(1)}, u32[]{:S(2)}) copy-start(bf16[4,128,2048]{2,1,0:T(8,128)(2,1)S(1)} %collective-permute-done.2.refs_1_) | copy-start | bytes 6291460
  45.9 0.9 copy-start.9
  46.8 10.5 %copy-start.2 = (bf16[256,2048]{1,0:T(8,128)(2,1)}, bf16[256,2048]{1,0:T(8,128)(2,1)S(1)}, u32[]{:S(2)}) copy-start(bf16[256,2048]{1,0:T(8,128)(2,1)S(1)} %get-tuple-element.30.refs_6_.refs_7_) | copy-start | bytes 3145732
  46.8 10.5 %copy-start.4 = (bf16[256,2048]{1,0:T(8,128)(2,1)}, bf16[256,2048]{1,0:T(8,128)(2,1)S(1)}, u32[]{:S(2)}) copy-start(bf16[256,2048]{1,0:T(8,128)(2,1)S(1)} %get-tuple-element.31.refs_7_.refs_9_) | copy-start | bytes 3145732
  46.8 10.5 %copy-start.17 = (bf16[128,2048]{1,0:T(8,128)(2,1)}, bf16[128,2048]{1,0:T(8,128)(2,1)S(1)}, u32[]{:S(2)}) copy-start(bf16[128,2048]{1,0:T(8,128)(2,1)S(1)} %get-tuple-element.34) | copy-start | bytes 1572868
  54.5 2.8 %copy-start.7 = (bf16[128,2048]{1,0:T(8,128)(2,1)}, bf16[128,2048]{1,0:T(8,128)(2,1)S(1)}, u32[]{:S(2)}) copy-start(bf16[128,2048]{1,0:T(8,128)(2,1)S(1)} %collective-permute-done.10.refs_5_) | copy-start | bytes 1572868
  57.3 2.8 %copy-start.10 = (f32[2,18,32,128]{3,2,1,0:T(8,128)}, f32[2,18,32,128]{3,2,1,0:T(8,128)S(1)}, u32[]{:S(2)}) copy-start(f32[2,18,32,128]{3,2,1,0:T(8,128)S(1)} %get-tuple-element.32) | copy-start | bytes 1769476
  57.3 3.2 %copy-start.12 = (bf16[128,2048]{1,0:T(8,128)(2,1)}, bf16[128,2048]{1,0:T(8,128)(2,1)S(1)}, u32[]{:S(2)}) copy-start(bf16[128,2048]{1,0:T(8,128)(2,1)S(1)} %get-tuple-element.35.refs_8_) | copy-start | bytes 1572868
  57.3 3.2 %copy-start.14 = (bf16[128,2048]{1,0:T(8,128)(2,1)}, bf16[128,2048]{1,0:T(8,128)(2,1)S(1)}, u32[]{:S(2)}) copy-start(bf16[128,2048]{1,0:T(8,128)(2,1)S(1)} %get-tuple-element.36.refs_10_) | copy-start | bytes 1572868
  58.2 7.1 %collective-permute-start.11 = (f16[2,18,32,128]{3,2,1,0:T(8,128)(2,1)}, f16[2,18,32,128]{3,2,1,0:T(8,128)(2,1)}, u32[]{:S(2)}, u32[]{:S(2)}) collective-permute-start(f16[2,18,32,128]{3,2,1,0:T(8,128)(2,1)} %convert_element_type.80), channel_id=1, source_target_pairs={{0,1},{1,0},{2,3},{3,2},{4,5},{5,4},{6,7},{7,6},{8,9},{9,8},{10,11... | collective-permute-start | bytes 884744 | tf_op jit(solution)/shard_map/ppermute | solution.py:21
  60.1 13.7 %collective-permute-start.6 = (f16[2,24,32,128]{3,2,1,0:T(8,128)(2,1)}, f16[2,24,32,128]{3,2,1,0:T(8,128)(2,1)}, u32[]{:S(2)}, u32[]{:S(2)}) collective-permute-start(f16[2,24,32,128]{3,2,1,0:T(8,128)(2,1)} %convert_element_type.76), channel_id=1, source_target_pairs={{0,1},{1,0},{2,3},{3,2},{4,5},{5,4},{6,7},{7,6},{8,9},{9,8},{10,11... | collective-permute-start | bytes 1179656 | tf_op jit(solution)/shard_map/ppermute | solution.py:21
  60.5 14.6 %collective-permute-start.15 = (bf16[128,2048]{1,0:T(8,128)(2,1)}, bf16[128,2048]{1,0:T(8,128)(2,1)S(1)}, u32[]{:S(2)}, u32[]{:S(2)}) collective-permute-start(bf16[128,2048]{1,0:T(8,128)(2,1)} %copy-done.17), channel_id=1, source_target_pairs={{0,16},{4,20},{8,24},{12,28},{16,0},{20,4},{24,8},{28,12},{1,17},{... | collective-permute-start | bytes 1572872 | tf_op jit(solution)/shard_map/ppermute | solution.py:21
  61.7 31.6 %collective-permute-start.17 = (bf16[128,2048]{1,0:T(8,128)(2,1)}, bf16[128,2048]{1,0:T(8,128)(2,1)S(1)}, u32[]{:S(2)}, u32[]{:S(2)}) collective-permute-start(bf16[128,2048]{1,0:T(8,128)(2,1)} %copy-done.17), channel_id=1, source_target_pairs={{0,8},{4,12},{8,0},{12,4},{16,24},{20,28},{24,16},{28,20},{1,9},{5... | collective-permute-start | bytes 1572872 | tf_op jit(solution)/shard_map/ppermute | solution.py:21
  65.3 28.1 %copy-start.5 = (bf16[256,2048]{1,0:T(8,128)(2,1)S(1)}, bf16[256,2048]{1,0:T(8,128)(2,1)}, u32[]{:S(2)}) copy-start(bf16[256,2048]{1,0:T(8,128)(2,1)} %copy-done.4) | copy-start | bytes 3145732
  65.3 28.1 %copy-start.13 = (bf16[128,2048]{1,0:T(8,128)(2,1)S(1)}, bf16[128,2048]{1,0:T(8,128)(2,1)}, u32[]{:S(2)}) copy-start(bf16[128,2048]{1,0:T(8,128)(2,1)} %copy-done.12) | copy-start | bytes 1572868
  66.7 26.7 %copy-start.1 = (bf16[4,128,2048]{2,1,0:T(8,128)(2,1)S(1)}, bf16[4,128,2048]{2,1,0:T(8,128)(2,1)}, u32[]{:S(2)}) copy-start(bf16[4,128,2048]{2,1,0:T(8,128)(2,1)} %copy-done) | copy-start | bytes 6291460
  66.7 26.7 %copy-start.3 = (bf16[256,2048]{1,0:T(8,128)(2,1)S(1)}, bf16[256,2048]{1,0:T(8,128)(2,1)}, u32[]{:S(2)}) copy-start(bf16[256,2048]{1,0:T(8,128)(2,1)} %copy-done.2) | copy-start | bytes 3145732
  66.7 26.7 %copy-start.8 = (bf16[128,2048]{1,0:T(8,128)(2,1)S(1)}, bf16[128,2048]{1,0:T(8,128)(2,1)}, u32[]{:S(2)}) copy-start(bf16[128,2048]{1,0:T(8,128)(2,1)} %copy-done.7) | copy-start | bytes 1572868
  75.1 18.3 %collective-permute-start.16 = (bf16[128,2048]{1,0:T(8,128)(2,1)S(1)}, bf16[128,2048]{1,0:T(8,128)(2,1)S(1)}, u32[]{:S(2)}, u32[]{:S(2)}) collective-permute-start(bf16[128,2048]{1,0:T(8,128)(2,1)S(1)} %collective-permute-done.15.refs_2_), channel_id=1, source_target_pairs={{0,4},{4,0},{8,12},{12,8},{16,20},{20,16},{24,28},{28,24},{1,5},{5... | collective-permute-start | bytes 1572872 | tf_op jit(solution)/shard_map/ppermute | solution.py:21
  77.8 15.5 %collective-permute-start.7 = (f16[24,32,128]{2,1,0:T(8,128)(2,1)S(1)}, f16[24,32,128]{2,1,0:T(8,128)(2,1)S(1)}, u32[]{:S(2)}, u32[]{:S(2)}) collective-permute-start(f16[24,32,128]{2,1,0:T(8,128)(2,1)S(1)} %fusion.4), channel_id=1, source_target_pairs={{0,2},{1,3},{2,0},{3,1},{4,6},{5,7},{6,4},{7,5},{8,10},{9,11},{10,... | collective-permute-start | bytes 589832 | tf_op jit(solution)/shard_map/ppermute | solution.py:21
  80.7 17.9 %collective-permute-start.12 = (f16[18,32,128]{2,1,0:T(8,128)(2,1)S(1)}, f16[18,32,128]{2,1,0:T(8,128)(2,1)S(1)}, u32[]{:S(2)}, u32[]{:S(2)}) collective-permute-start(f16[18,32,128]{2,1,0:T(8,128)(2,1)S(1)} %fusion.6), channel_id=1, source_target_pairs={{0,2},{1,3},{2,0},{3,1},{4,6},{5,7},{6,4},{7,5},{8,10},{9,11},{10,... | collective-permute-start | bytes 442376 | tf_op jit(solution)/shard_map/ppermute | solution.py:21
  93.4 1.0 copy-start.15
  97.9 9.2 %collective-permute-start.18 = (f16[2,22,32,128]{3,2,1,0:T(8,128)(2,1)S(1)}, f16[2,22,32,128]{3,2,1,0:T(8,128)(2,1)S(1)}, u32[]{:S(2)}, u32[]{:S(2)}) collective-permute-start(f16[2,22,32,128]{3,2,1,0:T(8,128)(2,1)S(1)} %convert_element_type.87), channel_id=1, source_target_pairs={{0,1},{1,0},{2,3},{3,2},{4,5},{5,4},{6,7},{7,6},{8,9},{9,8},{10,11... | collective-permute-start | bytes 1081352 | tf_op jit(solution)/shard_map/ppermute | solution.py:21
  107.3 10.9 %collective-permute-start.19 = (f16[22,32,128]{2,1,0:T(8,128)(2,1)S(1)}, f16[22,32,128]{2,1,0:T(8,128)(2,1)S(1)}, u32[]{:S(2)}, u32[]{:S(2)}) collective-permute-start(f16[22,32,128]{2,1,0:T(8,128)(2,1)S(1)} %fusion.5), channel_id=1, source_target_pairs={{0,2},{1,3},{2,0},{3,1},{4,6},{5,7},{6,4},{7,5},{8,10},{9,11},{10,... | collective-permute-start | bytes 540680 | tf_op jit(solution)/shard_map/ppermute | solution.py:21
  110.3 17.2 %collective-permute-start.13 = (f16[9,32,128]{2,1,0:T(8,128)(2,1)S(1)}, f16[9,32,128]{2,1,0:T(8,128)(2,1)S(1)}, u32[]{:S(2)}, u32[]{:S(2)}) collective-permute-start(f16[9,32,128]{2,1,0:T(8,128)(2,1)S(1)} %fusion.8), channel_id=1, source_target_pairs={{8,24},{12,28},{24,8},{28,12},{9,25},{13,29},{25,9},{29,13},{10,26... | collective-permute-start | bytes 221192 | tf_op jit(solution)/shard_map/ppermute | solution.py:21
  118.3 5.1 %collective-permute-start.20 = (f16[7,32,128]{2,1,0:T(8,128)(2,1)S(1)}, f16[7,32,128]{2,1,0:T(8,128)(2,1)S(1)}, u32[]{:S(2)}, u32[]{:S(2)}) collective-permute-start(f16[7,32,128]{2,1,0:T(8,128)(2,1)S(1)} %slice_convert_fusion.5), channel_id=1, source_target_pairs={{8,24},{12,28},{24,8},{28,12},{9,25},{13,29},{25,9},{29,13},{10,26... | collective-permute-start | bytes 172040 | tf_op jit(solution)/shard_map/ppermute | solution.py:21
  121.5 6.1 %collective-permute-start.14 = (f16[9,32,128]{2,1,0:T(8,128)(2,1)S(1)}, f16[9,32,128]{2,1,0:T(8,128)(2,1)S(1)}, u32[]{:S(2)}, u32[]{:S(2)}) collective-permute-start(f16[9,32,128]{2,1,0:T(8,128)(2,1)S(1)} %pad_maximum_fusion.1), channel_id=1, source_target_pairs={{0,4},{4,0},{8,28},{12,24},{16,20},{20,16},{24,12},{28,8},{1,5},{5... | collective-permute-start | bytes 221192 | tf_op jit(solution)/shard_map/ppermute | solution.py:353
  123.4 6.0 %collective-permute-start.21 = (f16[7,32,128]{2,1,0:T(8,128)(2,1)S(1)}, f16[7,32,128]{2,1,0:T(8,128)(2,1)S(1)}, u32[]{:S(2)}, u32[]{:S(2)}) collective-permute-start(f16[7,32,128]{2,1,0:T(8,128)(2,1)S(1)} %get-tuple-element.41), channel_id=1, source_target_pairs={{0,4},{4,0},{8,28},{12,24},{16,20},{20,16},{24,12},{28,8},{1,5},{5... | collective-permute-start | bytes 172040 | tf_op jit(solution)/shard_map/ppermute | solution.py:353

commit v4 on v3

--- a/solution.py
+++ b/solution.py
@@ -120,6 +120,7 @@
     out_shape = [jax.ShapeDtypeStruct((UNITS, length, points), jnp.bfloat16)]
     out_shape += [jax.ShapeDtypeStruct((len(units) * length, points), jnp.bfloat16) for units in STAGES[:first]]
     hbm = pl.BlockSpec(memory_space=pltpu.HBM)
+    stay_put = functools.partial(pltpu.with_memory_space_constraint, memory_space=pltpu.HBM)
     return pl.pallas_call(
         clean_kernel,
         out_shape=out_shape,
@@ -134,7 +135,7 @@
             pltpu.SemaphoreType.DMA((tile_rows,)),
         ],
         compiler_params=pltpu.CompilerParams(vmem_limit_bytes=40 << 20),
-    )(outlier_cols, threshold.reshape(1), snapshots, outlier_values)
+    )(stay_put(outlier_cols), threshold.reshape(1), stay_put(snapshots), stay_put(outlier_values))
 
 
 def columns_of(ref):
@@ -176,7 +177,7 @@
     return names + [("y", key) for key in y_blocks(stage)] + [("side", key) for key in y_blocks(stage)]
 
 
-def stage_kernel(down, stage, n_after, hands_on, *refs):
+def stage_kernel(down, stage, n_after, *refs):
     refs = list(refs)
 
     def take(n):
@@ -199,10 +200,6 @@
 
     def units_of(stage_refs):
         return [unit_of(ref, i) for s, ref in enumerate(stage_refs) for i in range(len(STAGES[s]))]
-
-    if hands_on is not None:
-        for i, unit in enumerate(STAGES[hands_on]):
-            refs[0][i * length : (i + 1) * length] = all_ref[unit]
 
     for i, unit in enumerate(fresh):
         rows = slice(i * length, (i + 1) * length)
@@ -315,29 +312,31 @@
     def summed(kept):
         return kept[0] + swapped(kept[1].astype(jnp.float16), "space", 2).astype(jnp.float32)
 
-    whole, *sent = clean_units(snapshots, outlier_cols, outlier_values, threshold, 2)
+    whole, *sent = clean_units(snapshots, outlier_cols, outlier_values, threshold, len(STAGES))
     out_shape = message(UNITS * UNITS) + [jax.ShapeDtypeStruct(whole.shape, whole.dtype)]
     stay, away, lent = in_order(functools.partial(own_kernel, down), out_shape, 1)(whole)
     sibling = swapped(lent, "tm", 1)
-    own = summed(half_summed(stay, away))
+    halves = [half_summed(stay, away)]
+    own = summed(halves[0])
     x_units, left, cross, totals = [], [], [], []
     for stage, fresh in enumerate(STAGES):
-        x_units.append(swapped(sent[stage], "tm", 2))
-        y_units = swapped(sent[stage], "tm", 4)
-        y_other = swapped(y_units, "tm", 1)
+        block = sent[stage]
+        if stage > 0:
+            block, *_ = lax.optimization_barrier((block, x_units[-1], y_units))
+        x_units.append(swapped(block, "tm", 2))
+        y_units = swapped(block, "tm", 4)
+        y_other = swapped(lax.optimization_barrier((y_units, x_units[-1]))[0], "tm", 1)
         operands = [whole, sibling, y_units, y_other, *x_units, *left, *cross]
-        after = ([], [own], totals[:1])[stage]
-        hands_on = stage + 2 if stage + 2 < len(STAGES) else None
+        after = [own] if stage == 1 else totals[:-1] if stage > 1 else []
+        after = after + halves[-1:]
         out_shape = message(len(stage_blocks(stage))) + [units(len(fresh))] * 3
-        if hands_on is not None:
-            out_shape.append(units(len(STAGES[hands_on])))
-        stay, away, left_now, cross_now, _, *later = in_order(
-            functools.partial(stage_kernel, down, stage, len(after), hands_on), out_shape, len(operands), len(after)
+        stay, away, left_now, cross_now, _ = in_order(
+            functools.partial(stage_kernel, down, stage, len(after)), out_shape, len(operands), len(after)
         )(*operands, *after)
         left.append(left_now)
         cross.append(cross_now)
-        sent.extend(later)
-        totals.append(summed(half_summed(stay, away)))
+        halves.append(half_summed(stay, away))
+        totals.append(summed(halves[-1]))
 
     parts = []
     for first, last in GOES:

time: 131 us -> 120 us (0.916)
  waiting for transfers between devices: 69.1 us -> 51 us
  starting transfers between devices: 35.1 us -> 39 us
  Pallas kernels: 15.4 us -> 17.6 us
    ppermute x20, waiting for transfers between devices: 67.3 us -> 48.6 us  [swapped(): return lax.ppermute(x, axis, pairs)]
    ppermute x20, starting transfers between devices: 29 us -> 31.6 us  [swapped(): return lax.ppermute(x, axis, pairs)]
    add x4, other arithmetic: 2.89 us -> 1.54 us  [half_summed(): stay + swapped(away.astype(jnp.float16), 'space', 1).astype(jnp.float32)]
    unnamed x36 -> x28, local copies, waits for them, and re-layouts: 5.27 us -> 6.09 us
  transfers between devices with their start and end apart: 22 -> 22, of which waited for: 9 -> 10; matrix products, arithmetic and copies ran while one was open for 3% -> 4% of each run, Pallas kernels for 7% -> 7%
where the time goes in v4:
time: 120 us
  waiting for transfers between devices  51 us (42%)
  starting transfers between devices  39 us (32%)
  Pallas kernels  17.6 us (15%)
  local copies, waits for them, and re-layouts  6.13 us (5%)
  other arithmetic  4.78 us (4%)
    ppermute x20, waiting for transfers between devices, swapped(): return lax.ppermute(x, axis, pairs)  48.6 us
    ppermute x20, starting transfers between devices, swapped(): return lax.ppermute(x, axis, pairs)  31.6 us
    pallas_call x3, Pallas kernels, square(): in_order(functools.partial(stage_kernel, down, stage, len(after)), out_sh...  9.99 us
    ppermute x2, starting transfers between devices, square(): lax.ppermute(other.astype(jnp.float16), 'tm', pairs).astype(jnp.float32)  7.36 us
    unnamed x28, local copies, waits for them, and re-layouts  6.09 us
    pallas_call x1, Pallas kernels, clean_units(): pl.pallas_call(clean_kernel, out_shape=out_shape, in_specs=[hbm, pl.Block...  3.13 us
    pallas_call x1, Pallas kernels, square(): in_order(functools.partial(own_kernel, down), out_shape, 1)(whole)  2.93 us
    ppermute x2, waiting for transfers between devices, square(): lax.ppermute(other.astype(jnp.float16), 'tm', pairs).astype(jnp.float32)  2.41 us
  transfers between devices with their start and end apart: 22, of which 10 were waited for; matrix products, arithmetic and copies ran while one was open for 4% of the time, Pallas kernels for 7%

profile of v4, /device:TPU:3, one launch (start us, length us, event | category | flops | bytes accessed | tf_op | source)
XLA Modules:
  0.0 119.5 jit_solution(17186967009241947365)
XLA Ops:
  0.7 3.1 %shard_map.46 = (bf16[4,128,2048]{2,1,0:T(8,128)(2,1)S(1)}, bf16[256,2048]{1,0:T(8,128)(2,1)S(1)}, bf16[128,2048]{1,0:T(8,128)(2,1)S(1)}, bf16[128,2048]{1,0:T(8,128)(2,1)}) custom-call(s32[4,4]{1,0:T(4,128)} %cols_hbm.1, f32[1]{0:T(128)} %bitcast.26.threshold_ref, bf16[512,2048]{1,0:T(8,128)(2,1)} %snapshots_hbm.1, bf16[4,4,128,128]{3,2,1,0:T(8,128)(2,1)} %values_hbm.1), custom_call_target="tpu_custom_call" | custom-call | tf_op jit(solution)/shard_map/pallas_call | solution.py:124
  3.9 1.5 %collective-permute-start.3 = (bf16[256,2048]{1,0:T(8,128)(2,1)S(1)}, bf16[256,2048]{1,0:T(8,128)(2,1)S(1)}, u32[]{:S(2)}, u32[]{:S(2)}) collective-permute-start(bf16[256,2048]{1,0:T(8,128)(2,1)S(1)} %get-tuple-element.31), channel_id=1, source_target_pairs={{0,16},{4,20},{8,24},{12,28},{16,0},{20,4},{24,8},{28,12},{1,17},{... | collective-permute-start | bytes 3145736 | tf_op jit(solution)/shard_map/ppermute | solution.py:21
  5.4 2.9 %shard_map.47 = (f32[2,16,32,128]{3,2,1,0:T(8,128)S(1)}, f32[2,16,32,128]{3,2,1,0:T(8,128)S(1)}, bf16[4,128,2048]{2,1,0:T(8,128)(2,1)S(1)}) custom-call(bf16[4,128,2048]{2,1,0:T(8,128)(2,1)S(1)} %get-tuple-element.27.all_ref.refs_0_), custom_call_target="tpu_custom_call" | custom-call | flops 1000 | bytes 1000 | tf_op jit(solution)/shard_map/pallas_call | solution.py:317
  8.3 1.3 %collective-permute-start.2 = (bf16[4,128,2048]{2,1,0:T(8,128)(2,1)S(1)}, bf16[4,128,2048]{2,1,0:T(8,128)(2,1)S(1)}, u32[]{:S(2)}, u32[]{:S(2)}) collective-permute-start(bf16[4,128,2048]{2,1,0:T(8,128)(2,1)S(1)} %get-tuple-element.30), channel_id=1, source_target_pairs={{0,4},{4,0},{8,12},{12,8},{16,20},{20,16},{24,28},{28,24},{1,5},{5... | collective-permute-start | bytes 6291464 | tf_op jit(solution)/shard_map/ppermute | solution.py:21
  9.6 18.3 %collective-permute-done.4.refs_4_ = bf16[256,2048]{1,0:T(8,128)(2,1)S(1)} collective-permute-done((bf16[256,2048]{1,0:T(8,128)(2,1)S(1)}, bf16[256,2048]{1,0:T(8,128)(2,1)S(1)}, u32[]{:S(2)}, u32[]{:S(2)}) %collective-permute-start.4) | collective-permute-done | bytes 1048608 | tf_op jit(solution)/shard_map/ppermute | solution.py:21
  28.0 1.6 %collective-permute-start.5 = (bf16[256,2048]{1,0:T(8,128)(2,1)S(1)}, bf16[256,2048]{1,0:T(8,128)(2,1)S(1)}, u32[]{:S(2)}, u32[]{:S(2)}) collective-permute-start(bf16[256,2048]{1,0:T(8,128)(2,1)S(1)} %collective-permute-done.3.refs_2_), channel_id=1, source_target_pairs={{0,4},{4,0},{8,12},{12,8},{16,20},{20,16},{24,28},{28,24},{1,5},{5... | collective-permute-start | bytes 3145736 | tf_op jit(solution)/shard_map/ppermute | solution.py:21
  29.6 1.5 %collective-permute-start = (f16[2,16,32,128]{3,2,1,0:T(8,128)(2,1)S(1)}, f16[2,16,32,128]{3,2,1,0:T(8,128)(2,1)S(1)}, u32[]{:S(2)}, u32[]{:S(2)}) collective-permute-start(f16[2,16,32,128]{3,2,1,0:T(8,128)(2,1)S(1)} %convert_element_type.72), channel_id=1, source_target_pairs={{0,1},{1,0},{2,3},{3,2},{4,5},{5,4},{6,7},{7,6},{8,9},{9,8},{10,11... | collective-permute-start | bytes 786440 | tf_op jit(solution)/shard_map/ppermute | solution.py:21
  31.1 1.2 %collective-permute-start.9 = (bf16[128,2048]{1,0:T(8,128)(2,1)S(1)}, bf16[128,2048]{1,0:T(8,128)(2,1)S(1)}, u32[]{:S(2)}, u32[]{:S(2)}) collective-permute-start(bf16[128,2048]{1,0:T(8,128)(2,1)S(1)} %get-tuple-element.36), channel_id=1, source_target_pairs={{0,8},{4,12},{8,0},{12,4},{16,24},{20,28},{24,16},{28,20},{1,9},{5... | collective-permute-start | bytes 1572872 | tf_op jit(solution)/shard_map/ppermute | solution.py:21
  32.3 1.2 %collective-permute-start.8 = (bf16[128,2048]{1,0:T(8,128)(2,1)S(1)}, bf16[128,2048]{1,0:T(8,128)(2,1)S(1)}, u32[]{:S(2)}, u32[]{:S(2)}) collective-permute-start(bf16[128,2048]{1,0:T(8,128)(2,1)S(1)} %get-tuple-element.36), channel_id=1, source_target_pairs={{0,16},{4,20},{8,24},{12,28},{16,0},{20,4},{24,8},{28,12},{1,17},{... | collective-permute-start | bytes 1572872 | tf_op jit(solution)/shard_map/ppermute | solution.py:21
  33.5 4.1 %collective-permute-done = f16[2,16,32,128]{3,2,1,0:T(8,128)(2,1)S(1)} collective-permute-done((f16[2,16,32,128]{3,2,1,0:T(8,128)(2,1)S(1)}, f16[2,16,32,128]{3,2,1,0:T(8,128)(2,1)S(1)}, u32[]{:S(2)}, u32[]{:S(2)}) %collective-permute-start) | collective-permute-done | bytes 262176 | tf_op jit(solution)/shard_map/ppermute | solution.py:21
  37.7 2.7 %shard_map.48 = (f32[2,24,32,128]{3,2,1,0:T(8,128)S(1)}, f32[2,24,32,128]{3,2,1,0:T(8,128)S(1)}, bf16[256,2048]{1,0:T(8,128)(2,1)S(1)}, bf16[256,2048]{1,0:T(8,128)(2,1)S(1)}, bf16[256,2048]{1,0:T(8,128)(2,1)}) custom-call(bf16[4,128,2048]{2,1,0:T(8,128)(2,1)S(1)} %get-tuple-element.27.all_ref.refs_0_, ...), custom_call_target="tpu_custom_call" | custom-call | flops 1000 | bytes 1000 | tf_op jit(solution)/shard_map/pallas_call | solution.py:333
  40.5 1.5 %collective-permute-start.6 = (f16[2,24,32,128]{3,2,1,0:T(8,128)(2,1)S(1)}, f16[2,24,32,128]{3,2,1,0:T(8,128)(2,1)S(1)}, u32[]{:S(2)}, u32[]{:S(2)}) collective-permute-start(f16[2,24,32,128]{3,2,1,0:T(8,128)(2,1)S(1)} %convert_element_type.76), channel_id=1, source_target_pairs={{0,1},{1,0},{2,3},{3,2},{4,5},{5,4},{6,7},{7,6},{8,9},{9,8},{10,11... | collective-permute-start | bytes 1179656 | tf_op jit(solution)/shard_map/ppermute | solution.py:21
  42.0 2.4 %collective-permute-start.1 = (f16[16,32,128]{2,1,0:T(8,128)(2,1)S(1)}, f16[16,32,128]{2,1,0:T(8,128)(2,1)S(1)}, u32[]{:S(2)}, u32[]{:S(2)}) collective-permute-start(f16[16,32,128]{2,1,0:T(8,128)(2,1)S(1)} %fusion.7), channel_id=1, source_target_pairs={{0,2},{1,3},{2,0},{3,1},{4,6},{5,7},{6,4},{7,5},{8,10},{9,11},{10,... | collective-permute-start | bytes 393224 | tf_op jit(solution)/shard_map/ppermute | solution.py:21
  44.4 0.8 collective-permute-done.8.refs_2_
  45.2 1.2 %collective-permute-start.15 = (bf16[128,2048]{1,0:T(8,128)(2,1)}, bf16[128,2048]{1,0:T(8,128)(2,1)}, u32[]{:S(2)}, u32[]{:S(2)}) collective-permute-start(bf16[128,2048]{1,0:T(8,128)(2,1)} %get-tuple-element.43), channel_id=1, source_target_pairs={{0,16},{4,20},{8,24},{12,28},{16,0},{20,4},{24,8},{28,12},{1,17},{... | collective-permute-start | bytes 1572872 | tf_op jit(solution)/shard_map/ppermute | solution.py:21
  46.5 0.4 collective-permute-start.16
  46.9 1.9 %collective-permute-start.10 = (bf16[128,2048]{1,0:T(8,128)(2,1)S(1)}, bf16[128,2048]{1,0:T(8,128)(2,1)S(1)}, u32[]{:S(2)}, u32[]{:S(2)}) collective-permute-start(bf16[128,2048]{1,0:T(8,128)(2,1)S(1)} %collective-permute-done.8.refs_2_), channel_id=1, source_target_pairs={{0,4},{4,0},{8,12},{12,8},{16,20},{20,16},{24,28},{28,24},{1,5},{5... | collective-permute-start | bytes 1572872 | tf_op jit(solution)/shard_map/ppermute | solution.py:21
  48.8 4.5 %collective-permute-done.6 = f16[2,24,32,128]{3,2,1,0:T(8,128)(2,1)S(1)} collective-permute-done((f16[2,24,32,128]{3,2,1,0:T(8,128)(2,1)S(1)}, f16[2,24,32,128]{3,2,1,0:T(8,128)(2,1)S(1)}, u32[]{:S(2)}, u32[]{:S(2)}) %collective-permute-start.6) | collective-permute-done | bytes 393248 | tf_op jit(solution)/shard_map/ppermute | solution.py:21
  53.4 0.1 convert_add_fusion.refs_9_
  53.5 0.8 fusion.4
  54.3 1.4 %collective-permute-start.7 = (f16[24,32,128]{2,1,0:T(8,128)(2,1)}, f16[24,32,128]{2,1,0:T(8,128)(2,1)}, u32[]{:S(2)}, u32[]{:S(2)}) collective-permute-start(f16[24,32,128]{2,1,0:T(8,128)(2,1)} %fusion.4), channel_id=1, source_target_pairs={{0,2},{1,3},{2,0},{3,1},{4,6},{5,7},{6,4},{7,5},{8,10},{9,11},{10,... | collective-permute-start | bytes 589832 | tf_op jit(solution)/shard_map/ppermute | solution.py:21
  55.8 2.7 %shard_map.49 = (f32[2,18,32,128]{3,2,1,0:T(8,128)S(1)}, f32[2,18,32,128]{3,2,1,0:T(8,128)S(1)}, bf16[128,2048]{1,0:T(8,128)(2,1)S(1)}, bf16[128,2048]{1,0:T(8,128)(2,1)S(1)}, bf16[128,2048]{1,0:T(8,128)(2,1)}) custom-call(bf16[4,128,2048]{2,1,0:T(8,128)(2,1)S(1)} %get-tuple-element.27.all_ref.refs_0_, ...), custom_call_target="tpu_custom_call" | custom-call | flops 1000 | bytes 1000 | tf_op jit(solution)/shard_map/pallas_call | solution.py:333
  58.5 0.8 copy-done.10
  59.3 0.8 copy-done.12
  60.1 0.8 convert_element_type.80
  60.9 0.1 copy-done.9
  61.0 2.3 %collective-permute-start.11 = (f16[2,18,32,128]{3,2,1,0:T(8,128)(2,1)}, f16[2,18,32,128]{3,2,1,0:T(8,128)(2,1)}, u32[]{:S(2)}, u32[]{:S(2)}) collective-permute-start(f16[2,18,32,128]{3,2,1,0:T(8,128)(2,1)} %convert_element_type.80), channel_id=1, source_target_pairs={{0,1},{1,0},{2,3},{3,2},{4,5},{5,4},{6,7},{7,6},{8,9},{9,8},{10,11... | collective-permute-start | bytes 884744 | tf_op jit(solution)/shard_map/ppermute | solution.py:21
  63.4 2.2 %collective-permute-start.17 = (bf16[128,2048]{1,0:T(8,128)(2,1)}, bf16[128,2048]{1,0:T(8,128)(2,1)S(1)}, u32[]{:S(2)}, u32[]{:S(2)}) collective-permute-start(bf16[128,2048]{1,0:T(8,128)(2,1)} %collective-permute-done.15.refs_2_), channel_id=1, source_target_pairs={{0,4},{4,0},{8,12},{12,8},{16,20},{20,16},{24,28},{28,24},{1,5},{5... | collective-permute-start | bytes 1572872 | tf_op jit(solution)/shard_map/ppermute | solution.py:21
  65.6 1.1 fusion.refs_11_
  66.7 6.0 %collective-permute-done.11 = f16[2,18,32,128]{3,2,1,0:T(8,128)(2,1)} collective-permute-done((f16[2,18,32,128]{3,2,1,0:T(8,128)(2,1)}, f16[2,18,32,128]{3,2,1,0:T(8,128)(2,1)}, u32[]{:S(2)}, u32[]{:S(2)}) %collective-permute-start.11) | collective-permute-done | bytes 294944 | tf_op jit(solution)/shard_map/ppermute | solution.py:21
  72.7 1.2 %convert_add_fusion.2.refs_12_ = f32[2,18,32,128]{3,2,1,0:T(8,128)S(1)} fusion(f32[2,18,32,128]{3,2,1,0:T(8,128)} %copy-done.9, f16[2,18,32,128]{3,2,1,0:T(8,128)(2,1)} %collective-permute-done.11), kind=kLoop, calls=%fused_computation.2 | loop fusion | flops 294912 | bytes 1474560 | tf_op jit(solution)/shard_map/add | solution.py:310
  74.0 1.2 %copy-done.6 = bf16[256,2048]{1,0:T(8,128)(2,1)S(1)} copy-done((bf16[256,2048]{1,0:T(8,128)(2,1)S(1)}, bf16[256,2048]{1,0:T(8,128)(2,1)}, u32[]{:S(2)}) %copy-start.6) | copy-done | bytes 1048600
  75.2 1.0 copy-done.8
  76.2 1.0 copy-done.11
  77.3 1.0 copy-done.13
  78.3 4.6 %shard_map.50 = (f32[2,22,32,128]{3,2,1,0:T(8,128)S(1)}, f32[2,22,32,128]{3,2,1,0:T(8,128)S(1)}, bf16[128,2048]{1,0:T(8,128)(2,1)}, bf16[128,2048]{1,0:T(8,128)(2,1)}, bf16[128,2048]{1,0:T(8,128)(2,1)}) custom-call(bf16[4,128,2048]{2,1,0:T(8,128)(2,1)S(1)} %get-tuple-element.27.all_ref.refs_0_, bf16[4,128,2048]{2,1,0:T(8,128)(2,1)S(1)} %copy-done.1, ...), custom_call_target="tpu_custom_call" | custom-call | flops 1000 | bytes 1000 | tf_op jit(solution)/shard_map/pallas_call | solution.py:333
  83.0 2.8 %collective-permute-start.12 = (f16[18,32,128]{2,1,0:T(8,128)(2,1)S(1)}, f16[18,32,128]{2,1,0:T(8,128)(2,1)S(1)}, u32[]{:S(2)}, u32[]{:S(2)}) collective-permute-start(f16[18,32,128]{2,1,0:T(8,128)(2,1)S(1)} %fusion.6), channel_id=1, source_target_pairs={{0,2},{1,3},{2,0},{3,1},{4,6},{5,7},{6,4},{7,5},{8,10},{9,11},{10,... | collective-permute-start | bytes 442376 | tf_op jit(solution)/shard_map/ppermute | solution.py:21
  85.8 7.7 %collective-permute-done.12 = f16[18,32,128]{2,1,0:T(8,128)(2,1)S(1)} collective-permute-done((f16[18,32,128]{2,1,0:T(8,128)(2,1)S(1)}, f16[18,32,128]{2,1,0:T(8,128)(2,1)S(1)}, u32[]{:S(2)}, u32[]{:S(2)}) %collective-permute-start.12) | collective-permute-done | bytes 147488 | tf_op jit(solution)/shard_map/ppermute | solution.py:21
  93.6 1.9 %collective-permute-done.18 = f16[2,22,32,128]{3,2,1,0:T(8,128)(2,1)S(1)} collective-permute-done((f16[2,22,32,128]{3,2,1,0:T(8,128)(2,1)S(1)}, f16[2,22,32,128]{3,2,1,0:T(8,128)(2,1)S(1)}, u32[]{:S(2)}, u32[]{:S(2)}) %collective-permute-start.18) | collective-permute-done | bytes 360480 | tf_op jit(solution)/shard_map/ppermute | solution.py:21
  95.5 0.1 convert_add_fusion.1
  95.6 1.3 %collective-permute-start.19 = (f16[22,32,128]{2,1,0:T(8,128)(2,1)S(1)}, f16[22,32,128]{2,1,0:T(8,128)(2,1)S(1)}, u32[]{:S(2)}, u32[]{:S(2)}) collective-permute-start(f16[22,32,128]{2,1,0:T(8,128)(2,1)S(1)} %fusion.5), channel_id=1, source_target_pairs={{0,2},{1,3},{2,0},{3,1},{4,6},{5,7},{6,4},{7,5},{8,10},{9,11},{10,... | collective-permute-start | bytes 540680 | tf_op jit(solution)/shard_map/ppermute | solution.py:21
  97.0 2.9 %collective-permute-start.14 = (f16[9,32,128]{2,1,0:T(8,128)(2,1)S(1)}, f16[9,32,128]{2,1,0:T(8,128)(2,1)S(1)}, u32[]{:S(2)}, u32[]{:S(2)}) collective-permute-start(f16[9,32,128]{2,1,0:T(8,128)(2,1)S(1)} %pad_maximum_fusion.1), channel_id=1, source_target_pairs={{0,4},{4,0},{8,28},{12,24},{16,20},{20,16},{24,12},{28,8},{1,5},{5... | collective-permute-start | bytes 221192 | tf_op jit(solution)/shard_map/ppermute | solution.py:352
  99.9 5.3 %collective-permute-done.19 = f16[22,32,128]{2,1,0:T(8,128)(2,1)S(1)} collective-permute-done((f16[22,32,128]{2,1,0:T(8,128)(2,1)S(1)}, f16[22,32,128]{2,1,0:T(8,128)(2,1)S(1)}, u32[]{:S(2)}, u32[]{:S(2)}) %collective-permute-start.19) | collective-permute-done | bytes 180256 | tf_op jit(solution)/shard_map/ppermute | solution.py:21
  105.3 3.8 %collective-permute-start.20 = (f16[7,32,128]{2,1,0:T(8,128)(2,1)S(1)}, f16[7,32,128]{2,1,0:T(8,128)(2,1)S(1)}, u32[]{:S(2)}, u32[]{:S(2)}) collective-permute-start(f16[7,32,128]{2,1,0:T(8,128)(2,1)S(1)} %slice_convert_fusion.5), channel_id=1, source_target_pairs={{8,24},{12,28},{24,8},{28,12},{9,25},{13,29},{25,9},{29,13},{10,26... | collective-permute-start | bytes 172040 | tf_op jit(solution)/shard_map/ppermute | solution.py:21
  109.1 1.9 %collective-permute-start.13 = (f16[9,32,128]{2,1,0:T(8,128)(2,1)S(1)}, f16[9,32,128]{2,1,0:T(8,128)(2,1)S(1)}, u32[]{:S(2)}, u32[]{:S(2)}) collective-permute-start(f16[9,32,128]{2,1,0:T(8,128)(2,1)S(1)} %fusion.8), channel_id=1, source_target_pairs={{8,24},{12,28},{24,8},{28,12},{9,25},{13,29},{25,9},{29,13},{10,26... | collective-permute-start | bytes 221192 | tf_op jit(solution)/shard_map/ppermute | solution.py:21
  111.0 4.4 %collective-permute-start.21 = (f16[7,32,128]{2,1,0:T(8,128)(2,1)S(1)}, f16[7,32,128]{2,1,0:T(8,128)(2,1)S(1)}, u32[]{:S(2)}, u32[]{:S(2)}) collective-permute-start(f16[7,32,128]{2,1,0:T(8,128)(2,1)S(1)} %get-tuple-element.51), channel_id=1, source_target_pairs={{0,4},{4,0},{8,28},{12,24},{16,20},{20,16},{24,12},{28,8},{1,5},{5... | collective-permute-start | bytes 172040 | tf_op jit(solution)/shard_map/ppermute | solution.py:352
  115.5 2.4 %collective-permute-done.21 = f16[7,32,128]{2,1,0:T(8,128)(2,1)S(1)} collective-permute-done((f16[7,32,128]{2,1,0:T(8,128)(2,1)S(1)}, f16[7,32,128]{2,1,0:T(8,128)(2,1)S(1)}, u32[]{:S(2)}, u32[]{:S(2)}) %collective-permute-start.21) | collective-permute-done | bytes 57376 | tf_op jit(solution)/shard_map/ppermute | solution.py:352
  118.0 1.5 %shard_map.51 = f32[5,512,128]{2,1,0:T(8,128)} custom-call(f32[16,32,128]{2,1,0:T(8,128)S(1)} %fusion.3.refs_8_.refs_0_, f32[9,32,128]{2,1,0:T(8,128)S(1)} %convert_select_fusion.refs_1_, f32[9,32,128]{2,1,0:T(8,128)S(1)} %convert_element_type.86.refs_2_, f32[7,32,128]{2,1,0:T(8,128)S(1)} %get-tuple-element.52.refs_3_, ...), custom_call_target="tpu_custom_call" | custom-call | flops 1000 | bytes 1000 | tf_op jit(solution)/shard_map/pallas_call | solution.py:356
  (58 shorter events, 0.9 us)
Async XLA Ops:
  3.8 24.1 %collective-permute-start.4 = (bf16[256,2048]{1,0:T(8,128)(2,1)S(1)}, bf16[256,2048]{1,0:T(8,128)(2,1)S(1)}, u32[]{:S(2)}, u32[]{:S(2)}) collective-permute-start(bf16[256,2048]{1,0:T(8,128)(2,1)S(1)} %get-tuple-element.31), channel_id=1, source_target_pairs={{0,8},{4,12},{8,0},{12,4},{16,24},{20,28},{24,16},{28,20},{1,9},{5... | collective-permute-start | bytes 3145736 | tf_op jit(solution)/shard_map/ppermute | solution.py:21
  3.9 24.1 %collective-permute-start.3 = (bf16[256,2048]{1,0:T(8,128)(2,1)S(1)}, bf16[256,2048]{1,0:T(8,128)(2,1)S(1)}, u32[]{:S(2)}, u32[]{:S(2)}) collective-permute-start(bf16[256,2048]{1,0:T(8,128)(2,1)S(1)} %get-tuple-element.31), channel_id=1, source_target_pairs={{0,16},{4,20},{8,24},{12,28},{16,0},{20,4},{24,8},{28,12},{1,17},{... | collective-permute-start | bytes 3145736 | tf_op jit(solution)/shard_map/ppermute | solution.py:21
  8.3 29.4 %collective-permute-start.2 = (bf16[4,128,2048]{2,1,0:T(8,128)(2,1)S(1)}, bf16[4,128,2048]{2,1,0:T(8,128)(2,1)S(1)}, u32[]{:S(2)}, u32[]{:S(2)}) collective-permute-start(bf16[4,128,2048]{2,1,0:T(8,128)(2,1)S(1)} %get-tuple-element.30), channel_id=1, source_target_pairs={{0,4},{4,0},{8,12},{12,8},{16,20},{20,16},{24,28},{28,24},{1,5},{5... | collective-permute-start | bytes 6291464 | tf_op jit(solution)/shard_map/ppermute | solution.py:21
  28.0 9.7 %collective-permute-start.5 = (bf16[256,2048]{1,0:T(8,128)(2,1)S(1)}, bf16[256,2048]{1,0:T(8,128)(2,1)S(1)}, u32[]{:S(2)}, u32[]{:S(2)}) collective-permute-start(bf16[256,2048]{1,0:T(8,128)(2,1)S(1)} %collective-permute-done.3.refs_2_), channel_id=1, source_target_pairs={{0,4},{4,0},{8,12},{12,8},{16,20},{20,16},{24,28},{28,24},{1,5},{5... | collective-permute-start | bytes 3145736 | tf_op jit(solution)/shard_map/ppermute | solution.py:21
  29.6 8.0 %collective-permute-start = (f16[2,16,32,128]{3,2,1,0:T(8,128)(2,1)S(1)}, f16[2,16,32,128]{3,2,1,0:T(8,128)(2,1)S(1)}, u32[]{:S(2)}, u32[]{:S(2)}) collective-permute-start(f16[2,16,32,128]{3,2,1,0:T(8,128)(2,1)S(1)} %convert_element_type.72), channel_id=1, source_target_pairs={{0,1},{1,0},{2,3},{3,2},{4,5},{5,4},{6,7},{7,6},{8,9},{9,8},{10,11... | collective-permute-start | bytes 786440 | tf_op jit(solution)/shard_map/ppermute | solution.py:21
  31.1 13.3 %collective-permute-start.9 = (bf16[128,2048]{1,0:T(8,128)(2,1)S(1)}, bf16[128,2048]{1,0:T(8,128)(2,1)S(1)}, u32[]{:S(2)}, u32[]{:S(2)}) collective-permute-start(bf16[128,2048]{1,0:T(8,128)(2,1)S(1)} %get-tuple-element.36), channel_id=1, source_target_pairs={{0,8},{4,12},{8,0},{12,4},{16,24},{20,28},{24,16},{28,20},{1,9},{5... | collective-permute-start | bytes 1572872 | tf_op jit(solution)/shard_map/ppermute | solution.py:21
  32.3 12.9 %collective-permute-start.8 = (bf16[128,2048]{1,0:T(8,128)(2,1)S(1)}, bf16[128,2048]{1,0:T(8,128)(2,1)S(1)}, u32[]{:S(2)}, u32[]{:S(2)}) collective-permute-start(bf16[128,2048]{1,0:T(8,128)(2,1)S(1)} %get-tuple-element.36), channel_id=1, source_target_pairs={{0,16},{4,20},{8,24},{12,28},{16,0},{20,4},{24,8},{28,12},{1,17},{... | collective-permute-start | bytes 1572872 | tf_op jit(solution)/shard_map/ppermute | solution.py:21
  37.7 18.0 %copy-start = (bf16[4,128,2048]{2,1,0:T(8,128)(2,1)}, bf16[4,128,2048]{2,1,0:T(8,128)(2,1)S(1)}, u32[]{:S(2)}) copy-start(bf16[4,128,2048]{2,1,0:T(8,128)(2,1)S(1)} %collective-permute-done.2.refs_1_) | copy-start | bytes 6291460
  40.4 15.4 %copy-start.3 = (bf16[256,2048]{1,0:T(8,128)(2,1)}, bf16[256,2048]{1,0:T(8,128)(2,1)S(1)}, u32[]{:S(2)}) copy-start(bf16[256,2048]{1,0:T(8,128)(2,1)S(1)} %get-tuple-element.38.refs_6_.refs_7_) | copy-start | bytes 3145732
  40.4 15.4 %copy-start.5 = (bf16[256,2048]{1,0:T(8,128)(2,1)}, bf16[256,2048]{1,0:T(8,128)(2,1)S(1)}, u32[]{:S(2)}) copy-start(bf16[256,2048]{1,0:T(8,128)(2,1)S(1)} %get-tuple-element.39.refs_7_.refs_9_) | copy-start | bytes 3145732
  40.5 12.9 %collective-permute-start.6 = (f16[2,24,32,128]{3,2,1,0:T(8,128)(2,1)S(1)}, f16[2,24,32,128]{3,2,1,0:T(8,128)(2,1)S(1)}, u32[]{:S(2)}, u32[]{:S(2)}) collective-permute-start(f16[2,24,32,128]{3,2,1,0:T(8,128)(2,1)S(1)} %convert_element_type.76), channel_id=1, source_target_pairs={{0,1},{1,0},{2,3},{3,2},{4,5},{5,4},{6,7},{7,6},{8,9},{9,8},{10,11... | collective-permute-start | bytes 1179656 | tf_op jit(solution)/shard_map/ppermute | solution.py:21
  42.0 13.7 %collective-permute-start.1 = (f16[16,32,128]{2,1,0:T(8,128)(2,1)S(1)}, f16[16,32,128]{2,1,0:T(8,128)(2,1)S(1)}, u32[]{:S(2)}, u32[]{:S(2)}) collective-permute-start(f16[16,32,128]{2,1,0:T(8,128)(2,1)S(1)} %fusion.7), channel_id=1, source_target_pairs={{0,2},{1,3},{2,0},{3,1},{4,6},{5,7},{6,4},{7,5},{8,10},{9,11},{10,... | collective-permute-start | bytes 393224 | tf_op jit(solution)/shard_map/ppermute | solution.py:21
  44.4 14.1 %copy-start.7 = (bf16[128,2048]{1,0:T(8,128)(2,1)}, bf16[128,2048]{1,0:T(8,128)(2,1)S(1)}, u32[]{:S(2)}) copy-start(bf16[128,2048]{1,0:T(8,128)(2,1)S(1)} %collective-permute-done.9.refs_5_) | copy-start | bytes 1572868
  45.2 18.1 %collective-permute-start.15 = (bf16[128,2048]{1,0:T(8,128)(2,1)}, bf16[128,2048]{1,0:T(8,128)(2,1)}, u32[]{:S(2)}, u32[]{:S(2)}) collective-permute-start(bf16[128,2048]{1,0:T(8,128)(2,1)} %get-tuple-element.43), channel_id=1, source_target_pairs={{0,16},{4,20},{8,24},{12,28},{16,0},{20,4},{24,8},{28,12},{1,17},{... | collective-permute-start | bytes 1572872 | tf_op jit(solution)/shard_map/ppermute | solution.py:21
  46.5 16.9 %collective-permute-start.16 = (bf16[128,2048]{1,0:T(8,128)(2,1)}, bf16[128,2048]{1,0:T(8,128)(2,1)}, u32[]{:S(2)}, u32[]{:S(2)}) collective-permute-start(bf16[128,2048]{1,0:T(8,128)(2,1)} %get-tuple-element.43), channel_id=1, source_target_pairs={{0,8},{4,12},{8,0},{12,4},{16,24},{20,28},{24,16},{28,20},{1,9},{5... | collective-permute-start | bytes 1572872 | tf_op jit(solution)/shard_map/ppermute | solution.py:21
  46.9 8.8 %collective-permute-start.10 = (bf16[128,2048]{1,0:T(8,128)(2,1)S(1)}, bf16[128,2048]{1,0:T(8,128)(2,1)S(1)}, u32[]{:S(2)}, u32[]{:S(2)}) collective-permute-start(bf16[128,2048]{1,0:T(8,128)(2,1)S(1)} %collective-permute-done.8.refs_2_), channel_id=1, source_target_pairs={{0,4},{4,0},{8,12},{12,8},{16,20},{20,16},{24,28},{28,24},{1,5},{5... | collective-permute-start | bytes 1572872 | tf_op jit(solution)/shard_map/ppermute | solution.py:21
  53.5 5.0 %copy-start.2 = (f32[2,24,32,128]{3,2,1,0:T(8,128)}, f32[2,24,32,128]{3,2,1,0:T(8,128)S(1)}, u32[]{:S(2)}) copy-start(f32[2,24,32,128]{3,2,1,0:T(8,128)S(1)} %convert_add_fusion.refs_9_) | copy-start | bytes 2359300
  54.3 11.3 %collective-permute-start.7 = (f16[24,32,128]{2,1,0:T(8,128)(2,1)}, f16[24,32,128]{2,1,0:T(8,128)(2,1)}, u32[]{:S(2)}, u32[]{:S(2)}) collective-permute-start(f16[24,32,128]{2,1,0:T(8,128)(2,1)} %fusion.4), channel_id=1, source_target_pairs={{0,2},{1,3},{2,0},{3,1},{4,6},{5,7},{6,4},{7,5},{8,10},{9,11},{10,... | collective-permute-start | bytes 589832 | tf_op jit(solution)/shard_map/ppermute | solution.py:21
  58.5 0.8 copy-start.10
  59.3 0.8 copy-start.12
  60.1 0.9 copy-start.9
  61.0 11.6 %collective-permute-start.11 = (f16[2,18,32,128]{3,2,1,0:T(8,128)(2,1)}, f16[2,18,32,128]{3,2,1,0:T(8,128)(2,1)}, u32[]{:S(2)}, u32[]{:S(2)}) collective-permute-start(f16[2,18,32,128]{3,2,1,0:T(8,128)(2,1)} %convert_element_type.80), channel_id=1, source_target_pairs={{0,1},{1,0},{2,3},{3,2},{4,5},{5,4},{6,7},{7,6},{8,9},{9,8},{10,11... | collective-permute-start | bytes 884744 | tf_op jit(solution)/shard_map/ppermute | solution.py:21
  63.4 10.6 %copy-start.1 = (bf16[4,128,2048]{2,1,0:T(8,128)(2,1)S(1)}, bf16[4,128,2048]{2,1,0:T(8,128)(2,1)}, u32[]{:S(2)}) copy-start(bf16[4,128,2048]{2,1,0:T(8,128)(2,1)} %copy-done) | copy-start | bytes 6291460
  63.4 10.6 %copy-start.4 = (bf16[256,2048]{1,0:T(8,128)(2,1)S(1)}, bf16[256,2048]{1,0:T(8,128)(2,1)}, u32[]{:S(2)}) copy-start(bf16[256,2048]{1,0:T(8,128)(2,1)} %copy-done.3) | copy-start | bytes 3145732
  63.4 10.6 %collective-permute-start.17 = (bf16[128,2048]{1,0:T(8,128)(2,1)}, bf16[128,2048]{1,0:T(8,128)(2,1)S(1)}, u32[]{:S(2)}, u32[]{:S(2)}) collective-permute-start(bf16[128,2048]{1,0:T(8,128)(2,1)} %collective-permute-done.15.refs_2_), channel_id=1, source_target_pairs={{0,4},{4,0},{8,12},{12,8},{16,20},{20,16},{24,28},{28,24},{1,5},{5... | collective-permute-start | bytes 1572872 | tf_op jit(solution)/shard_map/ppermute | solution.py:21
  74.0 1.2 %copy-start.6 = (bf16[256,2048]{1,0:T(8,128)(2,1)S(1)}, bf16[256,2048]{1,0:T(8,128)(2,1)}, u32[]{:S(2)}) copy-start(bf16[256,2048]{1,0:T(8,128)(2,1)} %copy-done.5) | copy-start | bytes 3145732
  75.2 1.0 copy-start.8
  76.2 1.0 copy-start.11
  77.3 1.0 copy-start.13
  83.0 12.5 %collective-permute-start.18 = (f16[2,22,32,128]{3,2,1,0:T(8,128)(2,1)S(1)}, f16[2,22,32,128]{3,2,1,0:T(8,128)(2,1)S(1)}, u32[]{:S(2)}, u32[]{:S(2)}) collective-permute-start(f16[2,22,32,128]{3,2,1,0:T(8,128)(2,1)S(1)} %convert_element_type.87), channel_id=1, source_target_pairs={{0,1},{1,0},{2,3},{3,2},{4,5},{5,4},{6,7},{7,6},{8,9},{9,8},{10,11... | collective-permute-start | bytes 1081352 | tf_op jit(solution)/shard_map/ppermute | solution.py:21
  83.0 10.5 %collective-permute-start.12 = (f16[18,32,128]{2,1,0:T(8,128)(2,1)S(1)}, f16[18,32,128]{2,1,0:T(8,128)(2,1)S(1)}, u32[]{:S(2)}, u32[]{:S(2)}) collective-permute-start(f16[18,32,128]{2,1,0:T(8,128)(2,1)S(1)} %fusion.6), channel_id=1, source_target_pairs={{0,2},{1,3},{2,0},{3,1},{4,6},{5,7},{6,4},{7,5},{8,10},{9,11},{10,... | collective-permute-start | bytes 442376 | tf_op jit(solution)/shard_map/ppermute | solution.py:21
  95.6 9.6 %collective-permute-start.19 = (f16[22,32,128]{2,1,0:T(8,128)(2,1)S(1)}, f16[22,32,128]{2,1,0:T(8,128)(2,1)S(1)}, u32[]{:S(2)}, u32[]{:S(2)}) collective-permute-start(f16[22,32,128]{2,1,0:T(8,128)(2,1)S(1)} %fusion.5), channel_id=1, source_target_pairs={{0,2},{1,3},{2,0},{3,1},{4,6},{5,7},{6,4},{7,5},{8,10},{9,11},{10,... | collective-permute-start | bytes 540680 | tf_op jit(solution)/shard_map/ppermute | solution.py:21
  97.0 18.5 %collective-permute-start.14 = (f16[9,32,128]{2,1,0:T(8,128)(2,1)S(1)}, f16[9,32,128]{2,1,0:T(8,128)(2,1)S(1)}, u32[]{:S(2)}, u32[]{:S(2)}) collective-permute-start(f16[9,32,128]{2,1,0:T(8,128)(2,1)S(1)} %pad_maximum_fusion.1), channel_id=1, source_target_pairs={{0,4},{4,0},{8,28},{12,24},{16,20},{20,16},{24,12},{28,8},{1,5},{5... | collective-permute-start | bytes 221192 | tf_op jit(solution)/shard_map/ppermute | solution.py:352
  105.3 5.7 %collective-permute-start.20 = (f16[7,32,128]{2,1,0:T(8,128)(2,1)S(1)}, f16[7,32,128]{2,1,0:T(8,128)(2,1)S(1)}, u32[]{:S(2)}, u32[]{:S(2)}) collective-permute-start(f16[7,32,128]{2,1,0:T(8,128)(2,1)S(1)} %slice_convert_fusion.5), channel_id=1, source_target_pairs={{8,24},{12,28},{24,8},{28,12},{9,25},{13,29},{25,9},{29,13},{10,26... | collective-permute-start | bytes 172040 | tf_op jit(solution)/shard_map/ppermute | solution.py:21
  109.1 6.4 %collective-permute-start.13 = (f16[9,32,128]{2,1,0:T(8,128)(2,1)S(1)}, f16[9,32,128]{2,1,0:T(8,128)(2,1)S(1)}, u32[]{:S(2)}, u32[]{:S(2)}) collective-permute-start(f16[9,32,128]{2,1,0:T(8,128)(2,1)S(1)} %fusion.8), channel_id=1, source_target_pairs={{8,24},{12,28},{24,8},{28,12},{9,25},{13,29},{25,9},{29,13},{10,26... | collective-permute-start | bytes 221192 | tf_op jit(solution)/shard_map/ppermute | solution.py:21
  111.0 6.9 %collective-permute-start.21 = (f16[7,32,128]{2,1,0:T(8,128)(2,1)S(1)}, f16[7,32,128]{2,1,0:T(8,128)(2,1)S(1)}, u32[]{:S(2)}, u32[]{:S(2)}) collective-permute-start(f16[7,32,128]{2,1,0:T(8,128)(2,1)S(1)} %get-tuple-element.51), channel_id=1, source_target_pairs={{0,4},{4,0},{8,28},{12,24},{16,20},{20,16},{24,12},{28,8},{1,5},{5... | collective-permute-start | bytes 172040 | tf_op jit(solution)/shard_map/ppermute | solution.py:352

commit v5 on v4

v5 whole, which is shorter than its diff:
```python
import functools
import math

import jax
import jax.numpy as jnp
from jax import lax
from jax.experimental import pallas as pl
from jax.experimental.pallas import tpu as pltpu
from jax.sharding import PartitionSpec as P

ST = 128
SNAP_MAX = 6.0
OUTLIER_MAX = 12.0
UNITS = 4
GOES = ((0, UNITS - 1), (UNITS - 1, UNITS + 1))


def swapped(x, axis, bit, only=None):
    pairs = [(i, i ^ bit) for i in range(lax.axis_size(axis)) if only is None or only(i)]
    return lax.ppermute(x, axis, pairs)


def passed_along(x, axis, by):
    size = lax.axis_size(axis)
    return lax.ppermute(x, axis, [(i, (i + by) % size) for i in range(size)])


def tile_product(own, other):
    return lax.dot_general(own, other, (((1,), (1,)), ((), ())), preferred_element_type=jnp.float32)


def clean(snapshots, outlier_cols, outlier_values, threshold):
    block_rows, points = snapshots.shape
    tiles_dev = points // ST
    onehot = (
        outlier_cols[:, :, None] == jnp.arange(tiles_dev, dtype=jnp.int32)[None, None, :]
    ).astype(jnp.bfloat16)
    dense = jnp.einsum("rkos,rkn->rons", outlier_values, onehot, preferred_element_type=jnp.float32)
    dense = dense.reshape(block_rows, points)
    diff = snapshots.astype(jnp.float32) - dense
    return (jnp.sign(diff) * jnp.maximum(jnp.abs(diff) - threshold, 0.0)).astype(jnp.bfloat16)


def ring(cleaned):
    kept = [tile_product(cleaned, cleaned)]
    moving = cleaned
    for step in range(lax.axis_size("tm") // 2):
        moving = passed_along(moving, "tm", -1)
        kept.append(tile_product(cleaned, moving))
    return lax.psum_scatter(jnp.stack(kept, axis=1), "space", scatter_dimension=2, tiled=True)


def on_units(body, out_shape, n_in):
    whole = pl.BlockSpec(memory_space=pltpu.VMEM)
    return pl.pallas_call(
        body,
        out_shape=out_shape,
        in_specs=[whole] * n_in,
        out_specs=jax.tree.map(lambda _: whole, out_shape),
        compiler_params=pltpu.CompilerParams(vmem_limit_bytes=18 << 20),
        cost_estimate=pl.CostEstimate(flops=1000, bytes_accessed=1000, transcendentals=0),
    )


def clean_kernel(
    cols_hbm, threshold_ref, snapshots_hbm, values_hbm, all_ref, rest_ref, *refs
):
    *sent_refs, cols_ref, snapshots_ref, values_ref, cols_sem, row_sems, value_sems = refs
    tile_rows, listed, height, _ = values_ref.shape
    width = height // UNITS
    threshold = threshold_ref[0]
    cols_copy = pltpu.make_async_copy(cols_hbm, cols_ref, cols_sem)
    cols_copy.start()
    row_copies, value_copies = [], []
    for g in range(tile_rows):
        rows = pl.ds(g * height, height)
        row_copies.append(pltpu.make_async_copy(snapshots_hbm.at[rows], snapshots_ref.at[rows], row_sems.at[g]))
        value_copies.append(pltpu.make_async_copy(values_hbm.at[g], values_ref.at[g], value_sems.at[g]))
        row_copies[-1].start()
        value_copies[-1].start()
    cols_copy.wait()

    def shrunk(d):
        return (d - jnp.clip(d, -threshold, threshold)).astype(jnp.bfloat16)

    for g in range(tile_rows):
        row_copies[g].wait()

        def put(unit, columns, value):
            all_ref[unit, g * width : (g + 1) * width, columns] = value
            sent_refs[unit][g * width : (g + 1) * width, columns] = value
            if unit > 0:
                rest_ref[unit - 1, g * width : (g + 1) * width, columns] = value

        for unit in range(UNITS):
            rows = slice(g * height + unit * width, g * height + (unit + 1) * width)
            put(unit, slice(None), shrunk(snapshots_ref[rows, :].astype(jnp.float32)))
        value_copies[g].wait()
        for k in range(listed):
            col = cols_ref[g, k]
            columns = pl.ds(pl.multiple_of(col * ST, ST), ST)
            for unit in range(UNITS):
                rows = slice(unit * width, (unit + 1) * width)
                total = values_ref[g, k, rows, :].astype(jnp.float32)
                for other in range(listed):
                    if other != k:
                        same = jnp.where(cols_ref[g, other] == col, 1.0, 0.0)
                        total = total + same * values_ref[g, other, rows, :].astype(jnp.float32)
                rows = slice(g * height + unit * width, g * height + (unit + 1) * width)
                put(unit, columns, shrunk(snapshots_ref[rows, columns].astype(jnp.float32) - total))


def clean_units(snapshots, outlier_cols, outlier_values, threshold):
    rows, points = snapshots.shape
    tile_rows = outlier_values.shape[0]
    length = rows // UNITS
    out_shape = [jax.ShapeDtypeStruct((n, length, points), jnp.bfloat16) for n in (UNITS, UNITS - 1)]
    out_shape += [jax.ShapeDtypeStruct((length, points), jnp.bfloat16)] * UNITS
    hbm = pl.BlockSpec(memory_space=pltpu.HBM)
    stay_put = functools.partial(pltpu.with_memory_space_constraint, memory_space=pltpu.HBM)
    return pl.pallas_call(
        clean_kernel,
        out_shape=out_shape,
        in_specs=[hbm, pl.BlockSpec(memory_space=pltpu.SMEM), hbm, hbm],
        out_specs=[pl.BlockSpec(memory_space=pltpu.VMEM)] * len(out_shape),
        scratch_shapes=[
            pltpu.SMEM(outlier_cols.shape, jnp.int32),
            pltpu.VMEM(snapshots.shape, jnp.bfloat16),
            pltpu.VMEM(outlier_values.shape, jnp.bfloat16),
            pltpu.SemaphoreType.DMA,
            pltpu.SemaphoreType.DMA((tile_rows,)),
            pltpu.SemaphoreType.DMA((tile_rows,)),
        ],
        compiler_params=pltpu.CompilerParams(vmem_limit_bytes=18 << 20),
    )(stay_put(outlier_cols), threshold.reshape(1), stay_put(snapshots), stay_put(outlier_values))


def columns_of(ref):
    here = lax.axis_index("space")
    width = ref.shape[0] // 4
    return [ref[pl.ds(pl.multiple_of((here ^ q) * width, width), width), :] for q in (0, 2, 1, 3)]


def multiply(cols, rows, stay_ref, away_ref, places):
    cols = [piece for ref in cols for piece in columns_of(ref)]
    product = tile_product(jnp.concatenate(cols, axis=0), jnp.concatenate([ref[...] for ref in rows], axis=0))
    width, length = stay_ref.shape[2:]
    for c, line in enumerate(places):
        for s, place in enumerate(line):
            for q in range(4):
                top = (c * 4 + q) * width
                block = product[top : top + width, s * length : (s + 1) * length]
                (stay_ref, stay_ref, away_ref, away_ref)[q][q % 2, place] = block


def own_kernel(all_ref, stay_ref, away_ref):
    units = [all_ref.at[s] for s in range(UNITS)]
    for c in range(UNITS):
        multiply([units[c]], units, stay_ref, away_ref, [[c * UNITS + s for s in range(UNITS)]])


def x_blocks(unit):
    return [(unit, s) for s in range(unit + 1)] + [(c, unit) for c in range(unit)]


def message_blocks(step):
    fresh, late = step < UNITS, step > 0
    keys = [("near", key) for key in x_blocks(step)] * fresh + [("cross", key) for key in x_blocks(step - 1)] * late
    return keys + [("y", (step, s)) for s in range(UNITS)] * fresh + [("side", (step - 1, s)) for s in range(UNITS)] * late


def step_kernel(step, *refs):
    refs = list(refs)

    def take(n):
        out, refs[:n] = refs[:n], []
        return out

    fresh, late = step < UNITS, step > 0
    (all_ref,) = take(1)
    x_refs = take(min(step + 1, UNITS))
    y_ref = take(1)[0] if fresh else None
    sibling_ref, other_ref = take(2) if late else (None, None)
    left_refs, cross_refs = take(step if fresh else 0), take(step - 1 if late else 0)
    stay_ref, away_ref = take(2)
    core = lax.rem(lax.axis_index("tm"), 2)
    far = lax.rem(lax.div(lax.axis_index("tm"), 2), 2)
    units = [all_ref.at[s] for s in range(UNITS)]

    def choose(out_ref, flag, yes_ref, no_ref):
        @pl.when(flag == 1)
        def _():
            out_ref[...] = yes_ref[...]

        @pl.when(flag == 0)
        def _():
            out_ref[...] = no_ref[...]

    if fresh:
        left_refs += take(1)
        choose(left_refs[-1], far, y_ref, units[step])
    if late:
        cross_refs += take(1)
        (side_ref,) = take(1)
        if step > 1:
            sibling_ref = sibling_ref.at[step - 2]
        choose(cross_refs[-1], far, other_ref, sibling_ref)
        choose(side_ref, core, other_ref, sibling_ref)

    place = {key: i for i, key in enumerate(message_blocks(step))}

    def product(cols, rows):
        places = [[place[name, (c, s)] for name, s, _ in rows] for c, _ in cols]
        multiply([ref for _, ref in cols], [ref for *_, ref in rows], stay_ref, away_ref, places)

    x = list(enumerate(x_refs))
    left = [("near", s, ref) for s, ref in enumerate(left_refs)]
    cross = [("cross", s, ref) for s, ref in enumerate(cross_refs)]
    if fresh:
        product(x[step:], left)
    if late:
        product(x[step - 1 : step], left[step:] + cross)
    if step > 1:
        product(x[: step - 1], left[step:] + cross[step - 1 :])
    cols, places = [], []
    if fresh:
        cols.append(y_ref)
        places.append([place["y", (step, s)] for s in range(UNITS)])
    if late:
        cols.append(side_ref)
        places.append([place["side", (step - 1, s)] for s in range(UNITS)])
    multiply(cols, units, stay_ref, away_ref, places)


def pieces_of_result():
    pieces = []
    for first, last in GOES:
        for name in ("near", "cross"):
            pieces.append((name, [key for step in range(first, last) for key in message_blocks(step) if key[0] == name]))
    for step in range(UNITS + 1):
        pieces.append(("y", [key for key in message_blocks(step) if key[0] in ("y", "side")]))
    return pieces


def assemble_kernel(scale, *refs):
    own_ref, out_ref = refs[0], refs[-1]
    core = lax.rem(lax.axis_index("tm"), 2)
    where = {("own", (c, s)): (own_ref, c * UNITS + s) for c in range(UNITS) for s in range(UNITS)}
    for (_, keys), ref in zip(pieces_of_result(), refs[1:-1]):
        where.update({key: (ref, i) for i, key in enumerate(keys)})
    width = own_ref.shape[1]
    quarter = width * UNITS

    def put(k, name):
        for s in range(UNITS):
            pieces = [where[name, (c, s)] for c in range(UNITS)]
            tile = jnp.concatenate([ref[i] for ref, i in pieces], axis=0).T * scale
            for g in range(4):
                out_ref[k, g * quarter + s * width : g * quarter + (s + 1) * width, :] = tile[g * width : (g + 1) * width]

    put(0, "own")
    put(2, "near")
    put(4, "y")

    @pl.when(core == 0)
    def _():
        put(1, "side")
        put(3, "cross")

    @pl.when(core == 1)
    def _():
        put(1, "cross")
        put(3, "side")


def square(snapshots, outlier_cols, outlier_values, threshold):
    rows, points = snapshots.shape
    width, length = rows // (4 * UNITS), rows // UNITS
    far = (lax.axis_index("tm") // 2) % 2
    most = SNAP_MAX + outlier_cols.shape[1] * OUTLIER_MAX
    down = 2.0 ** -max(0, math.ceil(math.log2(2 * points * most * most / 6e4)))
    scale = 1.0 / (math.sqrt(points * lax.axis_size("space")) * down)

    def message(blocks):
        return [jax.ShapeDtypeStruct((2, blocks, width, length), jnp.float32)] * 2

    def units(n):
        return jax.ShapeDtypeStruct((n * length, points), jnp.bfloat16)

    def half_summed(stay, away):
        came = swapped((away * down).astype(jnp.float16), "space", 1)
        return stay * down + came.astype(jnp.float32), came

    def summed(kept, *others):
        came = swapped(behind(kept[1].astype(jnp.float16), *others), "space", 2)
        return kept[0] + came.astype(jnp.float32), came

    def behind(value, *others):
        return lax.optimization_barrier((value, *others))[0]

    whole, rest, *sent = clean_units(snapshots, outlier_cols, outlier_values, threshold)
    sibling = [swapped(sent[0], "tm", 1), swapped(rest, "tm", 1)]
    stay, away = on_units(own_kernel, message(UNITS * UNITS), 1)(behind(whole, sibling[0]))
    own_half, own_came = half_summed(stay, away)
    own, _ = summed(own_half)
    x_units, by_y, left, cross, totals, kept, other = [], [], [], [], [], [], None
    came = []
    came_last = []
    for step in range(UNITS + 1):
        fresh, late = step < UNITS, step > 0
        if fresh:
            block = sent[step]
            if step > 1:
                seen = 0 if step == 2 else step - 1
                block = behind(block, x_units[seen], by_y[seen])
            x_units.append(swapped(block, "tm", 2))
            by_y.append(swapped(block, "tm", 4))
        whole = behind(whole, *((own_came,), came_last, came_last, came[-1:], left[-1:])[step])
        operands = [whole, *x_units] + by_y[step:] + ([sibling[step > 1], other] if late else [])
        operands += (left if fresh else []) + cross
        out_shape = message(len(message_blocks(step))) + [units(1)] * (fresh + 2 * late)
        stay, away, *chosen = on_units(
            functools.partial(step_kernel, step), out_shape, len(operands)
        )(*operands)
        if fresh:
            left.append(chosen[0])
            other = swapped(behind(by_y[step], x_units[step], *came[-1:]), "tm", 1)
        if late:
            cross.append(chosen[-2])
        half, arrived = half_summed(stay, away)
        came.append(arrived)
        kept.append(half)
        if step < UNITS - 1:
            total, last = summed(half)
            totals.append(total)
            came_last = [last]
    totals += [summed(kept[-2], stay)[0], summed(kept[-1])[0]]

    def blocks_of(step, names):
        taken = [i for i, key in enumerate(message_blocks(step)) if key[0] in names]
        runs = [i for i in taken if i - 1 not in taken]
        return [totals[step][i : next(j for j in range(i, i + len(taken) + 1) if j not in taken)] for i in runs]

    parts = []
    for first, last in GOES:
        near = jnp.concatenate([part for step in range(first, last) for part in blocks_of(step, ("near",))])
        cross = jnp.concatenate([part for step in range(first, last) for part in blocks_of(step, ("cross",))])
        near, cross = (behind(part, *(parts or came[-2:-1])) for part in (near, cross))
        handed = swapped(near.astype(jnp.float16), "tm", 4, lambda i: i & 2)
        parts.append(jnp.where(far == 1, handed.astype(jnp.float32), near))
        pairs = [(i, i ^ (5 if i & 2 else 1)) for i in range(lax.axis_size("tm"))]
        parts.append(lax.ppermute(cross.astype(jnp.float16), "tm", pairs).astype(jnp.float32))
    parts += [jnp.concatenate(blocks_of(step, ("y", "side"))) for step in range(UNITS + 1)]
    out_shape = jax.ShapeDtypeStruct((5, rows, rows // 4), jnp.float32)
    operands = [own, *parts]
    band = on_units(functools.partial(assemble_kernel, scale), out_shape, len(operands))(*operands)
    return band.transpose(1, 0, 2)


def local(snapshots, outlier_cols, outlier_values, threshold):
    if lax.axis_size("tm") == 8 and lax.axis_size("space") == 4:
        return square(snapshots, outlier_cols, outlier_values, threshold)
    points = snapshots.shape[1] * lax.axis_size("space")
    band = ring(clean(snapshots, outlier_cols, outlier_values, threshold))
    return band * (1.0 / jnp.sqrt(jnp.float32(points)))


def solution(mesh):
    placed = (P("tm", "space"), P("tm", "space"), P("tm", "space", None, None), P())
    return jax.shard_map(
        local, mesh=mesh, in_specs=placed, out_specs=P("tm", None, "space"), check_vma=False
    )
```

time: 120 us -> 123 us (1.025)
  starting transfers between devices: 39 us -> 56.6 us
  waiting for transfers between devices: 51 us -> 34 us
  Pallas kernels: 17.6 us -> 25.3 us
  local copies, waits for them, and re-layouts: 6.13 us -> 3.31 us
  other arithmetic: 4.78 us -> 2.26 us
    ppermute x20 -> x28, waiting for transfers between devices: 48.6 us -> 26.6 us  [swapped(): return lax.ppermute(x, axis, pairs)]
    ppermute x20 -> x28, starting transfers between devices: 31.6 us -> 48.3 us  [swapped(): return lax.ppermute(x, axis, pairs)]
    pallas_call x5 -> x7, Pallas kernels: 14.4 us -> 21.6 us  [the longest x5 17.1 us: square(): on_units(functools.partial(step_kernel, step), out_shape, len(operands))]
    ppermute x2, waiting for transfers between devices: 2.41 us -> 7.42 us  [square(): lax.ppermute(cross.astype(jnp.float16), 'tm', pairs).astype(jnp.float32)]
    unnamed x28 -> x26, local copies, waits for them, and re-layouts: 6.09 us -> 3.22 us
    convert_element_type x10 -> x16, other arithmetic: 1.89 us -> 0.47 us  [the longest x6 0.31 us: half_summed(): came = swapped((away * down).astype(jnp.float16), 'space', 1)]
    add x8 -> x12, other arithmetic: 2.76 us -> 1.69 us  [the longest x6 1.51 us: half_summed(): return (stay * down + came.astype(jnp.float32), came)]
  transfers between devices with their start and end apart: 22 -> 30, of which waited for: 10 -> 11; matrix products, arithmetic and copies ran while one was open for 4% -> 2% of each run, Pallas kernels for 7% -> 16%
where the time goes in v5:
time: 123 us
  starting transfers between devices  56.6 us (46%)
  waiting for transfers between devices  34 us (28%)
  Pallas kernels  25.3 us (21%)
  local copies, waits for them, and re-layouts  3.31 us (3%)
  other arithmetic  2.26 us (2%)
    ppermute x28, starting transfers between devices, swapped(): return lax.ppermute(x, axis, pairs)  48.3 us
    ppermute x28, waiting for transfers between devices, swapped(): return lax.ppermute(x, axis, pairs)  26.6 us
    pallas_call x5, Pallas kernels, square(): on_units(functools.partial(step_kernel, step), out_shape, len(operands))  17.1 us
    ppermute x2, starting transfers between devices, square(): lax.ppermute(cross.astype(jnp.float16), 'tm', pairs).astype(jnp.float32)  8.36 us
    ppermute x2, waiting for transfers between devices, square(): lax.ppermute(cross.astype(jnp.float16), 'tm', pairs).astype(jnp.float32)  7.42 us
    pallas_call x1, Pallas kernels, clean_units(): pl.pallas_call(clean_kernel, out_shape=out_shape, in_specs=[hbm, pl.Block...  3.71 us
    unnamed x26, local copies, waits for them, and re-layouts  3.22 us
    pallas_call x1, Pallas kernels, square(): on_units(own_kernel, message(UNITS * UNITS), 1)(behind(whole, sibling[0]))  2.89 us
  transfers between devices with their start and end apart: 30, of which 11 were waited for; matrix products, arithmetic and copies ran while one was open for 2% of the time, Pallas kernels for 16%

profile of v5, /device:TPU:3, one launch (start us, length us, event | category | flops | bytes accessed | tf_op | source)
XLA Modules:
  0.0 122.8 jit_solution(17661998344676930225)
XLA Ops:
  0.7 3.7 %shard_map.46 = (bf16[4,128,2048]{2,1,0:T(8,128)(2,1)S(1)}, bf16[3,128,2048]{2,1,0:T(8,128)(2,1)}, bf16[128,2048]{1,0:T(8,128)(2,1)S(1)}, bf16[128,2048]{1,0:T(8...) custom-call(s32[4,4]{1,0:T(4,128)} %cols_hbm.1, f32[1]{0:T(128)} %bitcast.38.threshold_ref, ...), custom_call_target="tpu_custom_call" | custom-call | tf_op jit(solution)/shard_map/pallas_call | solution.py:121
  4.4 0.8 copy-done.6
  5.2 0.8 copy-done.8
  5.9 0.7 collective-permute-start
  6.6 1.5 %collective-permute-start.4 = (bf16[128,2048]{1,0:T(8,128)(2,1)S(1)}, bf16[128,2048]{1,0:T(8,128)(2,1)S(1)}, u32[]{:S(2)}, u32[]{:S(2)}) collective-permute-start(bf16[128,2048]{1,0:T(8,128)(2,1)S(1)} %get-tuple-element.46), channel_id=1, source_target_pairs={{0,16},{4,20},{8,24},{12,28},{16,0},{20,4},{24,8},{28,12},{1,17},{... | collective-permute-start | bytes 1572872 | tf_op jit(solution)/shard_map/ppermute | solution.py:20
  8.2 0.8 copy-done.2
  9.0 2.9 %shard_map.47 = (f32[2,16,32,128]{3,2,1,0:T(8,128)S(1)}, f32[2,16,32,128]{3,2,1,0:T(8,128)S(1)}) custom-call(bf16[4,128,2048]{2,1,0:T(8,128)(2,1)S(1)} %get-tuple-element.68.all_ref.refs_0_), custom_call_target="tpu_custom_call" | custom-call | flops 1000 | bytes 1000 | tf_op jit(solution)/shard_map/pallas_call | solution.py:303
  11.9 1.4 %collective-permute-start.1 = (f16[2,16,32,128]{3,2,1,0:T(8,128)(2,1)S(1)}, f16[2,16,32,128]{3,2,1,0:T(8,128)(2,1)S(1)}, u32[]{:S(2)}, u32[]{:S(2)}) collective-permute-start(f16[2,16,32,128]{3,2,1,0:T(8,128)(2,1)S(1)} %multiply_convert_fusion.2), channel_id=1, source_target_pairs={{0,1},{1,0},{2,3},{3,2},{4,5},{5,4},{6,7},{7,6},{8,9},{9,8},{10,11... | collective-permute-start | bytes 786440 | tf_op jit(solution)/shard_map/ppermute | solution.py:20
  13.3 6.0 %collective-permute-done.1 = f16[2,16,32,128]{3,2,1,0:T(8,128)(2,1)S(1)} collective-permute-done((f16[2,16,32,128]{3,2,1,0:T(8,128)(2,1)S(1)}, f16[2,16,32,128]{3,2,1,0:T(8,128)(2,1)S(1)}, u32[]{:S(2)}, u32[]{:S(2)}) %collective-permute-start.1) | collective-permute-done | bytes 262176 | tf_op jit(solution)/shard_map/ppermute | solution.py:20
  19.3 0.8 collective-permute-done.3.refs_1_
  20.2 1.0 shard_map.48
  21.2 0.8 copy-done
  22.1 1.3 %collective-permute-start.5 = (f16[2,5,32,128]{3,2,1,0:T(8,128)(2,1)S(1)}, f16[2,5,32,128]{3,2,1,0:T(8,128)(2,1)S(1)}, u32[]{:S(2)}, u32[]{:S(2)}) collective-permute-start(f16[2,5,32,128]{3,2,1,0:T(8,128)(2,1)S(1)} %multiply_convert_fusion.5), channel_id=1, source_target_pairs={{0,1},{1,0},{2,3},{3,2},{4,5},{5,4},{6,7},{7,6},{8,9},{9,8},{10,11... | collective-permute-start | bytes 245768 | tf_op jit(solution)/shard_map/ppermute | solution.py:20
  23.4 1.1 collective-permute-start.7
  24.5 1.2 %collective-permute-start.8 = (bf16[128,2048]{1,0:T(8,128)(2,1)}, bf16[128,2048]{1,0:T(8,128)(2,1)}, u32[]{:S(2)}, u32[]{:S(2)}) collective-permute-start(bf16[128,2048]{1,0:T(8,128)(2,1)} %get-tuple-element.54), channel_id=1, source_target_pairs={{0,16},{4,20},{8,24},{12,28},{16,0},{20,4},{24,8},{28,12},{1,17},{... | collective-permute-start | bytes 1572872 | tf_op jit(solution)/shard_map/ppermute | solution.py:20
  25.8 1.9 %collective-permute-start.14 = (bf16[3,128,2048]{2,1,0:T(8,128)(2,1)}, bf16[3,128,2048]{2,1,0:T(8,128)(2,1)}, u32[]{:S(2)}, u32[]{:S(2)}) collective-permute-start(bf16[3,128,2048]{2,1,0:T(8,128)(2,1)} %get-tuple-element.62), channel_id=1, source_target_pairs={{0,4},{4,0},{8,12},{12,8},{16,20},{20,16},{24,28},{28,24},{1,5},{5... | collective-permute-start | bytes 4718600 | tf_op jit(solution)/shard_map/ppermute | solution.py:20
  27.8 2.4 %collective-permute-start.6 = (f16[5,32,128]{2,1,0:T(8,128)(2,1)S(1)}, f16[5,32,128]{2,1,0:T(8,128)(2,1)S(1)}, u32[]{:S(2)}, u32[]{:S(2)}) collective-permute-start(f16[5,32,128]{2,1,0:T(8,128)(2,1)S(1)} %fusion.11), channel_id=1, source_target_pairs={{0,2},{1,3},{2,0},{3,1},{4,6},{5,7},{6,4},{7,5},{8,10},{9,11},{10,... | collective-permute-start | bytes 122888 | tf_op jit(solution)/shard_map/ppermute | solution.py:20
  30.2 1.2 convert_add_fusion.2
  31.4 0.6 collective-permute-done.6
  32.0 0.3 collective-permute-start.12
  32.2 3.6 %collective-permute-done.7.refs_2_ = bf16[128,2048]{1,0:T(8,128)(2,1)S(1)} collective-permute-done((bf16[128,2048]{1,0:T(8,128)(2,1)}, bf16[128,2048]{1,0:T(8,128)(2,1)S(1)}, u32[]{:S(2)}, u32[]{:S(2)}) %collective-permute-start.7) | collective-permute-done | bytes 524320 | tf_op jit(solution)/shard_map/ppermute | solution.py:20
  35.8 1.2 %collective-permute-start.13 = (bf16[128,2048]{1,0:T(8,128)(2,1)S(1)}, bf16[128,2048]{1,0:T(8,128)(2,1)S(1)}, u32[]{:S(2)}, u32[]{:S(2)}) collective-permute-start(bf16[128,2048]{1,0:T(8,128)(2,1)S(1)} %copy-done.9), channel_id=1, source_target_pairs={{0,16},{4,20},{8,24},{12,28},{16,0},{20,4},{24,8},{28,12},{1,17},{... | collective-permute-start | bytes 1572872 | tf_op jit(solution)/shard_map/ppermute | solution.py:20
  37.1 3.2 %shard_map.49 = (f32[2,12,32,128]{3,2,1,0:T(8,128)S(1)}, f32[2,12,32,128]{3,2,1,0:T(8,128)S(1)}, bf16[128,2048]{1,0:T(8,128)(2,1)S(1)}, bf16[128,2048]{1,0:T(8,128)(2,1)S(1)}, bf16[128,2048]{1,0:T(8,128)(2,1)}) custom-call(bf16[4,128,2048]{2,1,0:T(8,128)(2,1)S(1)} %get-tuple-element.68.all_ref.refs_0_, bf16[128,2048]{1,0:T(8,128)(2,1)S(1)} %collective-permute-done.3.refs_1_, ...), custom_call_target="tpu_custom_call" | custom-call | flops 1000 | bytes 1000 | tf_op jit(solution)/shard_map/pallas_call | solution.py:322
  40.3 0.2 collective-permute-start.10
  40.6 4.6 %collective-permute-start.15 = (bf16[128,2048]{1,0:T(8,128)(2,1)}, bf16[128,2048]{1,0:T(8,128)(2,1)S(1)}, u32[]{:S(2)}, u32[]{:S(2)}) collective-permute-start(bf16[128,2048]{1,0:T(8,128)(2,1)} %collective-permute-done.8.refs_3_), channel_id=1, source_target_pairs={{0,4},{4,0},{8,12},{12,8},{16,20},{20,16},{24,28},{28,24},{1,5},{5... | collective-permute-start | bytes 1572872 | tf_op jit(solution)/shard_map/ppermute | solution.py:20
  45.3 2.4 %collective-permute-start.11 = (f16[12,32,128]{2,1,0:T(8,128)(2,1)S(1)}, f16[12,32,128]{2,1,0:T(8,128)(2,1)S(1)}, u32[]{:S(2)}, u32[]{:S(2)}) collective-permute-start(f16[12,32,128]{2,1,0:T(8,128)(2,1)S(1)} %fusion.8), channel_id=1, source_target_pairs={{0,2},{1,3},{2,0},{3,1},{4,6},{5,7},{6,4},{7,5},{8,10},{9,11},{10,... | collective-permute-start | bytes 294920 | tf_op jit(solution)/shard_map/ppermute | solution.py:20
  47.7 2.1 %collective-permute-done.11 = f16[12,32,128]{2,1,0:T(8,128)(2,1)S(1)} collective-permute-done((f16[12,32,128]{2,1,0:T(8,128)(2,1)S(1)}, f16[12,32,128]{2,1,0:T(8,128)(2,1)S(1)}, u32[]{:S(2)}, u32[]{:S(2)}) %collective-permute-start.11) | collective-permute-done | bytes 98336 | tf_op jit(solution)/shard_map/ppermute | solution.py:20
  49.8 2.3 %collective-permute-start.2 = (f16[16,32,128]{2,1,0:T(8,128)(2,1)S(1)}, f16[16,32,128]{2,1,0:T(8,128)(2,1)S(1)}, u32[]{:S(2)}, u32[]{:S(2)}) collective-permute-start(f16[16,32,128]{2,1,0:T(8,128)(2,1)S(1)} %fusion.6), channel_id=1, source_target_pairs={{0,2},{1,3},{2,0},{3,1},{4,6},{5,7},{6,4},{7,5},{8,10},{9,11},{10,... | collective-permute-start | bytes 393224 | tf_op jit(solution)/shard_map/ppermute | solution.py:20
  52.2 4.2 %shard_map.50 = (f32[2,16,32,128]{3,2,1,0:T(8,128)S(1)}, f32[2,16,32,128]{3,2,1,0:T(8,128)S(1)}, bf16[128,2048]{1,0:T(8,128)(2,1)S(1)}, bf16[128,2048]{1,0:T(8,128)(2,1)S(1)}, bf16[128,2048]{1,0:T(8,128)(2,1)}) custom-call(bf16[4,128,2048]{2,1,0:T(8,128)(2,1)S(1)} %get-tuple-element.68.all_ref.refs_0_, bf16[128,2048]{1,0:T(8,128)(2,1)S(1)} %collective-permute-done.3.refs_1_, ...), custom_call_target="tpu_custom_call" | custom-call | flops 1000 | bytes 1000 | tf_op jit(solution)/shard_map/pallas_call | solution.py:322
  56.4 2.2 %collective-permute-start.16 = (f16[2,16,32,128]{3,2,1,0:T(8,128)(2,1)S(1)}, f16[2,16,32,128]{3,2,1,0:T(8,128)(2,1)S(1)}, u32[]{:S(2)}, u32[]{:S(2)}) collective-permute-start(f16[2,16,32,128]{3,2,1,0:T(8,128)(2,1)S(1)} %multiply_convert_fusion.1), channel_id=1, source_target_pairs={{0,1},{1,0},{2,3},{3,2},{4,5},{5,4},{6,7},{7,6},{8,9},{9,8},{10,11... | collective-permute-start | bytes 786440 | tf_op jit(solution)/shard_map/ppermute | solution.py:20
  58.7 1.2 collective-permute-start.18
  59.9 0.2 collective-permute-start.19
  60.1 8.7 %collective-permute-start.20 = (bf16[128,2048]{1,0:T(8,128)(2,1)S(1)}, bf16[128,2048]{1,0:T(8,128)(2,1)S(1)}, u32[]{:S(2)}, u32[]{:S(2)}) collective-permute-start(bf16[128,2048]{1,0:T(8,128)(2,1)S(1)} %collective-permute-done.13.refs_4_), channel_id=1, source_target_pairs={{0,4},{4,0},{8,12},{12,8},{16,20},{20,16},{24,28},{28,24},{1,5},{5... | collective-permute-start | bytes 1572872 | tf_op jit(solution)/shard_map/ppermute | solution.py:20
  69.1 1.2 %collective-permute-done.20.refs_7_ = bf16[128,2048]{1,0:T(8,128)(2,1)S(1)} collective-permute-done((bf16[128,2048]{1,0:T(8,128)(2,1)S(1)}, bf16[128,2048]{1,0:T(8,128)(2,1)S(1)}, u32[]{:S(2)}, u32[]{:S(2)}) %collective-permute-start.20) | collective-permute-done | bytes 524320 | tf_op jit(solution)/shard_map/ppermute | solution.py:20
  70.3 4.6 %shard_map.51 = (f32[2,20,32,128]{3,2,1,0:T(8,128)S(1)}, f32[2,20,32,128]{3,2,1,0:T(8,128)S(1)}, bf16[128,2048]{1,0:T(8,128)(2,1)}, bf16[128,2048]{1,0:T(8,128)(2,1)S(1)}, bf16[128,2048]{1,0:T(8,128)(2,1)}) custom-call(bf16[4,128,2048]{2,1,0:T(8,128)(2,1)S(1)} %get-tuple-element.68.all_ref.refs_0_, bf16[128,2048]{1,0:T(8,128)(2,1)S(1)} %collective-permute-done.3.refs_1_, ...), custom_call_target="tpu_custom_call" | custom-call | flops 1000 | bytes 1000 | tf_op jit(solution)/shard_map/pallas_call | solution.py:322
  75.0 0.6 collective-permute-start.21
  75.6 6.7 %collective-permute-start.24 = (bf16[128,2048]{1,0:T(8,128)(2,1)S(1)}, bf16[128,2048]{1,0:T(8,128)(2,1)S(1)}, u32[]{:S(2)}, u32[]{:S(2)}) collective-permute-start(bf16[128,2048]{1,0:T(8,128)(2,1)S(1)} %collective-permute-done.19.refs_5_), channel_id=1, source_target_pairs={{0,4},{4,0},{8,12},{12,8},{16,20},{20,16},{24,28},{28,24},{1,5},{5... | collective-permute-start | bytes 1572872 | tf_op jit(solution)/shard_map/ppermute | solution.py:20
  82.5 2.1 %collective-permute-start.22 = (f16[9,32,128]{2,1,0:T(8,128)(2,1)S(1)}, f16[9,32,128]{2,1,0:T(8,128)(2,1)S(1)}, u32[]{:S(2)}, u32[]{:S(2)}) collective-permute-start(f16[9,32,128]{2,1,0:T(8,128)(2,1)S(1)} %convert_element_type.119), channel_id=1, source_target_pairs={{8,24},{12,28},{24,8},{28,12},{9,25},{13,29},{25,9},{29,13},{10,26... | collective-permute-start | bytes 221192 | tf_op jit(solution)/shard_map/ppermute | solution.py:20
  84.7 8.3 %collective-permute-start.23 = (f16[4,32,128]{2,1,0:T(8,128)(2,1)S(1)}, f16[4,32,128]{2,1,0:T(8,128)(2,1)S(1)}, u32[]{:S(2)}, u32[]{:S(2)}) collective-permute-start(f16[4,32,128]{2,1,0:T(8,128)(2,1)S(1)} %convert_element_type.121), channel_id=1, source_target_pairs={{0,4},{4,0},{8,28},{12,24},{16,20},{20,16},{24,12},{28,8},{1,5},{5... | collective-permute-start | bytes 98312 | tf_op jit(solution)/shard_map/ppermute | solution.py:352
  93.1 2.5 %collective-permute-done.23 = f16[4,32,128]{2,1,0:T(8,128)(2,1)S(1)} collective-permute-done((f16[4,32,128]{2,1,0:T(8,128)(2,1)S(1)}, f16[4,32,128]{2,1,0:T(8,128)(2,1)S(1)}, u32[]{:S(2)}, u32[]{:S(2)}) %collective-permute-start.23) | collective-permute-done | bytes 32800 | tf_op jit(solution)/shard_map/ppermute | solution.py:352
  95.6 4.2 %shard_map.52 = (f32[2,11,32,128]{3,2,1,0:T(8,128)S(1)}, f32[2,11,32,128]{3,2,1,0:T(8,128)S(1)}, bf16[128,2048]{1,0:T(8,128)(2,1)}, bf16[128,2048]{1,0:T(8,128)(2,1)}) custom-call(bf16[4,128,2048]{2,1,0:T(8,128)(2,1)S(1)} %get-tuple-element.68.all_ref.refs_0_, bf16[128,2048]{1,0:T(8,128)(2,1)S(1)} %collective-permute-done.3.refs_1_, ...), custom_call_target="tpu_custom_call" | custom-call | flops 1000 | bytes 1000 | tf_op jit(solution)/shard_map/pallas_call | solution.py:322
  100.0 1.8 %collective-permute-start.25 = (f16[20,32,128]{2,1,0:T(8,128)(2,1)S(1)}, f16[20,32,128]{2,1,0:T(8,128)(2,1)S(1)}, u32[]{:S(2)}, u32[]{:S(2)}) collective-permute-start(f16[20,32,128]{2,1,0:T(8,128)(2,1)S(1)} %fusion.5), channel_id=1, source_target_pairs={{0,2},{1,3},{2,0},{3,1},{4,6},{5,7},{6,4},{7,5},{8,10},{9,11},{10,... | collective-permute-start | bytes 491528 | tf_op jit(solution)/shard_map/ppermute | solution.py:20
  101.8 7.3 %collective-permute-done.27 = f16[2,11,32,128]{3,2,1,0:T(8,128)(2,1)S(1)} collective-permute-done((f16[2,11,32,128]{3,2,1,0:T(8,128)(2,1)S(1)}, f16[2,11,32,128]{3,2,1,0:T(8,128)(2,1)S(1)}, u32[]{:S(2)}, u32[]{:S(2)}) %collective-permute-start.27) | collective-permute-done | bytes 180256 | tf_op jit(solution)/shard_map/ppermute | solution.py:20
  109.2 1.1 collective-permute-done.25
  110.5 1.9 %collective-permute-start.26 = (f16[7,32,128]{2,1,0:T(8,128)(2,1)S(1)}, f16[7,32,128]{2,1,0:T(8,128)(2,1)S(1)}, u32[]{:S(2)}, u32[]{:S(2)}) collective-permute-start(f16[7,32,128]{2,1,0:T(8,128)(2,1)S(1)} %convert_element_type.126), channel_id=1, source_target_pairs={{8,24},{12,28},{24,8},{28,12},{9,25},{13,29},{25,9},{29,13},{10,26... | collective-permute-start | bytes 172040 | tf_op jit(solution)/shard_map/ppermute | solution.py:20
  112.4 3.6 %collective-permute-done.28 = f16[11,32,128]{2,1,0:T(8,128)(2,1)S(1)} collective-permute-done((f16[11,32,128]{2,1,0:T(8,128)(2,1)S(1)}, f16[11,32,128]{2,1,0:T(8,128)(2,1)S(1)}, u32[]{:S(2)}, u32[]{:S(2)}) %collective-permute-start.28) | collective-permute-done | bytes 90144 | tf_op jit(solution)/shard_map/ppermute | solution.py:20
  116.3 4.9 %collective-permute-done.29 = f16[12,32,128]{2,1,0:T(8,128)(2,1)S(1)} collective-permute-done((f16[12,32,128]{2,1,0:T(8,128)(2,1)S(1)}, f16[12,32,128]{2,1,0:T(8,128)(2,1)S(1)}, u32[]{:S(2)}, u32[]{:S(2)}) %collective-permute-start.29) | collective-permute-done | bytes 98336 | tf_op jit(solution)/shard_map/ppermute | solution.py:352
  121.2 1.5 %shard_map.53 = f32[5,512,128]{2,1,0:T(8,128)} custom-call(f32[16,32,128]{2,1,0:T(8,128)S(1)} %fusion.2.refs_0_, f32[9,32,128]{2,1,0:T(8,128)S(1)} %convert_select_fusion.refs_1_, f32[4,32,128]{2,1,0:T(8,128)S(1)} %convert_element_type.122.refs_2_, f32[7,32,128]{2,1,0:T(8,128)S(1)} %convert_select_fusion.1.refs_3_, ...), custom_call_target="tpu_custom_call" | custom-call | flops 1000 | bytes 1000 | tf_op jit(solution)/shard_map/pallas_call | solution.py:356
  (97 shorter events, 1.7 us)
Async XLA Ops:
  4.4 0.8 copy-start.6
  5.2 0.8 copy-start.8
  5.9 2.2 %collective-permute-start = (bf16[128,2048]{1,0:T(8,128)(2,1)S(1)}, bf16[128,2048]{1,0:T(8,128)(2,1)S(1)}, u32[]{:S(2)}, u32[]{:S(2)}) collective-permute-start(bf16[128,2048]{1,0:T(8,128)(2,1)S(1)} %get-tuple-element.46), channel_id=1, source_target_pairs={{0,4},{4,0},{8,12},{12,8},{16,20},{20,16},{24,28},{28,24},{1,5},{5... | collective-permute-start | bytes 1572872 | tf_op jit(solution)/shard_map/ppermute | solution.py:20
  6.6 13.6 %collective-permute-start.3 = (bf16[128,2048]{1,0:T(8,128)(2,1)S(1)}, bf16[128,2048]{1,0:T(8,128)(2,1)S(1)}, u32[]{:S(2)}, u32[]{:S(2)}) collective-permute-start(bf16[128,2048]{1,0:T(8,128)(2,1)S(1)} %get-tuple-element.46), channel_id=1, source_target_pairs={{0,8},{4,12},{8,0},{12,4},{16,24},{20,28},{24,16},{28,20},{1,9},{5... | collective-permute-start | bytes 1572872 | tf_op jit(solution)/shard_map/ppermute | solution.py:20
  6.6 13.6 %collective-permute-start.4 = (bf16[128,2048]{1,0:T(8,128)(2,1)S(1)}, bf16[128,2048]{1,0:T(8,128)(2,1)S(1)}, u32[]{:S(2)}, u32[]{:S(2)}) collective-permute-start(bf16[128,2048]{1,0:T(8,128)(2,1)S(1)} %get-tuple-element.46), channel_id=1, source_target_pairs={{0,16},{4,20},{8,24},{12,28},{16,0},{20,4},{24,8},{28,12},{1,17},{... | collective-permute-start | bytes 1572872 | tf_op jit(solution)/shard_map/ppermute | solution.py:20
  8.2 0.8 copy-start.2
  11.9 8.3 %copy-start.4 = (f32[2,16,32,128]{3,2,1,0:T(8,128)}, f32[2,16,32,128]{3,2,1,0:T(8,128)S(1)}, u32[]{:S(2)}) copy-start(f32[2,16,32,128]{3,2,1,0:T(8,128)S(1)} %get-tuple-element.48) | copy-start | bytes 1572868
  11.9 7.4 %collective-permute-start.1 = (f16[2,16,32,128]{3,2,1,0:T(8,128)(2,1)S(1)}, f16[2,16,32,128]{3,2,1,0:T(8,128)(2,1)S(1)}, u32[]{:S(2)}, u32[]{:S(2)}) collective-permute-start(f16[2,16,32,128]{3,2,1,0:T(8,128)(2,1)S(1)} %multiply_convert_fusion.2), channel_id=1, source_target_pairs={{0,1},{1,0},{2,3},{3,2},{4,5},{5,4},{6,7},{7,6},{8,9},{9,8},{10,11... | collective-permute-start | bytes 786440 | tf_op jit(solution)/shard_map/ppermute | solution.py:20
  19.3 1.8 %copy-start.12 = (f16[2,16,32,128]{3,2,1,0:T(8,128)(2,1)}, f16[2,16,32,128]{3,2,1,0:T(8,128)(2,1)S(1)}, u32[]{:S(2)}) copy-start(f16[2,16,32,128]{3,2,1,0:T(8,128)(2,1)S(1)} %collective-permute-done.1) | copy-start | bytes 786436
  20.2 1.0 copy-start.5
  21.2 0.8 copy-start
  22.1 5.7 %collective-permute-start.5 = (f16[2,5,32,128]{3,2,1,0:T(8,128)(2,1)S(1)}, f16[2,5,32,128]{3,2,1,0:T(8,128)(2,1)S(1)}, u32[]{:S(2)}, u32[]{:S(2)}) collective-permute-start(f16[2,5,32,128]{3,2,1,0:T(8,128)(2,1)S(1)} %multiply_convert_fusion.5), channel_id=1, source_target_pairs={{0,1},{1,0},{2,3},{3,2},{4,5},{5,4},{6,7},{7,6},{8,9},{9,8},{10,11... | collective-permute-start | bytes 245768 | tf_op jit(solution)/shard_map/ppermute | solution.py:20
  23.4 12.4 %collective-permute-start.7 = (bf16[128,2048]{1,0:T(8,128)(2,1)}, bf16[128,2048]{1,0:T(8,128)(2,1)S(1)}, u32[]{:S(2)}, u32[]{:S(2)}) collective-permute-start(bf16[128,2048]{1,0:T(8,128)(2,1)} %get-tuple-element.54), channel_id=1, source_target_pairs={{0,8},{4,12},{8,0},{12,4},{16,24},{20,28},{24,16},{28,20},{1,9},{5... | collective-permute-start | bytes 1572872 | tf_op jit(solution)/shard_map/ppermute | solution.py:20
  24.5 12.6 %collective-permute-start.8 = (bf16[128,2048]{1,0:T(8,128)(2,1)}, bf16[128,2048]{1,0:T(8,128)(2,1)}, u32[]{:S(2)}, u32[]{:S(2)}) collective-permute-start(bf16[128,2048]{1,0:T(8,128)(2,1)} %get-tuple-element.54), channel_id=1, source_target_pairs={{0,16},{4,20},{8,24},{12,28},{16,0},{20,4},{24,8},{28,12},{1,17},{... | collective-permute-start | bytes 1572872 | tf_op jit(solution)/shard_map/ppermute | solution.py:20
  25.8 26.4 %collective-permute-start.14 = (bf16[3,128,2048]{2,1,0:T(8,128)(2,1)}, bf16[3,128,2048]{2,1,0:T(8,128)(2,1)}, u32[]{:S(2)}, u32[]{:S(2)}) collective-permute-start(bf16[3,128,2048]{2,1,0:T(8,128)(2,1)} %get-tuple-element.62), channel_id=1, source_target_pairs={{0,4},{4,0},{8,12},{12,8},{16,20},{20,16},{24,28},{28,24},{1,5},{5... | collective-permute-start | bytes 4718600 | tf_op jit(solution)/shard_map/ppermute | solution.py:20
  27.7 4.3 %copy-start.9 = (bf16[128,2048]{1,0:T(8,128)(2,1)S(1)}, bf16[128,2048]{1,0:T(8,128)(2,1)}, u32[]{:S(2)}) copy-start(bf16[128,2048]{1,0:T(8,128)(2,1)} %copy-done.8) | copy-start | bytes 1572868
  27.7 9.4 %copy-start.1 = (bf16[128,2048]{1,0:T(8,128)(2,1)S(1)}, bf16[128,2048]{1,0:T(8,128)(2,1)}, u32[]{:S(2)}) copy-start(bf16[128,2048]{1,0:T(8,128)(2,1)} %copy-done) | copy-start | bytes 1572868
  27.7 9.4 %copy-start.3 = (bf16[128,2048]{1,0:T(8,128)(2,1)S(1)}, bf16[128,2048]{1,0:T(8,128)(2,1)}, u32[]{:S(2)}) copy-start(bf16[128,2048]{1,0:T(8,128)(2,1)} %copy-done.2) | copy-start | bytes 1572868
  27.7 9.4 %collective-permute-start.9 = (bf16[128,2048]{1,0:T(8,128)(2,1)}, bf16[128,2048]{1,0:T(8,128)(2,1)S(1)}, u32[]{:S(2)}, u32[]{:S(2)}) collective-permute-start(bf16[128,2048]{1,0:T(8,128)(2,1)} %copy-done.5), channel_id=1, source_target_pairs={{0,4},{4,0},{8,12},{12,8},{16,20},{20,16},{24,28},{28,24},{1,5},{5... | collective-permute-start | bytes 1572872 | tf_op jit(solution)/shard_map/ppermute | solution.py:20
  27.8 4.1 %collective-permute-start.6 = (f16[5,32,128]{2,1,0:T(8,128)(2,1)S(1)}, f16[5,32,128]{2,1,0:T(8,128)(2,1)S(1)}, u32[]{:S(2)}, u32[]{:S(2)}) collective-permute-start(f16[5,32,128]{2,1,0:T(8,128)(2,1)S(1)} %fusion.11), channel_id=1, source_target_pairs={{0,2},{1,3},{2,0},{3,1},{4,6},{5,7},{6,4},{7,5},{8,10},{9,11},{10,... | collective-permute-start | bytes 122888 | tf_op jit(solution)/shard_map/ppermute | solution.py:20
  32.0 20.1 %collective-permute-start.12 = (bf16[128,2048]{1,0:T(8,128)(2,1)S(1)}, bf16[128,2048]{1,0:T(8,128)(2,1)S(1)}, u32[]{:S(2)}, u32[]{:S(2)}) collective-permute-start(bf16[128,2048]{1,0:T(8,128)(2,1)S(1)} %copy-done.9), channel_id=1, source_target_pairs={{0,8},{4,12},{8,0},{12,4},{16,24},{20,28},{24,16},{28,20},{1,9},{5... | collective-permute-start | bytes 1572872 | tf_op jit(solution)/shard_map/ppermute | solution.py:20
  35.8 16.3 %collective-permute-start.13 = (bf16[128,2048]{1,0:T(8,128)(2,1)S(1)}, bf16[128,2048]{1,0:T(8,128)(2,1)S(1)}, u32[]{:S(2)}, u32[]{:S(2)}) collective-permute-start(bf16[128,2048]{1,0:T(8,128)(2,1)S(1)} %copy-done.9), channel_id=1, source_target_pairs={{0,16},{4,20},{8,24},{12,28},{16,0},{20,4},{24,8},{28,12},{1,17},{... | collective-permute-start | bytes 1572872 | tf_op jit(solution)/shard_map/ppermute | solution.py:20
  40.3 4.9 %collective-permute-start.10 = (f16[2,12,32,128]{3,2,1,0:T(8,128)(2,1)S(1)}, f16[2,12,32,128]{3,2,1,0:T(8,128)(2,1)S(1)}, u32[]{:S(2)}, u32[]{:S(2)}) collective-permute-start(f16[2,12,32,128]{3,2,1,0:T(8,128)(2,1)S(1)} %multiply_convert_fusion.3), channel_id=1, source_target_pairs={{0,1},{1,0},{2,3},{3,2},{4,5},{5,4},{6,7},{7,6},{8,9},{9,8},{10,11... | collective-permute-start | bytes 589832 | tf_op jit(solution)/shard_map/ppermute | solution.py:20
  40.6 11.6 %collective-permute-start.15 = (bf16[128,2048]{1,0:T(8,128)(2,1)}, bf16[128,2048]{1,0:T(8,128)(2,1)S(1)}, u32[]{:S(2)}, u32[]{:S(2)}) collective-permute-start(bf16[128,2048]{1,0:T(8,128)(2,1)} %collective-permute-done.8.refs_3_), channel_id=1, source_target_pairs={{0,4},{4,0},{8,12},{12,8},{16,20},{20,16},{24,28},{28,24},{1,5},{5... | collective-permute-start | bytes 1572872 | tf_op jit(solution)/shard_map/ppermute | solution.py:20
  45.3 4.5 %collective-permute-start.11 = (f16[12,32,128]{2,1,0:T(8,128)(2,1)S(1)}, f16[12,32,128]{2,1,0:T(8,128)(2,1)S(1)}, u32[]{:S(2)}, u32[]{:S(2)}) collective-permute-start(f16[12,32,128]{2,1,0:T(8,128)(2,1)S(1)} %fusion.8), channel_id=1, source_target_pairs={{0,2},{1,3},{2,0},{3,1},{4,6},{5,7},{6,4},{7,5},{8,10},{9,11},{10,... | collective-permute-start | bytes 294920 | tf_op jit(solution)/shard_map/ppermute | solution.py:20
  47.7 8.7 %copy-start.11 = (f32[5,32,128]{2,1,0:T(8,128)}, f32[5,32,128]{2,1,0:T(8,128)S(1)}, u32[]{:S(2)}) copy-start(f32[5,32,128]{2,1,0:T(8,128)S(1)} %fusion.10) | copy-start | bytes 245764
  49.8 8.8 %collective-permute-start.2 = (f16[16,32,128]{2,1,0:T(8,128)(2,1)S(1)}, f16[16,32,128]{2,1,0:T(8,128)(2,1)S(1)}, u32[]{:S(2)}, u32[]{:S(2)}) collective-permute-start(f16[16,32,128]{2,1,0:T(8,128)(2,1)S(1)} %fusion.6), channel_id=1, source_target_pairs={{0,2},{1,3},{2,0},{3,1},{4,6},{5,7},{6,4},{7,5},{8,10},{9,11},{10,... | collective-permute-start | bytes 393224 | tf_op jit(solution)/shard_map/ppermute | solution.py:20
  52.1 6.5 %copy-start.7 = (bf16[128,2048]{1,0:T(8,128)(2,1)S(1)}, bf16[128,2048]{1,0:T(8,128)(2,1)}, u32[]{:S(2)}) copy-start(bf16[128,2048]{1,0:T(8,128)(2,1)} %copy-done.6) | copy-start | bytes 1572868
  56.4 12.4 %collective-permute-start.16 = (f16[2,16,32,128]{3,2,1,0:T(8,128)(2,1)S(1)}, f16[2,16,32,128]{3,2,1,0:T(8,128)(2,1)S(1)}, u32[]{:S(2)}, u32[]{:S(2)}) collective-permute-start(f16[2,16,32,128]{3,2,1,0:T(8,128)(2,1)S(1)} %multiply_convert_fusion.1), channel_id=1, source_target_pairs={{0,1},{1,0},{2,3},{3,2},{4,5},{5,4},{6,7},{7,6},{8,9},{9,8},{10,11... | collective-permute-start | bytes 786440 | tf_op jit(solution)/shard_map/ppermute | solution.py:20
  58.7 10.4 %collective-permute-start.18 = (bf16[128,2048]{1,0:T(8,128)(2,1)S(1)}, bf16[128,2048]{1,0:T(8,128)(2,1)S(1)}, u32[]{:S(2)}, u32[]{:S(2)}) collective-permute-start(bf16[128,2048]{1,0:T(8,128)(2,1)S(1)} %copy-done.7), channel_id=1, source_target_pairs={{0,8},{4,12},{8,0},{12,4},{16,24},{20,28},{24,16},{28,20},{1,9},{5... | collective-permute-start | bytes 1572872 | tf_op jit(solution)/shard_map/ppermute | solution.py:20
  59.9 9.2 %collective-permute-start.19 = (bf16[128,2048]{1,0:T(8,128)(2,1)S(1)}, bf16[128,2048]{1,0:T(8,128)(2,1)S(1)}, u32[]{:S(2)}, u32[]{:S(2)}) collective-permute-start(bf16[128,2048]{1,0:T(8,128)(2,1)S(1)} %copy-done.7), channel_id=1, source_target_pairs={{0,16},{4,20},{8,24},{12,28},{16,0},{20,4},{24,8},{28,12},{1,17},{... | collective-permute-start | bytes 1572872 | tf_op jit(solution)/shard_map/ppermute | solution.py:20
  60.1 10.2 %collective-permute-start.20 = (bf16[128,2048]{1,0:T(8,128)(2,1)S(1)}, bf16[128,2048]{1,0:T(8,128)(2,1)S(1)}, u32[]{:S(2)}, u32[]{:S(2)}) collective-permute-start(bf16[128,2048]{1,0:T(8,128)(2,1)S(1)} %collective-permute-done.13.refs_4_), channel_id=1, source_target_pairs={{0,4},{4,0},{8,12},{12,8},{16,20},{20,16},{24,28},{28,24},{1,5},{5... | collective-permute-start | bytes 1572872 | tf_op jit(solution)/shard_map/ppermute | solution.py:20
  68.8 6.1 %copy-start.10 = (f32[12,32,128]{2,1,0:T(8,128)}, f32[12,32,128]{2,1,0:T(8,128)S(1)}, u32[]{:S(2)}) copy-start(f32[12,32,128]{2,1,0:T(8,128)S(1)} %fusion.3) | copy-start | bytes 589828
  69.0 13.3 %collective-permute-start.17 = (f16[16,32,128]{2,1,0:T(8,128)(2,1)S(1)}, f16[16,32,128]{2,1,0:T(8,128)(2,1)S(1)}, u32[]{:S(2)}, u32[]{:S(2)}) collective-permute-start(f16[16,32,128]{2,1,0:T(8,128)(2,1)S(1)} %fusion.7), channel_id=1, source_target_pairs={{0,2},{1,3},{2,0},{3,1},{4,6},{5,7},{6,4},{7,5},{8,10},{9,11},{10,... | collective-permute-start | bytes 393224 | tf_op jit(solution)/shard_map/ppermute | solution.py:20
  74.9 7.4 %slice-start.2 = ((f32[5,32,128]{2,1,0:T(8,128)}), f32[1,32,128]{2,1,0:T(8,128)S(1)}, s32[]{:S(2)}) async-start(f32[5,32,128]{2,1,0:T(8,128)} %copy-done.11), calls=%async_computation.2 | async-start | bytes 32768 | tf_op jit(solution)/shard_map/slice | solution.py:342
  74.9 7.5 %slice-start = ((f32[12,32,128]{2,1,0:T(8,128)}), f32[3,32,128]{2,1,0:T(8,128)S(1)}, s32[]{:S(2)}) async-start(f32[12,32,128]{2,1,0:T(8,128)} %copy-done.10), calls=%async_computation | async-start | bytes 98304 | tf_op jit(solution)/shard_map/slice | solution.py:342
  74.9 7.5 %slice-start.1 = ((f32[12,32,128]{2,1,0:T(8,128)}), f32[1,32,128]{2,1,0:T(8,128)S(1)}, s32[]{:S(2)}) async-start(f32[12,32,128]{2,1,0:T(8,128)} %copy-done.10), calls=%async_computation.1 | async-start | bytes 32768 | tf_op jit(solution)/shard_map/slice | solution.py:342
  75.0 7.4 %collective-permute-start.21 = (f16[2,20,32,128]{3,2,1,0:T(8,128)(2,1)S(1)}, f16[2,20,32,128]{3,2,1,0:T(8,128)(2,1)S(1)}, u32[]{:S(2)}, u32[]{:S(2)}) collective-permute-start(f16[2,20,32,128]{3,2,1,0:T(8,128)(2,1)S(1)} %multiply_convert_fusion), channel_id=1, source_target_pairs={{0,1},{1,0},{2,3},{3,2},{4,5},{5,4},{6,7},{7,6},{8,9},{9,8},{10,11... | collective-permute-start | bytes 983048 | tf_op jit(solution)/shard_map/ppermute | solution.py:20
  75.6 20.0 %collective-permute-start.24 = (bf16[128,2048]{1,0:T(8,128)(2,1)S(1)}, bf16[128,2048]{1,0:T(8,128)(2,1)S(1)}, u32[]{:S(2)}, u32[]{:S(2)}) collective-permute-start(bf16[128,2048]{1,0:T(8,128)(2,1)S(1)} %collective-permute-done.19.refs_5_), channel_id=1, source_target_pairs={{0,4},{4,0},{8,12},{12,8},{16,20},{20,16},{24,28},{28,24},{1,5},{5... | collective-permute-start | bytes 1572872 | tf_op jit(solution)/shard_map/ppermute | solution.py:20
  82.5 17.4 %collective-permute-start.22 = (f16[9,32,128]{2,1,0:T(8,128)(2,1)S(1)}, f16[9,32,128]{2,1,0:T(8,128)(2,1)S(1)}, u32[]{:S(2)}, u32[]{:S(2)}) collective-permute-start(f16[9,32,128]{2,1,0:T(8,128)(2,1)S(1)} %convert_element_type.119), channel_id=1, source_target_pairs={{8,24},{12,28},{24,8},{28,12},{9,25},{13,29},{25,9},{29,13},{10,26... | collective-permute-start | bytes 221192 | tf_op jit(solution)/shard_map/ppermute | solution.py:20
  84.7 10.9 %collective-permute-start.23 = (f16[4,32,128]{2,1,0:T(8,128)(2,1)S(1)}, f16[4,32,128]{2,1,0:T(8,128)(2,1)S(1)}, u32[]{:S(2)}, u32[]{:S(2)}) collective-permute-start(f16[4,32,128]{2,1,0:T(8,128)(2,1)S(1)} %convert_element_type.121), channel_id=1, source_target_pairs={{0,4},{4,0},{8,28},{12,24},{16,20},{20,16},{24,12},{28,8},{1,5},{5... | collective-permute-start | bytes 98312 | tf_op jit(solution)/shard_map/ppermute | solution.py:352
  99.8 9.2 %collective-permute-start.27 = (f16[2,11,32,128]{3,2,1,0:T(8,128)(2,1)S(1)}, f16[2,11,32,128]{3,2,1,0:T(8,128)(2,1)S(1)}, u32[]{:S(2)}, u32[]{:S(2)}) collective-permute-start(f16[2,11,32,128]{3,2,1,0:T(8,128)(2,1)S(1)} %multiply_convert_fusion.4), channel_id=1, source_target_pairs={{0,1},{1,0},{2,3},{3,2},{4,5},{5,4},{6,7},{7,6},{8,9},{9,8},{10,11... | collective-permute-start | bytes 540680 | tf_op jit(solution)/shard_map/ppermute | solution.py:20
  100.0 10.4 %collective-permute-start.25 = (f16[20,32,128]{2,1,0:T(8,128)(2,1)S(1)}, f16[20,32,128]{2,1,0:T(8,128)(2,1)S(1)}, u32[]{:S(2)}, u32[]{:S(2)}) collective-permute-start(f16[20,32,128]{2,1,0:T(8,128)(2,1)S(1)} %fusion.5), channel_id=1, source_target_pairs={{0,2},{1,3},{2,0},{3,1},{4,6},{5,7},{6,4},{7,5},{8,10},{9,11},{10,... | collective-permute-start | bytes 491528 | tf_op jit(solution)/shard_map/ppermute | solution.py:20
  109.2 6.9 %collective-permute-start.28 = (f16[11,32,128]{2,1,0:T(8,128)(2,1)S(1)}, f16[11,32,128]{2,1,0:T(8,128)(2,1)S(1)}, u32[]{:S(2)}, u32[]{:S(2)}) collective-permute-start(f16[11,32,128]{2,1,0:T(8,128)(2,1)S(1)} %fusion.9), channel_id=1, source_target_pairs={{0,2},{1,3},{2,0},{3,1},{4,6},{5,7},{6,4},{7,5},{8,10},{9,11},{10,... | collective-permute-start | bytes 270344 | tf_op jit(solution)/shard_map/ppermute | solution.py:20
  110.5 5.7 %collective-permute-start.26 = (f16[7,32,128]{2,1,0:T(8,128)(2,1)S(1)}, f16[7,32,128]{2,1,0:T(8,128)(2,1)S(1)}, u32[]{:S(2)}, u32[]{:S(2)}) collective-permute-start(f16[7,32,128]{2,1,0:T(8,128)(2,1)S(1)} %convert_element_type.126), channel_id=1, source_target_pairs={{8,24},{12,28},{24,8},{28,12},{9,25},{13,29},{25,9},{29,13},{10,26... | collective-permute-start | bytes 172040 | tf_op jit(solution)/shard_map/ppermute | solution.py:20
  116.1 5.1 %collective-permute-start.29 = (f16[12,32,128]{2,1,0:T(8,128)(2,1)S(1)}, f16[12,32,128]{2,1,0:T(8,128)(2,1)S(1)}, u32[]{:S(2)}, u32[]{:S(2)}) collective-permute-start(f16[12,32,128]{2,1,0:T(8,128)(2,1)S(1)} %convert_element_type.132), channel_id=1, source_target_pairs={{0,4},{4,0},{8,28},{12,24},{16,20},{20,16},{24,12},{28,8},{1,5},{5... | collective-permute-start | bytes 294920 | tf_op jit(solution)/shard_map/ppermute | solution.py:352

commit v6 on v4

--- a/solution.py
+++ b/solution.py
@@ -51,21 +51,20 @@
     return lax.psum_scatter(jnp.stack(kept, axis=1), "space", scatter_dimension=2, tiled=True)
 
 
-def in_order(body, out_shape, n_in, n_after=0):
-    anywhere = pl.BlockSpec(memory_space=pl.ANY)
+def on_units(body, out_shape, n_in):
     whole = pl.BlockSpec(memory_space=pltpu.VMEM)
     return pl.pallas_call(
         body,
         out_shape=out_shape,
-        in_specs=[whole] * n_in + [anywhere] * n_after,
+        in_specs=[whole] * n_in,
         out_specs=jax.tree.map(lambda _: whole, out_shape),
-        compiler_params=pltpu.CompilerParams(vmem_limit_bytes=40 << 20),
+        compiler_params=pltpu.CompilerParams(vmem_limit_bytes=18 << 20),
         cost_estimate=pl.CostEstimate(flops=1000, bytes_accessed=1000, transcendentals=0),
     )
 
 
 def clean_kernel(
-    cols_hbm, threshold_ref, snapshots_hbm, values_hbm, all_ref, *refs
+    cols_hbm, threshold_ref, snapshots_hbm, values_hbm, rest_ref, *refs
 ):
     *sent_refs, cols_ref, snapshots_ref, values_ref, cols_sem, row_sems, value_sems = refs
     tile_rows, listed, height, _ = values_ref.shape
@@ -89,7 +88,9 @@
         row_copies[g].wait()
 
         def put(unit, columns, value):
-            all_ref[unit, g * width : (g + 1) * width, columns] = value
+            if unit >= len(STAGES[0]):
+                top = (unit - len(STAGES[0])) * height + g * width
+                rest_ref[top : top + width, columns] = value
             for stage, sent_ref in enumerate(sent_refs):
                 if unit in STAGES[stage]:
                     top = (unit - STAGES[stage][0]) * height + g * width
@@ -113,12 +114,12 @@
                 put(unit, columns, shrunk(snapshots_ref[rows, columns].astype(jnp.float32) - total))
 
 
-def clean_units(snapshots, outlier_cols, outlier_values, threshold, first):
+def clean_units(snapshots, outlier_cols, outlier_values, threshold):
     rows, points = snapshots.shape
     tile_rows = outlier_values.shape[0]
     length = rows // UNITS
-    out_shape = [jax.ShapeDtypeStruct((UNITS, length, points), jnp.bfloat16)]
-    out_shape += [jax.ShapeDtypeStruct((len(units) * length, points), jnp.bfloat16) for units in STAGES[:first]]
+    counts = [UNITS - len(STAGES[0])] + [len(units) for units in STAGES]
+    out_shape = [jax.ShapeDtypeStruct((n * length, points), jnp.bfloat16) for n in counts]
     hbm = pl.BlockSpec(memory_space=pltpu.HBM)
     stay_put = functools.partial(pltpu.with_memory_space_constraint, memory_space=pltpu.HBM)
     return pl.pallas_call(
@@ -134,7 +135,7 @@
             pltpu.SemaphoreType.DMA((tile_rows,)),
             pltpu.SemaphoreType.DMA((tile_rows,)),
         ],
-        compiler_params=pltpu.CompilerParams(vmem_limit_bytes=40 << 20),
+        compiler_params=pltpu.CompilerParams(vmem_limit_bytes=18 << 20),
     )(stay_put(outlier_cols), threshold.reshape(1), stay_put(snapshots), stay_put(outlier_values))
 
 
@@ -144,9 +145,9 @@
     return [ref[pl.ds(pl.multiple_of((here ^ q) * width, width), width), :] for q in (0, 2, 1, 3)]
 
 
-def multiply(cols, rows, down, stay_ref, away_ref, places):
+def multiply(cols, rows, stay_ref, away_ref, places):
     cols = [piece for ref in cols for piece in columns_of(ref)]
-    product = tile_product(jnp.concatenate(cols, axis=0), jnp.concatenate([ref[...] for ref in rows], axis=0)) * down
+    product = tile_product(jnp.concatenate(cols, axis=0), jnp.concatenate([ref[...] for ref in rows], axis=0))
     width, length = stay_ref.shape[2:]
     for c, line in enumerate(places):
         for s, place in enumerate(line):
@@ -156,11 +157,16 @@
                 (stay_ref, stay_ref, away_ref, away_ref)[q][q % 2, place] = block
 
 
-def own_kernel(down, all_ref, stay_ref, away_ref, copy_ref):
-    units = [all_ref.at[s] for s in range(UNITS)]
+def units_of(stage_refs):
+    length = stage_refs[0].shape[0] // len(STAGES[0])
+    return [ref.at[pl.ds(i * length, length)] for s, ref in enumerate(stage_refs) for i in range(len(STAGES[s]))]
+
+
+def own_kernel(*refs):
+    *own_refs, stay_ref, away_ref = refs
+    units = units_of(own_refs)
     for c in range(UNITS):
-        multiply([units[c]], units, down, stay_ref, away_ref, [[c * UNITS + s for s in range(UNITS)]])
-    copy_ref[...] = all_ref[...]
+        multiply([units[c]], units, stay_ref, away_ref, [[c * UNITS + s for s in range(UNITS)]])
 
 
 def x_blocks(stage):
@@ -177,32 +183,31 @@
     return names + [("y", key) for key in y_blocks(stage)] + [("side", key) for key in y_blocks(stage)]
 
 
-def stage_kernel(down, stage, n_after, *refs):
+def stage_kernel(stage, *refs):
     refs = list(refs)
 
     def take(n):
         out, refs[:n] = refs[:n], []
         return out
 
-    all_ref, sibling_ref, y_ref, y_other_ref = take(4)
+    own_refs = take(len(STAGES))
+    sibling_ref, y_ref, y_other_ref = take(3)
     x_refs = take(stage + 1)
     left_before, cross_before = take(stage), take(stage)
-    take(n_after)
     stay_ref, away_ref, left_ref, cross_ref, side_ref = take(5)
     core = lax.rem(lax.axis_index("tm"), 2)
     far = lax.rem(lax.div(lax.axis_index("tm"), 2), 2)
     fresh, before = STAGES[stage], STAGES[stage][0]
     first, count = fresh[0], len(fresh)
-    length = all_ref.shape[1]
+    length = own_refs[0].shape[0] // len(STAGES[0])
+    sibling_first = (first - len(STAGES[0])) * length if stage > 0 else 0
 
     def unit_of(ref, i):
         return ref.at[pl.ds(i * length, length)]
 
-    def units_of(stage_refs):
-        return [unit_of(ref, i) for s, ref in enumerate(stage_refs) for i in range(len(STAGES[s]))]
-
-    for i, unit in enumerate(fresh):
+    for i in range(count):
         rows = slice(i * length, (i + 1) * length)
+        sibling_rows = slice(sibling_first + i * length, sibling_first + (i + 1) * length)
 
         @pl.when(far == 1)
         def _():
@@ -211,12 +216,12 @@
 
         @pl.when(far == 0)
         def _():
-            left_ref[rows] = all_ref[unit]
-            cross_ref[rows] = sibling_ref[unit]
+            left_ref[rows] = own_refs[stage][rows]
+            cross_ref[rows] = sibling_ref[sibling_rows]
 
         @pl.when(core == 0)
         def _():
-            side_ref[rows] = sibling_ref[unit]
+            side_ref[rows] = sibling_ref[sibling_rows]
 
         @pl.when(core == 1)
         def _():
@@ -229,7 +234,6 @@
     multiply(
         x_units[first:],
         left + cross,
-        down,
         stay_ref,
         away_ref,
         [[place[name, (c, s)] for name in ("near", "cross") for s in range(n)] for c in fresh],
@@ -238,15 +242,13 @@
         multiply(
             x_units[:first],
             left[first:] + cross[first:],
-            down,
             stay_ref,
             away_ref,
             [[place[name, (c, s)] for name in ("near", "cross") for s in fresh] for c in range(before)],
         )
     multiply(
         [unit_of(ref, i) for ref in (y_ref, side_ref) for i in range(count)],
-        [all_ref.at[s] for s in range(UNITS)],
-        down,
+        units_of(own_refs),
         stay_ref,
         away_ref,
         [[place[name, (c, s)] for s in range(UNITS)] for name in ("y", "side") for c in fresh],
@@ -306,37 +308,42 @@
     def units(n):
         return jax.ShapeDtypeStruct((n * length, points), jnp.bfloat16)
 
+    def behind(value, *others):
+        return lax.optimization_barrier((value, *others))[0]
+
     def half_summed(stay, away):
-        return stay + swapped(away.astype(jnp.float16), "space", 1).astype(jnp.float32)
+        came = swapped((away * down).astype(jnp.float16), "space", 1)
+        return stay * down + came.astype(jnp.float32), came
 
     def summed(kept):
         return kept[0] + swapped(kept[1].astype(jnp.float16), "space", 2).astype(jnp.float32)
 
-    whole, *sent = clean_units(snapshots, outlier_cols, outlier_values, threshold, len(STAGES))
-    out_shape = message(UNITS * UNITS) + [jax.ShapeDtypeStruct(whole.shape, whole.dtype)]
-    stay, away, lent = in_order(functools.partial(own_kernel, down), out_shape, 1)(whole)
-    sibling = swapped(lent, "tm", 1)
-    halves = [half_summed(stay, away)]
-    own = summed(halves[0])
-    x_units, left, cross, totals = [], [], [], []
+    rest, *sent = clean_units(snapshots, outlier_cols, outlier_values, threshold)
+    stay, away = on_units(own_kernel, message(UNITS * UNITS), len(sent))(*sent)
+    sibling = swapped(sent[0], "tm", 1)
+    half, own_came = half_summed(stay, away)
+    own = summed(half)
+    x_units, by_y, left, cross, totals, came = [], [], [], [], [], None
     for stage, fresh in enumerate(STAGES):
         block = sent[stage]
         if stage > 0:
-            block, *_ = lax.optimization_barrier((block, x_units[-1], y_units))
+            block = behind(block, x_units[-1], by_y[-1])
         x_units.append(swapped(block, "tm", 2))
-        y_units = swapped(block, "tm", 4)
-        y_other = swapped(lax.optimization_barrier((y_units, x_units[-1]))[0], "tm", 1)
-        operands = [whole, sibling, y_units, y_other, *x_units, *left, *cross]
-        after = [own] if stage == 1 else totals[:-1] if stage > 1 else []
-        after = after + halves[-1:]
+        by_y.append(swapped(block, "tm", 4))
+        other = swapped(behind(by_y[-1], x_units[-1], *([own_came], left, left[1:])[stage]), "tm", 1)
+        if stage == 1:
+            sibling = swapped(behind(rest, left[0]), "tm", 1)
+        if stage > 0:
+            other = behind(other, came, *([own] if stage == 1 else totals[:-1]))
+        operands = [*sent, sibling, by_y[-1], other, *x_units, *left, *cross]
         out_shape = message(len(stage_blocks(stage))) + [units(len(fresh))] * 3
-        stay, away, left_now, cross_now, _ = in_order(
-            functools.partial(stage_kernel, down, stage, len(after)), out_shape, len(operands), len(after)
-        )(*operands, *after)
+        stay, away, left_now, cross_now, _ = on_units(
+            functools.partial(stage_kernel, stage), out_shape, len(operands)
+        )(*operands)
         left.append(left_now)
         cross.append(cross_now)
-        halves.append(half_summed(stay, away))
-        totals.append(summed(halves[-1]))
+        half, came = half_summed(stay, away)
+        totals.append(summed(half))
 
     parts = []
     for first, last in GOES:
@@ -345,7 +352,7 @@
             n = len(x_blocks(stage))
             near.append(totals[stage][:n])
             other.append(totals[stage][n : 2 * n])
-        near, other = jnp.concatenate(near), jnp.concatenate(other)
+        near, other = (behind(jnp.concatenate(part), *(parts or [came])) for part in (near, other))
         handed = swapped(near.astype(jnp.float16), "tm", 4, lambda i: i & 2)
         parts.append(jnp.where(far == 1, handed.astype(jnp.float32), near))
         pairs = [(i, i ^ (5 if i & 2 else 1)) for i in range(lax.axis_size("tm"))]
@@ -353,7 +360,7 @@
     parts += [total[2 * len(x_blocks(stage)) :] for stage, total in enumerate(totals)]
     out_shape = jax.ShapeDtypeStruct((5, rows, rows // 4), jnp.float32)
     operands = [own, *parts]
-    band = in_order(functools.partial(assemble_kernel, scale), out_shape, len(operands))(*operands)
+    band = on_units(functools.partial(assemble_kernel, scale), out_shape, len(operands))(*operands)
     return band.transpose(1, 0, 2)
 
 

time: 120 us -> 114 us (0.950)
  starting transfers between devices: 39 us -> 33.3 us
  local copies, waits for them, and re-layouts: 6.13 us -> 2.46 us
  waiting for transfers between devices: 51 us -> 53.8 us
  Pallas kernels: 17.6 us -> 19.5 us
    unnamed x28 -> x12, local copies, waits for them, and re-layouts: 6.09 us -> 2.38 us
    ppermute x2, starting transfers between devices: 7.36 us -> 3.7 us  [square(): lax.ppermute(other.astype(jnp.float16), 'tm', pairs).astype(jnp.float32)]
    ppermute x2, waiting for transfers between devices: 2.41 us -> 5.24 us  [square(): lax.ppermute(other.astype(jnp.float16), 'tm', pairs).astype(jnp.float32)]
    ppermute x20 -> x21, starting transfers between devices: 31.6 us -> 29.6 us  [swapped(): return lax.ppermute(x, axis, pairs)]
    pallas_call x5, Pallas kernels: 14.4 us -> 16.2 us  [the longest x3 11.8 us: square(): on_units(functools.partial(stage_kernel, stage), out_shape, len(operands))]
    ppermute x20 -> x21, waiting for transfers between devices: 48.6 us -> 48.6 us  [swapped(): return lax.ppermute(x, axis, pairs)]
  transfers between devices with their start and end apart: 22 -> 23, of which waited for: 10 -> 13; matrix products, arithmetic and copies ran while one was open for 4% -> 3% of each run, Pallas kernels for 7% -> 13%
where the time goes in v6:
time: 114 us
  waiting for transfers between devices  53.8 us (47%)
  starting transfers between devices  33.3 us (29%)
  Pallas kernels  19.5 us (17%)
  other arithmetic  4.01 us (4%)
  local copies, waits for them, and re-layouts  2.46 us (2%)
    ppermute x21, waiting for transfers between devices, swapped(): return lax.ppermute(x, axis, pairs)  48.6 us
    ppermute x21, starting transfers between devices, swapped(): return lax.ppermute(x, axis, pairs)  29.6 us
    pallas_call x3, Pallas kernels, square(): on_units(functools.partial(stage_kernel, stage), out_shape, len(operands))  11.8 us
    ppermute x2, waiting for transfers between devices, square(): lax.ppermute(other.astype(jnp.float16), 'tm', pairs).astype(jnp.float32)  5.24 us
    ppermute x2, starting transfers between devices, square(): lax.ppermute(other.astype(jnp.float16), 'tm', pairs).astype(jnp.float32)  3.7 us
    pallas_call x1, Pallas kernels, clean_units(): pl.pallas_call(clean_kernel, out_shape=out_shape, in_specs=[hbm, pl.Block...  3.27 us
    pallas_call x1, Pallas kernels, square(): stay, away = on_units(own_kernel, message(UNITS * UNITS), len(sent))(*sent)  2.9 us
    unnamed x12, local copies, waits for them, and re-layouts  2.38 us
  transfers between devices with their start and end apart: 23, of which 13 were waited for; matrix products, arithmetic and copies ran while one was open for 3% of the time, Pallas kernels for 13%

profile of v6, /device:TPU:3, one launch (start us, length us, event | category | flops | bytes accessed | tf_op | source)
XLA Modules:
  0.0 114.1 jit_solution(13040014245288821857)
XLA Ops:
  0.7 3.3 %shard_map.46 = (bf16[256,2048]{1,0:T(8,128)(2,1)}, bf16[256,2048]{1,0:T(8,128)(2,1)S(1)}, bf16[128,2048]{1,0:T(8,128)(2,1)S(1)}, bf16[128,2048]{1,0:T(8,128)(2,1)S(1)}) custom-call(s32[4,4]{1,0:T(4,128)} %cols_hbm.1, f32[1]{0:T(128)} %bitcast.26.threshold_ref, bf16[512,2048]{1,0:T(8,128)(2,1)} %snapshots_hbm.1, bf16[4,4,128,128]{3,2,1,0:T(8,128)(2,1)} %values_hbm.1), custom_call_target="tpu_custom_call" | custom-call | tf_op jit(solution)/shard_map/pallas_call | solution.py:125
  3.9 1.3 %collective-permute-start.3 = (bf16[256,2048]{1,0:T(8,128)(2,1)S(1)}, bf16[256,2048]{1,0:T(8,128)(2,1)S(1)}, u32[]{:S(2)}, u32[]{:S(2)}) collective-permute-start(bf16[256,2048]{1,0:T(8,128)(2,1)S(1)} %get-tuple-element.33.refs_0_), channel_id=1, source_target_pairs={{0,16},{4,20},{8,24},{12,28},{16,0},{20,4},{24,8},{28,12},{1,17},{... | collective-permute-start | bytes 3145736 | tf_op jit(solution)/shard_map/ppermute | solution.py:21
  5.2 0.3 collective-permute-start.4
  5.5 2.9 %shard_map.47 = (f32[2,16,32,128]{3,2,1,0:T(8,128)S(1)}, f32[2,16,32,128]{3,2,1,0:T(8,128)S(1)}) custom-call(bf16[256,2048]{1,0:T(8,128)(2,1)S(1)} %get-tuple-element.33.refs_0_, bf16[128,2048]{1,0:T(8,128)(2,1)S(1)} %get-tuple-element.44.refs_1_, bf16[128,2048]{1,0:T(8,128)(2,1)S(1)} %get-tuple-element.50.refs_2_), custom_call_target="tpu_custom_call" | custom-call | flops 1000 | bytes 1000 | tf_op jit(solution)/shard_map/pallas_call | solution.py:322
  8.5 1.4 %collective-permute-start = (f16[2,16,32,128]{3,2,1,0:T(8,128)(2,1)S(1)}, f16[2,16,32,128]{3,2,1,0:T(8,128)(2,1)S(1)}, u32[]{:S(2)}, u32[]{:S(2)}) collective-permute-start(f16[2,16,32,128]{3,2,1,0:T(8,128)(2,1)S(1)} %multiply_convert_fusion.3), channel_id=1, source_target_pairs={{0,1},{1,0},{2,3},{3,2},{4,5},{5,4},{6,7},{7,6},{8,9},{9,8},{10,11... | collective-permute-start | bytes 786440 | tf_op jit(solution)/shard_map/ppermute | solution.py:21
  9.8 1.5 %collective-permute-start.2 = (bf16[256,2048]{1,0:T(8,128)(2,1)S(1)}, bf16[256,2048]{1,0:T(8,128)(2,1)S(1)}, u32[]{:S(2)}, u32[]{:S(2)}) collective-permute-start(bf16[256,2048]{1,0:T(8,128)(2,1)S(1)} %get-tuple-element.33.refs_0_), channel_id=1, source_target_pairs={{0,4},{4,0},{8,12},{12,8},{16,20},{20,16},{24,28},{28,24},{1,5},{5... | collective-permute-start | bytes 3145736 | tf_op jit(solution)/shard_map/ppermute | solution.py:21
  11.3 3.8 %collective-permute-done = f16[2,16,32,128]{3,2,1,0:T(8,128)(2,1)S(1)} collective-permute-done((f16[2,16,32,128]{3,2,1,0:T(8,128)(2,1)S(1)}, f16[2,16,32,128]{3,2,1,0:T(8,128)(2,1)S(1)}, u32[]{:S(2)}, u32[]{:S(2)}) %collective-permute-start) | collective-permute-done | bytes 262176 | tf_op jit(solution)/shard_map/ppermute | solution.py:21
  15.1 12.9 %collective-permute-done.3.refs_4_ = bf16[256,2048]{1,0:T(8,128)(2,1)S(1)} collective-permute-done((bf16[256,2048]{1,0:T(8,128)(2,1)S(1)}, bf16[256,2048]{1,0:T(8,128)(2,1)S(1)}, u32[]{:S(2)}, u32[]{:S(2)}) %collective-permute-start.3) | collective-permute-done | bytes 1048608 | tf_op jit(solution)/shard_map/ppermute | solution.py:21
  28.0 0.9 collective-permute-done.4.refs_6_
  28.9 1.9 %collective-permute-start.5 = (bf16[256,2048]{1,0:T(8,128)(2,1)S(1)}, bf16[256,2048]{1,0:T(8,128)(2,1)S(1)}, u32[]{:S(2)}, u32[]{:S(2)}) collective-permute-start(bf16[256,2048]{1,0:T(8,128)(2,1)S(1)} %collective-permute-done.3.refs_4_), channel_id=1, source_target_pairs={{0,4},{4,0},{8,12},{12,8},{16,20},{20,16},{24,28},{28,24},{1,5},{5... | collective-permute-start | bytes 3145736 | tf_op jit(solution)/shard_map/ppermute | solution.py:21
  30.9 0.3 collective-permute-start.9
  31.2 0.1 collective-permute-start.10
  31.3 1.8 %collective-permute-done.5.refs_5_ = bf16[256,2048]{1,0:T(8,128)(2,1)S(1)} collective-permute-done((bf16[256,2048]{1,0:T(8,128)(2,1)S(1)}, bf16[256,2048]{1,0:T(8,128)(2,1)S(1)}, u32[]{:S(2)}, u32[]{:S(2)}) %collective-permute-start.5) | collective-permute-done | bytes 1048608 | tf_op jit(solution)/shard_map/ppermute | solution.py:21
  33.1 2.8 %shard_map.48 = (f32[2,24,32,128]{3,2,1,0:T(8,128)S(1)}, f32[2,24,32,128]{3,2,1,0:T(8,128)S(1)}, bf16[256,2048]{1,0:T(8,128)(2,1)S(1)}, bf16[256,2048]{1,0:T(8,128)(2,1)S(1)}, bf16[256,2048]{1,0:T(8,128)(2,1)}) custom-call(bf16[256,2048]{1,0:T(8,128)(2,1)S(1)} %get-tuple-element.33.refs_0_, bf16[128,2048]{1,0:T(8,128)(2,1)S(1)} %get-tuple-element.44.refs_1_, ...), custom_call_target="tpu_custom_call" | custom-call | flops 1000 | bytes 1000 | tf_op jit(solution)/shard_map/pallas_call | solution.py:340
  35.9 1.0 copy-done
  36.9 1.0 copy-done.2
  37.8 0.4 collective-permute-start.8
  38.3 0.4 copy-done.4
  38.7 1.3 %collective-permute-start.6 = (f16[2,24,32,128]{3,2,1,0:T(8,128)(2,1)S(1)}, f16[2,24,32,128]{3,2,1,0:T(8,128)(2,1)}, u32[]{:S(2)}, u32[]{:S(2)}) collective-permute-start(f16[2,24,32,128]{3,2,1,0:T(8,128)(2,1)S(1)} %multiply_convert_fusion), channel_id=1, source_target_pairs={{0,1},{1,0},{2,3},{3,2},{4,5},{5,4},{6,7},{7,6},{8,9},{9,8},{10,11... | collective-permute-start | bytes 1179656 | tf_op jit(solution)/shard_map/ppermute | solution.py:21
  40.0 0.7 fusion.7
  40.7 2.3 %collective-permute-start.1 = (f16[16,32,128]{2,1,0:T(8,128)(2,1)}, f16[16,32,128]{2,1,0:T(8,128)(2,1)}, u32[]{:S(2)}, u32[]{:S(2)}) collective-permute-start(f16[16,32,128]{2,1,0:T(8,128)(2,1)} %fusion.7), channel_id=1, source_target_pairs={{0,2},{1,3},{2,0},{3,1},{4,6},{5,7},{6,4},{7,5},{8,10},{9,11},{10,... | collective-permute-start | bytes 393224 | tf_op jit(solution)/shard_map/ppermute | solution.py:21
  43.0 1.6 %collective-permute-done.9.refs_4_ = bf16[128,2048]{1,0:T(8,128)(2,1)} collective-permute-done((bf16[128,2048]{1,0:T(8,128)(2,1)S(1)}, bf16[128,2048]{1,0:T(8,128)(2,1)}, u32[]{:S(2)}, u32[]{:S(2)}) %collective-permute-start.9) | collective-permute-done | bytes 524320 | tf_op jit(solution)/shard_map/ppermute | solution.py:21
  44.6 1.0 collective-permute-start.11
  45.6 5.4 %collective-permute-done.1 = f16[16,32,128]{2,1,0:T(8,128)(2,1)} collective-permute-done((f16[16,32,128]{2,1,0:T(8,128)(2,1)}, f16[16,32,128]{2,1,0:T(8,128)(2,1)}, u32[]{:S(2)}, u32[]{:S(2)}) %collective-permute-start.1) | collective-permute-done | bytes 131104 | tf_op jit(solution)/shard_map/ppermute | solution.py:21
  51.1 1.0 fusion.3.refs_0_
  52.1 0.3 collective-permute-start.14
  52.4 0.4 collective-permute-start.15
  52.7 1.4 %convert_add_fusion = f32[2,24,32,128]{3,2,1,0:T(8,128)S(1)} fusion(f16[2,24,32,128]{3,2,1,0:T(8,128)(2,1)} %collective-permute-done.6, f32[2,24,32,128]{3,2,1,0:T(8,128)} %copy-done.4), kind=kLoop, calls=%fused_computation | loop fusion | flops 589824 | bytes 1966080 | tf_op jit(solution)/shard_map/add | solution.py:316
  54.2 3.2 %collective-permute-start.7 = (f16[24,32,128]{2,1,0:T(8,128)(2,1)S(1)}, f16[24,32,128]{2,1,0:T(8,128)(2,1)S(1)}, u32[]{:S(2)}, u32[]{:S(2)}) collective-permute-start(f16[24,32,128]{2,1,0:T(8,128)(2,1)S(1)} %fusion.4), channel_id=1, source_target_pairs={{0,2},{1,3},{2,0},{3,1},{4,6},{5,7},{6,4},{7,5},{8,10},{9,11},{10,... | collective-permute-start | bytes 589832 | tf_op jit(solution)/shard_map/ppermute | solution.py:21
  57.4 4.2 %shard_map.49 = (f32[2,18,32,128]{3,2,1,0:T(8,128)S(1)}, f32[2,18,32,128]{3,2,1,0:T(8,128)S(1)}, bf16[128,2048]{1,0:T(8,128)(2,1)S(1)}, bf16[128,2048]{1,0:T(8,128)(2,1)S(1)}, bf16[128,2048]{1,0:T(8,128)(2,1)}) custom-call(bf16[256,2048]{1,0:T(8,128)(2,1)S(1)} %get-tuple-element.33.refs_0_, bf16[128,2048]{1,0:T(8,128)(2,1)S(1)} %get-tuple-element.44.refs_1_, ...), custom_call_target="tpu_custom_call" | custom-call | flops 1000 | bytes 1000 | tf_op jit(solution)/shard_map/pallas_call | solution.py:340
  61.6 0.2 collective-permute-start.12
  61.9 2.4 %collective-permute-done.14.refs_4_ = bf16[128,2048]{1,0:T(8,128)(2,1)S(1)} collective-permute-done((bf16[128,2048]{1,0:T(8,128)(2,1)S(1)}, bf16[128,2048]{1,0:T(8,128)(2,1)S(1)}, u32[]{:S(2)}, u32[]{:S(2)}) %collective-permute-start.14) | collective-permute-done | bytes 524320 | tf_op jit(solution)/shard_map/ppermute | solution.py:21
  64.4 3.4 %collective-permute-start.16 = (bf16[128,2048]{1,0:T(8,128)(2,1)S(1)}, bf16[128,2048]{1,0:T(8,128)(2,1)S(1)}, u32[]{:S(2)}, u32[]{:S(2)}) collective-permute-start(bf16[128,2048]{1,0:T(8,128)(2,1)S(1)} %collective-permute-done.14.refs_4_), channel_id=1, source_target_pairs={{0,4},{4,0},{8,12},{12,8},{16,20},{20,16},{24,28},{28,24},{1,5},{5... | collective-permute-start | bytes 1572872 | tf_op jit(solution)/shard_map/ppermute | solution.py:21
  67.7 3.7 %collective-permute-done.12 = f16[2,18,32,128]{3,2,1,0:T(8,128)(2,1)S(1)} collective-permute-done((f16[2,18,32,128]{3,2,1,0:T(8,128)(2,1)S(1)}, f16[2,18,32,128]{3,2,1,0:T(8,128)(2,1)S(1)}, u32[]{:S(2)}, u32[]{:S(2)}) %collective-permute-start.12) | collective-permute-done | bytes 294944 | tf_op jit(solution)/shard_map/ppermute | solution.py:21
  71.5 2.2 %collective-permute-start.13 = (f16[18,32,128]{2,1,0:T(8,128)(2,1)S(1)}, f16[18,32,128]{2,1,0:T(8,128)(2,1)S(1)}, u32[]{:S(2)}, u32[]{:S(2)}) collective-permute-start(f16[18,32,128]{2,1,0:T(8,128)(2,1)S(1)} %fusion.6), channel_id=1, source_target_pairs={{0,2},{1,3},{2,0},{3,1},{4,6},{5,7},{6,4},{7,5},{8,10},{9,11},{10,... | collective-permute-start | bytes 442376 | tf_op jit(solution)/shard_map/ppermute | solution.py:21
  73.7 4.8 %shard_map.50 = (f32[2,22,32,128]{3,2,1,0:T(8,128)S(1)}, f32[2,22,32,128]{3,2,1,0:T(8,128)S(1)}, bf16[128,2048]{1,0:T(8,128)(2,1)}, bf16[128,2048]{1,0:T(8,128)(2,1)}, bf16[128,2048]{1,0:T(8,128)(2,1)}) custom-call(bf16[256,2048]{1,0:T(8,128)(2,1)S(1)} %get-tuple-element.33.refs_0_, bf16[128,2048]{1,0:T(8,128)(2,1)S(1)} %get-tuple-element.44.refs_1_, ...), custom_call_target="tpu_custom_call" | custom-call | flops 1000 | bytes 1000 | tf_op jit(solution)/shard_map/pallas_call | solution.py:340
  78.6 2.3 %collective-permute-start.17 = (f16[2,22,32,128]{3,2,1,0:T(8,128)(2,1)S(1)}, f16[2,22,32,128]{3,2,1,0:T(8,128)(2,1)S(1)}, u32[]{:S(2)}, u32[]{:S(2)}) collective-permute-start(f16[2,22,32,128]{3,2,1,0:T(8,128)(2,1)S(1)} %multiply_convert_fusion.1), channel_id=1, source_target_pairs={{0,1},{1,0},{2,3},{3,2},{4,5},{5,4},{6,7},{7,6},{8,9},{9,8},{10,11... | collective-permute-start | bytes 1081352 | tf_op jit(solution)/shard_map/ppermute | solution.py:21
  81.0 7.9 %collective-permute-done.17 = f16[2,22,32,128]{3,2,1,0:T(8,128)(2,1)S(1)} collective-permute-done((f16[2,22,32,128]{3,2,1,0:T(8,128)(2,1)S(1)}, f16[2,22,32,128]{3,2,1,0:T(8,128)(2,1)S(1)}, u32[]{:S(2)}, u32[]{:S(2)}) %collective-permute-start.17) | collective-permute-done | bytes 360480 | tf_op jit(solution)/shard_map/ppermute | solution.py:21
  88.9 3.1 %collective-permute-start.18 = (f16[9,32,128]{2,1,0:T(8,128)(2,1)S(1)}, f16[9,32,128]{2,1,0:T(8,128)(2,1)S(1)}, u32[]{:S(2)}, u32[]{:S(2)}) collective-permute-start(f16[9,32,128]{2,1,0:T(8,128)(2,1)S(1)} %convert_element_type.89), channel_id=1, source_target_pairs={{8,24},{12,28},{24,8},{28,12},{9,25},{13,29},{25,9},{29,13},{10,26... | collective-permute-start | bytes 221192 | tf_op jit(solution)/shard_map/ppermute | solution.py:21
  92.0 1.9 %collective-permute-start.19 = (f16[9,32,128]{2,1,0:T(8,128)(2,1)S(1)}, f16[9,32,128]{2,1,0:T(8,128)(2,1)S(1)}, u32[]{:S(2)}, u32[]{:S(2)}) collective-permute-start(f16[9,32,128]{2,1,0:T(8,128)(2,1)S(1)} %convert_element_type.91), channel_id=1, source_target_pairs={{0,4},{4,0},{8,28},{12,24},{16,20},{20,16},{24,12},{28,8},{1,5},{5... | collective-permute-start | bytes 221192 | tf_op jit(solution)/shard_map/ppermute | solution.py:359
  94.0 0.6 collective-permute-start.20
  94.6 2.9 %collective-permute-done.19 = f16[9,32,128]{2,1,0:T(8,128)(2,1)S(1)} collective-permute-done((f16[9,32,128]{2,1,0:T(8,128)(2,1)S(1)}, f16[9,32,128]{2,1,0:T(8,128)(2,1)S(1)}, u32[]{:S(2)}, u32[]{:S(2)}) %collective-permute-start.19) | collective-permute-done | bytes 73760 | tf_op jit(solution)/shard_map/ppermute | solution.py:359
  97.6 7.6 %collective-permute-done.20 = f16[22,32,128]{2,1,0:T(8,128)(2,1)S(1)} collective-permute-done((f16[22,32,128]{2,1,0:T(8,128)(2,1)S(1)}, f16[22,32,128]{2,1,0:T(8,128)(2,1)S(1)}, u32[]{:S(2)}, u32[]{:S(2)}) %collective-permute-start.20) | collective-permute-done | bytes 180256 | tf_op jit(solution)/shard_map/ppermute | solution.py:21
  105.3 2.5 %collective-permute-start.21 = (f16[7,32,128]{2,1,0:T(8,128)(2,1)S(1)}, f16[7,32,128]{2,1,0:T(8,128)(2,1)S(1)}, u32[]{:S(2)}, u32[]{:S(2)}) collective-permute-start(f16[7,32,128]{2,1,0:T(8,128)(2,1)S(1)} %convert_element_type.96), channel_id=1, source_target_pairs={{8,24},{12,28},{24,8},{28,12},{9,25},{13,29},{25,9},{29,13},{10,26... | collective-permute-start | bytes 172040 | tf_op jit(solution)/shard_map/ppermute | solution.py:21
  107.8 1.8 %collective-permute-start.22 = (f16[7,32,128]{2,1,0:T(8,128)(2,1)S(1)}, f16[7,32,128]{2,1,0:T(8,128)(2,1)S(1)}, u32[]{:S(2)}, u32[]{:S(2)}) collective-permute-start(f16[7,32,128]{2,1,0:T(8,128)(2,1)S(1)} %convert_element_type.98), channel_id=1, source_target_pairs={{0,4},{4,0},{8,28},{12,24},{16,20},{20,16},{24,12},{28,8},{1,5},{5... | collective-permute-start | bytes 172040 | tf_op jit(solution)/shard_map/ppermute | solution.py:359
  109.6 0.6 collective-permute-done.21
  110.2 2.3 %collective-permute-done.22 = f16[7,32,128]{2,1,0:T(8,128)(2,1)S(1)} collective-permute-done((f16[7,32,128]{2,1,0:T(8,128)(2,1)S(1)}, f16[7,32,128]{2,1,0:T(8,128)(2,1)S(1)}, u32[]{:S(2)}, u32[]{:S(2)}) %collective-permute-start.22) | collective-permute-done | bytes 57376 | tf_op jit(solution)/shard_map/ppermute | solution.py:359
  112.5 1.5 %shard_map.51 = f32[5,512,128]{2,1,0:T(8,128)} custom-call(f32[16,32,128]{2,1,0:T(8,128)S(1)} %fusion.3.refs_0_, f32[9,32,128]{2,1,0:T(8,128)S(1)} %convert_select_fusion.refs_1_, f32[9,32,128]{2,1,0:T(8,128)S(1)} %convert_element_type.92.refs_2_, f32[7,32,128]{2,1,0:T(8,128)S(1)} %convert_select_fusion.1.refs_3_, ...), custom_call_target="tpu_custom_call" | custom-call | flops 1000 | bytes 1000 | tf_op jit(solution)/shard_map/pallas_call | solution.py:363
  (47 shorter events, 1.1 us)
Async XLA Ops:
  3.9 24.1 %collective-permute-start.3 = (bf16[256,2048]{1,0:T(8,128)(2,1)S(1)}, bf16[256,2048]{1,0:T(8,128)(2,1)S(1)}, u32[]{:S(2)}, u32[]{:S(2)}) collective-permute-start(bf16[256,2048]{1,0:T(8,128)(2,1)S(1)} %get-tuple-element.33.refs_0_), channel_id=1, source_target_pairs={{0,16},{4,20},{8,24},{12,28},{16,0},{20,4},{24,8},{28,12},{1,17},{... | collective-permute-start | bytes 3145736 | tf_op jit(solution)/shard_map/ppermute | solution.py:21
  5.2 23.7 %collective-permute-start.4 = (bf16[256,2048]{1,0:T(8,128)(2,1)S(1)}, bf16[256,2048]{1,0:T(8,128)(2,1)S(1)}, u32[]{:S(2)}, u32[]{:S(2)}) collective-permute-start(bf16[256,2048]{1,0:T(8,128)(2,1)S(1)} %get-tuple-element.33.refs_0_), channel_id=1, source_target_pairs={{0,8},{4,12},{8,0},{12,4},{16,24},{20,28},{24,16},{28,20},{1,9},{5... | collective-permute-start | bytes 3145736 | tf_op jit(solution)/shard_map/ppermute | solution.py:21
  8.5 6.6 %collective-permute-start = (f16[2,16,32,128]{3,2,1,0:T(8,128)(2,1)S(1)}, f16[2,16,32,128]{3,2,1,0:T(8,128)(2,1)S(1)}, u32[]{:S(2)}, u32[]{:S(2)}) collective-permute-start(f16[2,16,32,128]{3,2,1,0:T(8,128)(2,1)S(1)} %multiply_convert_fusion.3), channel_id=1, source_target_pairs={{0,1},{1,0},{2,3},{3,2},{4,5},{5,4},{6,7},{7,6},{8,9},{9,8},{10,11... | collective-permute-start | bytes 786440 | tf_op jit(solution)/shard_map/ppermute | solution.py:21
  9.8 21.5 %collective-permute-start.2 = (bf16[256,2048]{1,0:T(8,128)(2,1)S(1)}, bf16[256,2048]{1,0:T(8,128)(2,1)S(1)}, u32[]{:S(2)}, u32[]{:S(2)}) collective-permute-start(bf16[256,2048]{1,0:T(8,128)(2,1)S(1)} %get-tuple-element.33.refs_0_), channel_id=1, source_target_pairs={{0,4},{4,0},{8,12},{12,8},{16,20},{20,16},{24,28},{28,24},{1,5},{5... | collective-permute-start | bytes 3145736 | tf_op jit(solution)/shard_map/ppermute | solution.py:21
  28.9 4.2 %collective-permute-start.5 = (bf16[256,2048]{1,0:T(8,128)(2,1)S(1)}, bf16[256,2048]{1,0:T(8,128)(2,1)S(1)}, u32[]{:S(2)}, u32[]{:S(2)}) collective-permute-start(bf16[256,2048]{1,0:T(8,128)(2,1)S(1)} %collective-permute-done.3.refs_4_), channel_id=1, source_target_pairs={{0,4},{4,0},{8,12},{12,8},{16,20},{20,16},{24,28},{28,24},{1,5},{5... | collective-permute-start | bytes 3145736 | tf_op jit(solution)/shard_map/ppermute | solution.py:21
  30.9 9.1 %copy-start.5 = (f32[2,16,32,128]{3,2,1,0:T(8,128)}, f32[2,16,32,128]{3,2,1,0:T(8,128)S(1)}, u32[]{:S(2)}) copy-start(f32[2,16,32,128]{3,2,1,0:T(8,128)S(1)} %convert_add_fusion.3) | copy-start | bytes 1572868
  30.9 13.7 %collective-permute-start.9 = (bf16[128,2048]{1,0:T(8,128)(2,1)S(1)}, bf16[128,2048]{1,0:T(8,128)(2,1)}, u32[]{:S(2)}, u32[]{:S(2)}) collective-permute-start(bf16[128,2048]{1,0:T(8,128)(2,1)S(1)} %get-tuple-element.44.refs_1_), channel_id=1, source_target_pairs={{0,16},{4,20},{8,24},{12,28},{16,0},{20,4},{24,8},{28,12},{1,17},{... | collective-permute-start | bytes 1572872 | tf_op jit(solution)/shard_map/ppermute | solution.py:21
  31.2 13.4 %collective-permute-start.10 = (bf16[128,2048]{1,0:T(8,128)(2,1)S(1)}, bf16[128,2048]{1,0:T(8,128)(2,1)}, u32[]{:S(2)}, u32[]{:S(2)}) collective-permute-start(bf16[128,2048]{1,0:T(8,128)(2,1)S(1)} %get-tuple-element.44.refs_1_), channel_id=1, source_target_pairs={{0,8},{4,12},{8,0},{12,4},{16,24},{20,28},{24,16},{28,20},{1,9},{5... | collective-permute-start | bytes 1572872 | tf_op jit(solution)/shard_map/ppermute | solution.py:21
  35.9 1.0 copy-start
  36.8 1.0 copy-start.2
  37.8 0.9 copy-start.4
  37.8 19.5 %collective-permute-start.8 = (bf16[256,2048]{1,0:T(8,128)(2,1)}, bf16[256,2048]{1,0:T(8,128)(2,1)}, u32[]{:S(2)}, u32[]{:S(2)}) collective-permute-start(bf16[256,2048]{1,0:T(8,128)(2,1)} %get-tuple-element.43), channel_id=1, source_target_pairs={{0,4},{4,0},{8,12},{12,8},{16,20},{20,16},{24,28},{28,24},{1,5},{5... | collective-permute-start | bytes 3145736 | tf_op jit(solution)/shard_map/ppermute | solution.py:21
  38.7 14.0 %collective-permute-start.6 = (f16[2,24,32,128]{3,2,1,0:T(8,128)(2,1)S(1)}, f16[2,24,32,128]{3,2,1,0:T(8,128)(2,1)}, u32[]{:S(2)}, u32[]{:S(2)}) collective-permute-start(f16[2,24,32,128]{3,2,1,0:T(8,128)(2,1)S(1)} %multiply_convert_fusion), channel_id=1, source_target_pairs={{0,1},{1,0},{2,3},{3,2},{4,5},{5,4},{6,7},{7,6},{8,9},{9,8},{10,11... | collective-permute-start | bytes 1179656 | tf_op jit(solution)/shard_map/ppermute | solution.py:21
  40.7 10.4 %collective-permute-start.1 = (f16[16,32,128]{2,1,0:T(8,128)(2,1)}, f16[16,32,128]{2,1,0:T(8,128)(2,1)}, u32[]{:S(2)}, u32[]{:S(2)}) collective-permute-start(f16[16,32,128]{2,1,0:T(8,128)(2,1)} %fusion.7), channel_id=1, source_target_pairs={{0,2},{1,3},{2,0},{3,1},{4,6},{5,7},{6,4},{7,5},{8,10},{9,11},{10,... | collective-permute-start | bytes 393224 | tf_op jit(solution)/shard_map/ppermute | solution.py:21
  43.0 14.3 %copy-start.1 = (bf16[256,2048]{1,0:T(8,128)(2,1)S(1)}, bf16[256,2048]{1,0:T(8,128)(2,1)}, u32[]{:S(2)}) copy-start(bf16[256,2048]{1,0:T(8,128)(2,1)} %copy-done) | copy-start | bytes 3145732
  43.0 14.3 %copy-start.3 = (bf16[256,2048]{1,0:T(8,128)(2,1)S(1)}, bf16[256,2048]{1,0:T(8,128)(2,1)}, u32[]{:S(2)}) copy-start(bf16[256,2048]{1,0:T(8,128)(2,1)} %copy-done.2) | copy-start | bytes 3145732
  44.6 12.7 %collective-permute-start.11 = (bf16[128,2048]{1,0:T(8,128)(2,1)}, bf16[128,2048]{1,0:T(8,128)(2,1)S(1)}, u32[]{:S(2)}, u32[]{:S(2)}) collective-permute-start(bf16[128,2048]{1,0:T(8,128)(2,1)} %collective-permute-done.9.refs_4_), channel_id=1, source_target_pairs={{0,4},{4,0},{8,12},{12,8},{16,20},{20,16},{24,28},{28,24},{1,5},{5... | collective-permute-start | bytes 1572872 | tf_op jit(solution)/shard_map/ppermute | solution.py:21
  52.1 12.3 %collective-permute-start.14 = (bf16[128,2048]{1,0:T(8,128)(2,1)S(1)}, bf16[128,2048]{1,0:T(8,128)(2,1)S(1)}, u32[]{:S(2)}, u32[]{:S(2)}) collective-permute-start(bf16[128,2048]{1,0:T(8,128)(2,1)S(1)} %get-tuple-element.50.refs_2_), channel_id=1, source_target_pairs={{0,16},{4,20},{8,24},{12,28},{16,0},{20,4},{24,8},{28,12},{1,17},{... | collective-permute-start | bytes 1572872 | tf_op jit(solution)/shard_map/ppermute | solution.py:21
  52.4 12.0 %collective-permute-start.15 = (bf16[128,2048]{1,0:T(8,128)(2,1)S(1)}, bf16[128,2048]{1,0:T(8,128)(2,1)S(1)}, u32[]{:S(2)}, u32[]{:S(2)}) collective-permute-start(bf16[128,2048]{1,0:T(8,128)(2,1)S(1)} %get-tuple-element.50.refs_2_), channel_id=1, source_target_pairs={{0,8},{4,12},{8,0},{12,4},{16,24},{20,28},{24,16},{28,20},{1,9},{5... | collective-permute-start | bytes 1572872 | tf_op jit(solution)/shard_map/ppermute | solution.py:21
  54.2 7.7 %collective-permute-start.7 = (f16[24,32,128]{2,1,0:T(8,128)(2,1)S(1)}, f16[24,32,128]{2,1,0:T(8,128)(2,1)S(1)}, u32[]{:S(2)}, u32[]{:S(2)}) collective-permute-start(f16[24,32,128]{2,1,0:T(8,128)(2,1)S(1)} %fusion.4), channel_id=1, source_target_pairs={{0,2},{1,3},{2,0},{3,1},{4,6},{5,7},{6,4},{7,5},{8,10},{9,11},{10,... | collective-permute-start | bytes 589832 | tf_op jit(solution)/shard_map/ppermute | solution.py:21
  61.6 9.7 %collective-permute-start.12 = (f16[2,18,32,128]{3,2,1,0:T(8,128)(2,1)S(1)}, f16[2,18,32,128]{3,2,1,0:T(8,128)(2,1)S(1)}, u32[]{:S(2)}, u32[]{:S(2)}) collective-permute-start(f16[2,18,32,128]{3,2,1,0:T(8,128)(2,1)S(1)} %multiply_convert_fusion.2), channel_id=1, source_target_pairs={{0,1},{1,0},{2,3},{3,2},{4,5},{5,4},{6,7},{7,6},{8,9},{9,8},{10,11... | collective-permute-start | bytes 884744 | tf_op jit(solution)/shard_map/ppermute | solution.py:21
  64.4 9.3 %collective-permute-start.16 = (bf16[128,2048]{1,0:T(8,128)(2,1)S(1)}, bf16[128,2048]{1,0:T(8,128)(2,1)S(1)}, u32[]{:S(2)}, u32[]{:S(2)}) collective-permute-start(bf16[128,2048]{1,0:T(8,128)(2,1)S(1)} %collective-permute-done.14.refs_4_), channel_id=1, source_target_pairs={{0,4},{4,0},{8,12},{12,8},{16,20},{20,16},{24,28},{28,24},{1,5},{5... | collective-permute-start | bytes 1572872 | tf_op jit(solution)/shard_map/ppermute | solution.py:21
  71.5 9.3 %collective-permute-start.13 = (f16[18,32,128]{2,1,0:T(8,128)(2,1)S(1)}, f16[18,32,128]{2,1,0:T(8,128)(2,1)S(1)}, u32[]{:S(2)}, u32[]{:S(2)}) collective-permute-start(f16[18,32,128]{2,1,0:T(8,128)(2,1)S(1)} %fusion.6), channel_id=1, source_target_pairs={{0,2},{1,3},{2,0},{3,1},{4,6},{5,7},{6,4},{7,5},{8,10},{9,11},{10,... | collective-permute-start | bytes 442376 | tf_op jit(solution)/shard_map/ppermute | solution.py:21
  78.6 10.3 %collective-permute-start.17 = (f16[2,22,32,128]{3,2,1,0:T(8,128)(2,1)S(1)}, f16[2,22,32,128]{3,2,1,0:T(8,128)(2,1)S(1)}, u32[]{:S(2)}, u32[]{:S(2)}) collective-permute-start(f16[2,22,32,128]{3,2,1,0:T(8,128)(2,1)S(1)} %multiply_convert_fusion.1), channel_id=1, source_target_pairs={{0,1},{1,0},{2,3},{3,2},{4,5},{5,4},{6,7},{7,6},{8,9},{9,8},{10,11... | collective-permute-start | bytes 1081352 | tf_op jit(solution)/shard_map/ppermute | solution.py:21
  88.9 8.7 %collective-permute-start.18 = (f16[9,32,128]{2,1,0:T(8,128)(2,1)S(1)}, f16[9,32,128]{2,1,0:T(8,128)(2,1)S(1)}, u32[]{:S(2)}, u32[]{:S(2)}) collective-permute-start(f16[9,32,128]{2,1,0:T(8,128)(2,1)S(1)} %convert_element_type.89), channel_id=1, source_target_pairs={{8,24},{12,28},{24,8},{28,12},{9,25},{13,29},{25,9},{29,13},{10,26... | collective-permute-start | bytes 221192 | tf_op jit(solution)/shard_map/ppermute | solution.py:21
  92.0 5.5 %collective-permute-start.19 = (f16[9,32,128]{2,1,0:T(8,128)(2,1)S(1)}, f16[9,32,128]{2,1,0:T(8,128)(2,1)S(1)}, u32[]{:S(2)}, u32[]{:S(2)}) collective-permute-start(f16[9,32,128]{2,1,0:T(8,128)(2,1)S(1)} %convert_element_type.91), channel_id=1, source_target_pairs={{0,4},{4,0},{8,28},{12,24},{16,20},{20,16},{24,12},{28,8},{1,5},{5... | collective-permute-start | bytes 221192 | tf_op jit(solution)/shard_map/ppermute | solution.py:359
  94.0 11.1 %collective-permute-start.20 = (f16[22,32,128]{2,1,0:T(8,128)(2,1)S(1)}, f16[22,32,128]{2,1,0:T(8,128)(2,1)S(1)}, u32[]{:S(2)}, u32[]{:S(2)}) collective-permute-start(f16[22,32,128]{2,1,0:T(8,128)(2,1)S(1)} %fusion.5), channel_id=1, source_target_pairs={{0,2},{1,3},{2,0},{3,1},{4,6},{5,7},{6,4},{7,5},{8,10},{9,11},{10,... | collective-permute-start | bytes 540680 | tf_op jit(solution)/shard_map/ppermute | solution.py:21
  105.3 4.9 %collective-permute-start.21 = (f16[7,32,128]{2,1,0:T(8,128)(2,1)S(1)}, f16[7,32,128]{2,1,0:T(8,128)(2,1)S(1)}, u32[]{:S(2)}, u32[]{:S(2)}) collective-permute-start(f16[7,32,128]{2,1,0:T(8,128)(2,1)S(1)} %convert_element_type.96), channel_id=1, source_target_pairs={{8,24},{12,28},{24,8},{28,12},{9,25},{13,29},{25,9},{29,13},{10,26... | collective-permute-start | bytes 172040 | tf_op jit(solution)/shard_map/ppermute | solution.py:21
  107.8 4.7 %collective-permute-start.22 = (f16[7,32,128]{2,1,0:T(8,128)(2,1)S(1)}, f16[7,32,128]{2,1,0:T(8,128)(2,1)S(1)}, u32[]{:S(2)}, u32[]{:S(2)}) collective-permute-start(f16[7,32,128]{2,1,0:T(8,128)(2,1)S(1)} %convert_element_type.98), channel_id=1, source_target_pairs={{0,4},{4,0},{8,28},{12,24},{16,20},{20,16},{24,12},{28,8},{1,5},{5... | collective-permute-start | bytes 172040 | tf_op jit(solution)/shard_map/ppermute | solution.py:359

commit v7 on v6

--- a/solution.py
+++ b/solution.py
@@ -13,7 +13,6 @@
 OUTLIER_MAX = 12.0
 UNITS = 4
 STAGES = ((0, 1), (2,), (3,))
-GOES = ((0, 2), (2, 3))
 
 
 def swapped(x, axis, bit, only=None):
@@ -255,20 +254,16 @@
     )
 
 
-def assemble_kernel(scale, *refs):
-    own_ref, out_ref = refs[0], refs[-1]
+def assemble_kernel(scale, own_ref, *refs):
+    *total_refs, handed_ref, crossed_ref, out_ref = refs
     core = lax.rem(lax.axis_index("tm"), 2)
+    far = lax.rem(lax.div(lax.axis_index("tm"), 2), 2)
     where = {("own", (c, s)): (own_ref, c * UNITS + s) for c in range(UNITS) for s in range(UNITS)}
-    rest = iter(refs[1:-1])
-    for first, last in GOES:
-        for name in ("near", "cross"):
-            keys = [key for stage in range(first, last) for key in x_blocks(stage)]
-            ref = next(rest)
-            where.update({(name, key): (ref, i) for i, key in enumerate(keys)})
-    for stage in range(len(STAGES)):
-        ref = next(rest)
-        keys = [(name, key) for name in ("y", "side") for key in y_blocks(stage)]
-        where.update({key: (ref, i) for i, key in enumerate(keys)})
+    for stage, ref in enumerate(total_refs):
+        where.update({key: (ref, i) for i, key in enumerate(stage_blocks(stage))})
+    keys = [key for stage in range(len(STAGES)) for key in x_blocks(stage)]
+    where.update({("handed", key): (handed_ref, i) for i, key in enumerate(keys)})
+    where.update({("crossed", key): (crossed_ref, i) for i, key in enumerate(keys)})
     width = own_ref.shape[1]
     quarter = width * UNITS
 
@@ -280,24 +275,30 @@
                 out_ref[k, g * quarter + s * width : g * quarter + (s + 1) * width, :] = tile[g * width : (g + 1) * width]
 
     put(0, "own")
-    put(2, "near")
     put(4, "y")
+
+    @pl.when(far == 0)
+    def _():
+        put(2, "near")
+
+    @pl.when(far == 1)
+    def _():
+        put(2, "handed")
 
     @pl.when(core == 0)
     def _():
         put(1, "side")
-        put(3, "cross")
+        put(3, "crossed")
 
     @pl.when(core == 1)
     def _():
-        put(1, "cross")
+        put(1, "crossed")
         put(3, "side")
 
 
 def square(snapshots, outlier_cols, outlier_values, threshold):
     rows, points = snapshots.shape
     width, length = rows // (4 * UNITS), rows // UNITS
-    far = (lax.axis_index("tm") // 2) % 2
     most = SNAP_MAX + outlier_cols.shape[1] * OUTLIER_MAX
     down = 2.0 ** -max(0, math.ceil(math.log2(2 * points * most * most / 6e4)))
     scale = 1.0 / (math.sqrt(points * lax.axis_size("space")) * down)
@@ -330,11 +331,10 @@
             block = behind(block, x_units[-1], by_y[-1])
         x_units.append(swapped(block, "tm", 2))
         by_y.append(swapped(block, "tm", 4))
-        other = swapped(behind(by_y[-1], x_units[-1], *([own_came], left, left[1:])[stage]), "tm", 1)
+        other = swapped(behind(by_y[-1], x_units[-1], *([own_came, sibling], left, left[1:])[stage]), "tm", 1)
         if stage == 1:
             sibling = swapped(behind(rest, left[0]), "tm", 1)
-        if stage > 0:
-            other = behind(other, came, *([own] if stage == 1 else totals[:-1]))
+        other = behind(other, *([], [came], [own, *totals[:-1]])[stage])
         operands = [*sent, sibling, by_y[-1], other, *x_units, *left, *cross]
         out_shape = message(len(stage_blocks(stage))) + [units(len(fresh))] * 3
         stay, away, left_now, cross_now, _ = on_units(
@@ -345,21 +345,14 @@
         half, came = half_summed(stay, away)
         totals.append(summed(half))
 
-    parts = []
-    for first, last in GOES:
-        near, other = [], []
-        for stage in range(first, last):
-            n = len(x_blocks(stage))
-            near.append(totals[stage][:n])
-            other.append(totals[stage][n : 2 * n])
-        near, other = (behind(jnp.concatenate(part), *(parts or [came])) for part in (near, other))
-        handed = swapped(near.astype(jnp.float16), "tm", 4, lambda i: i & 2)
-        parts.append(jnp.where(far == 1, handed.astype(jnp.float32), near))
-        pairs = [(i, i ^ (5 if i & 2 else 1)) for i in range(lax.axis_size("tm"))]
-        parts.append(lax.ppermute(other.astype(jnp.float16), "tm", pairs).astype(jnp.float32))
-    parts += [total[2 * len(x_blocks(stage)) :] for stage, total in enumerate(totals)]
+    counts = [len(x_blocks(stage)) for stage in range(len(STAGES))]
+    near = jnp.concatenate([total[:n] for n, total in zip(counts, totals)]).astype(jnp.float16)
+    crossing = jnp.concatenate([total[n : 2 * n] for n, total in zip(counts, totals)]).astype(jnp.float16)
+    handed = swapped(near, "tm", 4, lambda i: i & 2)
+    pairs = [(i, i ^ (5 if i & 2 else 1)) for i in range(lax.axis_size("tm"))]
+    crossed = lax.ppermute(crossing, "tm", pairs)
     out_shape = jax.ShapeDtypeStruct((5, rows, rows // 4), jnp.float32)
-    operands = [own, *parts]
+    operands = [own, *totals, handed.astype(jnp.float32), crossed.astype(jnp.float32)]
     band = on_units(functools.partial(assemble_kernel, scale), out_shape, len(operands))(*operands)
     return band.transpose(1, 0, 2)
 

time: 114 us -> 106 us (0.930)
  Pallas kernels: 19.5 us -> 15.6 us
  other arithmetic: 4.01 us -> 1.17 us
  local copies, waits for them, and re-layouts: 2.46 us -> 0.06 us
    pallas_call x3, Pallas kernels: 11.8 us -> 8.85 us  [square(): on_units(functools.partial(stage_kernel, stage), out_shape, len(operands))]
    unnamed x12 -> x0, local copies, waits for them, and re-layouts: 2.38 us -> none
    add x4, other arithmetic: 1.66 us -> 0.4 us  [half_summed(): return (stay * down + came.astype(jnp.float32), came)]
    ppermute x21 -> x20, starting transfers between devices: 29.6 us -> 30.1 us  [swapped(): return lax.ppermute(x, axis, pairs)]
    ppermute x2 -> x1, waiting for transfers between devices: 5.24 us -> 4.86 us  [square(): crossed = lax.ppermute(crossing, 'tm', pairs)]
    ppermute x21 -> x20, waiting for transfers between devices: 48.6 us -> 48.8 us  [swapped(): return lax.ppermute(x, axis, pairs)]
    ppermute x2 -> x1, starting transfers between devices: 3.7 us -> 3.63 us  [square(): crossed = lax.ppermute(crossing, 'tm', pairs)]
  transfers between devices with their start and end apart: 23 -> 21, of which waited for: 13 -> 12; matrix products, arithmetic and copies ran while one was open for 3% -> 1% of each run, Pallas kernels for 13% -> 11%
where the time goes in v7:
time: 106 us; the launch traced here: 105 us
  waiting for transfers between devices  53.7 us (51%)
  starting transfers between devices  33.8 us (32%)
  Pallas kernels  15.6 us (15%)
  other arithmetic  1.17 us (1%)
    ppermute x20, waiting for transfers between devices, swapped(): return lax.ppermute(x, axis, pairs)  48.8 us
    ppermute x20, starting transfers between devices, swapped(): return lax.ppermute(x, axis, pairs)  30.1 us
    pallas_call x3, Pallas kernels, square(): on_units(functools.partial(stage_kernel, stage), out_shape, len(operands))  8.85 us
    ppermute x1, waiting for transfers between devices, square(): crossed = lax.ppermute(crossing, 'tm', pairs)  4.86 us
    ppermute x1, starting transfers between devices, square(): crossed = lax.ppermute(crossing, 'tm', pairs)  3.63 us
    pallas_call x1, Pallas kernels, square(): stay, away = on_units(own_kernel, message(UNITS * UNITS), len(sent))(*sent)  2.89 us
    pallas_call x1, Pallas kernels, clean_units(): pl.pallas_call(clean_kernel, out_shape=out_shape, in_specs=[hbm, pl.Block...  2.3 us
  transfers between devices with their start and end apart: 21, of which 12 were waited for; matrix products, arithmetic and copies ran while one was open for 1% of the time, Pallas kernels for 11%

profile of v7, /device:TPU:3, one launch (start us, length us, event | category | flops | bytes accessed | tf_op | source)
XLA Modules:
  0.0 105.2 jit_solution(11174288797364924803)
XLA Ops:
  0.7 2.3 %shard_map.46 = (bf16[256,2048]{1,0:T(8,128)(2,1)S(1)}, bf16[256,2048]{1,0:T(8,128)(2,1)S(1)}, bf16[128,2048]{1,0:T(8,128)(2,1)S(1)}, bf16[128,2048]{1,0:T(8,128)(2,1)S(1)}) custom-call(s32[4,4]{1,0:T(4,128)} %cols_hbm.1, f32[1]{0:T(128)} %bitcast.29.threshold_ref, bf16[512,2048]{1,0:T(8,128)(2,1)} %snapshots_hbm.1, bf16[4,4,128,128]{3,2,1,0:T(8,128)(2,1)} %values_hbm.1), custom_call_target="tpu_custom_call" | custom-call | tf_op jit(solution)/shard_map/pallas_call | solution.py:124
  3.0 0.7 collective-permute-start.2
  3.7 1.3 %collective-permute-start.3 = (bf16[256,2048]{1,0:T(8,128)(2,1)S(1)}, bf16[256,2048]{1,0:T(8,128)(2,1)S(1)}, u32[]{:S(2)}, u32[]{:S(2)}) collective-permute-start(bf16[256,2048]{1,0:T(8,128)(2,1)S(1)} %get-tuple-element.29.refs_0_), channel_id=1, source_target_pairs={{0,16},{4,20},{8,24},{12,28},{16,0},{20,4},{24,8},{28,12},{1,17},{... | collective-permute-start | bytes 3145736 | tf_op jit(solution)/shard_map/ppermute | solution.py:20
  5.0 0.3 collective-permute-start.4
  5.2 2.9 %shard_map.47 = (f32[2,16,32,128]{3,2,1,0:T(8,128)S(1)}, f32[2,16,32,128]{3,2,1,0:T(8,128)S(1)}) custom-call(bf16[256,2048]{1,0:T(8,128)(2,1)S(1)} %get-tuple-element.29.refs_0_, bf16[128,2048]{1,0:T(8,128)(2,1)S(1)} %get-tuple-element.40.refs_1_, bf16[128,2048]{1,0:T(8,128)(2,1)S(1)} %get-tuple-element.46.refs_2_), custom_call_target="tpu_custom_call" | custom-call | flops 1000 | bytes 1000 | tf_op jit(solution)/shard_map/pallas_call | solution.py:323
  8.1 0.1 multiply_convert_fusion.3
  8.2 1.4 %collective-permute-start = (f16[2,16,32,128]{3,2,1,0:T(8,128)(2,1)S(1)}, f16[2,16,32,128]{3,2,1,0:T(8,128)(2,1)S(1)}, u32[]{:S(2)}, u32[]{:S(2)}) collective-permute-start(f16[2,16,32,128]{3,2,1,0:T(8,128)(2,1)S(1)} %multiply_convert_fusion.3), channel_id=1, source_target_pairs={{0,1},{1,0},{2,3},{3,2},{4,5},{5,4},{6,7},{7,6},{8,9},{9,8},{10,11... | collective-permute-start | bytes 786440 | tf_op jit(solution)/shard_map/ppermute | solution.py:20
  9.5 5.9 %collective-permute-done = f16[2,16,32,128]{3,2,1,0:T(8,128)(2,1)S(1)} collective-permute-done((f16[2,16,32,128]{3,2,1,0:T(8,128)(2,1)S(1)}, f16[2,16,32,128]{3,2,1,0:T(8,128)(2,1)S(1)}, u32[]{:S(2)}, u32[]{:S(2)}) %collective-permute-start) | collective-permute-done | bytes 262176 | tf_op jit(solution)/shard_map/ppermute | solution.py:20
  15.5 13.0 %collective-permute-done.3.refs_4_ = bf16[256,2048]{1,0:T(8,128)(2,1)S(1)} collective-permute-done((bf16[256,2048]{1,0:T(8,128)(2,1)S(1)}, bf16[256,2048]{1,0:T(8,128)(2,1)S(1)}, u32[]{:S(2)}, u32[]{:S(2)}) %collective-permute-start.3) | collective-permute-done | bytes 1048608 | tf_op jit(solution)/shard_map/ppermute | solution.py:20
  28.4 0.9 collective-permute-done.4.refs_6_
  29.4 1.2 %collective-permute-start.5 = (bf16[256,2048]{1,0:T(8,128)(2,1)S(1)}, bf16[256,2048]{1,0:T(8,128)(2,1)S(1)}, u32[]{:S(2)}, u32[]{:S(2)}) collective-permute-start(bf16[256,2048]{1,0:T(8,128)(2,1)S(1)} %collective-permute-done.3.refs_4_), channel_id=1, source_target_pairs={{0,4},{4,0},{8,12},{12,8},{16,20},{20,16},{24,28},{28,24},{1,5},{5... | collective-permute-start | bytes 3145736 | tf_op jit(solution)/shard_map/ppermute | solution.py:20
  30.5 0.2 collective-permute-start.9
  30.8 2.0 %collective-permute-done.5.refs_5_ = bf16[256,2048]{1,0:T(8,128)(2,1)S(1)} collective-permute-done((bf16[256,2048]{1,0:T(8,128)(2,1)S(1)}, bf16[256,2048]{1,0:T(8,128)(2,1)S(1)}, u32[]{:S(2)}, u32[]{:S(2)}) %collective-permute-start.5) | collective-permute-done | bytes 1048608 | tf_op jit(solution)/shard_map/ppermute | solution.py:20
  32.8 2.8 %shard_map.48 = (f32[2,24,32,128]{3,2,1,0:T(8,128)S(1)}, f32[2,24,32,128]{3,2,1,0:T(8,128)S(1)}, bf16[256,2048]{1,0:T(8,128)(2,1)S(1)}, bf16[256,2048]{1,0:T(8,128)(2,1)S(1)}, bf16[256,2048]{1,0:T(8,128)(2,1)}) custom-call(bf16[256,2048]{1,0:T(8,128)(2,1)S(1)} %get-tuple-element.29.refs_0_, bf16[128,2048]{1,0:T(8,128)(2,1)S(1)} %get-tuple-element.40.refs_1_, ...), custom_call_target="tpu_custom_call" | custom-call | flops 1000 | bytes 1000 | tf_op jit(solution)/shard_map/pallas_call | solution.py:340
  35.6 0.4 collective-permute-start.8
  36.0 0.1 multiply_convert_fusion
  36.1 1.4 %collective-permute-start.6 = (f16[2,24,32,128]{3,2,1,0:T(8,128)(2,1)S(1)}, f16[2,24,32,128]{3,2,1,0:T(8,128)(2,1)S(1)}, u32[]{:S(2)}, u32[]{:S(2)}) collective-permute-start(f16[2,24,32,128]{3,2,1,0:T(8,128)(2,1)S(1)} %multiply_convert_fusion), channel_id=1, source_target_pairs={{0,1},{1,0},{2,3},{3,2},{4,5},{5,4},{6,7},{7,6},{8,9},{9,8},{10,11... | collective-permute-start | bytes 1179656 | tf_op jit(solution)/shard_map/ppermute | solution.py:20
  37.4 0.1 convert_add_fusion.3
  37.5 6.6 %collective-permute-done.9.refs_4_ = bf16[128,2048]{1,0:T(8,128)(2,1)S(1)} collective-permute-done((bf16[128,2048]{1,0:T(8,128)(2,1)S(1)}, bf16[128,2048]{1,0:T(8,128)(2,1)S(1)}, u32[]{:S(2)}, u32[]{:S(2)}) %collective-permute-start.9) | collective-permute-done | bytes 524320 | tf_op jit(solution)/shard_map/ppermute | solution.py:20
  44.1 1.0 collective-permute-start.11
  45.1 2.4 %collective-permute-start.1 = (f16[16,32,128]{2,1,0:T(8,128)(2,1)S(1)}, f16[16,32,128]{2,1,0:T(8,128)(2,1)S(1)}, u32[]{:S(2)}, u32[]{:S(2)}) collective-permute-start(f16[16,32,128]{2,1,0:T(8,128)(2,1)S(1)} %fusion.7), channel_id=1, source_target_pairs={{0,2},{1,3},{2,0},{3,1},{4,6},{5,7},{6,4},{7,5},{8,10},{9,11},{10,... | collective-permute-start | bytes 393224 | tf_op jit(solution)/shard_map/ppermute | solution.py:20
  47.5 1.2 %collective-permute-start.14 = (bf16[128,2048]{1,0:T(8,128)(2,1)S(1)}, bf16[128,2048]{1,0:T(8,128)(2,1)S(1)}, u32[]{:S(2)}, u32[]{:S(2)}) collective-permute-start(bf16[128,2048]{1,0:T(8,128)(2,1)S(1)} %get-tuple-element.46.refs_2_), channel_id=1, source_target_pairs={{0,16},{4,20},{8,24},{12,28},{16,0},{20,4},{24,8},{28,12},{1,17},{... | collective-permute-start | bytes 1572872 | tf_op jit(solution)/shard_map/ppermute | solution.py:20
  48.7 0.3 collective-permute-start.15
  49.0 0.1 convert_add_fusion
  49.2 0.3 collective-permute-start.7
  49.5 2.7 %shard_map.49 = (f32[2,18,32,128]{3,2,1,0:T(8,128)S(1)}, f32[2,18,32,128]{3,2,1,0:T(8,128)S(1)}, bf16[128,2048]{1,0:T(8,128)(2,1)S(1)}, bf16[128,2048]{1,0:T(8,128)(2,1)S(1)}, bf16[128,2048]{1,0:T(8,128)(2,1)}) custom-call(bf16[256,2048]{1,0:T(8,128)(2,1)S(1)} %get-tuple-element.29.refs_0_, bf16[128,2048]{1,0:T(8,128)(2,1)S(1)} %get-tuple-element.40.refs_1_, ...), custom_call_target="tpu_custom_call" | custom-call | flops 1000 | bytes 1000 | tf_op jit(solution)/shard_map/pallas_call | solution.py:340
  52.2 0.1 multiply_convert_fusion.2
  52.3 1.4 %collective-permute-start.12 = (f16[2,18,32,128]{3,2,1,0:T(8,128)(2,1)S(1)}, f16[2,18,32,128]{3,2,1,0:T(8,128)(2,1)S(1)}, u32[]{:S(2)}, u32[]{:S(2)}) collective-permute-start(f16[2,18,32,128]{3,2,1,0:T(8,128)(2,1)S(1)} %multiply_convert_fusion.2), channel_id=1, source_target_pairs={{0,1},{1,0},{2,3},{3,2},{4,5},{5,4},{6,7},{7,6},{8,9},{9,8},{10,11... | collective-permute-start | bytes 884744 | tf_op jit(solution)/shard_map/ppermute | solution.py:20
  53.6 3.5 %collective-permute-done.1 = f16[16,32,128]{2,1,0:T(8,128)(2,1)S(1)} collective-permute-done((f16[16,32,128]{2,1,0:T(8,128)(2,1)S(1)}, f16[16,32,128]{2,1,0:T(8,128)(2,1)S(1)}, u32[]{:S(2)}, u32[]{:S(2)}) %collective-permute-start.1) | collective-permute-done | bytes 131104 | tf_op jit(solution)/shard_map/ppermute | solution.py:20
  57.2 3.5 %collective-permute-done.14.refs_4_ = bf16[128,2048]{1,0:T(8,128)(2,1)S(1)} collective-permute-done((bf16[128,2048]{1,0:T(8,128)(2,1)S(1)}, bf16[128,2048]{1,0:T(8,128)(2,1)S(1)}, u32[]{:S(2)}, u32[]{:S(2)}) %collective-permute-start.14) | collective-permute-done | bytes 524320 | tf_op jit(solution)/shard_map/ppermute | solution.py:20
  60.7 0.9 collective-permute-done.15.refs_8_
  61.7 1.4 %collective-permute-start.16 = (bf16[128,2048]{1,0:T(8,128)(2,1)S(1)}, bf16[128,2048]{1,0:T(8,128)(2,1)S(1)}, u32[]{:S(2)}, u32[]{:S(2)}) collective-permute-start(bf16[128,2048]{1,0:T(8,128)(2,1)S(1)} %collective-permute-done.14.refs_4_), channel_id=1, source_target_pairs={{0,4},{4,0},{8,12},{12,8},{16,20},{20,16},{24,28},{28,24},{1,5},{5... | collective-permute-start | bytes 1572872 | tf_op jit(solution)/shard_map/ppermute | solution.py:20
  63.1 0.1 fusion.8
  63.2 0.8 collective-permute-done.12
  64.0 0.1 convert_add_fusion.2
  64.1 4.6 %collective-permute-start.13 = (f16[18,32,128]{2,1,0:T(8,128)(2,1)S(1)}, f16[18,32,128]{2,1,0:T(8,128)(2,1)S(1)}, u32[]{:S(2)}, u32[]{:S(2)}) collective-permute-start(f16[18,32,128]{2,1,0:T(8,128)(2,1)S(1)} %fusion.6), channel_id=1, source_target_pairs={{0,2},{1,3},{2,0},{3,1},{4,6},{5,7},{6,4},{7,5},{8,10},{9,11},{10,... | collective-permute-start | bytes 442376 | tf_op jit(solution)/shard_map/ppermute | solution.py:20
  68.7 3.4 %shard_map.50 = (f32[2,22,32,128]{3,2,1,0:T(8,128)S(1)}, f32[2,22,32,128]{3,2,1,0:T(8,128)S(1)}, bf16[128,2048]{1,0:T(8,128)(2,1)}, bf16[128,2048]{1,0:T(8,128)(2,1)}, bf16[128,2048]{1,0:T(8,128)(2,1)}) custom-call(bf16[256,2048]{1,0:T(8,128)(2,1)S(1)} %get-tuple-element.29.refs_0_, bf16[128,2048]{1,0:T(8,128)(2,1)S(1)} %get-tuple-element.40.refs_1_, ...), custom_call_target="tpu_custom_call" | custom-call | flops 1000 | bytes 1000 | tf_op jit(solution)/shard_map/pallas_call | solution.py:340
  72.1 0.1 multiply_convert_fusion.1
  72.2 2.3 %collective-permute-start.17 = (f16[2,22,32,128]{3,2,1,0:T(8,128)(2,1)S(1)}, f16[2,22,32,128]{3,2,1,0:T(8,128)(2,1)S(1)}, u32[]{:S(2)}, u32[]{:S(2)}) collective-permute-start(f16[2,22,32,128]{3,2,1,0:T(8,128)(2,1)S(1)} %multiply_convert_fusion.1), channel_id=1, source_target_pairs={{0,1},{1,0},{2,3},{3,2},{4,5},{5,4},{6,7},{7,6},{8,9},{9,8},{10,11... | collective-permute-start | bytes 1081352 | tf_op jit(solution)/shard_map/ppermute | solution.py:20
  74.6 8.2 %collective-permute-done.17 = f16[2,22,32,128]{3,2,1,0:T(8,128)(2,1)S(1)} collective-permute-done((f16[2,22,32,128]{3,2,1,0:T(8,128)(2,1)S(1)}, f16[2,22,32,128]{3,2,1,0:T(8,128)(2,1)S(1)}, u32[]{:S(2)}, u32[]{:S(2)}) %collective-permute-start.17) | collective-permute-done | bytes 360480 | tf_op jit(solution)/shard_map/ppermute | solution.py:20
  82.7 0.1 convert_add_fusion.1
  82.9 2.6 %collective-permute-start.18 = (f16[22,32,128]{2,1,0:T(8,128)(2,1)S(1)}, f16[22,32,128]{2,1,0:T(8,128)(2,1)S(1)}, u32[]{:S(2)}, u32[]{:S(2)}) collective-permute-start(f16[22,32,128]{2,1,0:T(8,128)(2,1)S(1)} %fusion.5), channel_id=1, source_target_pairs={{0,2},{1,3},{2,0},{3,1},{4,6},{5,7},{6,4},{7,5},{8,10},{9,11},{10,... | collective-permute-start | bytes 540680 | tf_op jit(solution)/shard_map/ppermute | solution.py:20
  85.5 3.4 %collective-permute-done.18 = f16[22,32,128]{2,1,0:T(8,128)(2,1)S(1)} collective-permute-done((f16[22,32,128]{2,1,0:T(8,128)(2,1)S(1)}, f16[22,32,128]{2,1,0:T(8,128)(2,1)S(1)}, u32[]{:S(2)}, u32[]{:S(2)}) %collective-permute-start.18) | collective-permute-done | bytes 180256 | tf_op jit(solution)/shard_map/ppermute | solution.py:20
  88.9 0.1 fusion.12
  89.1 5.9 %collective-permute-start.19 = (f16[16,32,128]{2,1,0:T(8,128)(2,1)S(1)}, f16[16,32,128]{2,1,0:T(8,128)(2,1)S(1)}, u32[]{:S(2)}, u32[]{:S(2)}) collective-permute-start(f16[16,32,128]{2,1,0:T(8,128)(2,1)S(1)} %pad_maximum_fusion), channel_id=1, source_target_pairs={{8,24},{12,28},{24,8},{28,12},{9,25},{13,29},{25,9},{29,13},{10,26... | collective-permute-start | bytes 393224 | tf_op jit(solution)/shard_map/ppermute | solution.py:20
  95.1 3.6 %collective-permute-start.20 = (f16[16,32,128]{2,1,0:T(8,128)(2,1)S(1)}, f16[16,32,128]{2,1,0:T(8,128)(2,1)S(1)}, u32[]{:S(2)}, u32[]{:S(2)}) collective-permute-start(f16[16,32,128]{2,1,0:T(8,128)(2,1)S(1)} %pad_maximum_fusion.1), channel_id=1, source_target_pairs={{0,4},{4,0},{8,28},{12,24},{16,20},{20,16},{24,12},{28,8},{1,5},{5... | collective-permute-start | bytes 393224 | tf_op jit(solution)/shard_map/ppermute | solution.py:353
  98.7 4.9 %collective-permute-done.20 = f16[16,32,128]{2,1,0:T(8,128)(2,1)S(1)} collective-permute-done((f16[16,32,128]{2,1,0:T(8,128)(2,1)S(1)}, f16[16,32,128]{2,1,0:T(8,128)(2,1)S(1)}, u32[]{:S(2)}, u32[]{:S(2)}) %collective-permute-start.20) | collective-permute-done | bytes 131104 | tf_op jit(solution)/shard_map/ppermute | solution.py:353
  103.6 1.6 %shard_map.51 = f32[5,512,128]{2,1,0:T(8,128)} custom-call(f32[16,32,128]{2,1,0:T(8,128)S(1)} %fusion.3.own_ref, f32[24,32,128]{2,1,0:T(8,128)S(1)} %get-tuple-element.54.refs_0_, f32[18,32,128]{2,1,0:T(8,128)S(1)} %get-tuple-element.56.refs_1_, f32[22,32,128]{2,1,0:T(8,128)S(1)} %get-tuple-element.58.refs_2_, ...), custom_call_target="tpu_custom_call" | custom-call | flops 1000 | bytes 1000 | tf_op jit(solution)/shard_map/pallas_call | solution.py:356
  (23 shorter events, 0.4 us)
Async XLA Ops:
  3.0 12.5 %collective-permute-start.2 = (bf16[256,2048]{1,0:T(8,128)(2,1)S(1)}, bf16[256,2048]{1,0:T(8,128)(2,1)S(1)}, u32[]{:S(2)}, u32[]{:S(2)}) collective-permute-start(bf16[256,2048]{1,0:T(8,128)(2,1)S(1)} %get-tuple-element.29.refs_0_), channel_id=1, source_target_pairs={{0,4},{4,0},{8,12},{12,8},{16,20},{20,16},{24,28},{28,24},{1,5},{5... | collective-permute-start | bytes 3145736 | tf_op jit(solution)/shard_map/ppermute | solution.py:20
  3.7 24.7 %collective-permute-start.3 = (bf16[256,2048]{1,0:T(8,128)(2,1)S(1)}, bf16[256,2048]{1,0:T(8,128)(2,1)S(1)}, u32[]{:S(2)}, u32[]{:S(2)}) collective-permute-start(bf16[256,2048]{1,0:T(8,128)(2,1)S(1)} %get-tuple-element.29.refs_0_), channel_id=1, source_target_pairs={{0,16},{4,20},{8,24},{12,28},{16,0},{20,4},{24,8},{28,12},{1,17},{... | collective-permute-start | bytes 3145736 | tf_op jit(solution)/shard_map/ppermute | solution.py:20
  5.0 24.4 %collective-permute-start.4 = (bf16[256,2048]{1,0:T(8,128)(2,1)S(1)}, bf16[256,2048]{1,0:T(8,128)(2,1)S(1)}, u32[]{:S(2)}, u32[]{:S(2)}) collective-permute-start(bf16[256,2048]{1,0:T(8,128)(2,1)S(1)} %get-tuple-element.29.refs_0_), channel_id=1, source_target_pairs={{0,8},{4,12},{8,0},{12,4},{16,24},{20,28},{24,16},{28,20},{1,9},{5... | collective-permute-start | bytes 3145736 | tf_op jit(solution)/shard_map/ppermute | solution.py:20
  8.2 7.3 %collective-permute-start = (f16[2,16,32,128]{3,2,1,0:T(8,128)(2,1)S(1)}, f16[2,16,32,128]{3,2,1,0:T(8,128)(2,1)S(1)}, u32[]{:S(2)}, u32[]{:S(2)}) collective-permute-start(f16[2,16,32,128]{3,2,1,0:T(8,128)(2,1)S(1)} %multiply_convert_fusion.3), channel_id=1, source_target_pairs={{0,1},{1,0},{2,3},{3,2},{4,5},{5,4},{6,7},{7,6},{8,9},{9,8},{10,11... | collective-permute-start | bytes 786440 | tf_op jit(solution)/shard_map/ppermute | solution.py:20
  29.4 3.5 %collective-permute-start.5 = (bf16[256,2048]{1,0:T(8,128)(2,1)S(1)}, bf16[256,2048]{1,0:T(8,128)(2,1)S(1)}, u32[]{:S(2)}, u32[]{:S(2)}) collective-permute-start(bf16[256,2048]{1,0:T(8,128)(2,1)S(1)} %collective-permute-done.3.refs_4_), channel_id=1, source_target_pairs={{0,4},{4,0},{8,12},{12,8},{16,20},{20,16},{24,28},{28,24},{1,5},{5... | collective-permute-start | bytes 3145736 | tf_op jit(solution)/shard_map/ppermute | solution.py:20
  30.5 13.6 %collective-permute-start.9 = (bf16[128,2048]{1,0:T(8,128)(2,1)S(1)}, bf16[128,2048]{1,0:T(8,128)(2,1)S(1)}, u32[]{:S(2)}, u32[]{:S(2)}) collective-permute-start(bf16[128,2048]{1,0:T(8,128)(2,1)S(1)} %get-tuple-element.40.refs_1_), channel_id=1, source_target_pairs={{0,16},{4,20},{8,24},{12,28},{16,0},{20,4},{24,8},{28,12},{1,17},{... | collective-permute-start | bytes 1572872 | tf_op jit(solution)/shard_map/ppermute | solution.py:20
  30.8 13.3 %collective-permute-start.10 = (bf16[128,2048]{1,0:T(8,128)(2,1)S(1)}, bf16[128,2048]{1,0:T(8,128)(2,1)S(1)}, u32[]{:S(2)}, u32[]{:S(2)}) collective-permute-start(bf16[128,2048]{1,0:T(8,128)(2,1)S(1)} %get-tuple-element.40.refs_1_), channel_id=1, source_target_pairs={{0,8},{4,12},{8,0},{12,4},{16,24},{20,28},{24,16},{28,20},{1,9},{5... | collective-permute-start | bytes 1572872 | tf_op jit(solution)/shard_map/ppermute | solution.py:20
  35.6 13.9 %collective-permute-start.8 = (bf16[256,2048]{1,0:T(8,128)(2,1)S(1)}, bf16[256,2048]{1,0:T(8,128)(2,1)S(1)}, u32[]{:S(2)}, u32[]{:S(2)}) collective-permute-start(bf16[256,2048]{1,0:T(8,128)(2,1)S(1)} %get-tuple-element.39), channel_id=1, source_target_pairs={{0,4},{4,0},{8,12},{12,8},{16,20},{20,16},{24,28},{28,24},{1,5},{5... | collective-permute-start | bytes 3145736 | tf_op jit(solution)/shard_map/ppermute | solution.py:20
  36.1 12.7 %collective-permute-start.6 = (f16[2,24,32,128]{3,2,1,0:T(8,128)(2,1)S(1)}, f16[2,24,32,128]{3,2,1,0:T(8,128)(2,1)S(1)}, u32[]{:S(2)}, u32[]{:S(2)}) collective-permute-start(f16[2,24,32,128]{3,2,1,0:T(8,128)(2,1)S(1)} %multiply_convert_fusion), channel_id=1, source_target_pairs={{0,1},{1,0},{2,3},{3,2},{4,5},{5,4},{6,7},{7,6},{8,9},{9,8},{10,11... | collective-permute-start | bytes 1179656 | tf_op jit(solution)/shard_map/ppermute | solution.py:20
  44.1 5.1 %collective-permute-start.11 = (bf16[128,2048]{1,0:T(8,128)(2,1)S(1)}, bf16[128,2048]{1,0:T(8,128)(2,1)S(1)}, u32[]{:S(2)}, u32[]{:S(2)}) collective-permute-start(bf16[128,2048]{1,0:T(8,128)(2,1)S(1)} %collective-permute-done.9.refs_4_), channel_id=1, source_target_pairs={{0,4},{4,0},{8,12},{12,8},{16,20},{20,16},{24,28},{28,24},{1,5},{5... | collective-permute-start | bytes 1572872 | tf_op jit(solution)/shard_map/ppermute | solution.py:20
  45.1 12.0 %collective-permute-start.1 = (f16[16,32,128]{2,1,0:T(8,128)(2,1)S(1)}, f16[16,32,128]{2,1,0:T(8,128)(2,1)S(1)}, u32[]{:S(2)}, u32[]{:S(2)}) collective-permute-start(f16[16,32,128]{2,1,0:T(8,128)(2,1)S(1)} %fusion.7), channel_id=1, source_target_pairs={{0,2},{1,3},{2,0},{3,1},{4,6},{5,7},{6,4},{7,5},{8,10},{9,11},{10,... | collective-permute-start | bytes 393224 | tf_op jit(solution)/shard_map/ppermute | solution.py:20
  47.5 13.2 %collective-permute-start.14 = (bf16[128,2048]{1,0:T(8,128)(2,1)S(1)}, bf16[128,2048]{1,0:T(8,128)(2,1)S(1)}, u32[]{:S(2)}, u32[]{:S(2)}) collective-permute-start(bf16[128,2048]{1,0:T(8,128)(2,1)S(1)} %get-tuple-element.46.refs_2_), channel_id=1, source_target_pairs={{0,16},{4,20},{8,24},{12,28},{16,0},{20,4},{24,8},{28,12},{1,17},{... | collective-permute-start | bytes 1572872 | tf_op jit(solution)/shard_map/ppermute | solution.py:20
  48.7 12.9 %collective-permute-start.15 = (bf16[128,2048]{1,0:T(8,128)(2,1)S(1)}, bf16[128,2048]{1,0:T(8,128)(2,1)S(1)}, u32[]{:S(2)}, u32[]{:S(2)}) collective-permute-start(bf16[128,2048]{1,0:T(8,128)(2,1)S(1)} %get-tuple-element.46.refs_2_), channel_id=1, source_target_pairs={{0,8},{4,12},{8,0},{12,4},{16,24},{20,28},{24,16},{28,20},{1,9},{5... | collective-permute-start | bytes 1572872 | tf_op jit(solution)/shard_map/ppermute | solution.py:20
  49.2 13.9 %collective-permute-start.7 = (f16[24,32,128]{2,1,0:T(8,128)(2,1)S(1)}, f16[24,32,128]{2,1,0:T(8,128)(2,1)S(1)}, u32[]{:S(2)}, u32[]{:S(2)}) collective-permute-start(f16[24,32,128]{2,1,0:T(8,128)(2,1)S(1)} %fusion.4), channel_id=1, source_target_pairs={{0,2},{1,3},{2,0},{3,1},{4,6},{5,7},{6,4},{7,5},{8,10},{9,11},{10,... | collective-permute-start | bytes 589832 | tf_op jit(solution)/shard_map/ppermute | solution.py:20
  52.3 11.7 %collective-permute-start.12 = (f16[2,18,32,128]{3,2,1,0:T(8,128)(2,1)S(1)}, f16[2,18,32,128]{3,2,1,0:T(8,128)(2,1)S(1)}, u32[]{:S(2)}, u32[]{:S(2)}) collective-permute-start(f16[2,18,32,128]{3,2,1,0:T(8,128)(2,1)S(1)} %multiply_convert_fusion.2), channel_id=1, source_target_pairs={{0,1},{1,0},{2,3},{3,2},{4,5},{5,4},{6,7},{7,6},{8,9},{9,8},{10,11... | collective-permute-start | bytes 884744 | tf_op jit(solution)/shard_map/ppermute | solution.py:20
  61.7 7.1 %collective-permute-start.16 = (bf16[128,2048]{1,0:T(8,128)(2,1)S(1)}, bf16[128,2048]{1,0:T(8,128)(2,1)S(1)}, u32[]{:S(2)}, u32[]{:S(2)}) collective-permute-start(bf16[128,2048]{1,0:T(8,128)(2,1)S(1)} %collective-permute-done.14.refs_4_), channel_id=1, source_target_pairs={{0,4},{4,0},{8,12},{12,8},{16,20},{20,16},{24,28},{28,24},{1,5},{5... | collective-permute-start | bytes 1572872 | tf_op jit(solution)/shard_map/ppermute | solution.py:20
  64.1 10.4 %collective-permute-start.13 = (f16[18,32,128]{2,1,0:T(8,128)(2,1)S(1)}, f16[18,32,128]{2,1,0:T(8,128)(2,1)S(1)}, u32[]{:S(2)}, u32[]{:S(2)}) collective-permute-start(f16[18,32,128]{2,1,0:T(8,128)(2,1)S(1)} %fusion.6), channel_id=1, source_target_pairs={{0,2},{1,3},{2,0},{3,1},{4,6},{5,7},{6,4},{7,5},{8,10},{9,11},{10,... | collective-permute-start | bytes 442376 | tf_op jit(solution)/shard_map/ppermute | solution.py:20
  72.2 10.5 %collective-permute-start.17 = (f16[2,22,32,128]{3,2,1,0:T(8,128)(2,1)S(1)}, f16[2,22,32,128]{3,2,1,0:T(8,128)(2,1)S(1)}, u32[]{:S(2)}, u32[]{:S(2)}) collective-permute-start(f16[2,22,32,128]{3,2,1,0:T(8,128)(2,1)S(1)} %multiply_convert_fusion.1), channel_id=1, source_target_pairs={{0,1},{1,0},{2,3},{3,2},{4,5},{5,4},{6,7},{7,6},{8,9},{9,8},{10,11... | collective-permute-start | bytes 1081352 | tf_op jit(solution)/shard_map/ppermute | solution.py:20
  82.9 6.0 %collective-permute-start.18 = (f16[22,32,128]{2,1,0:T(8,128)(2,1)S(1)}, f16[22,32,128]{2,1,0:T(8,128)(2,1)S(1)}, u32[]{:S(2)}, u32[]{:S(2)}) collective-permute-start(f16[22,32,128]{2,1,0:T(8,128)(2,1)S(1)} %fusion.5), channel_id=1, source_target_pairs={{0,2},{1,3},{2,0},{3,1},{4,6},{5,7},{6,4},{7,5},{8,10},{9,11},{10,... | collective-permute-start | bytes 540680 | tf_op jit(solution)/shard_map/ppermute | solution.py:20
  89.1 9.6 %collective-permute-start.19 = (f16[16,32,128]{2,1,0:T(8,128)(2,1)S(1)}, f16[16,32,128]{2,1,0:T(8,128)(2,1)S(1)}, u32[]{:S(2)}, u32[]{:S(2)}) collective-permute-start(f16[16,32,128]{2,1,0:T(8,128)(2,1)S(1)} %pad_maximum_fusion), channel_id=1, source_target_pairs={{8,24},{12,28},{24,8},{28,12},{9,25},{13,29},{25,9},{29,13},{10,26... | collective-permute-start | bytes 393224 | tf_op jit(solution)/shard_map/ppermute | solution.py:20
  95.1 8.5 %collective-permute-start.20 = (f16[16,32,128]{2,1,0:T(8,128)(2,1)S(1)}, f16[16,32,128]{2,1,0:T(8,128)(2,1)S(1)}, u32[]{:S(2)}, u32[]{:S(2)}) collective-permute-start(f16[16,32,128]{2,1,0:T(8,128)(2,1)S(1)} %pad_maximum_fusion.1), channel_id=1, source_target_pairs={{0,4},{4,0},{8,28},{12,24},{16,20},{20,16},{24,12},{28,8},{1,5},{5... | collective-permute-start | bytes 393224 | tf_op jit(solution)/shard_map/ppermute | solution.py:353

commit v8 on v7

--- a/solution.py
+++ b/solution.py
@@ -255,15 +255,16 @@
 
 
 def assemble_kernel(scale, own_ref, *refs):
-    *total_refs, handed_ref, crossed_ref, out_ref = refs
+    *total_refs, handed_ref, crossed_ref, handed_last_ref, crossed_last_ref, out_ref = refs
     core = lax.rem(lax.axis_index("tm"), 2)
     far = lax.rem(lax.div(lax.axis_index("tm"), 2), 2)
     where = {("own", (c, s)): (own_ref, c * UNITS + s) for c in range(UNITS) for s in range(UNITS)}
     for stage, ref in enumerate(total_refs):
         where.update({key: (ref, i) for i, key in enumerate(stage_blocks(stage))})
-    keys = [key for stage in range(len(STAGES)) for key in x_blocks(stage)]
-    where.update({("handed", key): (handed_ref, i) for i, key in enumerate(keys)})
-    where.update({("crossed", key): (crossed_ref, i) for i, key in enumerate(keys)})
+    for i, key in enumerate(x_blocks(0) + x_blocks(1)):
+        where.update({("handed", key): (handed_ref, i), ("crossed", key): (crossed_ref, i)})
+    for i, key in enumerate(x_blocks(2)):
+        where.update({("handed", key): (handed_last_ref, i), ("crossed", key): (crossed_last_ref, i)})
     width = own_ref.shape[1]
     quarter = width * UNITS
 
@@ -312,19 +313,29 @@
     def behind(value, *others):
         return lax.optimization_barrier((value, *others))[0]
 
-    def half_summed(stay, away):
-        came = swapped((away * down).astype(jnp.float16), "space", 1)
-        return stay * down + came.astype(jnp.float32), came
-
-    def summed(kept):
-        return kept[0] + swapped(kept[1].astype(jnp.float16), "space", 2).astype(jnp.float32)
+    def exchanged(away):
+        return swapped((away * down).astype(jnp.float16), "space", 1)
+
+    def half_summed(stay, came):
+        return stay * down + came.astype(jnp.float32)
+
+    def summed(kept, after=()):
+        came = swapped(kept[1].astype(jnp.float16), "space", 2)
+        return kept[0] + behind(came, *after).astype(jnp.float32)
+
+    def handed_over(stages):
+        counts = [len(x_blocks(stage)) for stage in stages]
+        near = jnp.concatenate([totals[stage][:n] for n, stage in zip(counts, stages)]).astype(jnp.float16)
+        cross = jnp.concatenate([totals[stage][n : 2 * n] for n, stage in zip(counts, stages)]).astype(jnp.float16)
+        pairs = [(i, i ^ (5 if i & 2 else 1)) for i in range(lax.axis_size("tm"))]
+        return [swapped(near, "tm", 4, lambda i: i & 2), lax.ppermute(cross, "tm", pairs)]
 
     rest, *sent = clean_units(snapshots, outlier_cols, outlier_values, threshold)
     stay, away = on_units(own_kernel, message(UNITS * UNITS), len(sent))(*sent)
     sibling = swapped(sent[0], "tm", 1)
-    half, own_came = half_summed(stay, away)
-    own = summed(half)
-    x_units, by_y, left, cross, totals, came = [], [], [], [], [], None
+    own_came = exchanged(away)
+    own_half = half_summed(stay, own_came)
+    x_units, by_y, left, cross, halves, totals, came = [], [], [], [], [], [], None
     for stage, fresh in enumerate(STAGES):
         block = sent[stage]
         if stage > 0:
@@ -334,7 +345,12 @@
         other = swapped(behind(by_y[-1], x_units[-1], *([own_came, sibling], left, left[1:])[stage]), "tm", 1)
         if stage == 1:
             sibling = swapped(behind(rest, left[0]), "tm", 1)
-        other = behind(other, *([], [came], [own, *totals[:-1]])[stage])
+        if stage == 2:
+            own = summed(own_half, after=[came])
+            totals.append(summed(halves[0], after=left[1:]))
+            other = behind(other, own, *totals)
+        elif stage == 1:
+            other = behind(other, came)
         operands = [*sent, sibling, by_y[-1], other, *x_units, *left, *cross]
         out_shape = message(len(stage_blocks(stage))) + [units(len(fresh))] * 3
         stay, away, left_now, cross_now, _ = on_units(
@@ -342,17 +358,15 @@
         )(*operands)
         left.append(left_now)
         cross.append(cross_now)
-        half, came = half_summed(stay, away)
-        totals.append(summed(half))
-
-    counts = [len(x_blocks(stage)) for stage in range(len(STAGES))]
-    near = jnp.concatenate([total[:n] for n, total in zip(counts, totals)]).astype(jnp.float16)
-    crossing = jnp.concatenate([total[n : 2 * n] for n, total in zip(counts, totals)]).astype(jnp.float16)
-    handed = swapped(near, "tm", 4, lambda i: i & 2)
-    pairs = [(i, i ^ (5 if i & 2 else 1)) for i in range(lax.axis_size("tm"))]
-    crossed = lax.ppermute(crossing, "tm", pairs)
+        came = exchanged(away)
+        halves.append(half_summed(stay, came))
+    totals.append(summed(halves[1], after=[came]))
+    parts = handed_over([0, 1])
+    totals.append(summed(halves[2], after=parts))
+    parts += handed_over([2])
+
     out_shape = jax.ShapeDtypeStruct((5, rows, rows // 4), jnp.float32)
-    operands = [own, *totals, handed.astype(jnp.float32), crossed.astype(jnp.float32)]
+    operands = [own, *totals, *(part.astype(jnp.float32) for part in parts)]
     band = on_units(functools.partial(assemble_kernel, scale), out_shape, len(operands))(*operands)
     return band.transpose(1, 0, 2)
 

time: 106 us -> 102 us (0.962)
  starting transfers between devices: 33.8 us -> 27.4 us
  waiting for transfers between devices: 53.7 us -> 56.4 us
    ppermute x20 -> x21, starting transfers between devices: 30.1 us -> 21.1 us  [swapped(): return lax.ppermute(x, axis, pairs)]
    ppermute x1 -> x2, starting transfers between devices: 3.63 us -> 6.27 us  [handed_over(): lax.ppermute(cross, 'tm', pairs)]
    ppermute x20 -> x21, waiting for transfers between devices: 48.8 us -> 50.5 us  [swapped(): return lax.ppermute(x, axis, pairs)]
    ppermute x1 -> x2, waiting for transfers between devices: 4.86 us -> 5.89 us  [handed_over(): lax.ppermute(cross, 'tm', pairs)]
  transfers between devices with their start and end apart: 21 -> 23, of which waited for: 12 -> 15; matrix products, arithmetic and copies ran while one was open for 1% -> 1% of each run, Pallas kernels for 11% -> 8%
where the time goes in v8:
time: 102 us
  waiting for transfers between devices  56.4 us (55%)
  starting transfers between devices  27.4 us (27%)
  Pallas kernels  15.7 us (15%)
  other arithmetic  1.14 us (1%)
    ppermute x21, waiting for transfers between devices, swapped(): return lax.ppermute(x, axis, pairs)  50.5 us
    ppermute x21, starting transfers between devices, swapped(): return lax.ppermute(x, axis, pairs)  21.1 us
    pallas_call x3, Pallas kernels, square(): on_units(functools.partial(stage_kernel, stage), out_shape, len(operands))  8.87 us
    ppermute x2, starting transfers between devices, handed_over(): lax.ppermute(cross, 'tm', pairs)  6.27 us
    ppermute x2, waiting for transfers between devices, handed_over(): lax.ppermute(cross, 'tm', pairs)  5.89 us
    pallas_call x1, Pallas kernels, square(): stay, away = on_units(own_kernel, message(UNITS * UNITS), len(sent))(*sent)  2.89 us
    pallas_call x1, Pallas kernels, clean_units(): pl.pallas_call(clean_kernel, out_shape=out_shape, in_specs=[hbm, pl.Block...  2.3 us
  transfers between devices with their start and end apart: 23, of which 15 were waited for; matrix products, arithmetic and copies ran while one was open for 1% of the time, Pallas kernels for 8%

profile of v8, /device:TPU:3, one launch (start us, length us, event | category | flops | bytes accessed | tf_op | source)
XLA Modules:
  0.0 101.6 jit_solution(11544306817698235925)
XLA Ops:
  0.7 2.3 %shard_map.46 = (bf16[256,2048]{1,0:T(8,128)(2,1)S(1)}, bf16[256,2048]{1,0:T(8,128)(2,1)S(1)}, bf16[128,2048]{1,0:T(8,128)(2,1)S(1)}, bf16[128,2048]{1,0:T(8,128)(2,1)S(1)}) custom-call(s32[4,4]{1,0:T(4,128)} %cols_hbm.1, f32[1]{0:T(128)} %bitcast.29.threshold_ref, bf16[512,2048]{1,0:T(8,128)(2,1)} %snapshots_hbm.1, bf16[4,4,128,128]{3,2,1,0:T(8,128)(2,1)} %values_hbm.1), custom_call_target="tpu_custom_call" | custom-call | tf_op jit(solution)/shard_map/pallas_call | solution.py:124
  3.0 0.7 collective-permute-start.2
  3.7 1.3 %collective-permute-start.3 = (bf16[256,2048]{1,0:T(8,128)(2,1)S(1)}, bf16[256,2048]{1,0:T(8,128)(2,1)S(1)}, u32[]{:S(2)}, u32[]{:S(2)}) collective-permute-start(bf16[256,2048]{1,0:T(8,128)(2,1)S(1)} %get-tuple-element.33.refs_0_), channel_id=1, source_target_pairs={{0,16},{4,20},{8,24},{12,28},{16,0},{20,4},{24,8},{28,12},{1,17},{... | collective-permute-start | bytes 3145736 | tf_op jit(solution)/shard_map/ppermute | solution.py:20
  5.0 0.3 collective-permute-start.4
  5.2 2.9 %shard_map.47 = (f32[2,16,32,128]{3,2,1,0:T(8,128)S(1)}, f32[2,16,32,128]{3,2,1,0:T(8,128)S(1)}) custom-call(bf16[256,2048]{1,0:T(8,128)(2,1)S(1)} %get-tuple-element.33.refs_0_, bf16[128,2048]{1,0:T(8,128)(2,1)S(1)} %get-tuple-element.42.refs_1_, bf16[128,2048]{1,0:T(8,128)(2,1)S(1)} %get-tuple-element.53.refs_2_), custom_call_target="tpu_custom_call" | custom-call | flops 1000 | bytes 1000 | tf_op jit(solution)/shard_map/pallas_call | solution.py:334
  8.2 1.4 %collective-permute-start = (f16[2,16,32,128]{3,2,1,0:T(8,128)(2,1)S(1)}, f16[2,16,32,128]{3,2,1,0:T(8,128)(2,1)S(1)}, u32[]{:S(2)}, u32[]{:S(2)}) collective-permute-start(f16[2,16,32,128]{3,2,1,0:T(8,128)(2,1)S(1)} %multiply_convert_fusion.3), channel_id=1, source_target_pairs={{0,1},{1,0},{2,3},{3,2},{4,5},{5,4},{6,7},{7,6},{8,9},{9,8},{10,11... | collective-permute-start | bytes 786440 | tf_op jit(solution)/shard_map/ppermute | solution.py:20
  9.6 5.9 %collective-permute-done = f16[2,16,32,128]{3,2,1,0:T(8,128)(2,1)S(1)} collective-permute-done((f16[2,16,32,128]{3,2,1,0:T(8,128)(2,1)S(1)}, f16[2,16,32,128]{3,2,1,0:T(8,128)(2,1)S(1)}, u32[]{:S(2)}, u32[]{:S(2)}) %collective-permute-start) | collective-permute-done | bytes 262176 | tf_op jit(solution)/shard_map/ppermute | solution.py:20
  15.5 13.0 %collective-permute-done.3.refs_4_ = bf16[256,2048]{1,0:T(8,128)(2,1)S(1)} collective-permute-done((bf16[256,2048]{1,0:T(8,128)(2,1)S(1)}, bf16[256,2048]{1,0:T(8,128)(2,1)S(1)}, u32[]{:S(2)}, u32[]{:S(2)}) %collective-permute-start.3) | collective-permute-done | bytes 1048608 | tf_op jit(solution)/shard_map/ppermute | solution.py:20
  28.4 0.9 collective-permute-done.4.refs_6_
  29.4 1.2 %collective-permute-start.5 = (bf16[256,2048]{1,0:T(8,128)(2,1)S(1)}, bf16[256,2048]{1,0:T(8,128)(2,1)S(1)}, u32[]{:S(2)}, u32[]{:S(2)}) collective-permute-start(bf16[256,2048]{1,0:T(8,128)(2,1)S(1)} %collective-permute-done.3.refs_4_), channel_id=1, source_target_pairs={{0,4},{4,0},{8,12},{12,8},{16,20},{20,16},{24,28},{28,24},{1,5},{5... | collective-permute-start | bytes 3145736 | tf_op jit(solution)/shard_map/ppermute | solution.py:20
  30.5 0.2 collective-permute-start.7
  30.8 2.0 %collective-permute-done.5.refs_5_ = bf16[256,2048]{1,0:T(8,128)(2,1)S(1)} collective-permute-done((bf16[256,2048]{1,0:T(8,128)(2,1)S(1)}, bf16[256,2048]{1,0:T(8,128)(2,1)S(1)}, u32[]{:S(2)}, u32[]{:S(2)}) %collective-permute-start.5) | collective-permute-done | bytes 1048608 | tf_op jit(solution)/shard_map/ppermute | solution.py:20
  32.8 2.8 %shard_map.48 = (f32[2,24,32,128]{3,2,1,0:T(8,128)S(1)}, f32[2,24,32,128]{3,2,1,0:T(8,128)S(1)}, bf16[256,2048]{1,0:T(8,128)(2,1)S(1)}, bf16[256,2048]{1,0:T(8,128)(2,1)S(1)}, bf16[256,2048]{1,0:T(8,128)(2,1)}) custom-call(bf16[256,2048]{1,0:T(8,128)(2,1)S(1)} %get-tuple-element.33.refs_0_, bf16[128,2048]{1,0:T(8,128)(2,1)S(1)} %get-tuple-element.42.refs_1_, ...), custom_call_target="tpu_custom_call" | custom-call | flops 1000 | bytes 1000 | tf_op jit(solution)/shard_map/pallas_call | solution.py:356
  35.6 0.4 collective-permute-start.6
  36.0 0.1 multiply_convert_fusion
  36.1 1.4 %collective-permute-start.10 = (f16[2,24,32,128]{3,2,1,0:T(8,128)(2,1)S(1)}, f16[2,24,32,128]{3,2,1,0:T(8,128)(2,1)S(1)}, u32[]{:S(2)}, u32[]{:S(2)}) collective-permute-start(f16[2,24,32,128]{3,2,1,0:T(8,128)(2,1)S(1)} %multiply_convert_fusion), channel_id=1, source_target_pairs={{0,1},{1,0},{2,3},{3,2},{4,5},{5,4},{6,7},{7,6},{8,9},{9,8},{10,11... | collective-permute-start | bytes 1179656 | tf_op jit(solution)/shard_map/ppermute | solution.py:20
  37.4 6.7 %collective-permute-done.7.refs_4_ = bf16[128,2048]{1,0:T(8,128)(2,1)S(1)} collective-permute-done((bf16[128,2048]{1,0:T(8,128)(2,1)S(1)}, bf16[128,2048]{1,0:T(8,128)(2,1)S(1)}, u32[]{:S(2)}, u32[]{:S(2)}) %collective-permute-start.7) | collective-permute-done | bytes 524320 | tf_op jit(solution)/shard_map/ppermute | solution.py:20
  44.1 1.0 collective-permute-start.9
  45.1 0.1 convert_add_fusion.3
  45.2 1.3 %collective-permute-start.14 = (bf16[128,2048]{1,0:T(8,128)(2,1)S(1)}, bf16[128,2048]{1,0:T(8,128)(2,1)S(1)}, u32[]{:S(2)}, u32[]{:S(2)}) collective-permute-start(bf16[128,2048]{1,0:T(8,128)(2,1)S(1)} %get-tuple-element.53.refs_2_), channel_id=1, source_target_pairs={{0,16},{4,20},{8,24},{12,28},{16,0},{20,4},{24,8},{28,12},{1,17},{... | collective-permute-start | bytes 1572872 | tf_op jit(solution)/shard_map/ppermute | solution.py:20
  46.5 0.3 collective-permute-start.15
  46.7 0.1 convert_add_fusion
  46.9 2.4 %collective-permute-start.12 = (f16[24,32,128]{2,1,0:T(8,128)(2,1)S(1)}, f16[24,32,128]{2,1,0:T(8,128)(2,1)S(1)}, u32[]{:S(2)}, u32[]{:S(2)}) collective-permute-start(f16[24,32,128]{2,1,0:T(8,128)(2,1)S(1)} %fusion.4), channel_id=1, source_target_pairs={{0,2},{1,3},{2,0},{3,1},{4,6},{5,7},{6,4},{7,5},{8,10},{9,11},{10,... | collective-permute-start | bytes 589832 | tf_op jit(solution)/shard_map/ppermute | solution.py:20
  49.3 2.7 %shard_map.49 = (f32[2,18,32,128]{3,2,1,0:T(8,128)S(1)}, f32[2,18,32,128]{3,2,1,0:T(8,128)S(1)}, bf16[128,2048]{1,0:T(8,128)(2,1)S(1)}, bf16[128,2048]{1,0:T(8,128)(2,1)S(1)}, bf16[128,2048]{1,0:T(8,128)(2,1)}) custom-call(bf16[256,2048]{1,0:T(8,128)(2,1)S(1)} %get-tuple-element.33.refs_0_, bf16[128,2048]{1,0:T(8,128)(2,1)S(1)} %get-tuple-element.42.refs_1_, ...), custom_call_target="tpu_custom_call" | custom-call | flops 1000 | bytes 1000 | tf_op jit(solution)/shard_map/pallas_call | solution.py:356
  52.1 1.4 %collective-permute-start.11 = (f16[2,18,32,128]{3,2,1,0:T(8,128)(2,1)S(1)}, f16[2,18,32,128]{3,2,1,0:T(8,128)(2,1)S(1)}, u32[]{:S(2)}, u32[]{:S(2)}) collective-permute-start(f16[2,18,32,128]{3,2,1,0:T(8,128)(2,1)S(1)} %multiply_convert_fusion.2), channel_id=1, source_target_pairs={{0,1},{1,0},{2,3},{3,2},{4,5},{5,4},{6,7},{7,6},{8,9},{9,8},{10,11... | collective-permute-start | bytes 884744 | tf_op jit(solution)/shard_map/ppermute | solution.py:20
  53.5 0.1 collective-permute-start.1
  53.6 4.3 %collective-permute-done.12 = f16[24,32,128]{2,1,0:T(8,128)(2,1)S(1)} collective-permute-done((f16[24,32,128]{2,1,0:T(8,128)(2,1)S(1)}, f16[24,32,128]{2,1,0:T(8,128)(2,1)S(1)}, u32[]{:S(2)}, u32[]{:S(2)}) %collective-permute-start.12) | collective-permute-done | bytes 196640 | tf_op jit(solution)/shard_map/ppermute | solution.py:20
  57.9 1.0 collective-permute-done.14.refs_4_
  58.8 0.9 collective-permute-done.15.refs_8_
  59.7 1.1 %collective-permute-start.16 = (bf16[128,2048]{1,0:T(8,128)(2,1)S(1)}, bf16[128,2048]{1,0:T(8,128)(2,1)S(1)}, u32[]{:S(2)}, u32[]{:S(2)}) collective-permute-start(bf16[128,2048]{1,0:T(8,128)(2,1)S(1)} %collective-permute-done.14.refs_4_), channel_id=1, source_target_pairs={{0,4},{4,0},{8,12},{12,8},{16,20},{20,16},{24,28},{28,24},{1,5},{5... | collective-permute-start | bytes 1572872 | tf_op jit(solution)/shard_map/ppermute | solution.py:20
  60.9 0.7 collective-permute-done.1
  61.6 4.6 %collective-permute-done.11 = f16[2,18,32,128]{3,2,1,0:T(8,128)(2,1)S(1)} collective-permute-done((f16[2,18,32,128]{3,2,1,0:T(8,128)(2,1)S(1)}, f16[2,18,32,128]{3,2,1,0:T(8,128)(2,1)S(1)}, u32[]{:S(2)}, u32[]{:S(2)}) %collective-permute-start.11) | collective-permute-done | bytes 294944 | tf_op jit(solution)/shard_map/ppermute | solution.py:20
  66.2 0.1 convert_add_fusion.2
  66.3 3.4 %shard_map.50 = (f32[2,22,32,128]{3,2,1,0:T(8,128)S(1)}, f32[2,22,32,128]{3,2,1,0:T(8,128)S(1)}, bf16[128,2048]{1,0:T(8,128)(2,1)}, bf16[128,2048]{1,0:T(8,128)(2,1)}, bf16[128,2048]{1,0:T(8,128)(2,1)}) custom-call(bf16[256,2048]{1,0:T(8,128)(2,1)S(1)} %get-tuple-element.33.refs_0_, bf16[128,2048]{1,0:T(8,128)(2,1)S(1)} %get-tuple-element.42.refs_1_, ...), custom_call_target="tpu_custom_call" | custom-call | flops 1000 | bytes 1000 | tf_op jit(solution)/shard_map/pallas_call | solution.py:356
  69.7 0.1 multiply_convert_fusion.1
  69.9 2.0 %collective-permute-start.13 = (f16[18,32,128]{2,1,0:T(8,128)(2,1)S(1)}, f16[18,32,128]{2,1,0:T(8,128)(2,1)S(1)}, u32[]{:S(2)}, u32[]{:S(2)}) collective-permute-start(f16[18,32,128]{2,1,0:T(8,128)(2,1)S(1)} %fusion.6), channel_id=1, source_target_pairs={{0,2},{1,3},{2,0},{3,1},{4,6},{5,7},{6,4},{7,5},{8,10},{9,11},{10,... | collective-permute-start | bytes 442376 | tf_op jit(solution)/shard_map/ppermute | solution.py:20
  71.9 7.8 %collective-permute-done.13 = f16[18,32,128]{2,1,0:T(8,128)(2,1)S(1)} collective-permute-done((f16[18,32,128]{2,1,0:T(8,128)(2,1)S(1)}, f16[18,32,128]{2,1,0:T(8,128)(2,1)S(1)}, u32[]{:S(2)}, u32[]{:S(2)}) %collective-permute-start.13) | collective-permute-done | bytes 147488 | tf_op jit(solution)/shard_map/ppermute | solution.py:20
  79.7 2.6 %collective-permute-done.17 = f16[2,22,32,128]{3,2,1,0:T(8,128)(2,1)S(1)} collective-permute-done((f16[2,22,32,128]{3,2,1,0:T(8,128)(2,1)S(1)}, f16[2,22,32,128]{3,2,1,0:T(8,128)(2,1)S(1)}, u32[]{:S(2)}, u32[]{:S(2)}) %collective-permute-start.17) | collective-permute-done | bytes 360480 | tf_op jit(solution)/shard_map/ppermute | solution.py:20
  82.3 0.1 convert_add_fusion.1
  82.5 0.6 collective-permute-start.18
  83.1 2.2 %collective-permute-start.19 = (f16[9,32,128]{2,1,0:T(8,128)(2,1)S(1)}, f16[9,32,128]{2,1,0:T(8,128)(2,1)S(1)}, u32[]{:S(2)}, u32[]{:S(2)}) collective-permute-start(f16[9,32,128]{2,1,0:T(8,128)(2,1)S(1)} %pad_maximum_fusion), channel_id=1, source_target_pairs={{8,24},{12,28},{24,8},{28,12},{9,25},{13,29},{25,9},{29,13},{10,26... | collective-permute-start | bytes 221192 | tf_op jit(solution)/shard_map/ppermute | solution.py:20
  85.4 3.6 %collective-permute-start.20 = (f16[9,32,128]{2,1,0:T(8,128)(2,1)S(1)}, f16[9,32,128]{2,1,0:T(8,128)(2,1)S(1)}, u32[]{:S(2)}, u32[]{:S(2)}) collective-permute-start(f16[9,32,128]{2,1,0:T(8,128)(2,1)S(1)} %pad_maximum_fusion.1), channel_id=1, source_target_pairs={{0,4},{4,0},{8,28},{12,24},{16,20},{20,16},{24,12},{28,8},{1,5},{5... | collective-permute-start | bytes 221192 | tf_op jit(solution)/shard_map/ppermute | solution.py:331
  89.0 3.6 %collective-permute-done.20 = f16[9,32,128]{2,1,0:T(8,128)(2,1)S(1)} collective-permute-done((f16[9,32,128]{2,1,0:T(8,128)(2,1)S(1)}, f16[9,32,128]{2,1,0:T(8,128)(2,1)S(1)}, u32[]{:S(2)}, u32[]{:S(2)}) %collective-permute-start.20) | collective-permute-done | bytes 73760 | tf_op jit(solution)/shard_map/ppermute | solution.py:331
  92.7 1.9 %collective-permute-start.21 = (f16[7,32,128]{2,1,0:T(8,128)(2,1)S(1)}, f16[7,32,128]{2,1,0:T(8,128)(2,1)S(1)}, u32[]{:S(2)}, u32[]{:S(2)}) collective-permute-start(f16[7,32,128]{2,1,0:T(8,128)(2,1)S(1)} %get-tuple-element.70), channel_id=1, source_target_pairs={{8,24},{12,28},{24,8},{28,12},{9,25},{13,29},{25,9},{29,13},{10,26... | collective-permute-start | bytes 172040 | tf_op jit(solution)/shard_map/ppermute | solution.py:20
  94.6 2.7 %collective-permute-start.22 = (f16[7,32,128]{2,1,0:T(8,128)(2,1)S(1)}, f16[7,32,128]{2,1,0:T(8,128)(2,1)S(1)}, u32[]{:S(2)}, u32[]{:S(2)}) collective-permute-start(f16[7,32,128]{2,1,0:T(8,128)(2,1)S(1)} %get-tuple-element.69), channel_id=1, source_target_pairs={{0,4},{4,0},{8,28},{12,24},{16,20},{20,16},{24,12},{28,8},{1,5},{5... | collective-permute-start | bytes 172040 | tf_op jit(solution)/shard_map/ppermute | solution.py:331
  97.3 0.3 collective-permute-done.21
  97.6 2.3 %collective-permute-done.22 = f16[7,32,128]{2,1,0:T(8,128)(2,1)S(1)} collective-permute-done((f16[7,32,128]{2,1,0:T(8,128)(2,1)S(1)}, f16[7,32,128]{2,1,0:T(8,128)(2,1)S(1)}, u32[]{:S(2)}, u32[]{:S(2)}) %collective-permute-start.22) | collective-permute-done | bytes 57376 | tf_op jit(solution)/shard_map/ppermute | solution.py:331
  100.0 1.6 %shard_map.51 = f32[5,512,128]{2,1,0:T(8,128)} custom-call(f32[16,32,128]{2,1,0:T(8,128)S(1)} %fusion.3.own_ref, f32[24,32,128]{2,1,0:T(8,128)S(1)} %get-tuple-element.64.refs_0_, f32[18,32,128]{2,1,0:T(8,128)S(1)} %get-tuple-element.66.refs_1_, f32[22,32,128]{2,1,0:T(8,128)S(1)} %get-tuple-element.62.refs_2_, ...), custom_call_target="tpu_custom_call" | custom-call | flops 1000 | bytes 1000 | tf_op jit(solution)/shard_map/pallas_call | solution.py:370
  (29 shorter events, 0.7 us)
Async XLA Ops:
  3.0 12.5 %collective-permute-start.2 = (bf16[256,2048]{1,0:T(8,128)(2,1)S(1)}, bf16[256,2048]{1,0:T(8,128)(2,1)S(1)}, u32[]{:S(2)}, u32[]{:S(2)}) collective-permute-start(bf16[256,2048]{1,0:T(8,128)(2,1)S(1)} %get-tuple-element.33.refs_0_), channel_id=1, source_target_pairs={{0,4},{4,0},{8,12},{12,8},{16,20},{20,16},{24,28},{28,24},{1,5},{5... | collective-permute-start | bytes 3145736 | tf_op jit(solution)/shard_map/ppermute | solution.py:20
  3.7 24.7 %collective-permute-start.3 = (bf16[256,2048]{1,0:T(8,128)(2,1)S(1)}, bf16[256,2048]{1,0:T(8,128)(2,1)S(1)}, u32[]{:S(2)}, u32[]{:S(2)}) collective-permute-start(bf16[256,2048]{1,0:T(8,128)(2,1)S(1)} %get-tuple-element.33.refs_0_), channel_id=1, source_target_pairs={{0,16},{4,20},{8,24},{12,28},{16,0},{20,4},{24,8},{28,12},{1,17},{... | collective-permute-start | bytes 3145736 | tf_op jit(solution)/shard_map/ppermute | solution.py:20
  5.0 24.4 %collective-permute-start.4 = (bf16[256,2048]{1,0:T(8,128)(2,1)S(1)}, bf16[256,2048]{1,0:T(8,128)(2,1)S(1)}, u32[]{:S(2)}, u32[]{:S(2)}) collective-permute-start(bf16[256,2048]{1,0:T(8,128)(2,1)S(1)} %get-tuple-element.33.refs_0_), channel_id=1, source_target_pairs={{0,8},{4,12},{8,0},{12,4},{16,24},{20,28},{24,16},{28,20},{1,9},{5... | collective-permute-start | bytes 3145736 | tf_op jit(solution)/shard_map/ppermute | solution.py:20
  8.2 7.3 %collective-permute-start = (f16[2,16,32,128]{3,2,1,0:T(8,128)(2,1)S(1)}, f16[2,16,32,128]{3,2,1,0:T(8,128)(2,1)S(1)}, u32[]{:S(2)}, u32[]{:S(2)}) collective-permute-start(f16[2,16,32,128]{3,2,1,0:T(8,128)(2,1)S(1)} %multiply_convert_fusion.3), channel_id=1, source_target_pairs={{0,1},{1,0},{2,3},{3,2},{4,5},{5,4},{6,7},{7,6},{8,9},{9,8},{10,11... | collective-permute-start | bytes 786440 | tf_op jit(solution)/shard_map/ppermute | solution.py:20
  29.4 3.5 %collective-permute-start.5 = (bf16[256,2048]{1,0:T(8,128)(2,1)S(1)}, bf16[256,2048]{1,0:T(8,128)(2,1)S(1)}, u32[]{:S(2)}, u32[]{:S(2)}) collective-permute-start(bf16[256,2048]{1,0:T(8,128)(2,1)S(1)} %collective-permute-done.3.refs_4_), channel_id=1, source_target_pairs={{0,4},{4,0},{8,12},{12,8},{16,20},{20,16},{24,28},{28,24},{1,5},{5... | collective-permute-start | bytes 3145736 | tf_op jit(solution)/shard_map/ppermute | solution.py:20
  30.5 13.6 %collective-permute-start.7 = (bf16[128,2048]{1,0:T(8,128)(2,1)S(1)}, bf16[128,2048]{1,0:T(8,128)(2,1)S(1)}, u32[]{:S(2)}, u32[]{:S(2)}) collective-permute-start(bf16[128,2048]{1,0:T(8,128)(2,1)S(1)} %get-tuple-element.42.refs_1_), channel_id=1, source_target_pairs={{0,16},{4,20},{8,24},{12,28},{16,0},{20,4},{24,8},{28,12},{1,17},{... | collective-permute-start | bytes 1572872 | tf_op jit(solution)/shard_map/ppermute | solution.py:20
  30.8 13.3 %collective-permute-start.8 = (bf16[128,2048]{1,0:T(8,128)(2,1)S(1)}, bf16[128,2048]{1,0:T(8,128)(2,1)S(1)}, u32[]{:S(2)}, u32[]{:S(2)}) collective-permute-start(bf16[128,2048]{1,0:T(8,128)(2,1)S(1)} %get-tuple-element.42.refs_1_), channel_id=1, source_target_pairs={{0,8},{4,12},{8,0},{12,4},{16,24},{20,28},{24,16},{28,20},{1,9},{5... | collective-permute-start | bytes 1572872 | tf_op jit(solution)/shard_map/ppermute | solution.py:20
  35.6 13.7 %collective-permute-start.6 = (bf16[256,2048]{1,0:T(8,128)(2,1)S(1)}, bf16[256,2048]{1,0:T(8,128)(2,1)S(1)}, u32[]{:S(2)}, u32[]{:S(2)}) collective-permute-start(bf16[256,2048]{1,0:T(8,128)(2,1)S(1)} %get-tuple-element.41), channel_id=1, source_target_pairs={{0,4},{4,0},{8,12},{12,8},{16,20},{20,16},{24,28},{28,24},{1,5},{5... | collective-permute-start | bytes 3145736 | tf_op jit(solution)/shard_map/ppermute | solution.py:20
  36.1 10.7 %collective-permute-start.10 = (f16[2,24,32,128]{3,2,1,0:T(8,128)(2,1)S(1)}, f16[2,24,32,128]{3,2,1,0:T(8,128)(2,1)S(1)}, u32[]{:S(2)}, u32[]{:S(2)}) collective-permute-start(f16[2,24,32,128]{3,2,1,0:T(8,128)(2,1)S(1)} %multiply_convert_fusion), channel_id=1, source_target_pairs={{0,1},{1,0},{2,3},{3,2},{4,5},{5,4},{6,7},{7,6},{8,9},{9,8},{10,11... | collective-permute-start | bytes 1179656 | tf_op jit(solution)/shard_map/ppermute | solution.py:20
  44.1 5.2 %collective-permute-start.9 = (bf16[128,2048]{1,0:T(8,128)(2,1)S(1)}, bf16[128,2048]{1,0:T(8,128)(2,1)S(1)}, u32[]{:S(2)}, u32[]{:S(2)}) collective-permute-start(bf16[128,2048]{1,0:T(8,128)(2,1)S(1)} %collective-permute-done.7.refs_4_), channel_id=1, source_target_pairs={{0,4},{4,0},{8,12},{12,8},{16,20},{20,16},{24,28},{28,24},{1,5},{5... | collective-permute-start | bytes 1572872 | tf_op jit(solution)/shard_map/ppermute | solution.py:20
  45.2 13.6 %collective-permute-start.14 = (bf16[128,2048]{1,0:T(8,128)(2,1)S(1)}, bf16[128,2048]{1,0:T(8,128)(2,1)S(1)}, u32[]{:S(2)}, u32[]{:S(2)}) collective-permute-start(bf16[128,2048]{1,0:T(8,128)(2,1)S(1)} %get-tuple-element.53.refs_2_), channel_id=1, source_target_pairs={{0,16},{4,20},{8,24},{12,28},{16,0},{20,4},{24,8},{28,12},{1,17},{... | collective-permute-start | bytes 1572872 | tf_op jit(solution)/shard_map/ppermute | solution.py:20
  46.5 13.2 %collective-permute-start.15 = (bf16[128,2048]{1,0:T(8,128)(2,1)S(1)}, bf16[128,2048]{1,0:T(8,128)(2,1)S(1)}, u32[]{:S(2)}, u32[]{:S(2)}) collective-permute-start(bf16[128,2048]{1,0:T(8,128)(2,1)S(1)} %get-tuple-element.53.refs_2_), channel_id=1, source_target_pairs={{0,8},{4,12},{8,0},{12,4},{16,24},{20,28},{24,16},{28,20},{1,9},{5... | collective-permute-start | bytes 1572872 | tf_op jit(solution)/shard_map/ppermute | solution.py:20
  46.9 10.9 %collective-permute-start.12 = (f16[24,32,128]{2,1,0:T(8,128)(2,1)S(1)}, f16[24,32,128]{2,1,0:T(8,128)(2,1)S(1)}, u32[]{:S(2)}, u32[]{:S(2)}) collective-permute-start(f16[24,32,128]{2,1,0:T(8,128)(2,1)S(1)} %fusion.4), channel_id=1, source_target_pairs={{0,2},{1,3},{2,0},{3,1},{4,6},{5,7},{6,4},{7,5},{8,10},{9,11},{10,... | collective-permute-start | bytes 589832 | tf_op jit(solution)/shard_map/ppermute | solution.py:20
  52.1 14.1 %collective-permute-start.11 = (f16[2,18,32,128]{3,2,1,0:T(8,128)(2,1)S(1)}, f16[2,18,32,128]{3,2,1,0:T(8,128)(2,1)S(1)}, u32[]{:S(2)}, u32[]{:S(2)}) collective-permute-start(f16[2,18,32,128]{3,2,1,0:T(8,128)(2,1)S(1)} %multiply_convert_fusion.2), channel_id=1, source_target_pairs={{0,1},{1,0},{2,3},{3,2},{4,5},{5,4},{6,7},{7,6},{8,9},{9,8},{10,11... | collective-permute-start | bytes 884744 | tf_op jit(solution)/shard_map/ppermute | solution.py:20
  53.5 8.1 %collective-permute-start.1 = (f16[16,32,128]{2,1,0:T(8,128)(2,1)S(1)}, f16[16,32,128]{2,1,0:T(8,128)(2,1)S(1)}, u32[]{:S(2)}, u32[]{:S(2)}) collective-permute-start(f16[16,32,128]{2,1,0:T(8,128)(2,1)S(1)} %fusion.7), channel_id=1, source_target_pairs={{0,2},{1,3},{2,0},{3,1},{4,6},{5,7},{6,4},{7,5},{8,10},{9,11},{10,... | collective-permute-start | bytes 393224 | tf_op jit(solution)/shard_map/ppermute | solution.py:20
  59.7 6.6 %collective-permute-start.16 = (bf16[128,2048]{1,0:T(8,128)(2,1)S(1)}, bf16[128,2048]{1,0:T(8,128)(2,1)S(1)}, u32[]{:S(2)}, u32[]{:S(2)}) collective-permute-start(bf16[128,2048]{1,0:T(8,128)(2,1)S(1)} %collective-permute-done.14.refs_4_), channel_id=1, source_target_pairs={{0,4},{4,0},{8,12},{12,8},{16,20},{20,16},{24,28},{28,24},{1,5},{5... | collective-permute-start | bytes 1572872 | tf_op jit(solution)/shard_map/ppermute | solution.py:20
  69.8 12.5 %collective-permute-start.17 = (f16[2,22,32,128]{3,2,1,0:T(8,128)(2,1)S(1)}, f16[2,22,32,128]{3,2,1,0:T(8,128)(2,1)S(1)}, u32[]{:S(2)}, u32[]{:S(2)}) collective-permute-start(f16[2,22,32,128]{3,2,1,0:T(8,128)(2,1)S(1)} %multiply_convert_fusion.1), channel_id=1, source_target_pairs={{0,1},{1,0},{2,3},{3,2},{4,5},{5,4},{6,7},{7,6},{8,9},{9,8},{10,11... | collective-permute-start | bytes 1081352 | tf_op jit(solution)/shard_map/ppermute | solution.py:20
  69.9 9.8 %collective-permute-start.13 = (f16[18,32,128]{2,1,0:T(8,128)(2,1)S(1)}, f16[18,32,128]{2,1,0:T(8,128)(2,1)S(1)}, u32[]{:S(2)}, u32[]{:S(2)}) collective-permute-start(f16[18,32,128]{2,1,0:T(8,128)(2,1)S(1)} %fusion.6), channel_id=1, source_target_pairs={{0,2},{1,3},{2,0},{3,1},{4,6},{5,7},{6,4},{7,5},{8,10},{9,11},{10,... | collective-permute-start | bytes 442376 | tf_op jit(solution)/shard_map/ppermute | solution.py:20
  82.5 10.1 %collective-permute-start.18 = (f16[22,32,128]{2,1,0:T(8,128)(2,1)S(1)}, f16[22,32,128]{2,1,0:T(8,128)(2,1)S(1)}, u32[]{:S(2)}, u32[]{:S(2)}) collective-permute-start(f16[22,32,128]{2,1,0:T(8,128)(2,1)S(1)} %fusion.5), channel_id=1, source_target_pairs={{0,2},{1,3},{2,0},{3,1},{4,6},{5,7},{6,4},{7,5},{8,10},{9,11},{10,... | collective-permute-start | bytes 540680 | tf_op jit(solution)/shard_map/ppermute | solution.py:20
  83.1 5.9 %collective-permute-start.19 = (f16[9,32,128]{2,1,0:T(8,128)(2,1)S(1)}, f16[9,32,128]{2,1,0:T(8,128)(2,1)S(1)}, u32[]{:S(2)}, u32[]{:S(2)}) collective-permute-start(f16[9,32,128]{2,1,0:T(8,128)(2,1)S(1)} %pad_maximum_fusion), channel_id=1, source_target_pairs={{8,24},{12,28},{24,8},{28,12},{9,25},{13,29},{25,9},{29,13},{10,26... | collective-permute-start | bytes 221192 | tf_op jit(solution)/shard_map/ppermute | solution.py:20
  85.4 7.2 %collective-permute-start.20 = (f16[9,32,128]{2,1,0:T(8,128)(2,1)S(1)}, f16[9,32,128]{2,1,0:T(8,128)(2,1)S(1)}, u32[]{:S(2)}, u32[]{:S(2)}) collective-permute-start(f16[9,32,128]{2,1,0:T(8,128)(2,1)S(1)} %pad_maximum_fusion.1), channel_id=1, source_target_pairs={{0,4},{4,0},{8,28},{12,24},{16,20},{20,16},{24,12},{28,8},{1,5},{5... | collective-permute-start | bytes 221192 | tf_op jit(solution)/shard_map/ppermute | solution.py:331
  92.7 4.9 %collective-permute-start.21 = (f16[7,32,128]{2,1,0:T(8,128)(2,1)S(1)}, f16[7,32,128]{2,1,0:T(8,128)(2,1)S(1)}, u32[]{:S(2)}, u32[]{:S(2)}) collective-permute-start(f16[7,32,128]{2,1,0:T(8,128)(2,1)S(1)} %get-tuple-element.70), channel_id=1, source_target_pairs={{8,24},{12,28},{24,8},{28,12},{9,25},{13,29},{25,9},{29,13},{10,26... | collective-permute-start | bytes 172040 | tf_op jit(solution)/shard_map/ppermute | solution.py:20
  94.6 5.3 %collective-permute-start.22 = (f16[7,32,128]{2,1,0:T(8,128)(2,1)S(1)}, f16[7,32,128]{2,1,0:T(8,128)(2,1)S(1)}, u32[]{:S(2)}, u32[]{:S(2)}) collective-permute-start(f16[7,32,128]{2,1,0:T(8,128)(2,1)S(1)} %get-tuple-element.69), channel_id=1, source_target_pairs={{0,4},{4,0},{8,28},{12,24},{16,20},{20,16},{24,12},{28,8},{1,5},{5... | collective-permute-start | bytes 172040 | tf_op jit(solution)/shard_map/ppermute | solution.py:331

commit v9 on v8

--- a/solution.py
+++ b/solution.py
@@ -190,7 +190,8 @@
         return out
 
     own_refs = take(len(STAGES))
-    sibling_ref, y_ref, y_other_ref = take(3)
+    sibling_refs = take(len(STAGES[0]) if stage == 0 else 1)
+    y_ref, y_other_ref = take(2)
     x_refs = take(stage + 1)
     left_before, cross_before = take(stage), take(stage)
     stay_ref, away_ref, left_ref, cross_ref, side_ref = take(5)
@@ -206,7 +207,11 @@
 
     for i in range(count):
         rows = slice(i * length, (i + 1) * length)
-        sibling_rows = slice(sibling_first + i * length, sibling_first + (i + 1) * length)
+        if stage == 0:
+            sibling_ref, sibling_rows = sibling_refs[i], slice(None)
+        else:
+            sibling_ref = sibling_refs[0]
+            sibling_rows = slice(sibling_first + i * length, sibling_first + (i + 1) * length)
 
         @pl.when(far == 1)
         def _():
@@ -332,9 +337,9 @@
 
     rest, *sent = clean_units(snapshots, outlier_cols, outlier_values, threshold)
     stay, away = on_units(own_kernel, message(UNITS * UNITS), len(sent))(*sent)
-    sibling = swapped(sent[0], "tm", 1)
     own_came = exchanged(away)
-    own_half = half_summed(stay, own_came)
+    own = summed(half_summed(stay, own_came))
+    sibling = [swapped(behind(sent[0][i * length : (i + 1) * length], own), "tm", 1) for i in range(len(STAGES[0]))]
     x_units, by_y, left, cross, halves, totals, came = [], [], [], [], [], [], None
     for stage, fresh in enumerate(STAGES):
         block = sent[stage]
@@ -342,16 +347,15 @@
             block = behind(block, x_units[-1], by_y[-1])
         x_units.append(swapped(block, "tm", 2))
         by_y.append(swapped(block, "tm", 4))
-        other = swapped(behind(by_y[-1], x_units[-1], *([own_came, sibling], left, left[1:])[stage]), "tm", 1)
+        other = swapped(behind(by_y[-1], x_units[-1], *([own_came], left, left[1:])[stage]), "tm", 1)
         if stage == 1:
-            sibling = swapped(behind(rest, left[0]), "tm", 1)
+            sibling = [swapped(behind(rest, left[0]), "tm", 1)]
         if stage == 2:
-            own = summed(own_half, after=[came])
             totals.append(summed(halves[0], after=left[1:]))
-            other = behind(other, own, *totals)
+            other = behind(other, came, *totals)
         elif stage == 1:
             other = behind(other, came)
-        operands = [*sent, sibling, by_y[-1], other, *x_units, *left, *cross]
+        operands = [*sent, *sibling, by_y[-1], other, *x_units, *left, *cross]
         out_shape = message(len(stage_blocks(stage))) + [units(len(fresh))] * 3
         stay, away, left_now, cross_now, _ = on_units(
             functools.partial(stage_kernel, stage), out_shape, len(operands)

time: 102 us -> 99.7 us (0.977)
  waiting for transfers between devices: 56.4 us -> 52.1 us
  starting transfers between devices: 27.4 us -> 29.5 us
    ppermute x21 -> x22, waiting for transfers between devices: 50.5 us -> 46.2 us  [swapped(): return lax.ppermute(x, axis, pairs)]
    ppermute x21 -> x22, starting transfers between devices: 21.1 us -> 23.6 us  [swapped(): return lax.ppermute(x, axis, pairs)]
  transfers between devices with their start and end apart: 23 -> 24, of which waited for: 15 -> 15; matrix products, arithmetic and copies ran while one was open for 1% -> 1% of each run, Pallas kernels for 8% -> 8%
where the time goes in v9:
time: 99.7 us; the launch traced here: 99.5 us
  waiting for transfers between devices  52.1 us (52%)
  starting transfers between devices  29.5 us (30%)
  Pallas kernels  15.7 us (16%)
  other arithmetic  1.14 us (1%)
    ppermute x22, waiting for transfers between devices, swapped(): return lax.ppermute(x, axis, pairs)  46.2 us
    ppermute x22, starting transfers between devices, swapped(): return lax.ppermute(x, axis, pairs)  23.6 us
    pallas_call x3, Pallas kernels, square(): on_units(functools.partial(stage_kernel, stage), out_shape, len(operands))  8.88 us
    ppermute x2, waiting for transfers between devices, handed_over(): lax.ppermute(cross, 'tm', pairs)  5.91 us
    ppermute x2, starting transfers between devices, handed_over(): lax.ppermute(cross, 'tm', pairs)  5.83 us
    pallas_call x1, Pallas kernels, square(): stay, away = on_units(own_kernel, message(UNITS * UNITS), len(sent))(*sent)  2.89 us
    pallas_call x1, Pallas kernels, clean_units(): pl.pallas_call(clean_kernel, out_shape=out_shape, in_specs=[hbm, pl.Block...  2.3 us
  transfers between devices with their start and end apart: 24, of which 15 were waited for; matrix products, arithmetic and copies ran while one was open for 1% of the time, Pallas kernels for 8%

profile of v9, /device:TPU:3, one launch (start us, length us, event | category | flops | bytes accessed | tf_op | source)
XLA Modules:
  0.0 99.5 jit_solution(3497251405459850258)
XLA Ops:
  0.7 2.3 %shard_map.46 = (bf16[256,2048]{1,0:T(8,128)(2,1)S(1)}, bf16[256,2048]{1,0:T(8,128)(2,1)S(1)}, bf16[128,2048]{1,0:T(8,128)(2,1)S(1)}, bf16[128,2048]{1,0:T(8,128)(2,1)S(1)}) custom-call(s32[4,4]{1,0:T(4,128)} %cols_hbm.1, f32[1]{0:T(128)} %bitcast.29.threshold_ref, bf16[512,2048]{1,0:T(8,128)(2,1)} %snapshots_hbm.1, bf16[4,4,128,128]{3,2,1,0:T(8,128)(2,1)} %values_hbm.1), custom_call_target="tpu_custom_call" | custom-call | tf_op jit(solution)/shard_map/pallas_call | solution.py:124
  3.0 1.3 %collective-permute-start.4 = (bf16[256,2048]{1,0:T(8,128)(2,1)S(1)}, bf16[256,2048]{1,0:T(8,128)(2,1)S(1)}, u32[]{:S(2)}, u32[]{:S(2)}) collective-permute-start(bf16[256,2048]{1,0:T(8,128)(2,1)S(1)} %get-tuple-element.34.refs_0_), channel_id=1, source_target_pairs={{0,16},{4,20},{8,24},{12,28},{16,0},{20,4},{24,8},{28,12},{1,17},{... | collective-permute-start | bytes 3145736 | tf_op jit(solution)/shard_map/ppermute | solution.py:20
  4.3 0.3 collective-permute-start.5
  4.5 2.9 %shard_map.47 = (f32[2,16,32,128]{3,2,1,0:T(8,128)S(1)}, f32[2,16,32,128]{3,2,1,0:T(8,128)S(1)}) custom-call(bf16[256,2048]{1,0:T(8,128)(2,1)S(1)} %get-tuple-element.34.refs_0_, bf16[128,2048]{1,0:T(8,128)(2,1)S(1)} %get-tuple-element.47.refs_1_, bf16[128,2048]{1,0:T(8,128)(2,1)S(1)} %get-tuple-element.55.refs_2_), custom_call_target="tpu_custom_call" | custom-call | flops 1000 | bytes 1000 | tf_op jit(solution)/shard_map/pallas_call | solution.py:339
  7.5 1.4 %collective-permute-start = (f16[2,16,32,128]{3,2,1,0:T(8,128)(2,1)S(1)}, f16[2,16,32,128]{3,2,1,0:T(8,128)(2,1)S(1)}, u32[]{:S(2)}, u32[]{:S(2)}) collective-permute-start(f16[2,16,32,128]{3,2,1,0:T(8,128)(2,1)S(1)} %multiply_convert_fusion.3), channel_id=1, source_target_pairs={{0,1},{1,0},{2,3},{3,2},{4,5},{5,4},{6,7},{7,6},{8,9},{9,8},{10,11... | collective-permute-start | bytes 786440 | tf_op jit(solution)/shard_map/ppermute | solution.py:20
  8.9 5.3 %collective-permute-done = f16[2,16,32,128]{3,2,1,0:T(8,128)(2,1)S(1)} collective-permute-done((f16[2,16,32,128]{3,2,1,0:T(8,128)(2,1)S(1)}, f16[2,16,32,128]{3,2,1,0:T(8,128)(2,1)S(1)}, u32[]{:S(2)}, u32[]{:S(2)}) %collective-permute-start) | collective-permute-done | bytes 262176 | tf_op jit(solution)/shard_map/ppermute | solution.py:20
  14.2 2.4 %collective-permute-start.1 = (f16[16,32,128]{2,1,0:T(8,128)(2,1)S(1)}, f16[16,32,128]{2,1,0:T(8,128)(2,1)S(1)}, u32[]{:S(2)}, u32[]{:S(2)}) collective-permute-start(f16[16,32,128]{2,1,0:T(8,128)(2,1)S(1)} %fusion.7), channel_id=1, source_target_pairs={{0,2},{1,3},{2,0},{3,1},{4,6},{5,7},{6,4},{7,5},{8,10},{9,11},{10,... | collective-permute-start | bytes 393224 | tf_op jit(solution)/shard_map/ppermute | solution.py:20
  16.6 10.4 %collective-permute-done.4.refs_5_ = bf16[256,2048]{1,0:T(8,128)(2,1)S(1)} collective-permute-done((bf16[256,2048]{1,0:T(8,128)(2,1)S(1)}, bf16[256,2048]{1,0:T(8,128)(2,1)S(1)}, u32[]{:S(2)}, u32[]{:S(2)}) %collective-permute-start.4) | collective-permute-done | bytes 1048608 | tf_op jit(solution)/shard_map/ppermute | solution.py:20
  27.1 0.9 collective-permute-done.5.refs_7_.refs_6_
  28.0 1.9 %collective-permute-start.6 = (bf16[256,2048]{1,0:T(8,128)(2,1)S(1)}, bf16[256,2048]{1,0:T(8,128)(2,1)S(1)}, u32[]{:S(2)}, u32[]{:S(2)}) collective-permute-start(bf16[256,2048]{1,0:T(8,128)(2,1)S(1)} %collective-permute-done.4.refs_5_), channel_id=1, source_target_pairs={{0,4},{4,0},{8,12},{12,8},{16,20},{20,16},{24,28},{28,24},{1,5},{5... | collective-permute-start | bytes 3145736 | tf_op jit(solution)/shard_map/ppermute | solution.py:20
  29.8 0.1 fusion.14
  30.1 0.5 collective-permute-start.3
  30.6 0.2 collective-permute-start.10
  30.8 0.1 collective-permute-start.11
  30.9 2.0 %collective-permute-done.2.refs_3_ = bf16[128,2048]{1,0:T(8,128)(2,1)S(1)} collective-permute-done((bf16[128,2048]{1,0:T(8,128)(2,1)S(1)}, bf16[128,2048]{1,0:T(8,128)(2,1)S(1)}, u32[]{:S(2)}, u32[]{:S(2)}) %collective-permute-start.2) | collective-permute-done | bytes 524320 | tf_op jit(solution)/shard_map/ppermute | solution.py:20
  32.9 0.7 collective-permute-done.3.refs_4_
  33.6 2.8 %shard_map.48 = (f32[2,24,32,128]{3,2,1,0:T(8,128)S(1)}, f32[2,24,32,128]{3,2,1,0:T(8,128)S(1)}, bf16[256,2048]{1,0:T(8,128)(2,1)S(1)}, bf16[256,2048]{1,0:T(8,128)(2,1)S(1)}, bf16[256,2048]{1,0:T(8,128)(2,1)}) custom-call(bf16[256,2048]{1,0:T(8,128)(2,1)S(1)} %get-tuple-element.34.refs_0_, bf16[128,2048]{1,0:T(8,128)(2,1)S(1)} %get-tuple-element.47.refs_1_, ...), custom_call_target="tpu_custom_call" | custom-call | flops 1000 | bytes 1000 | tf_op jit(solution)/shard_map/pallas_call | solution.py:360
  36.4 0.4 collective-permute-start.9
  36.8 0.1 multiply_convert_fusion
  36.9 1.4 %collective-permute-start.7 = (f16[2,24,32,128]{3,2,1,0:T(8,128)(2,1)S(1)}, f16[2,24,32,128]{3,2,1,0:T(8,128)(2,1)S(1)}, u32[]{:S(2)}, u32[]{:S(2)}) collective-permute-start(f16[2,24,32,128]{3,2,1,0:T(8,128)(2,1)S(1)} %multiply_convert_fusion), channel_id=1, source_target_pairs={{0,1},{1,0},{2,3},{3,2},{4,5},{5,4},{6,7},{7,6},{8,9},{9,8},{10,11... | collective-permute-start | bytes 1179656 | tf_op jit(solution)/shard_map/ppermute | solution.py:20
  38.2 5.8 %collective-permute-done.10.refs_4_ = bf16[128,2048]{1,0:T(8,128)(2,1)S(1)} collective-permute-done((bf16[128,2048]{1,0:T(8,128)(2,1)S(1)}, bf16[128,2048]{1,0:T(8,128)(2,1)S(1)}, u32[]{:S(2)}, u32[]{:S(2)}) %collective-permute-start.10) | collective-permute-done | bytes 524320 | tf_op jit(solution)/shard_map/ppermute | solution.py:20
  44.1 1.1 %collective-permute-start.12 = (bf16[128,2048]{1,0:T(8,128)(2,1)S(1)}, bf16[128,2048]{1,0:T(8,128)(2,1)S(1)}, u32[]{:S(2)}, u32[]{:S(2)}) collective-permute-start(bf16[128,2048]{1,0:T(8,128)(2,1)S(1)} %collective-permute-done.10.refs_4_), channel_id=1, source_target_pairs={{0,4},{4,0},{8,12},{12,8},{16,20},{20,16},{24,28},{28,24},{1,5},{5... | collective-permute-start | bytes 1572872 | tf_op jit(solution)/shard_map/ppermute | solution.py:20
  45.2 1.2 %collective-permute-start.15 = (bf16[128,2048]{1,0:T(8,128)(2,1)S(1)}, bf16[128,2048]{1,0:T(8,128)(2,1)S(1)}, u32[]{:S(2)}, u32[]{:S(2)}) collective-permute-start(bf16[128,2048]{1,0:T(8,128)(2,1)S(1)} %get-tuple-element.55.refs_2_), channel_id=1, source_target_pairs={{0,16},{4,20},{8,24},{12,28},{16,0},{20,4},{24,8},{28,12},{1,17},{... | collective-permute-start | bytes 1572872 | tf_op jit(solution)/shard_map/ppermute | solution.py:20
  46.4 0.3 collective-permute-start.16
  46.7 0.9 collective-permute-done.7
  47.5 0.1 convert_add_fusion
  47.7 2.4 %collective-permute-start.8 = (f16[24,32,128]{2,1,0:T(8,128)(2,1)S(1)}, f16[24,32,128]{2,1,0:T(8,128)(2,1)S(1)}, u32[]{:S(2)}, u32[]{:S(2)}) collective-permute-start(f16[24,32,128]{2,1,0:T(8,128)(2,1)S(1)} %fusion.4), channel_id=1, source_target_pairs={{0,2},{1,3},{2,0},{3,1},{4,6},{5,7},{6,4},{7,5},{8,10},{9,11},{10,... | collective-permute-start | bytes 589832 | tf_op jit(solution)/shard_map/ppermute | solution.py:20
  50.1 2.7 %shard_map.49 = (f32[2,18,32,128]{3,2,1,0:T(8,128)S(1)}, f32[2,18,32,128]{3,2,1,0:T(8,128)S(1)}, bf16[128,2048]{1,0:T(8,128)(2,1)S(1)}, bf16[128,2048]{1,0:T(8,128)(2,1)S(1)}, bf16[128,2048]{1,0:T(8,128)(2,1)}) custom-call(bf16[256,2048]{1,0:T(8,128)(2,1)S(1)} %get-tuple-element.34.refs_0_, bf16[128,2048]{1,0:T(8,128)(2,1)S(1)} %get-tuple-element.47.refs_1_, ...), custom_call_target="tpu_custom_call" | custom-call | flops 1000 | bytes 1000 | tf_op jit(solution)/shard_map/pallas_call | solution.py:360
  52.8 1.4 %collective-permute-start.13 = (f16[2,18,32,128]{3,2,1,0:T(8,128)(2,1)S(1)}, f16[2,18,32,128]{3,2,1,0:T(8,128)(2,1)S(1)}, u32[]{:S(2)}, u32[]{:S(2)}) collective-permute-start(f16[2,18,32,128]{3,2,1,0:T(8,128)(2,1)S(1)} %multiply_convert_fusion.2), channel_id=1, source_target_pairs={{0,1},{1,0},{2,3},{3,2},{4,5},{5,4},{6,7},{7,6},{8,9},{9,8},{10,11... | collective-permute-start | bytes 884744 | tf_op jit(solution)/shard_map/ppermute | solution.py:20
  54.2 4.5 %collective-permute-done.15.refs_4_ = bf16[128,2048]{1,0:T(8,128)(2,1)S(1)} collective-permute-done((bf16[128,2048]{1,0:T(8,128)(2,1)S(1)}, bf16[128,2048]{1,0:T(8,128)(2,1)S(1)}, u32[]{:S(2)}, u32[]{:S(2)}) %collective-permute-start.15) | collective-permute-done | bytes 524320 | tf_op jit(solution)/shard_map/ppermute | solution.py:20
  58.7 0.9 collective-permute-done.16.refs_8_
  59.6 1.1 %collective-permute-start.17 = (bf16[128,2048]{1,0:T(8,128)(2,1)S(1)}, bf16[128,2048]{1,0:T(8,128)(2,1)S(1)}, u32[]{:S(2)}, u32[]{:S(2)}) collective-permute-start(bf16[128,2048]{1,0:T(8,128)(2,1)S(1)} %collective-permute-done.15.refs_4_), channel_id=1, source_target_pairs={{0,4},{4,0},{8,12},{12,8},{16,20},{20,16},{24,28},{28,24},{1,5},{5... | collective-permute-start | bytes 1572872 | tf_op jit(solution)/shard_map/ppermute | solution.py:20
  60.8 3.3 %collective-permute-done.13 = f16[2,18,32,128]{3,2,1,0:T(8,128)(2,1)S(1)} collective-permute-done((f16[2,18,32,128]{3,2,1,0:T(8,128)(2,1)S(1)}, f16[2,18,32,128]{3,2,1,0:T(8,128)(2,1)S(1)}, u32[]{:S(2)}, u32[]{:S(2)}) %collective-permute-start.13) | collective-permute-done | bytes 294944 | tf_op jit(solution)/shard_map/ppermute | solution.py:20
  64.1 0.1 convert_add_fusion.2
  64.2 3.4 %shard_map.50 = (f32[2,22,32,128]{3,2,1,0:T(8,128)S(1)}, f32[2,22,32,128]{3,2,1,0:T(8,128)S(1)}, bf16[128,2048]{1,0:T(8,128)(2,1)}, bf16[128,2048]{1,0:T(8,128)(2,1)}, bf16[128,2048]{1,0:T(8,128)(2,1)}) custom-call(bf16[256,2048]{1,0:T(8,128)(2,1)S(1)} %get-tuple-element.34.refs_0_, bf16[128,2048]{1,0:T(8,128)(2,1)S(1)} %get-tuple-element.47.refs_1_, ...), custom_call_target="tpu_custom_call" | custom-call | flops 1000 | bytes 1000 | tf_op jit(solution)/shard_map/pallas_call | solution.py:360
  67.8 1.7 %collective-permute-start.14 = (f16[18,32,128]{2,1,0:T(8,128)(2,1)S(1)}, f16[18,32,128]{2,1,0:T(8,128)(2,1)S(1)}, u32[]{:S(2)}, u32[]{:S(2)}) collective-permute-start(f16[18,32,128]{2,1,0:T(8,128)(2,1)S(1)} %fusion.6), channel_id=1, source_target_pairs={{0,2},{1,3},{2,0},{3,1},{4,6},{5,7},{6,4},{7,5},{8,10},{9,11},{10,... | collective-permute-start | bytes 442376 | tf_op jit(solution)/shard_map/ppermute | solution.py:20
  69.5 8.1 %collective-permute-done.14 = f16[18,32,128]{2,1,0:T(8,128)(2,1)S(1)} collective-permute-done((f16[18,32,128]{2,1,0:T(8,128)(2,1)S(1)}, f16[18,32,128]{2,1,0:T(8,128)(2,1)S(1)}, u32[]{:S(2)}, u32[]{:S(2)}) %collective-permute-start.14) | collective-permute-done | bytes 147488 | tf_op jit(solution)/shard_map/ppermute | solution.py:20
  77.6 2.6 %collective-permute-done.18 = f16[2,22,32,128]{3,2,1,0:T(8,128)(2,1)S(1)} collective-permute-done((f16[2,22,32,128]{3,2,1,0:T(8,128)(2,1)S(1)}, f16[2,22,32,128]{3,2,1,0:T(8,128)(2,1)S(1)}, u32[]{:S(2)}, u32[]{:S(2)}) %collective-permute-start.18) | collective-permute-done | bytes 360480 | tf_op jit(solution)/shard_map/ppermute | solution.py:20
  80.2 0.1 convert_add_fusion.1
  80.4 0.6 collective-permute-start.19
  81.0 2.1 %collective-permute-start.20 = (f16[9,32,128]{2,1,0:T(8,128)(2,1)S(1)}, f16[9,32,128]{2,1,0:T(8,128)(2,1)S(1)}, u32[]{:S(2)}, u32[]{:S(2)}) collective-permute-start(f16[9,32,128]{2,1,0:T(8,128)(2,1)S(1)} %pad_maximum_fusion), channel_id=1, source_target_pairs={{8,24},{12,28},{24,8},{28,12},{9,25},{13,29},{25,9},{29,13},{10,26... | collective-permute-start | bytes 221192 | tf_op jit(solution)/shard_map/ppermute | solution.py:20
  83.2 3.7 %collective-permute-start.21 = (f16[9,32,128]{2,1,0:T(8,128)(2,1)S(1)}, f16[9,32,128]{2,1,0:T(8,128)(2,1)S(1)}, u32[]{:S(2)}, u32[]{:S(2)}) collective-permute-start(f16[9,32,128]{2,1,0:T(8,128)(2,1)S(1)} %pad_maximum_fusion.1), channel_id=1, source_target_pairs={{0,4},{4,0},{8,28},{12,24},{16,20},{20,16},{24,12},{28,8},{1,5},{5... | collective-permute-start | bytes 221192 | tf_op jit(solution)/shard_map/ppermute | solution.py:336
  86.9 3.8 %collective-permute-done.21 = f16[9,32,128]{2,1,0:T(8,128)(2,1)S(1)} collective-permute-done((f16[9,32,128]{2,1,0:T(8,128)(2,1)S(1)}, f16[9,32,128]{2,1,0:T(8,128)(2,1)S(1)}, u32[]{:S(2)}, u32[]{:S(2)}) %collective-permute-start.21) | collective-permute-done | bytes 73760 | tf_op jit(solution)/shard_map/ppermute | solution.py:336
  90.8 1.9 %collective-permute-start.22 = (f16[7,32,128]{2,1,0:T(8,128)(2,1)S(1)}, f16[7,32,128]{2,1,0:T(8,128)(2,1)S(1)}, u32[]{:S(2)}, u32[]{:S(2)}) collective-permute-start(f16[7,32,128]{2,1,0:T(8,128)(2,1)S(1)} %get-tuple-element.74), channel_id=1, source_target_pairs={{8,24},{12,28},{24,8},{28,12},{9,25},{13,29},{25,9},{29,13},{10,26... | collective-permute-start | bytes 172040 | tf_op jit(solution)/shard_map/ppermute | solution.py:20
  92.7 2.1 %collective-permute-start.23 = (f16[7,32,128]{2,1,0:T(8,128)(2,1)S(1)}, f16[7,32,128]{2,1,0:T(8,128)(2,1)S(1)}, u32[]{:S(2)}, u32[]{:S(2)}) collective-permute-start(f16[7,32,128]{2,1,0:T(8,128)(2,1)S(1)} %get-tuple-element.73), channel_id=1, source_target_pairs={{0,4},{4,0},{8,28},{12,24},{16,20},{20,16},{24,12},{28,8},{1,5},{5... | collective-permute-start | bytes 172040 | tf_op jit(solution)/shard_map/ppermute | solution.py:336
  94.9 0.8 collective-permute-done.22
  95.8 2.1 %collective-permute-done.23 = f16[7,32,128]{2,1,0:T(8,128)(2,1)S(1)} collective-permute-done((f16[7,32,128]{2,1,0:T(8,128)(2,1)S(1)}, f16[7,32,128]{2,1,0:T(8,128)(2,1)S(1)}, u32[]{:S(2)}, u32[]{:S(2)}) %collective-permute-start.23) | collective-permute-done | bytes 57376 | tf_op jit(solution)/shard_map/ppermute | solution.py:336
  97.9 1.6 %shard_map.51 = f32[5,512,128]{2,1,0:T(8,128)} custom-call(f32[16,32,128]{2,1,0:T(8,128)S(1)} %fusion.3.own_ref, f32[24,32,128]{2,1,0:T(8,128)S(1)} %get-tuple-element.66.refs_0_, f32[18,32,128]{2,1,0:T(8,128)S(1)} %get-tuple-element.68.refs_1_, f32[22,32,128]{2,1,0:T(8,128)S(1)} %get-tuple-element.64.refs_2_, ...), custom_call_target="tpu_custom_call" | custom-call | flops 1000 | bytes 1000 | tf_op jit(solution)/shard_map/pallas_call | solution.py:374
  (32 shorter events, 1.0 us)
Async XLA Ops:
  3.0 24.1 %collective-permute-start.4 = (bf16[256,2048]{1,0:T(8,128)(2,1)S(1)}, bf16[256,2048]{1,0:T(8,128)(2,1)S(1)}, u32[]{:S(2)}, u32[]{:S(2)}) collective-permute-start(bf16[256,2048]{1,0:T(8,128)(2,1)S(1)} %get-tuple-element.34.refs_0_), channel_id=1, source_target_pairs={{0,16},{4,20},{8,24},{12,28},{16,0},{20,4},{24,8},{28,12},{1,17},{... | collective-permute-start | bytes 3145736 | tf_op jit(solution)/shard_map/ppermute | solution.py:20
  4.3 23.7 %collective-permute-start.5 = (bf16[256,2048]{1,0:T(8,128)(2,1)S(1)}, bf16[256,2048]{1,0:T(8,128)(2,1)S(1)}, u32[]{:S(2)}, u32[]{:S(2)}) collective-permute-start(bf16[256,2048]{1,0:T(8,128)(2,1)S(1)} %get-tuple-element.34.refs_0_), channel_id=1, source_target_pairs={{0,8},{4,12},{8,0},{12,4},{16,24},{20,28},{24,16},{28,20},{1,9},{5... | collective-permute-start | bytes 3145736 | tf_op jit(solution)/shard_map/ppermute | solution.py:20
  7.5 6.6 %collective-permute-start = (f16[2,16,32,128]{3,2,1,0:T(8,128)(2,1)S(1)}, f16[2,16,32,128]{3,2,1,0:T(8,128)(2,1)S(1)}, u32[]{:S(2)}, u32[]{:S(2)}) collective-permute-start(f16[2,16,32,128]{3,2,1,0:T(8,128)(2,1)S(1)} %multiply_convert_fusion.3), channel_id=1, source_target_pairs={{0,1},{1,0},{2,3},{3,2},{4,5},{5,4},{6,7},{7,6},{8,9},{9,8},{10,11... | collective-permute-start | bytes 786440 | tf_op jit(solution)/shard_map/ppermute | solution.py:20
  14.2 15.7 %collective-permute-start.1 = (f16[16,32,128]{2,1,0:T(8,128)(2,1)S(1)}, f16[16,32,128]{2,1,0:T(8,128)(2,1)S(1)}, u32[]{:S(2)}, u32[]{:S(2)}) collective-permute-start(f16[16,32,128]{2,1,0:T(8,128)(2,1)S(1)} %fusion.7), channel_id=1, source_target_pairs={{0,2},{1,3},{2,0},{3,1},{4,6},{5,7},{6,4},{7,5},{8,10},{9,11},{10,... | collective-permute-start | bytes 393224 | tf_op jit(solution)/shard_map/ppermute | solution.py:20
  28.0 5.7 %collective-permute-start.6 = (bf16[256,2048]{1,0:T(8,128)(2,1)S(1)}, bf16[256,2048]{1,0:T(8,128)(2,1)S(1)}, u32[]{:S(2)}, u32[]{:S(2)}) collective-permute-start(bf16[256,2048]{1,0:T(8,128)(2,1)S(1)} %collective-permute-done.4.refs_5_), channel_id=1, source_target_pairs={{0,4},{4,0},{8,12},{12,8},{16,20},{20,16},{24,28},{28,24},{1,5},{5... | collective-permute-start | bytes 3145736 | tf_op jit(solution)/shard_map/ppermute | solution.py:20
  30.0 2.9 %collective-permute-start.2 = (bf16[128,2048]{1,0:T(8,128)(2,1)S(1)}, bf16[128,2048]{1,0:T(8,128)(2,1)S(1)}, u32[]{:S(2)}, u32[]{:S(2)}) collective-permute-start(bf16[128,2048]{1,0:T(8,128)(2,1)S(1)} %get-tuple-element.39), channel_id=1, source_target_pairs={{0,4},{4,0},{8,12},{12,8},{16,20},{20,16},{24,28},{28,24},{1,5},{5... | collective-permute-start | bytes 1572872 | tf_op jit(solution)/shard_map/ppermute | solution.py:20
  30.1 3.5 %collective-permute-start.3 = (bf16[128,2048]{1,0:T(8,128)(2,1)S(1)}, bf16[128,2048]{1,0:T(8,128)(2,1)S(1)}, u32[]{:S(2)}, u32[]{:S(2)}) collective-permute-start(bf16[128,2048]{1,0:T(8,128)(2,1)S(1)} %get-tuple-element.40), channel_id=1, source_target_pairs={{0,4},{4,0},{8,12},{12,8},{16,20},{20,16},{24,28},{28,24},{1,5},{5... | collective-permute-start | bytes 1572872 | tf_op jit(solution)/shard_map/ppermute | solution.py:20
  30.6 13.5 %collective-permute-start.10 = (bf16[128,2048]{1,0:T(8,128)(2,1)S(1)}, bf16[128,2048]{1,0:T(8,128)(2,1)S(1)}, u32[]{:S(2)}, u32[]{:S(2)}) collective-permute-start(bf16[128,2048]{1,0:T(8,128)(2,1)S(1)} %get-tuple-element.47.refs_1_), channel_id=1, source_target_pairs={{0,16},{4,20},{8,24},{12,28},{16,0},{20,4},{24,8},{28,12},{1,17},{... | collective-permute-start | bytes 1572872 | tf_op jit(solution)/shard_map/ppermute | solution.py:20
  30.8 13.3 %collective-permute-start.11 = (bf16[128,2048]{1,0:T(8,128)(2,1)S(1)}, bf16[128,2048]{1,0:T(8,128)(2,1)S(1)}, u32[]{:S(2)}, u32[]{:S(2)}) collective-permute-start(bf16[128,2048]{1,0:T(8,128)(2,1)S(1)} %get-tuple-element.47.refs_1_), channel_id=1, source_target_pairs={{0,8},{4,12},{8,0},{12,4},{16,24},{20,28},{24,16},{28,20},{1,9},{5... | collective-permute-start | bytes 1572872 | tf_op jit(solution)/shard_map/ppermute | solution.py:20
  36.4 13.7 %collective-permute-start.9 = (bf16[256,2048]{1,0:T(8,128)(2,1)S(1)}, bf16[256,2048]{1,0:T(8,128)(2,1)S(1)}, u32[]{:S(2)}, u32[]{:S(2)}) collective-permute-start(bf16[256,2048]{1,0:T(8,128)(2,1)S(1)} %get-tuple-element.46), channel_id=1, source_target_pairs={{0,4},{4,0},{8,12},{12,8},{16,20},{20,16},{24,28},{28,24},{1,5},{5... | collective-permute-start | bytes 3145736 | tf_op jit(solution)/shard_map/ppermute | solution.py:20
  36.9 10.6 %collective-permute-start.7 = (f16[2,24,32,128]{3,2,1,0:T(8,128)(2,1)S(1)}, f16[2,24,32,128]{3,2,1,0:T(8,128)(2,1)S(1)}, u32[]{:S(2)}, u32[]{:S(2)}) collective-permute-start(f16[2,24,32,128]{3,2,1,0:T(8,128)(2,1)S(1)} %multiply_convert_fusion), channel_id=1, source_target_pairs={{0,1},{1,0},{2,3},{3,2},{4,5},{5,4},{6,7},{7,6},{8,9},{9,8},{10,11... | collective-permute-start | bytes 1179656 | tf_op jit(solution)/shard_map/ppermute | solution.py:20
  44.1 6.0 %collective-permute-start.12 = (bf16[128,2048]{1,0:T(8,128)(2,1)S(1)}, bf16[128,2048]{1,0:T(8,128)(2,1)S(1)}, u32[]{:S(2)}, u32[]{:S(2)}) collective-permute-start(bf16[128,2048]{1,0:T(8,128)(2,1)S(1)} %collective-permute-done.10.refs_4_), channel_id=1, source_target_pairs={{0,4},{4,0},{8,12},{12,8},{16,20},{20,16},{24,28},{28,24},{1,5},{5... | collective-permute-start | bytes 1572872 | tf_op jit(solution)/shard_map/ppermute | solution.py:20
  45.2 13.6 %collective-permute-start.15 = (bf16[128,2048]{1,0:T(8,128)(2,1)S(1)}, bf16[128,2048]{1,0:T(8,128)(2,1)S(1)}, u32[]{:S(2)}, u32[]{:S(2)}) collective-permute-start(bf16[128,2048]{1,0:T(8,128)(2,1)S(1)} %get-tuple-element.55.refs_2_), channel_id=1, source_target_pairs={{0,16},{4,20},{8,24},{12,28},{16,0},{20,4},{24,8},{28,12},{1,17},{... | collective-permute-start | bytes 1572872 | tf_op jit(solution)/shard_map/ppermute | solution.py:20
  46.4 13.2 %collective-permute-start.16 = (bf16[128,2048]{1,0:T(8,128)(2,1)S(1)}, bf16[128,2048]{1,0:T(8,128)(2,1)S(1)}, u32[]{:S(2)}, u32[]{:S(2)}) collective-permute-start(bf16[128,2048]{1,0:T(8,128)(2,1)S(1)} %get-tuple-element.55.refs_2_), channel_id=1, source_target_pairs={{0,8},{4,12},{8,0},{12,4},{16,24},{20,28},{24,16},{28,20},{1,9},{5... | collective-permute-start | bytes 1572872 | tf_op jit(solution)/shard_map/ppermute | solution.py:20
  47.7 13.0 %collective-permute-start.8 = (f16[24,32,128]{2,1,0:T(8,128)(2,1)S(1)}, f16[24,32,128]{2,1,0:T(8,128)(2,1)S(1)}, u32[]{:S(2)}, u32[]{:S(2)}) collective-permute-start(f16[24,32,128]{2,1,0:T(8,128)(2,1)S(1)} %fusion.4), channel_id=1, source_target_pairs={{0,2},{1,3},{2,0},{3,1},{4,6},{5,7},{6,4},{7,5},{8,10},{9,11},{10,... | collective-permute-start | bytes 589832 | tf_op jit(solution)/shard_map/ppermute | solution.py:20
  52.8 11.3 %collective-permute-start.13 = (f16[2,18,32,128]{3,2,1,0:T(8,128)(2,1)S(1)}, f16[2,18,32,128]{3,2,1,0:T(8,128)(2,1)S(1)}, u32[]{:S(2)}, u32[]{:S(2)}) collective-permute-start(f16[2,18,32,128]{3,2,1,0:T(8,128)(2,1)S(1)} %multiply_convert_fusion.2), channel_id=1, source_target_pairs={{0,1},{1,0},{2,3},{3,2},{4,5},{5,4},{6,7},{7,6},{8,9},{9,8},{10,11... | collective-permute-start | bytes 884744 | tf_op jit(solution)/shard_map/ppermute | solution.py:20
  59.6 4.6 %collective-permute-start.17 = (bf16[128,2048]{1,0:T(8,128)(2,1)S(1)}, bf16[128,2048]{1,0:T(8,128)(2,1)S(1)}, u32[]{:S(2)}, u32[]{:S(2)}) collective-permute-start(bf16[128,2048]{1,0:T(8,128)(2,1)S(1)} %collective-permute-done.15.refs_4_), channel_id=1, source_target_pairs={{0,4},{4,0},{8,12},{12,8},{16,20},{20,16},{24,28},{28,24},{1,5},{5... | collective-permute-start | bytes 1572872 | tf_op jit(solution)/shard_map/ppermute | solution.py:20
  67.7 12.5 %collective-permute-start.18 = (f16[2,22,32,128]{3,2,1,0:T(8,128)(2,1)S(1)}, f16[2,22,32,128]{3,2,1,0:T(8,128)(2,1)S(1)}, u32[]{:S(2)}, u32[]{:S(2)}) collective-permute-start(f16[2,22,32,128]{3,2,1,0:T(8,128)(2,1)S(1)} %multiply_convert_fusion.1), channel_id=1, source_target_pairs={{0,1},{1,0},{2,3},{3,2},{4,5},{5,4},{6,7},{7,6},{8,9},{9,8},{10,11... | collective-permute-start | bytes 1081352 | tf_op jit(solution)/shard_map/ppermute | solution.py:20
  67.8 9.8 %collective-permute-start.14 = (f16[18,32,128]{2,1,0:T(8,128)(2,1)S(1)}, f16[18,32,128]{2,1,0:T(8,128)(2,1)S(1)}, u32[]{:S(2)}, u32[]{:S(2)}) collective-permute-start(f16[18,32,128]{2,1,0:T(8,128)(2,1)S(1)} %fusion.6), channel_id=1, source_target_pairs={{0,2},{1,3},{2,0},{3,1},{4,6},{5,7},{6,4},{7,5},{8,10},{9,11},{10,... | collective-permute-start | bytes 442376 | tf_op jit(solution)/shard_map/ppermute | solution.py:20
  80.4 10.3 %collective-permute-start.19 = (f16[22,32,128]{2,1,0:T(8,128)(2,1)S(1)}, f16[22,32,128]{2,1,0:T(8,128)(2,1)S(1)}, u32[]{:S(2)}, u32[]{:S(2)}) collective-permute-start(f16[22,32,128]{2,1,0:T(8,128)(2,1)S(1)} %fusion.5), channel_id=1, source_target_pairs={{0,2},{1,3},{2,0},{3,1},{4,6},{5,7},{6,4},{7,5},{8,10},{9,11},{10,... | collective-permute-start | bytes 540680 | tf_op jit(solution)/shard_map/ppermute | solution.py:20
  81.0 5.9 %collective-permute-start.20 = (f16[9,32,128]{2,1,0:T(8,128)(2,1)S(1)}, f16[9,32,128]{2,1,0:T(8,128)(2,1)S(1)}, u32[]{:S(2)}, u32[]{:S(2)}) collective-permute-start(f16[9,32,128]{2,1,0:T(8,128)(2,1)S(1)} %pad_maximum_fusion), channel_id=1, source_target_pairs={{8,24},{12,28},{24,8},{28,12},{9,25},{13,29},{25,9},{29,13},{10,26... | collective-permute-start | bytes 221192 | tf_op jit(solution)/shard_map/ppermute | solution.py:20
  83.2 7.5 %collective-permute-start.21 = (f16[9,32,128]{2,1,0:T(8,128)(2,1)S(1)}, f16[9,32,128]{2,1,0:T(8,128)(2,1)S(1)}, u32[]{:S(2)}, u32[]{:S(2)}) collective-permute-start(f16[9,32,128]{2,1,0:T(8,128)(2,1)S(1)} %pad_maximum_fusion.1), channel_id=1, source_target_pairs={{0,4},{4,0},{8,28},{12,24},{16,20},{20,16},{24,12},{28,8},{1,5},{5... | collective-permute-start | bytes 221192 | tf_op jit(solution)/shard_map/ppermute | solution.py:336
  90.8 4.9 %collective-permute-start.22 = (f16[7,32,128]{2,1,0:T(8,128)(2,1)S(1)}, f16[7,32,128]{2,1,0:T(8,128)(2,1)S(1)}, u32[]{:S(2)}, u32[]{:S(2)}) collective-permute-start(f16[7,32,128]{2,1,0:T(8,128)(2,1)S(1)} %get-tuple-element.74), channel_id=1, source_target_pairs={{8,24},{12,28},{24,8},{28,12},{9,25},{13,29},{25,9},{29,13},{10,26... | collective-permute-start | bytes 172040 | tf_op jit(solution)/shard_map/ppermute | solution.py:20
  92.7 5.1 %collective-permute-start.23 = (f16[7,32,128]{2,1,0:T(8,128)(2,1)S(1)}, f16[7,32,128]{2,1,0:T(8,128)(2,1)S(1)}, u32[]{:S(2)}, u32[]{:S(2)}) collective-permute-start(f16[7,32,128]{2,1,0:T(8,128)(2,1)S(1)} %get-tuple-element.73), channel_id=1, source_target_pairs={{0,4},{4,0},{8,28},{12,24},{16,20},{20,16},{24,12},{28,8},{1,5},{5... | collective-permute-start | bytes 172040 | tf_op jit(solution)/shard_map/ppermute | solution.py:336

commit v10 on v9

--- a/solution.py
+++ b/solution.py
@@ -339,7 +339,8 @@
     stay, away = on_units(own_kernel, message(UNITS * UNITS), len(sent))(*sent)
     own_came = exchanged(away)
     own = summed(half_summed(stay, own_came))
-    sibling = [swapped(behind(sent[0][i * length : (i + 1) * length], own), "tm", 1) for i in range(len(STAGES[0]))]
+    sibling = [swapped(sent[0][:length], "tm", 1)]
+    sibling.append(swapped(behind(sent[0][length:], own), "tm", 1))
     x_units, by_y, left, cross, halves, totals, came = [], [], [], [], [], [], None
     for stage, fresh in enumerate(STAGES):
         block = sent[stage]

time: 99.7 us -> 99.7 us (level)
  no operation moved by 1% of the time
where the time goes in v10:
time: 99.7 us; the launch traced here: 99.5 us
  waiting for transfers between devices  52 us (52%)
  starting transfers between devices  29.6 us (30%)
  Pallas kernels  15.7 us (16%)
  other arithmetic  1.14 us (1%)
    ppermute x22, waiting for transfers between devices, swapped(): return lax.ppermute(x, axis, pairs)  46.1 us
    ppermute x22, starting transfers between devices, swapped(): return lax.ppermute(x, axis, pairs)  23.7 us
    pallas_call x3, Pallas kernels, square(): on_units(functools.partial(stage_kernel, stage), out_shape, len(operands))  8.87 us
    ppermute x2, waiting for transfers between devices, handed_over(): lax.ppermute(cross, 'tm', pairs)  5.91 us
    ppermute x2, starting transfers between devices, handed_over(): lax.ppermute(cross, 'tm', pairs)  5.84 us
    pallas_call x1, Pallas kernels, square(): stay, away = on_units(own_kernel, message(UNITS * UNITS), len(sent))(*sent)  2.89 us
    pallas_call x1, Pallas kernels, clean_units(): pl.pallas_call(clean_kernel, out_shape=out_shape, in_specs=[hbm, pl.Block...  2.31 us
  transfers between devices with their start and end apart: 24, of which 15 were waited for; matrix products, arithmetic and copies ran while one was open for 1% of the time, Pallas kernels for 8%

profile of v10, /device:TPU:3, one launch (start us, length us, event | category | flops | bytes accessed | tf_op | source)
XLA Modules:
  0.0 99.5 jit_solution(5918260484517161348)
XLA Ops:
  0.7 2.3 %shard_map.46 = (bf16[256,2048]{1,0:T(8,128)(2,1)S(1)}, bf16[256,2048]{1,0:T(8,128)(2,1)S(1)}, bf16[128,2048]{1,0:T(8,128)(2,1)S(1)}, bf16[128,2048]{1,0:T(8,128)(2,1)S(1)}) custom-call(s32[4,4]{1,0:T(4,128)} %cols_hbm.1, f32[1]{0:T(128)} %bitcast.29.threshold_ref, bf16[512,2048]{1,0:T(8,128)(2,1)} %snapshots_hbm.1, bf16[4,4,128,128]{3,2,1,0:T(8,128)(2,1)} %values_hbm.1), custom_call_target="tpu_custom_call" | custom-call | tf_op jit(solution)/shard_map/pallas_call | solution.py:124
  3.0 1.3 %collective-permute-start.4 = (bf16[256,2048]{1,0:T(8,128)(2,1)S(1)}, bf16[256,2048]{1,0:T(8,128)(2,1)S(1)}, u32[]{:S(2)}, u32[]{:S(2)}) collective-permute-start(bf16[256,2048]{1,0:T(8,128)(2,1)S(1)} %get-tuple-element.33.refs_0_), channel_id=1, source_target_pairs={{0,16},{4,20},{8,24},{12,28},{16,0},{20,4},{24,8},{28,12},{1,17},{... | collective-permute-start | bytes 3145736 | tf_op jit(solution)/shard_map/ppermute | solution.py:20
  4.3 0.3 collective-permute-start.5
  4.5 2.9 %shard_map.47 = (f32[2,16,32,128]{3,2,1,0:T(8,128)S(1)}, f32[2,16,32,128]{3,2,1,0:T(8,128)S(1)}) custom-call(bf16[256,2048]{1,0:T(8,128)(2,1)S(1)} %get-tuple-element.33.refs_0_, bf16[128,2048]{1,0:T(8,128)(2,1)S(1)} %get-tuple-element.45.refs_1_, bf16[128,2048]{1,0:T(8,128)(2,1)S(1)} %get-tuple-element.53.refs_2_), custom_call_target="tpu_custom_call" | custom-call | flops 1000 | bytes 1000 | tf_op jit(solution)/shard_map/pallas_call | solution.py:339
  7.5 1.4 %collective-permute-start = (f16[2,16,32,128]{3,2,1,0:T(8,128)(2,1)S(1)}, f16[2,16,32,128]{3,2,1,0:T(8,128)(2,1)S(1)}, u32[]{:S(2)}, u32[]{:S(2)}) collective-permute-start(f16[2,16,32,128]{3,2,1,0:T(8,128)(2,1)S(1)} %multiply_convert_fusion.3), channel_id=1, source_target_pairs={{0,1},{1,0},{2,3},{3,2},{4,5},{5,4},{6,7},{7,6},{8,9},{9,8},{10,11... | collective-permute-start | bytes 786440 | tf_op jit(solution)/shard_map/ppermute | solution.py:20
  8.9 5.3 %collective-permute-done = f16[2,16,32,128]{3,2,1,0:T(8,128)(2,1)S(1)} collective-permute-done((f16[2,16,32,128]{3,2,1,0:T(8,128)(2,1)S(1)}, f16[2,16,32,128]{3,2,1,0:T(8,128)(2,1)S(1)}, u32[]{:S(2)}, u32[]{:S(2)}) %collective-permute-start) | collective-permute-done | bytes 262176 | tf_op jit(solution)/shard_map/ppermute | solution.py:20
  14.2 2.4 %collective-permute-start.1 = (f16[16,32,128]{2,1,0:T(8,128)(2,1)S(1)}, f16[16,32,128]{2,1,0:T(8,128)(2,1)S(1)}, u32[]{:S(2)}, u32[]{:S(2)}) collective-permute-start(f16[16,32,128]{2,1,0:T(8,128)(2,1)S(1)} %fusion.7), channel_id=1, source_target_pairs={{0,2},{1,3},{2,0},{3,1},{4,6},{5,7},{6,4},{7,5},{8,10},{9,11},{10,... | collective-permute-start | bytes 393224 | tf_op jit(solution)/shard_map/ppermute | solution.py:20
  16.6 10.4 %collective-permute-done.4.refs_5_ = bf16[256,2048]{1,0:T(8,128)(2,1)S(1)} collective-permute-done((bf16[256,2048]{1,0:T(8,128)(2,1)S(1)}, bf16[256,2048]{1,0:T(8,128)(2,1)S(1)}, u32[]{:S(2)}, u32[]{:S(2)}) %collective-permute-start.4) | collective-permute-done | bytes 1048608 | tf_op jit(solution)/shard_map/ppermute | solution.py:20
  27.1 0.9 collective-permute-done.5.refs_7_.refs_6_
  28.0 1.9 %collective-permute-start.6 = (bf16[256,2048]{1,0:T(8,128)(2,1)S(1)}, bf16[256,2048]{1,0:T(8,128)(2,1)S(1)}, u32[]{:S(2)}, u32[]{:S(2)}) collective-permute-start(bf16[256,2048]{1,0:T(8,128)(2,1)S(1)} %collective-permute-done.4.refs_5_), channel_id=1, source_target_pairs={{0,4},{4,0},{8,12},{12,8},{16,20},{20,16},{24,28},{28,24},{1,5},{5... | collective-permute-start | bytes 3145736 | tf_op jit(solution)/shard_map/ppermute | solution.py:20
  29.8 0.1 fusion.14
  30.1 0.6 collective-permute-start.3
  30.6 0.2 collective-permute-start.10
  30.9 0.1 collective-permute-start.11
  31.0 1.9 %collective-permute-done.2.refs_3_ = bf16[128,2048]{1,0:T(8,128)(2,1)S(1)} collective-permute-done((bf16[128,2048]{1,0:T(8,128)(2,1)S(1)}, bf16[128,2048]{1,0:T(8,128)(2,1)S(1)}, u32[]{:S(2)}, u32[]{:S(2)}) %collective-permute-start.2) | collective-permute-done | bytes 524320 | tf_op jit(solution)/shard_map/ppermute | solution.py:20
  32.9 0.7 collective-permute-done.3.refs_4_
  33.6 2.8 %shard_map.48 = (f32[2,24,32,128]{3,2,1,0:T(8,128)S(1)}, f32[2,24,32,128]{3,2,1,0:T(8,128)S(1)}, bf16[256,2048]{1,0:T(8,128)(2,1)S(1)}, bf16[256,2048]{1,0:T(8,128)(2,1)S(1)}, bf16[256,2048]{1,0:T(8,128)(2,1)}) custom-call(bf16[256,2048]{1,0:T(8,128)(2,1)S(1)} %get-tuple-element.33.refs_0_, bf16[128,2048]{1,0:T(8,128)(2,1)S(1)} %get-tuple-element.45.refs_1_, ...), custom_call_target="tpu_custom_call" | custom-call | flops 1000 | bytes 1000 | tf_op jit(solution)/shard_map/pallas_call | solution.py:361
  36.4 0.4 collective-permute-start.9
  36.8 0.1 multiply_convert_fusion
  36.9 1.4 %collective-permute-start.7 = (f16[2,24,32,128]{3,2,1,0:T(8,128)(2,1)S(1)}, f16[2,24,32,128]{3,2,1,0:T(8,128)(2,1)S(1)}, u32[]{:S(2)}, u32[]{:S(2)}) collective-permute-start(f16[2,24,32,128]{3,2,1,0:T(8,128)(2,1)S(1)} %multiply_convert_fusion), channel_id=1, source_target_pairs={{0,1},{1,0},{2,3},{3,2},{4,5},{5,4},{6,7},{7,6},{8,9},{9,8},{10,11... | collective-permute-start | bytes 1179656 | tf_op jit(solution)/shard_map/ppermute | solution.py:20
  38.2 5.9 %collective-permute-done.10.refs_4_ = bf16[128,2048]{1,0:T(8,128)(2,1)S(1)} collective-permute-done((bf16[128,2048]{1,0:T(8,128)(2,1)S(1)}, bf16[128,2048]{1,0:T(8,128)(2,1)S(1)}, u32[]{:S(2)}, u32[]{:S(2)}) %collective-permute-start.10) | collective-permute-done | bytes 524320 | tf_op jit(solution)/shard_map/ppermute | solution.py:20
  44.1 1.1 %collective-permute-start.12 = (bf16[128,2048]{1,0:T(8,128)(2,1)S(1)}, bf16[128,2048]{1,0:T(8,128)(2,1)S(1)}, u32[]{:S(2)}, u32[]{:S(2)}) collective-permute-start(bf16[128,2048]{1,0:T(8,128)(2,1)S(1)} %collective-permute-done.10.refs_4_), channel_id=1, source_target_pairs={{0,4},{4,0},{8,12},{12,8},{16,20},{20,16},{24,28},{28,24},{1,5},{5... | collective-permute-start | bytes 1572872 | tf_op jit(solution)/shard_map/ppermute | solution.py:20
  45.2 1.2 %collective-permute-start.15 = (bf16[128,2048]{1,0:T(8,128)(2,1)S(1)}, bf16[128,2048]{1,0:T(8,128)(2,1)S(1)}, u32[]{:S(2)}, u32[]{:S(2)}) collective-permute-start(bf16[128,2048]{1,0:T(8,128)(2,1)S(1)} %get-tuple-element.53.refs_2_), channel_id=1, source_target_pairs={{0,16},{4,20},{8,24},{12,28},{16,0},{20,4},{24,8},{28,12},{1,17},{... | collective-permute-start | bytes 1572872 | tf_op jit(solution)/shard_map/ppermute | solution.py:20
  46.5 0.3 collective-permute-start.16
  46.7 0.8 collective-permute-done.7
  47.5 0.1 convert_add_fusion
  47.7 2.4 %collective-permute-start.8 = (f16[24,32,128]{2,1,0:T(8,128)(2,1)S(1)}, f16[24,32,128]{2,1,0:T(8,128)(2,1)S(1)}, u32[]{:S(2)}, u32[]{:S(2)}) collective-permute-start(f16[24,32,128]{2,1,0:T(8,128)(2,1)S(1)} %fusion.4), channel_id=1, source_target_pairs={{0,2},{1,3},{2,0},{3,1},{4,6},{5,7},{6,4},{7,5},{8,10},{9,11},{10,... | collective-permute-start | bytes 589832 | tf_op jit(solution)/shard_map/ppermute | solution.py:20
  50.1 2.7 %shard_map.49 = (f32[2,18,32,128]{3,2,1,0:T(8,128)S(1)}, f32[2,18,32,128]{3,2,1,0:T(8,128)S(1)}, bf16[128,2048]{1,0:T(8,128)(2,1)S(1)}, bf16[128,2048]{1,0:T(8,128)(2,1)S(1)}, bf16[128,2048]{1,0:T(8,128)(2,1)}) custom-call(bf16[256,2048]{1,0:T(8,128)(2,1)S(1)} %get-tuple-element.33.refs_0_, bf16[128,2048]{1,0:T(8,128)(2,1)S(1)} %get-tuple-element.45.refs_1_, ...), custom_call_target="tpu_custom_call" | custom-call | flops 1000 | bytes 1000 | tf_op jit(solution)/shard_map/pallas_call | solution.py:361
  52.8 1.4 %collective-permute-start.13 = (f16[2,18,32,128]{3,2,1,0:T(8,128)(2,1)S(1)}, f16[2,18,32,128]{3,2,1,0:T(8,128)(2,1)S(1)}, u32[]{:S(2)}, u32[]{:S(2)}) collective-permute-start(f16[2,18,32,128]{3,2,1,0:T(8,128)(2,1)S(1)} %multiply_convert_fusion.2), channel_id=1, source_target_pairs={{0,1},{1,0},{2,3},{3,2},{4,5},{5,4},{6,7},{7,6},{8,9},{9,8},{10,11... | collective-permute-start | bytes 884744 | tf_op jit(solution)/shard_map/ppermute | solution.py:20
  54.2 4.6 %collective-permute-done.15.refs_4_ = bf16[128,2048]{1,0:T(8,128)(2,1)S(1)} collective-permute-done((bf16[128,2048]{1,0:T(8,128)(2,1)S(1)}, bf16[128,2048]{1,0:T(8,128)(2,1)S(1)}, u32[]{:S(2)}, u32[]{:S(2)}) %collective-permute-start.15) | collective-permute-done | bytes 524320 | tf_op jit(solution)/shard_map/ppermute | solution.py:20
  58.8 0.9 collective-permute-done.16.refs_8_
  59.7 1.1 %collective-permute-start.17 = (bf16[128,2048]{1,0:T(8,128)(2,1)S(1)}, bf16[128,2048]{1,0:T(8,128)(2,1)S(1)}, u32[]{:S(2)}, u32[]{:S(2)}) collective-permute-start(bf16[128,2048]{1,0:T(8,128)(2,1)S(1)} %collective-permute-done.15.refs_4_), channel_id=1, source_target_pairs={{0,4},{4,0},{8,12},{12,8},{16,20},{20,16},{24,28},{28,24},{1,5},{5... | collective-permute-start | bytes 1572872 | tf_op jit(solution)/shard_map/ppermute | solution.py:20
  60.9 3.2 %collective-permute-done.13 = f16[2,18,32,128]{3,2,1,0:T(8,128)(2,1)S(1)} collective-permute-done((f16[2,18,32,128]{3,2,1,0:T(8,128)(2,1)S(1)}, f16[2,18,32,128]{3,2,1,0:T(8,128)(2,1)S(1)}, u32[]{:S(2)}, u32[]{:S(2)}) %collective-permute-start.13) | collective-permute-done | bytes 294944 | tf_op jit(solution)/shard_map/ppermute | solution.py:20
  64.1 0.1 convert_add_fusion.2
  64.2 3.4 %shard_map.50 = (f32[2,22,32,128]{3,2,1,0:T(8,128)S(1)}, f32[2,22,32,128]{3,2,1,0:T(8,128)S(1)}, bf16[128,2048]{1,0:T(8,128)(2,1)}, bf16[128,2048]{1,0:T(8,128)(2,1)}, bf16[128,2048]{1,0:T(8,128)(2,1)}) custom-call(bf16[256,2048]{1,0:T(8,128)(2,1)S(1)} %get-tuple-element.33.refs_0_, bf16[128,2048]{1,0:T(8,128)(2,1)S(1)} %get-tuple-element.45.refs_1_, ...), custom_call_target="tpu_custom_call" | custom-call | flops 1000 | bytes 1000 | tf_op jit(solution)/shard_map/pallas_call | solution.py:361
  67.8 1.7 %collective-permute-start.14 = (f16[18,32,128]{2,1,0:T(8,128)(2,1)S(1)}, f16[18,32,128]{2,1,0:T(8,128)(2,1)S(1)}, u32[]{:S(2)}, u32[]{:S(2)}) collective-permute-start(f16[18,32,128]{2,1,0:T(8,128)(2,1)S(1)} %fusion.6), channel_id=1, source_target_pairs={{0,2},{1,3},{2,0},{3,1},{4,6},{5,7},{6,4},{7,5},{8,10},{9,11},{10,... | collective-permute-start | bytes 442376 | tf_op jit(solution)/shard_map/ppermute | solution.py:20
  69.6 8.0 %collective-permute-done.14 = f16[18,32,128]{2,1,0:T(8,128)(2,1)S(1)} collective-permute-done((f16[18,32,128]{2,1,0:T(8,128)(2,1)S(1)}, f16[18,32,128]{2,1,0:T(8,128)(2,1)S(1)}, u32[]{:S(2)}, u32[]{:S(2)}) %collective-permute-start.14) | collective-permute-done | bytes 147488 | tf_op jit(solution)/shard_map/ppermute | solution.py:20
  77.6 2.6 %collective-permute-done.18 = f16[2,22,32,128]{3,2,1,0:T(8,128)(2,1)S(1)} collective-permute-done((f16[2,22,32,128]{3,2,1,0:T(8,128)(2,1)S(1)}, f16[2,22,32,128]{3,2,1,0:T(8,128)(2,1)S(1)}, u32[]{:S(2)}, u32[]{:S(2)}) %collective-permute-start.18) | collective-permute-done | bytes 360480 | tf_op jit(solution)/shard_map/ppermute | solution.py:20
  80.2 0.1 convert_add_fusion.1
  80.4 0.6 collective-permute-start.19
  81.0 2.1 %collective-permute-start.20 = (f16[9,32,128]{2,1,0:T(8,128)(2,1)S(1)}, f16[9,32,128]{2,1,0:T(8,128)(2,1)S(1)}, u32[]{:S(2)}, u32[]{:S(2)}) collective-permute-start(f16[9,32,128]{2,1,0:T(8,128)(2,1)S(1)} %pad_maximum_fusion), channel_id=1, source_target_pairs={{8,24},{12,28},{24,8},{28,12},{9,25},{13,29},{25,9},{29,13},{10,26... | collective-permute-start | bytes 221192 | tf_op jit(solution)/shard_map/ppermute | solution.py:20
  83.2 3.7 %collective-permute-start.21 = (f16[9,32,128]{2,1,0:T(8,128)(2,1)S(1)}, f16[9,32,128]{2,1,0:T(8,128)(2,1)S(1)}, u32[]{:S(2)}, u32[]{:S(2)}) collective-permute-start(f16[9,32,128]{2,1,0:T(8,128)(2,1)S(1)} %pad_maximum_fusion.1), channel_id=1, source_target_pairs={{0,4},{4,0},{8,28},{12,24},{16,20},{20,16},{24,12},{28,8},{1,5},{5... | collective-permute-start | bytes 221192 | tf_op jit(solution)/shard_map/ppermute | solution.py:336
  86.9 3.8 %collective-permute-done.21 = f16[9,32,128]{2,1,0:T(8,128)(2,1)S(1)} collective-permute-done((f16[9,32,128]{2,1,0:T(8,128)(2,1)S(1)}, f16[9,32,128]{2,1,0:T(8,128)(2,1)S(1)}, u32[]{:S(2)}, u32[]{:S(2)}) %collective-permute-start.21) | collective-permute-done | bytes 73760 | tf_op jit(solution)/shard_map/ppermute | solution.py:336
  90.8 1.9 %collective-permute-start.22 = (f16[7,32,128]{2,1,0:T(8,128)(2,1)S(1)}, f16[7,32,128]{2,1,0:T(8,128)(2,1)S(1)}, u32[]{:S(2)}, u32[]{:S(2)}) collective-permute-start(f16[7,32,128]{2,1,0:T(8,128)(2,1)S(1)} %get-tuple-element.72), channel_id=1, source_target_pairs={{8,24},{12,28},{24,8},{28,12},{9,25},{13,29},{25,9},{29,13},{10,26... | collective-permute-start | bytes 172040 | tf_op jit(solution)/shard_map/ppermute | solution.py:20
  92.8 2.1 %collective-permute-start.23 = (f16[7,32,128]{2,1,0:T(8,128)(2,1)S(1)}, f16[7,32,128]{2,1,0:T(8,128)(2,1)S(1)}, u32[]{:S(2)}, u32[]{:S(2)}) collective-permute-start(f16[7,32,128]{2,1,0:T(8,128)(2,1)S(1)} %get-tuple-element.71), channel_id=1, source_target_pairs={{0,4},{4,0},{8,28},{12,24},{16,20},{20,16},{24,12},{28,8},{1,5},{5... | collective-permute-start | bytes 172040 | tf_op jit(solution)/shard_map/ppermute | solution.py:336
  94.9 0.8 collective-permute-done.22
  95.8 2.1 %collective-permute-done.23 = f16[7,32,128]{2,1,0:T(8,128)(2,1)S(1)} collective-permute-done((f16[7,32,128]{2,1,0:T(8,128)(2,1)S(1)}, f16[7,32,128]{2,1,0:T(8,128)(2,1)S(1)}, u32[]{:S(2)}, u32[]{:S(2)}) %collective-permute-start.23) | collective-permute-done | bytes 57376 | tf_op jit(solution)/shard_map/ppermute | solution.py:336
  97.9 1.6 %shard_map.51 = f32[5,512,128]{2,1,0:T(8,128)} custom-call(f32[16,32,128]{2,1,0:T(8,128)S(1)} %fusion.3.own_ref, f32[24,32,128]{2,1,0:T(8,128)S(1)} %get-tuple-element.64.refs_0_, f32[18,32,128]{2,1,0:T(8,128)S(1)} %get-tuple-element.66.refs_1_, f32[22,32,128]{2,1,0:T(8,128)S(1)} %get-tuple-element.62.refs_2_, ...), custom_call_target="tpu_custom_call" | custom-call | flops 1000 | bytes 1000 | tf_op jit(solution)/shard_map/pallas_call | solution.py:375
  (32 shorter events, 1.0 us)
Async XLA Ops:
  3.0 24.1 %collective-permute-start.4 = (bf16[256,2048]{1,0:T(8,128)(2,1)S(1)}, bf16[256,2048]{1,0:T(8,128)(2,1)S(1)}, u32[]{:S(2)}, u32[]{:S(2)}) collective-permute-start(bf16[256,2048]{1,0:T(8,128)(2,1)S(1)} %get-tuple-element.33.refs_0_), channel_id=1, source_target_pairs={{0,16},{4,20},{8,24},{12,28},{16,0},{20,4},{24,8},{28,12},{1,17},{... | collective-permute-start | bytes 3145736 | tf_op jit(solution)/shard_map/ppermute | solution.py:20
  4.3 23.7 %collective-permute-start.5 = (bf16[256,2048]{1,0:T(8,128)(2,1)S(1)}, bf16[256,2048]{1,0:T(8,128)(2,1)S(1)}, u32[]{:S(2)}, u32[]{:S(2)}) collective-permute-start(bf16[256,2048]{1,0:T(8,128)(2,1)S(1)} %get-tuple-element.33.refs_0_), channel_id=1, source_target_pairs={{0,8},{4,12},{8,0},{12,4},{16,24},{20,28},{24,16},{28,20},{1,9},{5... | collective-permute-start | bytes 3145736 | tf_op jit(solution)/shard_map/ppermute | solution.py:20
  7.5 6.6 %collective-permute-start = (f16[2,16,32,128]{3,2,1,0:T(8,128)(2,1)S(1)}, f16[2,16,32,128]{3,2,1,0:T(8,128)(2,1)S(1)}, u32[]{:S(2)}, u32[]{:S(2)}) collective-permute-start(f16[2,16,32,128]{3,2,1,0:T(8,128)(2,1)S(1)} %multiply_convert_fusion.3), channel_id=1, source_target_pairs={{0,1},{1,0},{2,3},{3,2},{4,5},{5,4},{6,7},{7,6},{8,9},{9,8},{10,11... | collective-permute-start | bytes 786440 | tf_op jit(solution)/shard_map/ppermute | solution.py:20
  14.2 15.8 %collective-permute-start.1 = (f16[16,32,128]{2,1,0:T(8,128)(2,1)S(1)}, f16[16,32,128]{2,1,0:T(8,128)(2,1)S(1)}, u32[]{:S(2)}, u32[]{:S(2)}) collective-permute-start(f16[16,32,128]{2,1,0:T(8,128)(2,1)S(1)} %fusion.7), channel_id=1, source_target_pairs={{0,2},{1,3},{2,0},{3,1},{4,6},{5,7},{6,4},{7,5},{8,10},{9,11},{10,... | collective-permute-start | bytes 393224 | tf_op jit(solution)/shard_map/ppermute | solution.py:20
  28.0 5.7 %collective-permute-start.6 = (bf16[256,2048]{1,0:T(8,128)(2,1)S(1)}, bf16[256,2048]{1,0:T(8,128)(2,1)S(1)}, u32[]{:S(2)}, u32[]{:S(2)}) collective-permute-start(bf16[256,2048]{1,0:T(8,128)(2,1)S(1)} %collective-permute-done.4.refs_5_), channel_id=1, source_target_pairs={{0,4},{4,0},{8,12},{12,8},{16,20},{20,16},{24,28},{28,24},{1,5},{5... | collective-permute-start | bytes 3145736 | tf_op jit(solution)/shard_map/ppermute | solution.py:20
  30.0 2.9 %collective-permute-start.2 = (bf16[128,2048]{1,0:T(8,128)(2,1)S(1)}, bf16[128,2048]{1,0:T(8,128)(2,1)S(1)}, u32[]{:S(2)}, u32[]{:S(2)}) collective-permute-start(bf16[128,2048]{1,0:T(8,128)(2,1)S(1)} %get-tuple-element.68), channel_id=1, source_target_pairs={{0,4},{4,0},{8,12},{12,8},{16,20},{20,16},{24,28},{28,24},{1,5},{5... | collective-permute-start | bytes 1572872 | tf_op jit(solution)/shard_map/ppermute | solution.py:20
  30.1 3.5 %collective-permute-start.3 = (bf16[128,2048]{1,0:T(8,128)(2,1)S(1)}, bf16[128,2048]{1,0:T(8,128)(2,1)S(1)}, u32[]{:S(2)}, u32[]{:S(2)}) collective-permute-start(bf16[128,2048]{1,0:T(8,128)(2,1)S(1)} %get-tuple-element.38), channel_id=1, source_target_pairs={{0,4},{4,0},{8,12},{12,8},{16,20},{20,16},{24,28},{28,24},{1,5},{5... | collective-permute-start | bytes 1572872 | tf_op jit(solution)/shard_map/ppermute | solution.py:20
  30.6 13.5 %collective-permute-start.10 = (bf16[128,2048]{1,0:T(8,128)(2,1)S(1)}, bf16[128,2048]{1,0:T(8,128)(2,1)S(1)}, u32[]{:S(2)}, u32[]{:S(2)}) collective-permute-start(bf16[128,2048]{1,0:T(8,128)(2,1)S(1)} %get-tuple-element.45.refs_1_), channel_id=1, source_target_pairs={{0,16},{4,20},{8,24},{12,28},{16,0},{20,4},{24,8},{28,12},{1,17},{... | collective-permute-start | bytes 1572872 | tf_op jit(solution)/shard_map/ppermute | solution.py:20
  30.9 13.3 %collective-permute-start.11 = (bf16[128,2048]{1,0:T(8,128)(2,1)S(1)}, bf16[128,2048]{1,0:T(8,128)(2,1)S(1)}, u32[]{:S(2)}, u32[]{:S(2)}) collective-permute-start(bf16[128,2048]{1,0:T(8,128)(2,1)S(1)} %get-tuple-element.45.refs_1_), channel_id=1, source_target_pairs={{0,8},{4,12},{8,0},{12,4},{16,24},{20,28},{24,16},{28,20},{1,9},{5... | collective-permute-start | bytes 1572872 | tf_op jit(solution)/shard_map/ppermute | solution.py:20
  36.4 13.7 %collective-permute-start.9 = (bf16[256,2048]{1,0:T(8,128)(2,1)S(1)}, bf16[256,2048]{1,0:T(8,128)(2,1)S(1)}, u32[]{:S(2)}, u32[]{:S(2)}) collective-permute-start(bf16[256,2048]{1,0:T(8,128)(2,1)S(1)} %get-tuple-element.44), channel_id=1, source_target_pairs={{0,4},{4,0},{8,12},{12,8},{16,20},{20,16},{24,28},{28,24},{1,5},{5... | collective-permute-start | bytes 3145736 | tf_op jit(solution)/shard_map/ppermute | solution.py:20
  36.9 10.6 %collective-permute-start.7 = (f16[2,24,32,128]{3,2,1,0:T(8,128)(2,1)S(1)}, f16[2,24,32,128]{3,2,1,0:T(8,128)(2,1)S(1)}, u32[]{:S(2)}, u32[]{:S(2)}) collective-permute-start(f16[2,24,32,128]{3,2,1,0:T(8,128)(2,1)S(1)} %multiply_convert_fusion), channel_id=1, source_target_pairs={{0,1},{1,0},{2,3},{3,2},{4,5},{5,4},{6,7},{7,6},{8,9},{9,8},{10,11... | collective-permute-start | bytes 1179656 | tf_op jit(solution)/shard_map/ppermute | solution.py:20
  44.1 5.9 %collective-permute-start.12 = (bf16[128,2048]{1,0:T(8,128)(2,1)S(1)}, bf16[128,2048]{1,0:T(8,128)(2,1)S(1)}, u32[]{:S(2)}, u32[]{:S(2)}) collective-permute-start(bf16[128,2048]{1,0:T(8,128)(2,1)S(1)} %collective-permute-done.10.refs_4_), channel_id=1, source_target_pairs={{0,4},{4,0},{8,12},{12,8},{16,20},{20,16},{24,28},{28,24},{1,5},{5... | collective-permute-start | bytes 1572872 | tf_op jit(solution)/shard_map/ppermute | solution.py:20
  45.2 13.6 %collective-permute-start.15 = (bf16[128,2048]{1,0:T(8,128)(2,1)S(1)}, bf16[128,2048]{1,0:T(8,128)(2,1)S(1)}, u32[]{:S(2)}, u32[]{:S(2)}) collective-permute-start(bf16[128,2048]{1,0:T(8,128)(2,1)S(1)} %get-tuple-element.53.refs_2_), channel_id=1, source_target_pairs={{0,16},{4,20},{8,24},{12,28},{16,0},{20,4},{24,8},{28,12},{1,17},{... | collective-permute-start | bytes 1572872 | tf_op jit(solution)/shard_map/ppermute | solution.py:20
  46.5 13.2 %collective-permute-start.16 = (bf16[128,2048]{1,0:T(8,128)(2,1)S(1)}, bf16[128,2048]{1,0:T(8,128)(2,1)S(1)}, u32[]{:S(2)}, u32[]{:S(2)}) collective-permute-start(bf16[128,2048]{1,0:T(8,128)(2,1)S(1)} %get-tuple-element.53.refs_2_), channel_id=1, source_target_pairs={{0,8},{4,12},{8,0},{12,4},{16,24},{20,28},{24,16},{28,20},{1,9},{5... | collective-permute-start | bytes 1572872 | tf_op jit(solution)/shard_map/ppermute | solution.py:20
  47.7 13.1 %collective-permute-start.8 = (f16[24,32,128]{2,1,0:T(8,128)(2,1)S(1)}, f16[24,32,128]{2,1,0:T(8,128)(2,1)S(1)}, u32[]{:S(2)}, u32[]{:S(2)}) collective-permute-start(f16[24,32,128]{2,1,0:T(8,128)(2,1)S(1)} %fusion.4), channel_id=1, source_target_pairs={{0,2},{1,3},{2,0},{3,1},{4,6},{5,7},{6,4},{7,5},{8,10},{9,11},{10,... | collective-permute-start | bytes 589832 | tf_op jit(solution)/shard_map/ppermute | solution.py:20
  52.8 11.3 %collective-permute-start.13 = (f16[2,18,32,128]{3,2,1,0:T(8,128)(2,1)S(1)}, f16[2,18,32,128]{3,2,1,0:T(8,128)(2,1)S(1)}, u32[]{:S(2)}, u32[]{:S(2)}) collective-permute-start(f16[2,18,32,128]{3,2,1,0:T(8,128)(2,1)S(1)} %multiply_convert_fusion.2), channel_id=1, source_target_pairs={{0,1},{1,0},{2,3},{3,2},{4,5},{5,4},{6,7},{7,6},{8,9},{9,8},{10,11... | collective-permute-start | bytes 884744 | tf_op jit(solution)/shard_map/ppermute | solution.py:20
  59.7 4.5 %collective-permute-start.17 = (bf16[128,2048]{1,0:T(8,128)(2,1)S(1)}, bf16[128,2048]{1,0:T(8,128)(2,1)S(1)}, u32[]{:S(2)}, u32[]{:S(2)}) collective-permute-start(bf16[128,2048]{1,0:T(8,128)(2,1)S(1)} %collective-permute-done.15.refs_4_), channel_id=1, source_target_pairs={{0,4},{4,0},{8,12},{12,8},{16,20},{20,16},{24,28},{28,24},{1,5},{5... | collective-permute-start | bytes 1572872 | tf_op jit(solution)/shard_map/ppermute | solution.py:20
  67.7 12.5 %collective-permute-start.18 = (f16[2,22,32,128]{3,2,1,0:T(8,128)(2,1)S(1)}, f16[2,22,32,128]{3,2,1,0:T(8,128)(2,1)S(1)}, u32[]{:S(2)}, u32[]{:S(2)}) collective-permute-start(f16[2,22,32,128]{3,2,1,0:T(8,128)(2,1)S(1)} %multiply_convert_fusion.1), channel_id=1, source_target_pairs={{0,1},{1,0},{2,3},{3,2},{4,5},{5,4},{6,7},{7,6},{8,9},{9,8},{10,11... | collective-permute-start | bytes 1081352 | tf_op jit(solution)/shard_map/ppermute | solution.py:20
  67.8 9.8 %collective-permute-start.14 = (f16[18,32,128]{2,1,0:T(8,128)(2,1)S(1)}, f16[18,32,128]{2,1,0:T(8,128)(2,1)S(1)}, u32[]{:S(2)}, u32[]{:S(2)}) collective-permute-start(f16[18,32,128]{2,1,0:T(8,128)(2,1)S(1)} %fusion.6), channel_id=1, source_target_pairs={{0,2},{1,3},{2,0},{3,1},{4,6},{5,7},{6,4},{7,5},{8,10},{9,11},{10,... | collective-permute-start | bytes 442376 | tf_op jit(solution)/shard_map/ppermute | solution.py:20
  80.4 10.3 %collective-permute-start.19 = (f16[22,32,128]{2,1,0:T(8,128)(2,1)S(1)}, f16[22,32,128]{2,1,0:T(8,128)(2,1)S(1)}, u32[]{:S(2)}, u32[]{:S(2)}) collective-permute-start(f16[22,32,128]{2,1,0:T(8,128)(2,1)S(1)} %fusion.5), channel_id=1, source_target_pairs={{0,2},{1,3},{2,0},{3,1},{4,6},{5,7},{6,4},{7,5},{8,10},{9,11},{10,... | collective-permute-start | bytes 540680 | tf_op jit(solution)/shard_map/ppermute | solution.py:20
  81.0 5.9 %collective-permute-start.20 = (f16[9,32,128]{2,1,0:T(8,128)(2,1)S(1)}, f16[9,32,128]{2,1,0:T(8,128)(2,1)S(1)}, u32[]{:S(2)}, u32[]{:S(2)}) collective-permute-start(f16[9,32,128]{2,1,0:T(8,128)(2,1)S(1)} %pad_maximum_fusion), channel_id=1, source_target_pairs={{8,24},{12,28},{24,8},{28,12},{9,25},{13,29},{25,9},{29,13},{10,26... | collective-permute-start | bytes 221192 | tf_op jit(solution)/shard_map/ppermute | solution.py:20
  83.2 7.5 %collective-permute-start.21 = (f16[9,32,128]{2,1,0:T(8,128)(2,1)S(1)}, f16[9,32,128]{2,1,0:T(8,128)(2,1)S(1)}, u32[]{:S(2)}, u32[]{:S(2)}) collective-permute-start(f16[9,32,128]{2,1,0:T(8,128)(2,1)S(1)} %pad_maximum_fusion.1), channel_id=1, source_target_pairs={{0,4},{4,0},{8,28},{12,24},{16,20},{20,16},{24,12},{28,8},{1,5},{5... | collective-permute-start | bytes 221192 | tf_op jit(solution)/shard_map/ppermute | solution.py:336
  90.8 4.9 %collective-permute-start.22 = (f16[7,32,128]{2,1,0:T(8,128)(2,1)S(1)}, f16[7,32,128]{2,1,0:T(8,128)(2,1)S(1)}, u32[]{:S(2)}, u32[]{:S(2)}) collective-permute-start(f16[7,32,128]{2,1,0:T(8,128)(2,1)S(1)} %get-tuple-element.72), channel_id=1, source_target_pairs={{8,24},{12,28},{24,8},{28,12},{9,25},{13,29},{25,9},{29,13},{10,26... | collective-permute-start | bytes 172040 | tf_op jit(solution)/shard_map/ppermute | solution.py:20
  92.8 5.1 %collective-permute-start.23 = (f16[7,32,128]{2,1,0:T(8,128)(2,1)S(1)}, f16[7,32,128]{2,1,0:T(8,128)(2,1)S(1)}, u32[]{:S(2)}, u32[]{:S(2)}) collective-permute-start(f16[7,32,128]{2,1,0:T(8,128)(2,1)S(1)} %get-tuple-element.71), channel_id=1, source_target_pairs={{0,4},{4,0},{8,28},{12,24},{16,20},{20,16},{24,12},{28,8},{1,5},{5... | collective-permute-start | bytes 172040 | tf_op jit(solution)/shard_map/ppermute | solution.py:336
